TPU v7x, 128 devices: a whole 4x4x4 slice. The times are simulated.
128 devices in a mesh: section: 2 (over core), dp: 16 (over y, z), tensor: 4 (over x).
Axes of the slice: x: 4, y: 4, z: 4, core: 2. Of those that a mesh axis runs over, the one named last changes fastest.
Arguments:
- tokens: bfloat16 [2, 4096, 1024], P(None, ('dp', 'tensor')), may hold values from -6 to 6
- segment_ids: int32 [2, 4096], P(None, ('dp', 'tensor')), may hold values from 0 to 2, as said below
- w_qkv: bfloat16 [2, 3, 1024, 1024], P('section', None, 'dp', 'tensor'), may hold values from -0.1875 to 0.1875
- w_out: bfloat16 [2, 1024, 1024], P('section', 'dp', 'tensor'), may hold values from -3 to 3
- w_up: bfloat16 [2, 1024, 4096], P('section', 'dp', 'tensor'), may hold values from -0.1875 to 0.1875
- w_down: bfloat16 [2, 1024, 4096], P('section', 'dp', 'tensor'), may hold values from -0.09375 to 0.09375
- vectors: bfloat16 [2, 13, 1024], P('section', None, 'dp'), may hold values from -1.6 to 1.6
- out_bias: bfloat16 [2, 1024], P('section', 'dp'), may hold values from -1.5 to 1.5
- cotangent: bfloat16 [2, 4096, 1024], P(None, ('dp', 'tensor')), may hold values from -6 to 6
Outputs:
- section_out: bfloat16 [2, 2, 4096, 1024], P('section', None, ('dp', 'tensor'))
- input_grad: float32 [2, 2, 4096, 1024], P('section', None, ('dp', 'tensor'))
- grad_qkv: float32 [2, 3, 1024, 1024], P('section', None, 'dp', 'tensor')
- grad_out: float32 [2, 1024, 1024], P('section', 'dp', 'tensor')
- grad_up: float32 [2, 1024, 4096], P('section', 'dp', 'tensor')
- grad_down: float32 [2, 1024, 4096], P('section', 'dp', 'tensor')
- grad_vectors: float32 [2, 13, 1024], P('section', None, 'dp')
- grad_out_bias: float32 [2, 1024], P('section', 'dp')
Inputs may be any that keep to these rules, and one draw needn't show every extreme that they name: `segment_ids`: each micro-batch packs three images; within every aligned block of 256 tokens of a micro-batch the ids never fall and each of 0, 1 and 2 occurs.
All inputs are finite; a program needn't handle non-finite values.
Results may differ from a plain program's by a relative error of at most 0.02.
Values may be sent and summed in bfloat16 or wider, within the bound.
A program may use at most 192 MiB of HBM per device.

v0:
```python
import jax
import jax.numpy as jnp
from jax import lax
from jax.sharding import PartitionSpec as P

HEAD_DIM = 64


EPSILON = 1e-06
MASKED_SCORE = -1e30


def passed_along(value, axis, by):
    size = lax.axis_size(axis)
    pairs = [(i, i + by) for i in range(size) if 0 <= i + by < size]
    return lax.ppermute(value, axis, pairs)


def layer_norm(values, gain_row, shift_row):
    centre = values - jnp.mean(values, axis=-1, keepdims=True)
    spread = jnp.mean(centre * centre, axis=-1, keepdims=True)
    return centre * lax.rsqrt(spread + EPSILON) * gain_row + shift_row


def gelu_exact(values):
    return jax.nn.gelu(values, approximate=False)


def gather_weights(w_qkv, w_out, w_up, w_down, vectors, out_bias):
    gathered = (
        lax.all_gather(w_qkv[0], "dp", axis=1, tiled=True),
        lax.all_gather(w_out[0], "dp", axis=0, tiled=True),
        lax.all_gather(w_up[0], "dp", axis=0, tiled=True),
        lax.all_gather(w_down[0], "dp", axis=0, tiled=True),
        lax.all_gather(vectors[0], "dp", axis=1, tiled=True),
        lax.all_gather(out_bias[0], "dp", axis=0, tiled=True),
    )
    return (
        gathered[0],
        gathered[1],
        gathered[2],
        gathered[3],
        gathered[4].astype(jnp.float32),
        gathered[5].astype(jnp.float32),
    )


def reduce_weights(grad_tuple):
    return (
        lax.psum_scatter(
            grad_tuple[0].astype(jnp.bfloat16), "dp", scatter_dimension=1, tiled=True
        ).astype(jnp.float32),
        lax.psum_scatter(
            grad_tuple[1].astype(jnp.bfloat16), "dp", scatter_dimension=0, tiled=True
        ).astype(jnp.float32),
        lax.psum_scatter(
            grad_tuple[2].astype(jnp.bfloat16), "dp", scatter_dimension=0, tiled=True
        ).astype(jnp.float32),
        lax.psum_scatter(
            grad_tuple[3].astype(jnp.bfloat16), "dp", scatter_dimension=0, tiled=True
        ).astype(jnp.float32),
        lax.psum_scatter(
            grad_tuple[4].astype(jnp.bfloat16), "dp", scatter_dimension=1, tiled=True
        ).astype(jnp.float32),
        lax.psum_scatter(
            grad_tuple[5].astype(jnp.bfloat16), "dp", scatter_dimension=0, tiled=True
        ).astype(jnp.float32),
    )


def spread_rows(normed):
    return lax.all_gather(normed, "tensor", axis=0, tiled=True)


def spread_grads(branch_grad):
    return lax.all_gather(branch_grad, "tensor", axis=0, tiled=True)


def collect_rows(source, weight):
    return lax.psum_scatter(
        lax.dot_general(
            source, weight, (((1,), (1,)), ((), ())), preferred_element_type=jnp.float32
        ).astype(jnp.bfloat16),
        "tensor",
        scatter_dimension=0,
        tiled=True,
    ).astype(jnp.float32)


def return_rows(term_function, tok_rows):
    return lax.psum_scatter(
        term_function(jnp.int32(0), tok_rows * lax.axis_size("tensor")).astype(jnp.bfloat16),
        "tensor",
        scatter_dimension=0,
        tiled=True,
    ).astype(jnp.float32)


def attention_weights(queries, keys_full, seg_rows, seg_keys):
    heads_here = queries.shape[1] // HEAD_DIM
    query_heads = queries.reshape(queries.shape[0], heads_here, HEAD_DIM)
    key_heads = keys_full.reshape(keys_full.shape[0], heads_here, HEAD_DIM)
    raw_scores = jnp.einsum(
        "rhd,shd->hrs", query_heads, key_heads, preferred_element_type=jnp.float32
    ) * HEAD_DIM ** (-0.5)
    allowed = seg_rows[:, None] == seg_keys[None, :]
    masked = jnp.where(allowed[None], raw_scores, MASKED_SCORE)
    highest = jnp.max(masked, axis=-1, keepdims=True)
    exponent = jnp.exp(masked - highest)
    total = jnp.sum(exponent, axis=-1, keepdims=True)
    return (exponent / total, highest + jnp.log(total))


def forward_step(inputs, seg_rows, seg_keys, weights, tensor_rank):
    w_qkv, w_out, w_up, w_down, vectors, out_bias = weights
    local_width = w_qkv.shape[2]
    local_hidden = w_up.shape[1]
    heads_here = local_width // HEAD_DIM
    query_bias = lax.dynamic_slice_in_dim(vectors[2], tensor_rank * local_width, local_width)
    value_bias = lax.dynamic_slice_in_dim(vectors[3], tensor_rank * local_width, local_width)
    up_bias = lax.dynamic_slice_in_dim(
        vectors[9:].reshape(-1), tensor_rank * local_hidden, local_hidden
    )
    normed_rows = spread_rows(layer_norm(inputs, vectors[0], vectors[1]).astype(jnp.bfloat16))
    projected = jnp.einsum("rd,kdc->krc", normed_rows, w_qkv, preferred_element_type=jnp.float32)
    queries = (projected[0] + query_bias).astype(jnp.bfloat16)
    keys_local = projected[1].astype(jnp.bfloat16)
    values_local = (projected[2] + value_bias).astype(jnp.bfloat16)
    keys_full, values_full = (
        lax.all_gather(keys_local, "dp", axis=0, tiled=True),
        lax.all_gather(values_local, "dp", axis=0, tiled=True),
    )
    soft_weights = attention_weights(queries, keys_full, seg_rows, seg_keys)[0]
    mixed_heads = jnp.einsum(
        "hrs,shd->rhd",
        soft_weights.astype(jnp.bfloat16),
        values_full.reshape(-1, heads_here, HEAD_DIM),
        preferred_element_type=jnp.float32,
    )
    mixed_heads = mixed_heads.reshape(-1, local_width).astype(jnp.bfloat16)
    attn_out = collect_rows(mixed_heads, w_out) + out_bias
    hidden = inputs + vectors[4] * attn_out
    normed_two = spread_rows(layer_norm(hidden, vectors[5], vectors[6]).astype(jnp.bfloat16))
    pre_act = jnp.dot(normed_two, w_up, preferred_element_type=jnp.float32) + up_bias
    activated = gelu_exact(pre_act).astype(jnp.bfloat16)
    mlp_out = collect_rows(activated, w_down) + vectors[7]
    outputs = hidden + vectors[8] * mlp_out
    kept_step = (
        inputs,
        normed_rows,
        queries,
        keys_full,
        values_full,
        mixed_heads,
        attn_out,
        hidden,
        normed_two,
        pre_act,
        activated,
        mlp_out,
    )
    return (outputs, kept_step)


def backward_step(upstream, kept_step, seg_rows, seg_keys, weights, tensor_rank, tensor_count):
    w_qkv, w_out, w_up, w_down, vectors, out_bias = weights
    (
        inputs,
        normed_rows,
        queries,
        keys_full,
        values_full,
        mixed_heads,
        attn_out,
        hidden,
        normed_two,
        pre_act,
        activated,
        mlp_out,
    ) = kept_step
    tok_rows = inputs.shape[0]
    model_width = inputs.shape[1]
    local_width = w_qkv.shape[2]
    local_hidden = w_up.shape[1]
    heads_here = local_width // HEAD_DIM
    contract_rows = (((0,), (0,)), ((), ()))
    head_scale = HEAD_DIM ** (-0.5)
    mlp_grad = vectors[8] * upstream
    grad_scale_two = jnp.sum(upstream * mlp_out, axis=0)
    grad_down_bias = jnp.sum(mlp_grad, axis=0)
    mlp_rows = spread_grads(mlp_grad.astype(jnp.bfloat16))
    act_grad = jnp.dot(mlp_rows, w_down, preferred_element_type=jnp.float32)
    grad_down = lax.dot_general(
        mlp_rows, activated, contract_rows, preferred_element_type=jnp.float32
    )
    pre_grad = jax.vjp(gelu_exact, pre_act)[1](act_grad)[0]
    grad_up_bias = jnp.sum(pre_grad, axis=0)
    pre_low = pre_grad.astype(jnp.bfloat16)
    grad_up = lax.dot_general(
        normed_two, pre_low, contract_rows, preferred_element_type=jnp.float32
    )

    def up_term(offset, number):
        return lax.dot_general(
            pre_low, w_up, (((1,), (1,)), ((), ())), preferred_element_type=jnp.float32
        )

    normed_grad = return_rows(up_term, tok_rows)
    pull_two = jax.vjp(layer_norm, hidden, vectors[5], vectors[6])[1]
    hidden_part, grad_gain_two, grad_shift_two = pull_two(normed_grad)
    hidden_grad = upstream + hidden_part
    attn_grad = vectors[4] * hidden_grad
    grad_scale_one = jnp.sum(hidden_grad * attn_out, axis=0)
    grad_out_bias = jnp.sum(attn_grad, axis=0)
    attn_rows = spread_grads(attn_grad.astype(jnp.bfloat16))
    mixed_grad = jnp.dot(attn_rows, w_out, preferred_element_type=jnp.float32).astype(jnp.bfloat16)
    grad_out = lax.dot_general(
        attn_rows, mixed_heads, contract_rows, preferred_element_type=jnp.float32
    )
    soft_weights, log_total = attention_weights(queries, keys_full, seg_rows, seg_keys)
    mixed_split = mixed_grad.reshape(-1, heads_here, HEAD_DIM)
    value_heads = values_full.reshape(-1, heads_here, HEAD_DIM)
    key_heads = keys_full.reshape(-1, heads_here, HEAD_DIM)
    query_heads = queries.reshape(-1, heads_here, HEAD_DIM)
    prob_grad = jnp.einsum(
        "rhd,shd->hrs", mixed_split, value_heads, preferred_element_type=jnp.float32
    )
    row_delta = jnp.sum(prob_grad * soft_weights, axis=-1)
    score_grad = soft_weights * (prob_grad - row_delta[..., None])
    score_low = (score_grad * head_scale).astype(jnp.bfloat16)
    query_grad = jnp.einsum(
        "hrs,shd->rhd", score_low, key_heads, preferred_element_type=jnp.float32
    ).reshape(-1, local_width)
    values_grad_full = jnp.einsum(
        "hrs,rhd->shd",
        soft_weights.astype(jnp.bfloat16),
        mixed_split,
        preferred_element_type=jnp.float32,
    ).reshape(-1, local_width)
    keys_grad_full = jnp.einsum(
        "hrs,rhd->shd", score_low, query_heads, preferred_element_type=jnp.float32
    ).reshape(-1, local_width)
    keys_grad, values_grad = (
        lax.psum_scatter(
            keys_grad_full.astype(jnp.bfloat16), "dp", scatter_dimension=0, tiled=True
        ).astype(jnp.float32),
        lax.psum_scatter(
            values_grad_full.astype(jnp.bfloat16), "dp", scatter_dimension=0, tiled=True
        ).astype(jnp.float32),
    )
    grad_query_bias = jnp.sum(query_grad, axis=0)
    grad_value_bias = jnp.sum(values_grad, axis=0)
    triple_low = jnp.stack([query_grad, keys_grad, values_grad]).astype(jnp.bfloat16)
    grad_qkv = jnp.einsum(
        "rd,krc->kdc", normed_rows, triple_low, preferred_element_type=jnp.float32
    )

    def qkv_term(offset, number):
        return jnp.einsum("krc,kdc->rd", triple_low, w_qkv, preferred_element_type=jnp.float32)

    normed_grad_one = return_rows(qkv_term, tok_rows)
    pull_one = jax.vjp(layer_norm, inputs, vectors[0], vectors[1])[1]
    input_part, grad_gain_one, grad_shift_one = pull_one(normed_grad_one)
    input_grad = hidden_grad + input_part

    def placed(shard_values, full_length):
        empty = jnp.zeros((full_length,), jnp.float32)
        return lax.dynamic_update_slice(empty, shard_values, (tensor_rank * shard_values.shape[0],))

    vector_grads = jnp.concatenate(
        [
            jnp.stack(
                [
                    grad_gain_one,
                    grad_shift_one,
                    placed(grad_query_bias, model_width),
                    placed(grad_value_bias, model_width),
                    grad_scale_one,
                    grad_gain_two,
                    grad_shift_two,
                    grad_down_bias,
                    grad_scale_two,
                ]
            ),
            placed(grad_up_bias, local_hidden * tensor_count).reshape(-1, model_width),
        ],
        axis=0,
    )
    return (input_grad, (grad_qkv, grad_out, grad_up, grad_down, vector_grads, grad_out_bias))


def add_tuples(former, latter):
    if former is None:
        return latter
    return tuple((first_term + second_term for first_term, second_term in zip(former, latter)))


def shards(tokens, segment_ids, w_qkv, w_out, w_up, w_down, vectors, out_bias, cotangent):
    section_first = lax.axis_index("section") == 0
    tensor_rank = lax.axis_index("tensor")
    tensor_count = lax.axis_size("tensor")
    dp_rank = lax.axis_index("dp")
    micro_count = tokens.shape[0]
    tok_rows = tokens.shape[1]
    model_width = tokens.shape[2]
    group_rows = tok_rows * tensor_count
    segments = lax.all_gather(segment_ids, ("dp", "tensor"), axis=1, tiled=True)
    segment_rows = lax.dynamic_slice_in_dim(segments, dp_rank * group_rows, group_rows, 1)
    weights = gather_weights(w_qkv, w_out, w_up, w_down, vectors, out_bias)
    received = jnp.zeros((tok_rows, model_width), jnp.bfloat16)
    outputs_list = []
    kept_list = []
    for period in range(micro_count + 1):
        ahead_index = min(period, micro_count - 1)
        behind_index = max(period - 1, 0)
        section_input = jnp.where(
            section_first, tokens[ahead_index].astype(jnp.float32), received.astype(jnp.float32)
        )
        seg_here = jnp.where(section_first, segment_rows[ahead_index], segment_rows[behind_index])
        seg_keys = jnp.where(section_first, segments[ahead_index], segments[behind_index])
        produced, kept_step = forward_step(section_input, seg_here, seg_keys, weights, tensor_rank)
        outputs_list.append(produced)
        kept_list.append(kept_step)
        if period < micro_count:
            received = passed_along(produced.astype(jnp.bfloat16), "section", 1)
    section_out = jnp.stack(
        [
            jnp.where(section_first, outputs_list[micro_index], outputs_list[micro_index + 1])
            for micro_index in range(micro_count)
        ]
    ).astype(jnp.bfloat16)[None]
    weights = gather_weights(w_qkv, w_out, w_up, w_down, vectors, out_bias)
    grad_sums = None
    shard_sums = None
    received_grad = jnp.zeros((tok_rows, model_width), jnp.bfloat16)
    grads_list = []
    for period in range(micro_count + 1):
        late_index = min(period, micro_count - 1)
        early_index = max(period - 1, 0)
        kept_step = jax.tree.map(
            lambda early_value, late_value: jnp.where(section_first, early_value, late_value),
            kept_list[early_index],
            kept_list[late_index + 1],
        )
        seg_here = jnp.where(section_first, segment_rows[early_index], segment_rows[late_index])
        seg_keys = jnp.where(section_first, segments[early_index], segments[late_index])
        upstream = jnp.where(
            section_first,
            received_grad.astype(jnp.float32),
            cotangent[late_index].astype(jnp.float32),
        )
        valid_flag = jnp.where(section_first, period >= 1, period < micro_count).astype(jnp.float32)
        section_grad, param_grads = backward_step(
            upstream, kept_step, seg_here, seg_keys, weights, tensor_rank, tensor_count
        )
        grads_list.append(section_grad)
        param_grads = tuple((valid_flag * piece_grad for piece_grad in param_grads))
        grad_sums = add_tuples(grad_sums, param_grads)
        if period < micro_count:
            received_grad = passed_along(section_grad.astype(jnp.bfloat16), "section", -1)
    shard_sums = reduce_weights(grad_sums)
    vector_shard, bias_shard = lax.psum((shard_sums[4], shard_sums[5]), "tensor")
    input_grad = jnp.stack(
        [
            jnp.where(section_first, grads_list[micro_index + 1], grads_list[micro_index])
            for micro_index in range(micro_count)
        ]
    )[None]
    return (
        section_out,
        input_grad,
        shard_sums[0][None],
        shard_sums[1][None],
        shard_sums[2][None],
        shard_sums[3][None],
        vector_shard[None],
        bias_shard[None],
    )


def solution(mesh):
    in_specs = (
        P(None, ("dp", "tensor"), None),
        P(None, ("dp", "tensor")),
        P("section", None, "dp", "tensor"),
        P("section", "dp", "tensor"),
        P("section", "dp", "tensor"),
        P("section", "dp", "tensor"),
        P("section", None, "dp"),
        P("section", "dp"),
        P(None, ("dp", "tensor"), None),
    )
    out_specs = (
        P("section", None, ("dp", "tensor"), None),
        P("section", None, ("dp", "tensor"), None),
        P("section", None, "dp", "tensor"),
        P("section", "dp", "tensor"),
        P("section", "dp", "tensor"),
        P("section", "dp", "tensor"),
        P("section", None, "dp"),
        P("section", "dp"),
    )
    return jax.shard_map(shards, mesh=mesh, in_specs=in_specs, out_specs=out_specs, check_vma=False)
```

profile of v0, /device:TPU:1, one launch (start us, length us, event | category | flops | bytes accessed | tf_op | source)
XLA Modules:
  0.0 2023.4 jit_solution(8004961826600050525)
XLA Ops:
  8.8 21.5 %all-gather = bf16[1,13,1024]{1,0,2:T(2,128)(2,1)S(1)} all-gather(bf16[1,13,64]{1,0,2:T(2,128)(2,1)S(1)} %copy.73), channel_id=2, replica_groups=mesh['section'=2,'dp'=16,'tensor'=4] {'dp'}, dimensions={2}, use_global_device_ids=true | all-gather | bytes 28288 | tf_op jit(solution)/shard_map/all_gather | solution.py:35
  32.9 22.2 %slice_reduce_fusion.3 = (f32[1024]{0:T(1024)S(1)}, f32[1024]{0:T(1024)S(1)}, f32[1024]{0:T(1024)S(1)}, f32[1024]{0:T(1024)S(1)}, f32[1024]{0:T(1024)S(1)}, /*index=5*/f32[1024]{0:T(1024)S(1)}, f32[1024]{0:T(1024)S(1)}) fusion(f32[1,13,1024]{1,0,2:T(1,128)S(1)} %convert_element_type.518), kind=kLoop, calls=%fused_computation.292 | loop fusion | bytes 57344 | tf_op jit(solution)/shard_map/slice | solution.py:147
  72.7 146.0 %all-gather.9 = s32[64,64,2]{1,2,0:T(2,128)S(1)} all-gather(s32[1,64,2]{1,2,0:T(2,128)S(1)} %bitcast.533), channel_id=1, replica_groups=mesh['section'=2,'dp'=16,'tensor'=4] {'dp','tensor'}, dimensions={0}, use_global_device_ids=true | all-gather | bytes 33280 | tf_op jit(solution)/shard_map/all_gather | solution.py:307
  219.9 16.0 all-gather.3
  238.3 11.1 fusion.420
  263.6 30.9 %all-reduce = bf16[1024]{0:T(1024)(128)(2,1)S(1)} all-reduce(bf16[1024]{0:T(1024)(128)(2,1)S(1)} %dynamic-update-slice), channel_id=6, replica_groups=mesh['section'=2,'dp'=16,'tensor'=4] {'dp'}, use_global_device_ids=true, to_apply=%add | all-reduce | flops 1024 | bytes 4096
  294.8 23.5 %reduce-scatter.25.cloned.1.call-done = bf16[64,1024]{1,0:T(8,128)(2,1)} async-done(((bf16[256,1024]{1,0:T(8,128)(2,1)}), bf16[64,1024]{1,0:T(8,128)(2,1)}) %reduce-scatter.25.cloned.1.call-update) | async-done | bytes 131088 | tf_op jit(solution)/shard_map/reduce_scatter | solution.py:80
  331.7 34.1 %all-gather.30.cloned.1.call-done = bf16[1,1024,1024]{2,1,0:T(8,128)(2,1)} async-done(((bf16[1,64,1024]{2,1,0:T(8,128)(2,1)}), bf16[1,1024,1024]{2,1,0:T(8,128)(2,1)}) %all-gather.30.cloned.1.call-update) | async-done | bytes 2097168 | tf_op jit(solution)/shard_map/all_gather | solution.py:33
  371.3 41.1 %all-gather.32.cloned.1.call-done = bf16[1,1024,1024]{2,1,0:T(8,128)(2,1)} async-done(((bf16[1,64,1024]{2,1,0:T(8,128)(2,1)}), bf16[1,1024,1024]{2,1,0:T(8,128)(2,1)}) %all-gather.32.cloned.1.call-update) | async-done | bytes 2097168 | tf_op jit(solution)/shard_map/all_gather | solution.py:34
  415.6 20.1 reduce-scatter.27.cloned.1.call-done
  461.6 43.1 %all-gather.34.cloned.1.call-done = bf16[1,4096,256]{1,2,0:T(8,128)(2,1)} async-done(((bf16[1,256,256]{1,2,0:T(8,128)(2,1)}), bf16[1,4096,256]{1,2,0:T(8,128)(2,1)}) %all-gather.34.cloned.1.call-update) | async-done | bytes 2097168 | tf_op jit(solution)/shard_map/all_gather | solution.py:130
  504.7 10.8 fusion.421
  515.5 39.0 %all-gather.22.cloned.1.call-done = bf16[4096,256]{0,1:T(8,128)(2,1)} async-done(((bf16[256,256]{0,1:T(8,128)(2,1)}), bf16[4096,256]{0,1:T(8,128)(2,1)}) %all-gather.22.cloned.1.call-update) | async-done | bytes 2097168 | tf_op jit(solution)/shard_map/all_gather | solution.py:131
  564.8 19.9 reduce-scatter.29.cloned.1.call-done
  586.9 11.5 all_gather.94
  606.4 23.0 %reduce-scatter.31.cloned.1.call-done = bf16[64,1024]{1,0:T(8,128)(2,1)} async-done(((bf16[256,1024]{1,0:T(8,128)(2,1)}), bf16[64,1024]{1,0:T(8,128)(2,1)}) %reduce-scatter.31.cloned.1.call-update) | async-done | bytes 131088 | tf_op jit(solution)/shard_map/reduce_scatter | solution.py:80
  632.3 11.1 all_gather.99
  678.3 47.2 %all-gather.36.cloned.1.call-done = bf16[1,4096,256]{1,2,0:T(8,128)(2,1)} async-done(((bf16[1,256,256]{1,2,0:T(8,128)(2,1)}), bf16[1,4096,256]{1,2,0:T(8,128)(2,1)}) %all-gather.36.cloned.1.call-update) | async-done | bytes 2097168 | tf_op jit(solution)/shard_map/all_gather | solution.py:130
  725.6 10.8 fusion.422
  736.4 38.8 %all-gather.24.cloned.1.call-done = bf16[4096,256]{0,1:T(8,128)(2,1)} async-done(((bf16[256,256]{0,1:T(8,128)(2,1)}), bf16[4096,256]{0,1:T(8,128)(2,1)}) %all-gather.24.cloned.1.call-update) | async-done | bytes 2097168 | tf_op jit(solution)/shard_map/all_gather | solution.py:131
  791.3 11.4 fusion.423
  814.5 11.0 all_gather.100
  834.8 23.4 %fusion.75 = bf16[4,64,4096]{2,1,0:T(8,128)(2,1)} fusion(bf16[256,4,64]{0,2,1:T(8,128)(2,1)S(1)} %copy-done.87, f32[4,256,4096]{2,1,0:T(8,128)} %fusion.435, f32[4,256,4096]{2,1,0:T(8,128)} %get-tuple-element.178, f32[4,256]{1,0:T(4,128)S(1)} %copy-done.141), kind=kOutput, calls=%fused_computation.77 | convolution fusion | flops 567284736 | bytes 35786752 | tf_op jit(solution)/shard_map/hrs,rhd->shd/dot_general | solution.py:240
  875.3 23.6 %fusion.415 = (f32[4,64]{1,0:T(4,128)}, bf16[256,4,64]{0,2,1:T(8,128)(2,1)S(1)}) fusion(bf16[4096,4,64]{0,2,1:T(8,128)(2,1)} %bitcast.455, f32[4,256,4096]{2,1,0:T(8,128)} %fusion.435, f32[4,256,4096]{2,1,0:T(8,128)} %get-tuple-element.178, f32[4,256]{1,0:T(4,128)S(1)} %copy-done.141), kind=kOutput, calls=%fused_computation.606 | convolution fusion | flops 566366976 | bytes 35787776 | tf_op jit(solution)/shard_map/hrs,shd->rhd/dot_general | solution.py:231
  899.1 38.4 %reduce-scatter.39.cloned.1.call-done = bf16[256,256]{1,0:T(8,128)(2,1)} async-done(((bf16[4096,256]{1,0:T(8,128)(2,1)}), bf16[256,256]{1,0:T(8,128)(2,1)}) %reduce-scatter.39.cloned.1.call-update) | async-done | bytes 131088 | tf_op jit(solution)/shard_map/reduce_scatter | solution.py:244
  937.5 77.2 %reduce-scatter.41.cloned.1.call-done = bf16[256,256]{1,0:T(8,128)(2,1)} async-done(((bf16[4096,256]{1,0:T(8,128)(2,1)}), bf16[256,256]{1,0:T(8,128)(2,1)}) %reduce-scatter.41.cloned.1.call-update) | async-done | bytes 131088 | tf_op jit(solution)/shard_map/reduce_scatter | solution.py:247
  1051.7 12.0 all_gather.101
  1070.0 10.9 fusion.426
  1094.8 11.0 all_gather.102
  1115.1 23.4 %fusion.72 = bf16[4,64,4096]{2,1,0:T(8,128)(2,1)} fusion(bf16[256,4,64]{0,2,1:T(8,128)(2,1)S(1)} %copy-done.84, f32[4,256,4096]{2,1,0:T(8,128)} %fusion.436, f32[4,256,4096]{2,1,0:T(8,128)} %get-tuple-element.181, f32[4,256]{1,0:T(4,128)S(1)} %get-tuple-element.180), kind=kOutput, calls=%fused_computation.76 | convolution fusion | flops 567284736 | bytes 35786752 | tf_op jit(solution)/shard_map/hrs,rhd->shd/dot_general | solution.py:240
  1155.7 23.6 %fusion.416 = (f32[4,64]{1,0:T(4,128)}, bf16[256,4,64]{0,2,1:T(8,128)(2,1)S(1)}) fusion(bf16[4096,4,64]{0,2,1:T(8,128)(2,1)} %bitcast.451, f32[4,256,4096]{2,1,0:T(8,128)} %fusion.436, f32[4,256,4096]{2,1,0:T(8,128)} %get-tuple-element.181, f32[4,256]{1,0:T(4,128)S(1)} %get-tuple-element.180), kind=kOutput, calls=%fused_computation.607 | convolution fusion | flops 566366976 | bytes 35787776 | tf_op jit(solution)/shard_map/hrs,shd->rhd/dot_general | solution.py:231
  1179.5 39.3 %reduce-scatter.47.cloned.1.call-done = bf16[256,256]{1,0:T(8,128)(2,1)} async-done(((bf16[4096,256]{1,0:T(8,128)(2,1)}), bf16[256,256]{1,0:T(8,128)(2,1)}) %reduce-scatter.47.cloned.1.call-update) | async-done | bytes 131088 | tf_op jit(solution)/shard_map/reduce_scatter | solution.py:244
  1218.8 77.3 %reduce-scatter.49.cloned.1.call-done = bf16[256,256]{1,0:T(8,128)(2,1)} async-done(((bf16[4096,256]{1,0:T(8,128)(2,1)}), bf16[256,256]{1,0:T(8,128)(2,1)}) %reduce-scatter.49.cloned.1.call-update) | async-done | bytes 131088 | tf_op jit(solution)/shard_map/reduce_scatter | solution.py:247
  1303.2 15.9 reduce-scatter.51.cloned.1.call-done
  1329.3 13.4 reduce-scatter.35.cloned.1.call-done
  1345.3 11.0 all_gather.103
  1364.6 11.5 fusion.429
  1376.1 11.3 reduce-scatter.53.cloned.1.call-done
  1393.0 11.3 all_gather.104
  1412.8 23.4 %fusion.69 = bf16[4,64,4096]{2,1,0:T(8,128)(2,1)} fusion(bf16[256,4,64]{0,2,1:T(8,128)(2,1)S(1)} %copy-done.85, f32[4,256,4096]{2,1,0:T(8,128)} %fusion.437, f32[4,256,4096]{2,1,0:T(8,128)} %get-tuple-element.186, f32[4,256]{1,0:T(4,128)S(1)} %copy-done.140), kind=kOutput, calls=%fused_computation.75 | convolution fusion | flops 567284736 | bytes 35786752 | tf_op jit(solution)/shard_map/hrs,rhd->shd/dot_general | solution.py:240
  1453.2 23.6 %fusion.417 = (f32[4,64]{1,0:T(4,128)}, bf16[256,4,64]{0,2,1:T(8,128)(2,1)S(1)}) fusion(bf16[4096,4,64]{0,2,1:T(8,128)(2,1)} %bitcast.447, f32[4,256,4096]{2,1,0:T(8,128)} %fusion.437, f32[4,256,4096]{2,1,0:T(8,128)} %get-tuple-element.186, f32[4,256]{1,0:T(4,128)S(1)} %copy-done.140), kind=kOutput, calls=%fused_computation.608 | convolution fusion | flops 566366976 | bytes 35787776 | tf_op jit(solution)/shard_map/hrs,shd->rhd/dot_general | solution.py:231
  1477.0 39.5 %reduce-scatter.55.cloned.1.call-done = bf16[256,256]{1,0:T(8,128)(2,1)} async-done(((bf16[4096,256]{1,0:T(8,128)(2,1)}), bf16[256,256]{1,0:T(8,128)(2,1)}) %reduce-scatter.55.cloned.1.call-update) | async-done | bytes 131088 | tf_op jit(solution)/shard_map/reduce_scatter | solution.py:244
  1516.5 77.1 %reduce-scatter.57.cloned.1.call-done = bf16[256,256]{1,0:T(8,128)(2,1)} async-done(((bf16[4096,256]{1,0:T(8,128)(2,1)}), bf16[256,256]{1,0:T(8,128)(2,1)}) %reduce-scatter.57.cloned.1.call-update) | async-done | bytes 131088 | tf_op jit(solution)/shard_map/reduce_scatter | solution.py:247
  1640.0 31.6 %all-reduce.2 = bf16[1024]{0:T(1024)(128)(2,1)} all-reduce(bf16[1024]{0:T(1024)(128)(2,1)} %add_convert_fusion.13), channel_id=34, replica_groups=mesh['section'=2,'dp'=16,'tensor'=4] {'dp'}, use_global_device_ids=true, to_apply=%region_108.109.clone | all-reduce | flops 1024 | bytes 4096
  1693.6 76.1 %reduce-scatter.65.cloned.1.call-done = bf16[64,1024]{1,0:T(8,128)(2,1)} async-done(((bf16[1024,1024]{1,0:T(8,128)(2,1)}), bf16[64,1024]{1,0:T(8,128)(2,1)}) %reduce-scatter.65.cloned.1.call-update) | async-done | bytes 131088 | tf_op jit(solution)/shard_map/reduce_scatter | solution.py:59
  1771.3 75.2 %reduce-scatter.63.cloned.1.call-done = bf16[64,1024]{1,0:T(8,128)(2,1)} async-done(((bf16[1024,1024]{1,0:T(8,128)(2,1)}), bf16[64,1024]{1,0:T(8,128)(2,1)}) %reduce-scatter.63.cloned.1.call-update) | async-done | bytes 131088 | tf_op jit(solution)/shard_map/reduce_scatter | solution.py:56
  1849.1 72.0 %reduce-scatter.67.cloned.1.call-done = bf16[64,13]{1,0:T(8,128)(2,1)} async-done(((bf16[1024,13]{1,0:T(8,128)(2,1)}), bf16[64,13]{1,0:T(8,128)(2,1)}) %reduce-scatter.67.cloned.1.call-update) | async-done | bytes 1680
  1931.7 83.0 %all-reduce.6.cloned.1.call-done = bf16[3,1024,256]{2,0,1:T(4,128)(2,1)} async-done(((bf16[3,1024,256]{2,0,1:T(4,128)(2,1)}), bf16[3,1024,256]{2,0,1:T(4,128)(2,1)}) %all-reduce.6.cloned.1.call-update) | async-done | bytes 1572880
  (583 shorter events, 425.7 us)
Async XLA Ops:
  7.2 58.3 %all-gather.26.cloned.1.call-start = ((), (), s32[]{:S(2)}) async-start(), calls=%async_computation.46 | async-start | bytes 1671168 | tf_op jit(solution)/shard_map/all_gather | solution.py:31
  7.9 230.4 %all-gather.28.cloned.1.call-start = ((), (), s32[]{:S(2)}) async-start(), calls=%async_computation.47 | async-start | bytes 2228224 | tf_op jit(solution)/shard_map/all_gather | solution.py:130
  55.1 265.4 %copy-start.91 = (f32[1024]{0:T(1024)}, f32[1024]{0:T(1024)S(1)}, u32[]{:S(2)}) copy-start(f32[1024]{0:T(1024)S(1)} %get-tuple-element.41) | copy-start | bytes 12292
  55.1 380.6 %copy-start.82 = (f32[1024]{0:T(1024)}, f32[1024]{0:T(1024)S(1)}, u32[]{:S(2)}) copy-start(f32[1024]{0:T(1024)S(1)} %get-tuple-element.40) | copy-start | bytes 12292
  55.1 380.6 %copy-start.88 = (f32[1024]{0:T(1024)}, f32[1024]{0:T(1024)S(1)}, u32[]{:S(2)}) copy-start(f32[1024]{0:T(1024)S(1)} %get-tuple-element.46) | copy-start | bytes 12292
  55.2 386.4 %copy-start.93 = (f32[1024]{0:T(1024)}, f32[1024]{0:T(1024)S(1)}, u32[]{:S(2)}) copy-start(f32[1024]{0:T(1024)S(1)} %get-tuple-element.43) | copy-start | bytes 12292
  55.2 164.7 %copy-start.98 = (bf16[1,64,256]{2,1,0:T(8,128)(2,1)S(1)}, bf16[1,64,256]{2,1,0:T(8,128)(2,1)}, u32[]{:S(2)}) copy-start(bf16[1,64,256]{2,1,0:T(8,128)(2,1)} %param.12) | copy-start | bytes 98308
  68.5 180.8 %all-gather.20.cloned.1.call-start = ((), (), s32[]{:S(2)}) async-start(), calls=%async_computation.22 | async-start | bytes 2228224 | tf_op jit(solution)/shard_map/all_gather | solution.py:131
  71.9 383.3 %copy-start.99 = (f32[256]{0:T(256)}, f32[256]{0:T(256)S(1)}, u32[]{:S(2)}) copy-start(f32[256]{0:T(256)S(1)} %dynamic-slice_reduce_fusion.1) | copy-start | bytes 3076
  72.6 245.7 %reduce-scatter.25.cloned.1.call-start = ((), (), s32[]{:S(2)}) async-start(), calls=%async_computation.23 | async-start | bytes 655360 | tf_op jit(solution)/shard_map/reduce_scatter | solution.py:80
  235.9 221.0 %copy-start.106 = (s32[1,256]{1,0:T(1,128)}, s32[1,256]{1,0:T(1,128)S(1)}, u32[]{:S(2)}) copy-start(s32[1,256]{1,0:T(1,128)S(1)} %get-tuple-element.153) | copy-start | bytes 3076
  238.3 221.8 %copy-start.40 = (f32[1,256,256]{1,2,0:T(8,128)}, f32[1,256,256]{1,2,0:T(8,128)S(1)}, u32[]{:S(2)}) copy-start(f32[1,256,256]{1,2,0:T(8,128)S(1)} %slice.188) | copy-start | bytes 786436
  259.7 106.1 %all-gather.30.cloned.1.call-start = ((), (), s32[]{:S(2)}) async-start(), calls=%async_computation.48 | async-start | bytes 2228224 | tf_op jit(solution)/shard_map/all_gather | solution.py:33
  260.3 152.1 %all-gather.32.cloned.1.call-start = ((), (), s32[]{:S(2)}) async-start(), calls=%async_computation.49 | async-start | bytes 2228224 | tf_op jit(solution)/shard_map/all_gather | solution.py:34
  260.9 174.8 %reduce-scatter.27.cloned.1.call-start = ((), (), s32[]{:S(2)}) async-start(), calls=%async_computation.24 | async-start | bytes 655360 | tf_op jit(solution)/shard_map/reduce_scatter | solution.py:80
  294.5 517.2 %copy-start.80 = (f32[1024]{0:T(1024)}, f32[1024]{0:T(1024)S(1)}, u32[]{:S(2)}) copy-start(f32[1024]{0:T(1024)S(1)} %convert_element_type.520) | copy-start | bytes 12292
  415.6 89.1 %all-gather.34.cloned.1.call-start = ((), (), s32[]{:S(2)}) async-start(), calls=%async_computation.50 | async-start | bytes 2228224 | tf_op jit(solution)/shard_map/all_gather | solution.py:130
  436.7 4.4 collective-permute-start
  455.1 99.4 %all-gather.22.cloned.1.call-start = ((), (), s32[]{:S(2)}) async-start(), calls=%async_computation.25 | async-start | bytes 2228224 | tf_op jit(solution)/shard_map/all_gather | solution.py:131
  456.9 127.8 %reduce-scatter.29.cloned.1.call-start = ((), (), s32[]{:S(2)}) async-start(), calls=%async_computation.26 | async-start | bytes 655360 | tf_op jit(solution)/shard_map/reduce_scatter | solution.py:80
  564.8 64.6 %reduce-scatter.31.cloned.1.call-start = ((), (), s32[]{:S(2)}) async-start(), calls=%async_computation.27 | async-start | bytes 655360 | tf_op jit(solution)/shard_map/reduce_scatter | solution.py:80
  586.4 222.1 %copy-start.2 = (f32[64,1024]{1,0:T(8,128)}, f32[64,1024]{1,0:T(8,128)S(1)}, u32[]{:S(2)}) copy-start(f32[64,1024]{1,0:T(8,128)S(1)} %get-tuple-element.119) | copy-start | bytes 786436
  606.3 68.2 %reduce-scatter.37.cloned.1.call-start = ((), (), s32[]{:S(2)}) async-start(), calls=%async_computation.31 | async-start | bytes 655360 | tf_op jit(solution)/shard_map/reduce_scatter | solution.py:91
  631.0 20.5 %collective-permute-start.1 = (bf16[64,1024]{1,0:T(8,128)(2,1)}, bf16[64,1024]{1,0:T(8,128)(2,1)S(1)}, u32[]{:S(2)}, u32[]{:S(2)}) collective-permute-start(bf16[64,1024]{1,0:T(8,128)(2,1)} %get-tuple-element.150), channel_id=1, source_target_pairs={{0,64},{1,65},{2,66},{3,67},{4,68},{5,69},{6,70},{7,71},{8,72},{9,... | collective-permute-start | bytes 393224 | tf_op jit(solution)/shard_map/ppermute | solution.py:16
  651.5 74.1 %all-gather.36.cloned.1.call-start = ((), (), s32[]{:S(2)}) async-start(), calls=%async_computation.51 | async-start | bytes 2228224 | tf_op jit(solution)/shard_map/all_gather | solution.py:130
  666.6 108.6 %all-gather.24.cloned.1.call-start = ((), (), s32[]{:S(2)}) async-start(), calls=%async_computation.28 | async-start | bytes 2228224 | tf_op jit(solution)/shard_map/all_gather | solution.py:131
  668.4 140.0 %reduce-scatter.33.cloned.1.call-start = ((), (), s32[]{:S(2)}) async-start(), calls=%async_computation.29 | async-start | bytes 655360 | tf_op jit(solution)/shard_map/reduce_scatter | solution.py:80
  785.5 152.0 %reduce-scatter.39.cloned.1.call-start = ((), (), s32[]{:S(2)}) async-start(), calls=%async_computation.32 | async-start | bytes 2228224 | tf_op jit(solution)/shard_map/reduce_scatter | solution.py:244
  862.3 152.4 %reduce-scatter.41.cloned.1.call-start = ((), (), s32[]{:S(2)}) async-start(), calls=%async_computation.33 | async-start | bytes 2228224 | tf_op jit(solution)/shard_map/reduce_scatter | solution.py:247
  875.2 162.8 %reduce-scatter.43.cloned.1.call-start = ((), (), s32[]{:S(2)}) async-start(), calls=%async_computation.34 | async-start | bytes 655360 | tf_op jit(solution)/shard_map/reduce_scatter | solution.py:91
  1017.1 72.5 %reduce-scatter.45.cloned.1.call-start = ((), (), s32[]{:S(2)}) async-start(), calls=%async_computation.35 | async-start | bytes 655360 | tf_op jit(solution)/shard_map/reduce_scatter | solution.py:91
  1041.5 10.1 collective-permute-start.2
  1069.9 148.9 %reduce-scatter.47.cloned.1.call-start = ((), (), s32[]{:S(2)}) async-start(), calls=%async_computation.36 | async-start | bytes 2228224 | tf_op jit(solution)/shard_map/reduce_scatter | solution.py:244
  1142.6 153.5 %reduce-scatter.49.cloned.1.call-start = ((), (), s32[]{:S(2)}) async-start(), calls=%async_computation.37 | async-start | bytes 2228224 | tf_op jit(solution)/shard_map/reduce_scatter | solution.py:247
  1155.5 163.6 %reduce-scatter.51.cloned.1.call-start = ((), (), s32[]{:S(2)}) async-start(), calls=%async_computation.38 | async-start | bytes 655360 | tf_op jit(solution)/shard_map/reduce_scatter | solution.py:91
  1298.5 44.1 %reduce-scatter.35.cloned.1.call-start = ((), (), s32[]{:S(2)}) async-start(), calls=%async_computation.30 | async-start | bytes 655360 | tf_op jit(solution)/shard_map/reduce_scatter | solution.py:80
  1303.2 84.3 %reduce-scatter.53.cloned.1.call-start = ((), (), s32[]{:S(2)}) async-start(), calls=%async_computation.39 | async-start | bytes 655360 | tf_op jit(solution)/shard_map/reduce_scatter | solution.py:91
  1325.1 17.6 collective-permute-start.3
  1364.5 152.0 %reduce-scatter.55.cloned.1.call-start = ((), (), s32[]{:S(2)}) async-start(), calls=%async_computation.40 | async-start | bytes 2228224 | tf_op jit(solution)/shard_map/reduce_scatter | solution.py:244
  1440.3 153.4 %reduce-scatter.57.cloned.1.call-start = ((), (), s32[]{:S(2)}) async-start(), calls=%async_computation.41 | async-start | bytes 2228224 | tf_op jit(solution)/shard_map/reduce_scatter | solution.py:247
  1453.2 219.7 %reduce-scatter.59.cloned.1.call-start = ((), (), s32[]{:S(2)}) async-start(), calls=%async_computation.42 | async-start | bytes 655360 | tf_op jit(solution)/shard_map/reduce_scatter | solution.py:91
  1596.0 96.2 %reduce-scatter.61.cloned.1.call-start = ((), (), s32[]{:S(2)}) async-start(), calls=%async_computation.43 | async-start | bytes 557056 | tf_op jit(solution)/shard_map/reduce_scatter | solution.py:53
  1600.0 169.6 %reduce-scatter.65.cloned.1.call-start = ((), (), s32[]{:S(2)}) async-start(), calls=%async_computation.45 | async-start | bytes 2228224 | tf_op jit(solution)/shard_map/reduce_scatter | solution.py:59
  1605.5 241.0 %reduce-scatter.63.cloned.1.call-start = ((), (), s32[]{:S(2)}) async-start(), calls=%async_computation.44 | async-start | bytes 2228224 | tf_op jit(solution)/shard_map/reduce_scatter | solution.py:56
  1610.0 311.2 %reduce-scatter.67.cloned.1.call-start = ((), (), s32[]{:S(2)}) async-start(), calls=%async_computation.52 | async-start | bytes 278528
  1682.3 332.5 %all-reduce.6.cloned.1.call-start = ((), (), s32[]{:S(2)}) async-start(), calls=%async_computation.53 | async-start | bytes 4194304
  1686.5 161.6 %copy-start.108 = (f32[64]{0:T(128)S(1)}, f32[64]{0:T(128)}, u32[]{:S(2)}) copy-start(f32[64]{0:T(128)} %broadcast_multiply_fusion) | copy-start | bytes 772
  1686.5 161.8 %copy-start.62 = (f32[1,64,1024]{2,1,0:T(8,128)S(1)}, f32[1,64,1024]{2,1,0:T(8,128)}, u32[]{:S(2)}) copy-start(f32[1,64,1024]{2,1,0:T(8,128)} %get-tuple-element.94) | copy-start | bytes 786436
  (130 other events, 5059.4 us)
Sparse Core Ops, SparseCore 0:
  10.2 46.4 all-gather.25
  68.7 53.7 all-gather.27
  125.2 47.0 all-gather.19
  259.8 58.4 reduce-scatter.24
  320.3 45.4 all-gather.29
  367.8 44.5 all-gather.31
  415.7 19.9 reduce-scatter.26
  455.2 49.4 all-gather.33
  507.4 47.0 all-gather.21
  564.9 19.7 reduce-scatter.28
  606.4 22.8 reduce-scatter.30
  651.6 22.8 reduce-scatter.36
  677.2 48.3 all-gather.35
  728.1 47.0 all-gather.23
  785.6 19.7 reduce-scatter.32
  862.4 75.0 reduce-scatter.38
  940.9 73.6 reduce-scatter.40
  1017.5 20.4 reduce-scatter.42
  1070.0 19.5 reduce-scatter.44
  1142.7 76.0 reduce-scatter.46
  1222.4 73.6 reduce-scatter.48
  1298.6 20.4 reduce-scatter.50
  1321.5 21.1 reduce-scatter.34
  1364.6 22.7 reduce-scatter.52
  1440.4 76.0 reduce-scatter.54
  1520.0 73.6 reduce-scatter.56
  1596.1 20.4 reduce-scatter.58
  1619.8 72.2 reduce-scatter.60
  1695.8 73.7 reduce-scatter.64
  1772.7 73.6 reduce-scatter.62
  1849.9 71.1 reduce-scatter.66
  1924.5 90.1 all-reduce.5
where the time goes:
time: 2030 us; the launch traced here: 2020 us
  waiting for transfers between devices  1050 us (52%)
  blocking collectives  385 us (19%)
  matrix products  367 us (18%)
  local copies, waits for them, and re-layouts  102 us (5%)
  other arithmetic  87.7 us (4%)
    reduce_scatter x3, waiting for transfers between devices, backward_step(): lax.psum_scatter(values_grad_full.astype(jnp.bfloat16), 'dp', scatter_dim...  232 us
    unnamed x34, waiting for transfers between devices  157 us
    all_gather x1, blocking collectives, shards(): segments = lax.all_gather(segment_ids, ('dp', 'tensor'), axis=1, tiled=True)  146 us
    reduce_scatter x3, waiting for transfers between devices, backward_step(): lax.psum_scatter(keys_grad_full.astype(jnp.bfloat16), 'dp', scatter_dimen...  117 us
    reduce_scatter x6, waiting for transfers between devices, collect_rows(): lax.psum_scatter(lax.dot_general(source, weight, (((1,), (1,)), ((), ()))...  99.8 us
    all_gather x3, waiting for transfers between devices, forward_step(): lax.all_gather(keys_local, 'dp', axis=0, tiled=True)  90.4 us
    all_gather x3, waiting for transfers between devices, forward_step(): lax.all_gather(values_local, 'dp', axis=0, tiled=True)  77.8 us
    reduce_scatter x1, waiting for transfers between devices, reduce_weights(): lax.psum_scatter(grad_tuple[3].astype(jnp.bfloat16), 'dp', scatter_dimens...  76.1 us
  transfers between devices with their start and end apart: 36, of which 28 were waited for; matrix products, arithmetic and copies ran while one was open for 17% of the time, Pallas kernels for 0%

commit v1 on v0

v1 whole, which is shorter than its diff:
```python
import functools

import jax
import jax.numpy as jnp
from jax import lax
from jax.experimental import pallas as pl
from jax.experimental.pallas import tpu as pltpu
from jax.sharding import PartitionSpec as P

MESH = pl.DeviceIdType.MESH
HEAD_DIM = 64
EPSILON = 1e-06
MASKED_SCORE = -1e30
RING = 4
CHUNKS = 2
VMEM_LIMIT = 56 * 1024 * 1024
F32 = jnp.float32
BF16 = jnp.bfloat16


def vmem_spec():
    return pl.BlockSpec(memory_space=pltpu.VMEM)


def any_spec():
    return pl.BlockSpec(memory_space=pl.ANY)


def comm_params(cid):
    return pltpu.CompilerParams(
        collective_id=cid, has_side_effects=True, vmem_limit_bytes=VMEM_LIMIT
    )


def step(coord, by):
    return lax.rem(coord + by, RING)


def layer_norm(values, gain_row, shift_row):
    centre = values - jnp.mean(values, axis=-1, keepdims=True)
    spread = jnp.mean(centre * centre, axis=-1, keepdims=True)
    return centre * lax.rsqrt(spread + EPSILON) * gain_row + shift_row


def layer_norm_back(values, gain_row, grad):
    centre = values - jnp.mean(values, axis=-1, keepdims=True)
    spread = jnp.mean(centre * centre, axis=-1, keepdims=True)
    inverse = lax.rsqrt(spread + EPSILON)
    normed = centre * inverse
    scaled = grad * gain_row
    back = inverse * (
        scaled
        - jnp.mean(scaled, axis=-1, keepdims=True)
        - normed * jnp.mean(scaled * normed, axis=-1, keepdims=True)
    )
    return back, jnp.sum(grad * normed, axis=0, keepdims=True), jnp.sum(grad, axis=0, keepdims=True)


def tensor_kernel(function, n_rows, n_vecs, n_out, n_sums, reduce, gather, with_seg, *refs):
    refs = list(refs)
    take = lambda count: [refs.pop(0) for _ in range(count)]
    part = take(1)[0] if reduce else None
    rows_in = take(n_rows)
    vecs = take(n_vecs)
    seg_in = take(1)[0] if with_seg else None
    rows_out = take(n_out)
    sums_out = take(1)[0] if n_sums else None
    full = take(1)[0] if gather else None
    seg_out = take(1)[0] if with_seg else None
    landing = take(1)[0] if reduce else None
    send, recv, local = take(3)

    me = lax.axis_index("tensor")
    barrier = pltpu.get_barrier_semaphore()
    for k in range(1, RING):
        pl.semaphore_signal(
            barrier, inc=1, device_id={"tensor": step(me, k)}, device_id_type=MESH
        )
    pl.semaphore_wait(barrier, RING - 1)

    total_rows = (rows_in[0] if rows_in else part).shape[-2]
    chunk = total_rows // CHUNKS
    started = []

    def push(source, target, kind, index, k):
        copy = pltpu.make_async_remote_copy(
            src_ref=source,
            dst_ref=target,
            send_sem=send.at[kind, index, k - 1],
            recv_sem=recv.at[kind, index, k - 1],
            device_id={"tensor": step(me, k)},
            device_id_type=MESH,
        )
        copy.start()
        started.append(copy)
        return copy

    reduces = {}
    if reduce:
        for c in range(CHUNKS):
            here = pl.ds(c * chunk, chunk)
            for k in range(1, RING):
                reduces[c, k] = push(
                    part.at[step(me, k), here], landing.at[k - 1, here], 0, c, k
                )
    last = []
    if with_seg:
        own = pltpu.make_async_copy(seg_in, seg_out.at[me], local)
        own.start()
        last += [push(seg_in, seg_out.at[me], 2, 0, k) for k in range(1, RING)]
    sums = [None] * n_sums
    for c in range(CHUNKS):
        here = pl.ds(c * chunk, chunk)
        total = None
        if reduce:
            for k in range(1, RING):
                reduces[c, k].wait_recv()
            total = part[me, here].astype(F32)
            for k in range(1, RING):
                total = total + landing[k - 1, here].astype(F32)
        spread, outs, parts = function(
            total, [ref[here].astype(F32) for ref in rows_in], vecs
        )
        if gather:
            full[me, here] = spread.astype(BF16)
            last += [push(full.at[me, here], full.at[me, here], 1, c, k) for k in range(1, RING)]
        for ref, value in zip(rows_out, outs):
            ref[here] = value.astype(ref.dtype)
        sums = [new if old is None else old + new for old, new in zip(sums, parts)]
    if n_sums:
        sums_out[...] = jnp.concatenate(
            sums + [jnp.zeros((8 - n_sums, sums[0].shape[1]), F32)], axis=0
        ) if n_sums < 8 else jnp.concatenate(sums, axis=0)
    for copy in last:
        copy.wait_recv()
    if with_seg:
        own.wait()
    for copy in started:
        copy.wait_send()


def tensor_call(cid, function, part, rows, vecs, outs, n_sums, gather, seg=None):
    height, width = rows[0].shape
    reduce = part is not None
    with_seg = seg is not None
    args = ([part] if reduce else []) + list(rows) + list(vecs) + ([seg] if with_seg else [])
    shapes = [jax.ShapeDtypeStruct((height, width), dtype) for dtype in outs]
    if n_sums:
        shapes.append(jax.ShapeDtypeStruct((8, width), F32))
    if gather:
        shapes.append(jax.ShapeDtypeStruct((RING, height, width), BF16))
    if with_seg:
        shapes.append(jax.ShapeDtypeStruct((RING,) + seg.shape, seg.dtype))
    scratch = [pltpu.VMEM((RING - 1, height, width), BF16)] if reduce else []
    scratch += [
        pltpu.SemaphoreType.DMA((3, CHUNKS, RING - 1)),
        pltpu.SemaphoreType.DMA((3, CHUNKS, RING - 1)),
        pltpu.SemaphoreType.DMA,
    ]
    return pl.pallas_call(
        functools.partial(
            tensor_kernel, function, len(rows), len(vecs), len(outs), n_sums, reduce, gather, with_seg
        ),
        out_shape=shapes,
        in_specs=[vmem_spec()] * len(args),
        out_specs=[vmem_spec()] * len(shapes),
        scratch_shapes=scratch,
        compiler_params=comm_params(cid),
    )(*args)


def row(ref, index):
    return ref[pl.ds(index, 1), :]


def first_rows(total, rows, vecs):
    return layer_norm(rows[0], row(vecs[0], 0), row(vecs[0], 1)), [], []


def middle_rows(total, rows, vecs):
    vec = vecs[0]
    attn_out = total + row(vec, 13)
    hidden = rows[0] + row(vec, 4) * attn_out
    return layer_norm(hidden, row(vec, 5), row(vec, 6)), [attn_out, hidden], []


def end_rows_first(total, rows, vecs):
    vec, after = vecs
    mlp_out = total + row(vec, 7)
    outputs = (rows[0] + row(vec, 8) * mlp_out).astype(BF16)
    inputs = outputs.astype(F32)
    return layer_norm(inputs, row(after, 0), row(after, 1)), [mlp_out, outputs], []


def end_rows_last(total, rows, vecs):
    vec = vecs[0]
    hidden, upstream = rows
    mlp_out = total + row(vec, 7)
    outputs = hidden + row(vec, 8) * mlp_out
    mlp_grad = row(vec, 8) * upstream
    sums = [
        jnp.sum(upstream * mlp_out, axis=0, keepdims=True),
        jnp.sum(mlp_grad, axis=0, keepdims=True),
    ]
    return mlp_grad, [outputs], sums


def back_middle_rows(total, rows, vecs):
    vec = vecs[0]
    upstream, hidden, attn_out = rows
    part, gain, shift = layer_norm_back(hidden, row(vec, 5), total)
    hidden_grad = upstream + part
    attn_grad = row(vec, 4) * hidden_grad
    sums = [
        gain,
        shift,
        jnp.sum(hidden_grad * attn_out, axis=0, keepdims=True),
        jnp.sum(attn_grad, axis=0, keepdims=True),
    ]
    return attn_grad, [hidden_grad], sums


def back_end_rows_last(total, rows, vecs):
    vec, before = vecs
    hidden_grad, inputs, mlp_out = rows
    part, gain, shift = layer_norm_back(inputs, row(vec, 0), total)
    input_grad = hidden_grad + part
    upstream = input_grad.astype(BF16).astype(F32)
    mlp_grad = row(before, 8) * upstream
    sums = [
        gain,
        shift,
        jnp.sum(upstream * mlp_out, axis=0, keepdims=True),
        jnp.sum(mlp_grad, axis=0, keepdims=True),
    ]
    return mlp_grad, [input_grad], sums


def back_end_rows_first(total, rows, vecs):
    hidden_grad, inputs = rows
    part, gain, shift = layer_norm_back(inputs, row(vecs[0], 0), total)
    return None, [hidden_grad + part], [gain, shift]


def place(lane_first, own, other):
    return (other, own) if lane_first else (own, other)


def dp_neighbour(y, z, along_z, k):
    if along_z:
        return {"dp": y * RING + step(z, k)}
    return {"dp": step(y, k) * RING + z}


def dp_barrier(y, z, section):
    barrier = pltpu.get_barrier_semaphore()
    count = 0
    for along_z in (True, False):
        for k in range(1, RING):
            pl.semaphore_signal(
                barrier, inc=1, device_id=dp_neighbour(y, z, along_z, k), device_id_type=MESH
            )
            count += 1
    if section is not None:
        pl.semaphore_signal(
            barrier, inc=1, device_id={"section": 1 - section}, device_id_type=MESH
        )
        count += 1
    return barrier, count


def gather_kernel(pieces, n_in, n_out, with_sibling, *refs):
    ins, outs = refs[:n_in], refs[n_in : n_in + n_out]
    send, recv, local = refs[n_in + n_out :]
    rank = lax.axis_index("dp")
    y, z = rank // RING, lax.rem(rank, RING)
    section = lax.axis_index("section") if with_sibling else None
    barrier, count = dp_barrier(y, z, section)
    pl.semaphore_wait(barrier, count)
    started = []

    def push(index, stage, k, source, target, device):
        copy = pltpu.make_async_remote_copy(
            src_ref=source,
            dst_ref=target,
            send_sem=send.at[index, stage, k],
            recv_sem=recv.at[index, stage, k],
            device_id=device,
            device_id_type=MESH,
        )
        copy.start()
        started.append(copy)
        return copy

    def block(index, ys, zs):
        number, pre, along_z = pieces[index]
        lead = ((section,) if with_sibling else ()) + pre
        return outs[number].at[lead + (ys, zs)]

    own, first, second, across = [], {}, {}, []
    for index, (number, pre, along_z) in enumerate(pieces):
        source = ins[number].at[pre] if pre else ins[number]
        copy = pltpu.make_async_copy(source, block(index, y, z), local.at[index])
        copy.start()
        own.append(copy)
        for k in range(1, RING):
            first[index, k] = push(
                index, 0, k, source, block(index, y, z), dp_neighbour(y, z, along_z, k)
            )

    def line(index, k):
        along_z = pieces[index][2]
        return block(index, step(y, k), slice(None)) if along_z else block(index, slice(None), step(z, k))

    for index, (number, pre, along_z) in enumerate(pieces):
        own[index].wait()
        for k in range(1, RING):
            first[index, k].wait_recv()
        for k in range(1, RING):
            second[index, k] = push(
                index, 1, k, line(index, 0), line(index, 0), dp_neighbour(y, z, not along_z, k)
            )
        if with_sibling:
            across.append(
                push(index, 2, 0, line(index, 0), line(index, 0), {"section": 1 - section})
            )
    for index in range(len(pieces)):
        for k in range(1, RING):
            second[index, k].wait_recv()
            if with_sibling:
                came = line(index, RING - k)
                across.append(push(index, 2, k, came, came, {"section": 1 - section}))
    for copy in across:
        copy.wait_recv()
    for copy in started:
        copy.wait_send()


def gather_call(cid, pieces, ins, outs, with_sibling):
    return pl.pallas_call(
        functools.partial(gather_kernel, pieces, len(ins), len(outs), with_sibling),
        out_shape=outs,
        in_specs=[vmem_spec()] * len(ins),
        out_specs=[any_spec()] * len(outs),
        scratch_shapes=[
            pltpu.SemaphoreType.DMA((len(pieces), 3, RING)),
            pltpu.SemaphoreType.DMA((len(pieces), 3, RING)),
            pltpu.SemaphoreType.DMA((len(pieces),)),
        ],
        compiler_params=comm_params(cid),
    )(*ins)


def rows_loop(height, size, body):
    if height <= size:
        body(pl.ds(0, height))
        return

    def each(number, carry):
        body(pl.ds(pl.multiple_of(number * size, size), size))
        return carry

    lax.fori_loop(0, height // size, each, 0)


def scatter_first(index, along_z, source, landing, y, z, push):
    copies = []
    for k in range(1, RING):
        line = (
            source.at[:, step(z, k)] if along_z else source.at[step(y, k)]
        )
        copies.append(
            push(index, 0, k, line, landing.at[k - 1], dp_neighbour(y, z, along_z, k))
        )
    return copies


def scatter_second(index, along_z, source, landing, middle, arrivals, y, z, push, copies):
    for copy in copies:
        copy.wait_recv()
    height, width = source.shape[-2:]
    size = max(8, min(height, 65536 // width))
    second = []
    for k in list(range(1, RING)) + [0]:
        at = step(y, k) if along_z else step(z, k)

        def add(here):
            value = (source[at, z, here] if along_z else source[y, at, here]).astype(F32)
            for slot in range(RING - 1):
                value = value + landing[slot, at, here].astype(F32)
            middle[k, here] = value.astype(middle.dtype)

        rows_loop(height, size, add)
        if k:
            second.append(
                push(index, 1, k, middle.at[k], arrivals.at[k - 1], dp_neighbour(y, z, not along_z, k))
            )
    return second


def scatter_last(middle, arrivals, out, copies):
    for copy in copies:
        copy.wait_recv()
    height, width = middle.shape[-2:]
    size = max(8, min(height, 65536 // width))

    def add(here):
        value = middle[0, here].astype(F32)
        for slot in range(RING - 1):
            value = value + arrivals[slot, here].astype(F32)
        out[here] = value

    rows_loop(height, size, add)


def pusher(send, recv, started):
    def push(index, stage, k, source, target, device):
        copy = pltpu.make_async_remote_copy(
            src_ref=source,
            dst_ref=target,
            send_sem=send.at[index, stage, k],
            recv_sem=recv.at[index, stage, k],
            device_id=device,
            device_id_type=MESH,
        )
        copy.start()
        started.append(copy)
        return copy

    return push


def scatter_kernel(orders, *refs):
    n = len(orders)
    ins, outs = refs[:n], refs[n : 2 * n]
    landings, middles, arrivals = refs[2 * n : 3 * n], refs[3 * n : 4 * n], refs[4 * n : 5 * n]
    send, recv = refs[5 * n :]
    rank = lax.axis_index("dp")
    y, z = rank // RING, lax.rem(rank, RING)
    barrier, count = dp_barrier(y, z, None)
    pl.semaphore_wait(barrier, count)
    started = []
    push = pusher(send, recv, started)
    first = [
        scatter_first(i, orders[i], ins[i], landings[i], y, z, push) for i in range(n)
    ]
    second = [
        scatter_second(i, orders[i], ins[i], landings[i], middles[i], arrivals[i], y, z, push, first[i])
        for i in range(n)
    ]
    for i in range(n):
        scatter_last(middles[i], arrivals[i], outs[i], second[i])
    for copy in started:
        copy.wait_send()


def scatter_scratch(block, dtype):
    return (
        pltpu.VMEM((RING - 1, RING) + block, dtype),
        pltpu.VMEM((RING,) + block, dtype),
        pltpu.VMEM((RING - 1,) + block, dtype),
    )


def scatter_call(cid, orders, ins):
    blocks = [value.shape[2:] for value in ins]
    sets = [scatter_scratch(block, BF16) for block in blocks]
    return pl.pallas_call(
        functools.partial(scatter_kernel, orders),
        out_shape=[jax.ShapeDtypeStruct(block, F32) for block in blocks],
        in_specs=[vmem_spec()] * len(ins),
        out_specs=[vmem_spec()] * len(ins),
        scratch_shapes=[group[i] for i in range(3) for group in sets]
        + [
            pltpu.SemaphoreType.DMA((len(ins), 2, RING)),
            pltpu.SemaphoreType.DMA((len(ins), 2, RING)),
        ],
        compiler_params=comm_params(cid),
    )(*ins)


def final_kernel(orders, n_extra, *refs):
    n = len(orders)
    refs = list(refs)
    take = lambda count: [refs.pop(0) for _ in range(count)]
    ins, extras = take(n), take(n_extra)
    outs, extra_outs = take(n), take(n_extra)
    siblings, owns, landings, middles, arrivals = take(n), take(n), take(n), take(n), take(n)
    vector_own, vector_parts = take(2)
    send, recv, local, extra_send, extra_recv = take(5)
    rank = lax.axis_index("dp")
    y, z = rank // RING, lax.rem(rank, RING)
    section = lax.axis_index("section")
    me = lax.axis_index("tensor")
    barrier, count = dp_barrier(y, z, section)
    for k in range(1, RING):
        pl.semaphore_signal(
            barrier, inc=1, device_id={"tensor": step(me, k)}, device_id_type=MESH
        )
    pl.semaphore_wait(barrier, count + RING - 1)
    started = []
    push = pusher(send, recv, started)
    other = {"section": 1 - section}
    across, local_copies = [], []
    for i in range(n):
        across.append(push(i, 2, 0, ins[i].at[1 - section], siblings[i], other))
        copy = pltpu.make_async_copy(ins[i].at[section], owns[i], local.at[i])
        copy.start()
        local_copies.append(copy)
    extra_copies = []
    for i in range(n_extra):
        copy = pltpu.make_async_remote_copy(
            src_ref=extras[i],
            dst_ref=extra_outs[i],
            send_sem=extra_send.at[i],
            recv_sem=extra_recv.at[i],
            device_id=other,
            device_id_type=MESH,
        )
        copy.start()
        extra_copies.append(copy)
    first = []
    for i in range(n):
        local_copies[i].wait()
        across[i].wait_recv()
        own, sibling = owns[i], siblings[i]

        def add(number, carry):
            at_y, at_z = number // RING, lax.rem(number, RING)
            own[at_y, at_z] = (
                own[at_y, at_z].astype(F32) + sibling[at_y, at_z].astype(F32)
            ).astype(own.dtype)
            return carry

        lax.fori_loop(0, RING * RING, add, 0)
        first.append(scatter_first(i, orders[i], own, landings[i], y, z, push))
    second = [
        scatter_second(i, orders[i], owns[i], landings[i], middles[i], arrivals[i], y, z, push, first[i])
        for i in range(n)
    ]
    for i in range(n):
        scatter_last(
            middles[i], arrivals[i], vector_own if i == 0 else outs[i], second[i]
        )
        if i == 0:
            vector_parts[me] = vector_own[...]
            vector_copies = [
                push(
                    0, 3, k, vector_own, vector_parts.at[me], {"tensor": step(me, k)}
                )
                for k in range(1, RING)
            ]
    for copy in vector_copies:
        copy.wait_recv()
    total = vector_parts[0]
    for k in range(1, RING):
        total = total + vector_parts[k]
    outs[0][...] = total
    for copy in extra_copies:
        copy.wait()
    for copy in started:
        copy.wait_send()


def final_call(cid, orders, ins, extras):
    blocks = [value.shape[3:] for value in ins]
    sets = [scatter_scratch(block, value.dtype) for block, value in zip(blocks, ins)]
    square = [
        pltpu.VMEM((RING, RING) + block, value.dtype) for block, value in zip(blocks, ins)
    ]
    count, extra = len(ins), len(extras)
    return pl.pallas_call(
        functools.partial(final_kernel, orders, extra),
        out_shape=[jax.ShapeDtypeStruct(block, F32) for block in blocks]
        + [jax.ShapeDtypeStruct(value.shape, value.dtype) for value in extras],
        in_specs=[any_spec()] * count + [vmem_spec()] * extra,
        out_specs=[vmem_spec()] * (count + extra),
        scratch_shapes=square
        + square
        + [group[i] for i in range(3) for group in sets]
        + [
            pltpu.VMEM(blocks[0], F32),
            pltpu.VMEM((RING,) + blocks[0], F32),
            pltpu.SemaphoreType.DMA((count, 4, RING)),
            pltpu.SemaphoreType.DMA((count, 4, RING)),
            pltpu.SemaphoreType.DMA((count,)),
            pltpu.SemaphoreType.DMA((extra,)),
            pltpu.SemaphoreType.DMA((extra,)),
        ],
        compiler_params=comm_params(cid),
    )(*ins, *extras)


def gelu_exact(values):
    return jax.nn.gelu(values, approximate=False)


def flat_dot(former, latter):
    return lax.dot_general(former, latter, (((1,), (1,)), ((), ())), preferred_element_type=F32)


def rows_dot(former, latter):
    return lax.dot_general(former, latter, (((0,), (0,)), ((), ())), preferred_element_type=F32)


def attention_weights(queries, keys_full, seg_rows, seg_keys):
    heads_here = queries.shape[1] // HEAD_DIM
    query_heads = queries.reshape(queries.shape[0], heads_here, HEAD_DIM)
    key_heads = keys_full.reshape(keys_full.shape[0], heads_here, HEAD_DIM)
    raw_scores = jnp.einsum(
        "rhd,shd->hrs", query_heads, key_heads, preferred_element_type=F32
    ) * HEAD_DIM ** (-0.5)
    allowed = seg_rows[:, None] == seg_keys[None, :]
    masked = jnp.where(allowed[None], raw_scores, MASKED_SCORE)
    highest = jnp.max(masked, axis=-1, keepdims=True)
    exponent = jnp.exp(masked - highest)
    total = jnp.sum(exponent, axis=-1, keepdims=True)
    return exponent / total


def attention_forward(queries, keys_full, values_full, seg_rows, seg_keys):
    heads_here = queries.shape[1] // HEAD_DIM
    soft = attention_weights(queries, keys_full, seg_rows, seg_keys)
    mixed = jnp.einsum(
        "hrs,shd->rhd",
        soft.astype(BF16),
        values_full.reshape(-1, heads_here, HEAD_DIM),
        preferred_element_type=F32,
    )
    return mixed.reshape(queries.shape).astype(BF16)


def attention_backward(queries, keys_full, values_full, mixed_grad, seg_rows, seg_keys):
    local_width = queries.shape[1]
    heads_here = local_width // HEAD_DIM
    head_scale = HEAD_DIM ** (-0.5)
    soft = attention_weights(queries, keys_full, seg_rows, seg_keys)
    mixed_split = mixed_grad.reshape(-1, heads_here, HEAD_DIM)
    value_heads = values_full.reshape(-1, heads_here, HEAD_DIM)
    key_heads = keys_full.reshape(-1, heads_here, HEAD_DIM)
    query_heads = queries.reshape(-1, heads_here, HEAD_DIM)
    prob_grad = jnp.einsum("rhd,shd->hrs", mixed_split, value_heads, preferred_element_type=F32)
    row_delta = jnp.sum(prob_grad * soft, axis=-1)
    score_grad = soft * (prob_grad - row_delta[..., None])
    score_low = (score_grad * head_scale).astype(BF16)
    query_grad = jnp.einsum(
        "hrs,shd->rhd", score_low, key_heads, preferred_element_type=F32
    ).reshape(-1, local_width)
    values_grad = jnp.einsum(
        "hrs,rhd->shd", soft.astype(BF16), mixed_split, preferred_element_type=F32
    ).reshape(-1, local_width)
    keys_grad = jnp.einsum(
        "hrs,rhd->shd", score_low, query_heads, preferred_element_type=F32
    ).reshape(-1, local_width)
    return query_grad, keys_grad.astype(BF16), values_grad.astype(BF16)


WEIGHT_PIECES = (
    (0, (0,), True),
    (0, (1,), False),
    (0, (2,), True),
    (1, (), False),
    (4, (), True),
    (2, (), True),
    (3, (), False),
)


def shards(tokens, segment_ids, w_qkv, w_out, w_up, w_down, vectors, out_bias, cotangent):
    section = lax.axis_index("section")
    tensor_rank = lax.axis_index("tensor")
    own = lambda pair: jnp.where(section == 0, pair[0], pair[1])
    rows = tokens.shape[1]
    width = tokens.shape[2]
    group = rows * RING
    square = (RING, RING)
    local_width = w_qkv.shape[3]
    local_hidden = w_up.shape[2]

    depth = w_out.shape[1]
    small = jnp.pad(
        jnp.concatenate([vectors[0], out_bias], axis=0),
        ((0, 2), (0, 128 - depth)),
    )
    shape = lambda *dims: jax.ShapeDtypeStruct(dims, BF16)
    full_qkv, full_out, full_up, full_down, full_small = gather_call(
        0,
        WEIGHT_PIECES,
        [w_qkv[0], w_out[0], w_up[0], w_down[0], small],
        [
            shape(2, 3, *square, depth, local_width),
            shape(2, *square, depth, local_width),
            shape(2, *square, depth, local_hidden),
            shape(2, *square, depth, local_hidden),
            shape(2, *square, 16, 128),
        ],
        True,
    )
    full_qkv = full_qkv.reshape(2, 3, width, local_width)
    full_out = full_out.reshape(2, width, local_width)
    full_up = full_up.reshape(2, width, local_hidden)
    full_down = full_down.reshape(2, width, local_hidden)
    small_rows = (
        full_small.reshape(2, RING * RING, 16, 128)[..., :depth]
        .transpose(0, 2, 1, 3)
        .reshape(2, 16, width)
        .astype(F32)
    )

    my_tokens = own(tokens)
    my_cotangent = own(cotangent)
    my_segments = own(segment_ids)
    seg_block = jnp.zeros((8, 128), jnp.int32).at[0, :rows].set(my_segments)
    normed, seg_group = tensor_call(
        1, first_rows, None, [my_tokens], [small_rows[0]], [], 0, True, seg_block
    )
    seg_rows = seg_group[:, 0, :rows].reshape(group)
    seg_wide = jnp.broadcast_to(seg_rows[None], (8, group))
    inputs = my_tokens
    kept = []
    seg_keys = None
    for layer in range(2):
        vec = small_rows[layer]
        normed = normed.reshape(group, width)
        query_bias = lax.dynamic_slice_in_dim(vec[2], tensor_rank * local_width, local_width)
        value_bias = lax.dynamic_slice_in_dim(vec[3], tensor_rank * local_width, local_width)
        up_bias = lax.dynamic_slice_in_dim(
            vec[9:13].reshape(-1), tensor_rank * local_hidden, local_hidden
        )
        project = lambda which: jnp.dot(normed, full_qkv[layer, which], preferred_element_type=F32)
        queries = (project(0) + query_bias).astype(BF16)
        keys = project(1).astype(BF16)
        values = (project(2) + value_bias).astype(BF16)
        keys_full, values_full, seg_full = gather_call(
            2,
            ((2, (), True), (0, (), True), (1, (), False)),
            [keys, values, seg_wide],
            [
                shape(*square, group, local_width),
                shape(*square, group, local_width),
                jax.ShapeDtypeStruct(square + (8, group), jnp.int32),
            ],
            False,
        )
        keys_full = keys_full.reshape(-1, local_width)
        values_full = values_full.reshape(-1, local_width)
        if layer == 0:
            seg_keys = seg_full[:, :, 0].reshape(-1)
        mixed = attention_forward(queries, keys_full, values_full, seg_rows, seg_keys)
        part = flat_dot(mixed, full_out[layer]).astype(BF16).reshape(RING, rows, width)
        attn_out, hidden, normed_two = tensor_call(
            3, middle_rows, part, [inputs.astype(F32)], [vec], [F32, F32], 0, True
        )
        normed_two = normed_two.reshape(group, width)
        pre_act = jnp.dot(normed_two, full_up[layer], preferred_element_type=F32) + up_bias
        activated = gelu_exact(pre_act).astype(BF16)
        part = flat_dot(activated, full_down[layer]).astype(BF16).reshape(RING, rows, width)
        step_kept = [inputs, normed, queries, keys_full, values_full, mixed, attn_out, hidden]
        step_kept += [normed_two, pre_act, activated]
        if layer == 0:
            mlp_first, between, normed = tensor_call(
                4, end_rows_first, part, [hidden], [vec, small_rows[1]], [F32, BF16], 0, True
            )
            inputs = between
        else:
            outputs, sums_end, mlp_rows = tensor_call(
                5, end_rows_last, part, [hidden, my_cotangent], [vec], [BF16], 2, True
            )
        kept.append(step_kept)

    upstream = my_cotangent.astype(F32)
    grads = [None, None]
    scale_two, down_bias = sums_end[0], sums_end[1]
    for layer in (1, 0):
        vec = small_rows[layer]
        inputs, normed, queries, keys_full, values_full, mixed, attn_out, hidden = kept[layer][:8]
        normed_two, pre_act, activated = kept[layer][8:]
        mlp_rows = mlp_rows.reshape(group, width)
        act_grad = jnp.dot(mlp_rows, full_down[layer], preferred_element_type=F32)
        grad_down = rows_dot(mlp_rows, activated)
        pre_grad = jax.vjp(gelu_exact, pre_act)[1](act_grad)[0]
        up_bias_grad = jnp.sum(pre_grad, axis=0)
        pre_low = pre_grad.astype(BF16)
        grad_up = rows_dot(normed_two, pre_low)
        part = flat_dot(pre_low, full_up[layer]).astype(BF16).reshape(RING, rows, width)
        hidden_grad, sums_middle, attn_rows = tensor_call(
            6, back_middle_rows, part, [upstream, hidden, attn_out], [vec], [F32], 4, True
        )
        attn_rows = attn_rows.reshape(group, width)
        mixed_grad = jnp.dot(attn_rows, full_out[layer], preferred_element_type=F32).astype(BF16)
        grad_out = rows_dot(attn_rows, mixed)
        query_grad, keys_part, values_part = attention_backward(
            queries, keys_full, values_full, mixed_grad, seg_rows, seg_keys
        )
        keys_grad, values_grad = scatter_call(
            7,
            (True, False),
            [
                keys_part.reshape(*square, group, local_width),
                values_part.reshape(*square, group, local_width),
            ],
        )
        query_bias_grad = jnp.sum(query_grad, axis=0)
        value_bias_grad = jnp.sum(values_grad, axis=0)
        triple = [value.astype(BF16) for value in (query_grad, keys_grad, values_grad)]
        grad_qkv = [rows_dot(normed, value) for value in triple]
        part = sum(flat_dot(triple[which], full_qkv[layer, which]) for which in range(3))
        part = part.astype(BF16).reshape(RING, rows, width)
        if layer == 1:
            input_grad, sums_last, mlp_rows = tensor_call(
                8,
                back_end_rows_last,
                part,
                [hidden_grad, inputs.astype(F32), mlp_first],
                [vec, small_rows[0]],
                [F32],
                4,
                True,
            )
        else:
            input_grad, sums_last = tensor_call(
                9, back_end_rows_first, part, [hidden_grad, inputs.astype(F32)], [vec], [F32], 2, False
            )

        def placed(values, length):
            empty = jnp.zeros((length,), F32)
            return lax.dynamic_update_slice(empty, values, (tensor_rank * values.shape[0],))

        vector_rows = jnp.concatenate(
            [
                sums_last[0:2],
                placed(query_bias_grad, width)[None],
                placed(value_bias_grad, width)[None],
                sums_middle[2:3],
                sums_middle[0:2],
                down_bias[None],
                scale_two[None],
                placed(up_bias_grad, local_hidden * RING).reshape(-1, width),
                sums_middle[3:4],
                jnp.zeros((2, width), F32),
            ],
            axis=0,
        )
        vector_rows = jnp.pad(
            vector_rows.reshape(16, RING * RING, depth).transpose(1, 0, 2),
            ((0, 0), (0, 0), (0, 128 - depth)),
        ).reshape(*square, 16, 128)
        grads[layer] = [vector_rows] + [
            value.astype(BF16).reshape(*square, depth, value.shape[-1])
            for value in grad_qkv + [grad_out, grad_up, grad_down]
        ]
        if layer == 1:
            last_grad = input_grad
            upstream = input_grad.astype(BF16).astype(F32)
            scale_two, down_bias = sums_last[2], sums_last[3]
    first_grad = input_grad

    stacked = [jnp.stack(pair) for pair in zip(*grads)]
    extras = [
        jnp.where(section == 0, outputs, between),
        jnp.where(section == 0, last_grad, first_grad),
    ]
    results = final_call(10, (True, True, False, True, False, True, False), stacked, extras)
    small_sum, grad_q, grad_k, grad_v, grad_out, grad_up, grad_down, came_out, came_grad = results
    mine_out = jnp.where(section == 0, between, outputs)
    mine_grad = jnp.where(section == 0, first_grad, last_grad)
    pair = lambda mine, came: jnp.where(
        section == 0, jnp.stack([mine, came]), jnp.stack([came, mine])
    )[None]
    return (
        pair(mine_out, came_out),
        pair(mine_grad, came_grad),
        jnp.stack([grad_q, grad_k, grad_v])[None],
        grad_out[None],
        grad_up[None],
        grad_down[None],
        small_sum[:13, :depth][None],
        small_sum[13:14, :depth],
    )


def solution(mesh):
    in_specs = (
        P(None, ("dp", "tensor"), None),
        P(None, ("dp", "tensor")),
        P("section", None, "dp", "tensor"),
        P("section", "dp", "tensor"),
        P("section", "dp", "tensor"),
        P("section", "dp", "tensor"),
        P("section", None, "dp"),
        P("section", "dp"),
        P(None, ("dp", "tensor"), None),
    )
    out_specs = (
        P("section", None, ("dp", "tensor"), None),
        P("section", None, ("dp", "tensor"), None),
        P("section", None, "dp", "tensor"),
        P("section", "dp", "tensor"),
        P("section", "dp", "tensor"),
        P("section", "dp", "tensor"),
        P("section", None, "dp"),
        P("section", "dp"),
    )
    return jax.shard_map(shards, mesh=mesh, in_specs=in_specs, out_specs=out_specs, check_vma=False)
```

time: 2030 us -> 747 us (0.37)
  waiting for transfers between devices: 1050 us -> 0 us
  Pallas kernels: 0 us -> 394 us
  blocking collectives: 385 us -> 0 us
  matrix products: 367 us -> 222 us
  other arithmetic: 87.7 us -> 27.2 us
    reduce_scatter x21 -> x0, waiting for transfers between devices: 647 us -> none  [the longest x3 232 us: backward_step(): lax.psum_scatter(values_grad_full.astype(jnp.bfloat16), 'dp', scatter_dim...]
    pallas_call x0 -> x15, Pallas kernels: none -> 394 us  [the longest x3 131 us: gather_call(): pl.pallas_call(functools.partial(gather_kernel, pieces, len(ins), len(out...]
    all_gather x15 -> x0, blocking collectives: 314 us -> none  [the longest x1 146 us: shards(): segments = lax.all_gather(segment_ids, ('dp', 'tensor'), axis=1, tiled=True)]
    all_gather x9 -> x0, waiting for transfers between devices: 243 us -> none  [the longest x3 90.4 us: forward_step(): lax.all_gather(keys_local, 'dp', axis=0, tiled=True)]
    unnamed x34 -> x0, waiting for transfers between devices: 157 us -> none
    dot_general x51 -> x46, matrix products: 301 us -> 200 us  [the longest x2 46.7 us: attention_backward(): jnp.einsum('hrs,rhd->shd', score_low, query_heads, preferred_element_type...]
    unnamed x2 -> x0, blocking collectives: 62.5 us -> none
    sub x6 -> x2, matrix products: 66.4 us -> 21.4 us  [attention_weights(): exponent = jnp.exp(masked - highest)]
  transfers between devices with their start and end apart: 36 -> 0, of which waited for: 28 -> 0; matrix products, arithmetic and copies ran while one was open for 17% -> 0% of each run, Pallas kernels for 0% -> 0%
where the time goes in v1:
time: 747 us; the launch traced here: 735 us
  Pallas kernels  394 us (53%)
  matrix products  222 us (30%)
  local copies, waits for them, and re-layouts  90.4 us (12%)
  other arithmetic  27.2 us (4%)
    pallas_call x3, Pallas kernels, gather_call(): pl.pallas_call(functools.partial(gather_kernel, pieces, len(ins), len(out...  131 us
    pallas_call x9, Pallas kernels, tensor_call(): pl.pallas_call(functools.partial(tensor_kernel, function, len(rows), len(...  123 us
    pallas_call x2, Pallas kernels, scatter_call(): pl.pallas_call(functools.partial(scatter_kernel, orders), out_shape=[jax....  78.8 us
    pallas_call x1, Pallas kernels, final_call(): pl.pallas_call(functools.partial(final_kernel, orders, extra), out_shape=...  61.3 us
    dot_general x2, matrix products, attention_backward(): jnp.einsum('hrs,rhd->shd', score_low, query_heads, preferred_element_type...  46.7 us
    dot_general x2, matrix products, attention_backward(): jnp.einsum('hrs,shd->rhd', score_low, key_heads, preferred_element_type=F32)  45.1 us
    convert_element_type x8, local copies, waits for them, and re-layouts, attention_backward(): return (query_grad, keys_grad.astype(BF16), values_grad.astype(BF16))  30.3 us
    sub x2, matrix products, attention_weights(): exponent = jnp.exp(masked - highest)  21.4 us

profile of v1, /device:TPU:1, one launch (start us, length us, event | category | flops | bytes accessed | tf_op | source)
XLA Modules:
  0.0 735.3 jit_solution(14678781358009874768)
XLA Ops:
  1.9 59.5 %shard_map.152 = (bf16[2,3,4,4,64,256]{5,4,3,2,1,0:T(8,128)(2,1)}, bf16[2,4,4,64,256]{4,3,2,1,0:T(8,128)(2,1)}, bf16[2,4,4,64,1024]{4,3,2,1,0:T(8,128)(2,1)}, bf...) custom-call(bf16[3,64,256]{2,1,0:T(8,128)(2,1)} %bitcast.318, bf16[64,256]{1,0:T(8,128)(2,1)} %bitcast.324, ...), custom_call_target="tpu_custom_call" | custom-call | tf_op jit(solution)/shard_map/pallas_call | solution.py:340
  66.7 12.6 %shard_map.153 = (bf16[4,64,1024]{2,1,0:T(8,128)(2,1)}, s32[4,8,128]{2,1,0:T(8,128)}) custom-call(bf16[64,1024]{1,0:T(8,128)(2,1)} %get-tuple-element.187.refs_0_, f32[16,1024]{1,0:T(8,128)} %squeeze.43.refs_1_.refs_2_.refs_5_.refs_4_.refs_3_, s32[8,128]{1,0:T(8,128)} %scatter.4.refs_2_), custom_call_target="tpu_custom_call" | custom-call | tf_op jit(solution)/shard_map/pallas_call | solution.py:160
  85.1 34.1 %shard_map.154 = (bf16[4,4,256,256]{3,2,1,0:T(8,128)(2,1)}, bf16[4,4,256,256]{3,2,1,0:T(8,128)(2,1)}, s32[4,4,8,256]{3,2,1,0:T(8,128)}) custom-call(bf16[256,256]{1,0:T(8,128)(2,1)} %convolution_convert_fusion.23.refs_0_, bf16[256,256]{1,0:T(8,128)(2,1)} %fusion.68.refs_1_, s32[8,256]{1,0:T(8,128)} %broadcast_in_dim.84.refs_2_), custom_call_target="tpu_custom_call" | custom-call | tf_op jit(solution)/shard_map/pallas_call | solution.py:340
  119.2 4.6 copy.44
  123.9 3.3 reshape_reshape.8
  131.1 4.6 copy.45
  135.8 4.5 reshape_reshape.9
  140.2 10.5 %fusion.129 = (f32[4,256]{1,0:T(4,128)S(1)}, f32[4,256,4096]{2,1,0:T(8,128)}) fusion(pred[256,4096]{1,0:T(8,128)(4,1)S(1)} %copy-done.17, bf16[256,4,64]{0,2,1:T(8,128)(2,1)S(1)} %bitcast.332, bf16[4096,4,64]{0,2,1:T(8,128)(2,1)} %reshape_reshape.9), kind=kOutput, calls=%fused_computation.233 | convolution fusion | flops 553652224 | bytes 20058112 | tf_op jit(solution)/shard_map/sub | solution.py:616
  150.8 8.6 %fusion.62 = bf16[4,64,256]{2,1,0:T(8,128)(2,1)S(1)} fusion(bf16[4096,4,64]{0,2,1:T(8,128)(2,1)S(1)} %reshape_reshape.8, f32[4,256,4096]{2,1,0:T(8,128)} %get-tuple-element.175, f32[4,256]{1,0:T(4,128)S(1)} %get-tuple-element.174), kind=kOutput, calls=%fused_computation.81 | convolution fusion | flops 545325056 | bytes 19009536 | tf_op jit(solution)/shard_map/hrs,shd->rhd/dot_general | solution.py:624
  161.5 15.6 %shard_map.155 = (f32[64,1024]{1,0:T(8,128)}, f32[64,1024]{1,0:T(8,128)}, bf16[4,64,1024]{2,1,0:T(8,128)(2,1)}) custom-call(bf16[4,64,1024]{2,1,0:T(8,128)(2,1)} %bitcast.264, f32[64,1024]{1,0:T(8,128)} %get-tuple-element.186.refs_1_.refs_2_, f32[16,1024]{1,0:T(8,128)} %squeeze.43.refs_1_.refs_2_.refs_5_.refs_4_.refs_3_), custom_call_target="tpu_custom_call" | custom-call | tf_op jit(solution)/shard_map/pallas_call | solution.py:160
  177.1 4.5 fusion.122
  181.6 4.2 multiply_convert_fusion.3
  188.1 15.4 %shard_map.156 = (f32[64,1024]{1,0:T(8,128)}, bf16[64,1024]{1,0:T(8,128)(2,1)}, bf16[4,64,1024]{2,1,0:T(8,128)(2,1)}) custom-call(bf16[4,64,1024]{2,1,0:T(8,128)(2,1)} %bitcast.291, f32[64,1024]{1,0:T(8,128)} %get-tuple-element.79.refs_1_.refs_2_, f32[16,1024]{1,0:T(8,128)} %squeeze.43.refs_1_.refs_2_.refs_5_.refs_4_.refs_3_, ...), custom_call_target="tpu_custom_call" | custom-call | tf_op jit(solution)/shard_map/pallas_call | solution.py:160
  207.8 37.2 %shard_map.157 = (bf16[4,4,256,256]{3,2,1,0:T(8,128)(2,1)}, bf16[4,4,256,256]{3,2,1,0:T(8,128)(2,1)}, s32[4,4,8,256]{3,2,1,0:T(8,128)}) custom-call(bf16[256,256]{1,0:T(8,128)(2,1)} %convolution_convert_fusion.22.refs_0_, bf16[256,256]{1,0:T(8,128)(2,1)} %fusion.70.refs_1_, s32[8,256]{1,0:T(8,128)} %broadcast_in_dim.84.refs_2_), custom_call_target="tpu_custom_call" | custom-call | tf_op jit(solution)/shard_map/pallas_call | solution.py:340
  245.0 4.6 copy.47
  249.6 4.5 reshape_reshape.21
  254.1 4.6 copy.46
  258.8 4.4 reshape_reshape.20
  264.6 10.8 %fusion.130 = (f32[4,256]{1,0:T(4,128)S(1)}, f32[4,256,4096]{2,1,0:T(8,128)}) fusion(pred[256,4096]{1,0:T(8,128)(4,1)} %broadcast_compare_fusion, bf16[256,4,64]{0,2,1:T(8,128)(2,1)S(1)} %bitcast.334, bf16[4096,4,64]{0,2,1:T(8,128)(2,1)} %reshape_reshape.21), kind=kOutput, calls=%fused_computation.234 | convolution fusion | flops 553652224 | bytes 20058112 | tf_op jit(solution)/shard_map/sub | solution.py:616
  275.5 9.3 %fusion.65 = bf16[4,64,256]{2,1,0:T(8,128)(2,1)S(1)} fusion(bf16[4096,4,64]{0,2,1:T(8,128)(2,1)} %reshape_reshape.20, f32[4,256,4096]{2,1,0:T(8,128)} %get-tuple-element.178, f32[4,256]{1,0:T(4,128)S(1)} %get-tuple-element.177), kind=kOutput, calls=%fused_computation.82 | convolution fusion | flops 545325056 | bytes 19009536 | tf_op jit(solution)/shard_map/hrs,shd->rhd/dot_general | solution.py:624
  286.6 14.8 %shard_map.158 = (f32[64,1024]{1,0:T(8,128)}, f32[64,1024]{1,0:T(8,128)}, bf16[4,64,1024]{2,1,0:T(8,128)(2,1)}) custom-call(bf16[4,64,1024]{2,1,0:T(8,128)(2,1)} %bitcast.263, f32[64,1024]{1,0:T(8,128)} %convert_element_type.249.refs_1_.refs_2_, f32[16,1024]{1,0:T(8,128)} %squeeze.96.refs_3_.refs_2_.refs_4_), custom_call_target="tpu_custom_call" | custom-call | tf_op jit(solution)/shard_map/pallas_call | solution.py:160
  301.5 5.5 multiply_convert_fusion.2
  309.4 12.4 %shard_map.159 = (bf16[64,1024]{1,0:T(8,128)(2,1)}, f32[8,1024]{1,0:T(8,128)}, bf16[4,64,1024]{2,1,0:T(8,128)(2,1)}) custom-call(bf16[4,64,1024]{2,1,0:T(8,128)(2,1)} %bitcast.294, f32[64,1024]{1,0:T(8,128)} %get-tuple-element.85.refs_1_.refs_2_, bf16[64,1024]{1,0:T(8,128)(2,1)} %get-tuple-element.145.refs_2_, f32[16,1024]{1,0:T(8,128)} %squeeze.96.refs_3_.refs_2_.refs_4_), custom_call_target="tpu_custom_call" | custom-call | tf_op jit(solution)/shard_map/pallas_call | solution.py:160
  321.8 2.7 fusion.117
  326.0 14.2 %shard_map.160 = (f32[64,1024]{1,0:T(8,128)}, f32[8,1024]{1,0:T(8,128)}, bf16[4,64,1024]{2,1,0:T(8,128)(2,1)}) custom-call(bf16[4,64,1024]{2,1,0:T(8,128)(2,1)} %bitcast.292, f32[64,1024]{1,0:T(8,128)} %get-tuple-element.144.refs_1_, f32[64,1024]{1,0:T(8,128)} %get-tuple-element.85.refs_1_.refs_2_, f32[64,1024]{1,0:T(8,128)} %get-tuple-element.88.refs_3_, ...), custom_call_target="tpu_custom_call" | custom-call | tf_op jit(solution)/shard_map/pallas_call | solution.py:160
  341.7 8.1 %fusion.135 = f32[4,256,4096]{2,1,0:T(8,128)} fusion(bf16[256,4,64]{0,2,1:T(8,128)(2,1)S(1)} %bitcast.283, bf16[4096,4,64]{0,2,1:T(8,128)(2,1)S(1)} %copy-done), kind=kOutput, calls=%fused_computation.235 | convolution fusion | flops 536870912 | bytes 19005440 | tf_op jit(solution)/shard_map/rhd,shd->hrs/dot_general | solution.py:642
  349.7 22.6 %fusion.126 = (f32[4,64]{1,0:T(4,128)S(1)}, bf16[256,4,64]{0,2,1:T(8,128)(2,1)S(1)}) fusion(bf16[4096,4,64]{0,2,1:T(8,128)(2,1)} %reshape_reshape.21, f32[4,256,4096]{2,1,0:T(8,128)} %fusion.135, f32[4,256,4096]{2,1,0:T(8,128)} %get-tuple-element.178, f32[4,256]{1,0:T(4,128)S(1)} %get-tuple-element.177), kind=kOutput, calls=%fused_computation.230 | convolution fusion | flops 566366976 | bytes 35787776 | tf_op jit(solution)/shard_map/hrs,shd->rhd/dot_general | solution.py:646
  374.8 23.3 %fusion.38 = bf16[4096,4,64]{0,2,1:T(8,128)(2,1)} fusion(bf16[256,4,64]{0,2,1:T(8,128)(2,1)S(1)} %bitcast.335, f32[4,256,4096]{2,1,0:T(8,128)} %fusion.135, f32[4,256,4096]{2,1,0:T(8,128)} %get-tuple-element.178, f32[4,256]{1,0:T(4,128)S(1)} %get-tuple-element.177), kind=kOutput, calls=%fused_computation.34 | convolution fusion | flops 567284736 | bytes 35786752 | tf_op jit(solution)/shard_map/hrs,rhd->shd/dot_general | solution.py:652
  398.1 4.5 convert_element_type.261
  402.6 4.3 copy.48.refs_0_
  406.9 8.8 %fusion.36 = bf16[4096,4,64]{0,2,1:T(8,128)(2,1)} fusion(bf16[256,4,64]{0,2,1:T(8,128)(2,1)S(1)} %bitcast.284, f32[4,256,4096]{2,1,0:T(8,128)} %get-tuple-element.178, f32[4,256]{1,0:T(4,128)S(1)} %get-tuple-element.177), kind=kOutput, calls=%fused_computation.32 | convolution fusion | flops 546308096 | bytes 19009536 | tf_op jit(solution)/shard_map/hrs,rhd->shd/dot_general | solution.py:649
  415.7 4.5 convert_element_type.264
  420.2 4.7 copy.49.refs_1_
  425.0 41.7 %shard_map.161 = (f32[256,256]{1,0:T(8,128)}, f32[256,256]{1,0:T(8,128)}) custom-call(bf16[4,4,256,256]{3,2,1,0:T(8,128)(2,1)} %copy.48.refs_0_, bf16[4,4,256,256]{3,2,1,0:T(8,128)(2,1)} %copy.49.refs_1_), custom_call_target="tpu_custom_call" | custom-call | tf_op jit(solution)/shard_map/pallas_call | solution.py:468
  470.5 15.9 %shard_map.162 = (f32[64,1024]{1,0:T(8,128)}, f32[8,1024]{1,0:T(8,128)}, bf16[4,64,1024]{2,1,0:T(8,128)(2,1)}) custom-call(bf16[4,64,1024]{2,1,0:T(8,128)(2,1)} %bitcast.274, f32[64,1024]{1,0:T(8,128)} %get-tuple-element.92.refs_1_, f32[64,1024]{1,0:T(8,128)} %convert_element_type.249.refs_1_.refs_2_, f32[64,1024]{1,0:T(8,128)} %get-tuple-element.93.refs_3_, ...), custom_call_target="tpu_custom_call" | custom-call | tf_op jit(solution)/shard_map/pallas_call | solution.py:160
  491.7 3.4 fusion.116
  497.4 13.2 %shard_map.163 = (f32[64,1024]{1,0:T(8,128)}, f32[8,1024]{1,0:T(8,128)}, bf16[4,64,1024]{2,1,0:T(8,128)(2,1)}) custom-call(bf16[4,64,1024]{2,1,0:T(8,128)(2,1)} %bitcast.293, f32[64,1024]{1,0:T(8,128)} %convert_convert_fusion.refs_1_, f32[64,1024]{1,0:T(8,128)} %get-tuple-element.79.refs_1_.refs_2_, f32[64,1024]{1,0:T(8,128)} %get-tuple-element.96.refs_3_, ...), custom_call_target="tpu_custom_call" | custom-call | tf_op jit(solution)/shard_map/pallas_call | solution.py:160
  512.0 8.1 %fusion.136 = f32[4,256,4096]{2,1,0:T(8,128)} fusion(bf16[256,4,64]{0,2,1:T(8,128)(2,1)S(1)} %bitcast.285, bf16[4096,4,64]{0,2,1:T(8,128)(2,1)S(1)} %reshape_reshape.8), kind=kOutput, calls=%fused_computation.236 | convolution fusion | flops 536870912 | bytes 19005440 | tf_op jit(solution)/shard_map/rhd,shd->hrs/dot_general | solution.py:642
  520.1 22.5 %fusion.125 = (f32[4,64]{1,0:T(4,128)S(1)}, bf16[256,4,64]{0,2,1:T(8,128)(2,1)S(1)}) fusion(bf16[4096,4,64]{0,2,1:T(8,128)(2,1)} %reshape_reshape.9, f32[4,256,4096]{2,1,0:T(8,128)} %fusion.136, f32[4,256,4096]{2,1,0:T(8,128)} %get-tuple-element.175, f32[4,256]{1,0:T(4,128)S(1)} %get-tuple-element.174), kind=kOutput, calls=%fused_computation.229 | convolution fusion | flops 566366976 | bytes 35787776 | tf_op jit(solution)/shard_map/hrs,shd->rhd/dot_general | solution.py:646
  544.1 23.4 %fusion.41 = bf16[4096,4,64]{0,2,1:T(8,128)(2,1)} fusion(bf16[256,4,64]{0,2,1:T(8,128)(2,1)S(1)} %bitcast.333, f32[4,256,4096]{2,1,0:T(8,128)} %fusion.136, f32[4,256,4096]{2,1,0:T(8,128)} %get-tuple-element.175, f32[4,256]{1,0:T(4,128)S(1)} %get-tuple-element.174), kind=kOutput, calls=%fused_computation.35 | convolution fusion | flops 567284736 | bytes 35786752 | tf_op jit(solution)/shard_map/hrs,rhd->shd/dot_general | solution.py:652
  567.5 3.3 convert_element_type.278
  570.8 2.9 copy.50.refs_0_
  573.7 8.7 %fusion.37 = bf16[4096,4,64]{0,2,1:T(8,128)(2,1)} fusion(bf16[256,4,64]{0,2,1:T(8,128)(2,1)S(1)} %bitcast.286, f32[4,256,4096]{2,1,0:T(8,128)} %get-tuple-element.175, f32[4,256]{1,0:T(4,128)S(1)} %get-tuple-element.174), kind=kOutput, calls=%fused_computation.33 | convolution fusion | flops 546308096 | bytes 19009536 | tf_op jit(solution)/shard_map/hrs,rhd->shd/dot_general | solution.py:649
  582.5 3.3 convert_element_type.281
  585.8 2.7 copy.51.refs_1_
  588.5 37.1 %shard_map.164 = (f32[256,256]{1,0:T(8,128)}, f32[256,256]{1,0:T(8,128)}) custom-call(bf16[4,4,256,256]{3,2,1,0:T(8,128)(2,1)} %copy.50.refs_0_, bf16[4,4,256,256]{3,2,1,0:T(8,128)(2,1)} %copy.51.refs_1_), custom_call_target="tpu_custom_call" | custom-call | tf_op jit(solution)/shard_map/pallas_call | solution.py:468
  629.5 9.3 %shard_map.165 = (f32[64,1024]{1,0:T(8,128)}, f32[8,1024]{1,0:T(8,128)}) custom-call(bf16[4,64,1024]{2,1,0:T(8,128)(2,1)} %bitcast.265, f32[64,1024]{1,0:T(8,128)} %get-tuple-element.100.refs_1_, f32[64,1024]{1,0:T(8,128)} %get-tuple-element.186.refs_1_.refs_2_, f32[16,1024]{1,0:T(8,128)} %squeeze.43.refs_1_.refs_2_.refs_5_.refs_4_.refs_3_), custom_call_target="tpu_custom_call" | custom-call | tf_op jit(solution)/shard_map/pallas_call | solution.py:160
  661.4 61.3 %shard_map.166 = (f32[16,128]{1,0:T(8,128)}, f32[64,256]{1,0:T(8,128)}, f32[64,256]{1,0:T(8,128)}, f32[64,256]{1,0:T(8,128)}, f32[64,256]{1,0:T(8,128)}, /*index...) custom-call(f32[2,4,4,16,128]{4,3,2,1,0:T(8,128)} %pad_maximum_fusion.6.refs_0_, ...), custom_call_target="tpu_custom_call" | custom-call | tf_op jit(solution)/shard_map/pallas_call | solution.py:572
  (249 shorter events, 88.6 us)
Async XLA Ops:
  119.2 10.5 %copy-start.1 = (bf16[4,64,1024]{2,1,0:T(8,128)(2,1)S(1)}, bf16[4,64,1024]{2,1,0:T(8,128)(2,1)}, u32[]{:S(2)}) copy-start(bf16[4,64,1024]{2,1,0:T(8,128)(2,1)} %get-tuple-element.69) | copy-start | bytes 1572868
  131.1 9.1 %copy-start.50 = (bf16[256,256]{0,1:T(8,128)(2,1)}, bf16[256,256]{0,1:T(8,128)(2,1)S(1)}, u32[]{:S(2)}) copy-start(bf16[256,256]{0,1:T(8,128)(2,1)S(1)} %fusion.69) | copy-start | bytes 393220
  131.1 9.1 %copy-start.17 = (pred[256,4096]{1,0:T(8,128)(4,1)S(1)}, pred[256,4096]{1,0:T(8,128)(4,1)}, u32[]{:S(2)}) copy-start(pred[256,4096]{1,0:T(8,128)(4,1)} %broadcast_compare_fusion) | copy-start | bytes 3145732
  150.8 8.7 %copy-start.18 = (bf16[2,4,4,64,256]{4,3,2,1,0:T(8,128)(2,1)S(1)}, bf16[2,4,4,64,256]{4,3,2,1,0:T(8,128)(2,1)}, u32[]{:S(2)}) copy-start(bf16[2,4,4,64,256]{4,3,2,1,0:T(8,128)(2,1)} %get-tuple-element.75) | copy-start | bytes 3145732
  150.8 26.3 %copy-start.7 = (bf16[2,4,4,64,1024]{4,3,2,1,0:T(8,128)(2,1)S(1)}, bf16[2,4,4,64,1024]{4,3,2,1,0:T(8,128)(2,1)}, u32[]{:S(2)}) copy-start(bf16[2,4,4,64,1024]{4,3,2,1,0:T(8,128)(2,1)} %get-tuple-element.77) | copy-start | bytes 12582916
  159.4 22.1 %copy-start.22 = (bf16[4,64,256]{2,1,0:T(8,128)(2,1)}, bf16[4,64,256]{2,1,0:T(8,128)(2,1)S(1)}, u32[]{:S(2)}) copy-start(bf16[4,64,256]{2,1,0:T(8,128)(2,1)S(1)} %fusion.62) | copy-start | bytes 393220
  177.1 4.5 copy-start.29
  181.5 4.2 copy-start.12
  181.6 4.3 copy-start.14
  185.8 63.8 %copy-start.31 = (bf16[256,1024]{1,0:T(8,128)(2,1)}, bf16[256,1024]{1,0:T(8,128)(2,1)S(1)}, u32[]{:S(2)}) copy-start(bf16[256,1024]{1,0:T(8,128)(2,1)S(1)} %get-tuple-element.148) | copy-start | bytes 1572868
  254.1 9.1 %copy-start.3 = (bf16[4,64,1024]{2,1,0:T(8,128)(2,1)S(1)}, bf16[4,64,1024]{2,1,0:T(8,128)(2,1)}, u32[]{:S(2)}) copy-start(bf16[4,64,1024]{2,1,0:T(8,128)(2,1)} %get-tuple-element.81) | copy-start | bytes 1572868
  275.4 9.3 %copy-start.5 = (bf16[1,4,4,64,256]{4,3,2,1,0:T(8,128)(2,1)S(1)}, bf16[1,4,4,64,256]{4,3,2,1,0:T(8,128)(2,1)}, u32[]{:S(2)}) copy-start(bf16[1,4,4,64,256]{4,3,2,1,0:T(8,128)(2,1)} %get-tuple-element.156) | copy-start | bytes 1572868
  275.4 10.5 %copy-start.24 = (bf16[64,1024]{1,0:T(8,128)(2,1)S(1)}, bf16[64,1024]{1,0:T(8,128)(2,1)}, u32[]{:S(2)}) copy-start(bf16[64,1024]{1,0:T(8,128)(2,1)} %get-tuple-element.80) | copy-start | bytes 393220
  275.4 26.0 %copy-start.15 = (bf16[1,4,4,64,1024]{4,3,2,1,0:T(8,128)(2,1)S(1)}, bf16[1,4,4,64,1024]{4,3,2,1,0:T(8,128)(2,1)}, u32[]{:S(2)}) copy-start(bf16[1,4,4,64,1024]{4,3,2,1,0:T(8,128)(2,1)} %get-tuple-element.183) | copy-start | bytes 6291460
  284.7 22.3 %copy-start.26 = (bf16[4,64,256]{2,1,0:T(8,128)(2,1)}, bf16[4,64,256]{2,1,0:T(8,128)(2,1)S(1)}, u32[]{:S(2)}) copy-start(bf16[4,64,256]{2,1,0:T(8,128)(2,1)S(1)} %fusion.65) | copy-start | bytes 393220
  301.5 6.3 copy-start.16
  324.5 17.2 %copy-start.37 = (bf16[256,1024]{1,0:T(8,128)(2,1)}, bf16[256,1024]{1,0:T(8,128)(2,1)S(1)}, u32[]{:S(2)}) copy-start(bf16[256,1024]{1,0:T(8,128)(2,1)S(1)} %get-tuple-element.143) | copy-start | bytes 1572868
  324.5 17.2 %copy-start = (bf16[4096,4,64]{0,2,1:T(8,128)(2,1)S(1)}, bf16[4096,4,64]{0,2,1:T(8,128)(2,1)}, u32[]{:S(2)}) copy-start(bf16[4096,4,64]{0,2,1:T(8,128)(2,1)} %reshape_reshape.20) | copy-start | bytes 6291460
  372.3 25.8 %copy-start.42 = (bf16[256,4,64]{0,2,1:T(8,128)(2,1)}, bf16[256,4,64]{0,2,1:T(8,128)(2,1)S(1)}, u32[]{:S(2)}) copy-start(bf16[256,4,64]{0,2,1:T(8,128)(2,1)S(1)} %get-tuple-element.165) | copy-start | bytes 393220
  425.0 41.7 %copy-start.6 = (f32[256,1024]{1,0:T(8,128)S(1)}, f32[256,1024]{1,0:T(8,128)}, u32[]{:S(2)}) copy-start(f32[256,1024]{1,0:T(8,128)} %fusion.85) | copy-start | bytes 3145732
  466.7 21.9 %copy-start.8 = (f32[256,256]{1,0:T(8,128)S(1)}, f32[256,256]{1,0:T(8,128)}, u32[]{:S(2)}) copy-start(f32[256,256]{1,0:T(8,128)} %get-tuple-element.91) | copy-start | bytes 786436
  466.7 22.7 %copy-start.48 = (f32[8,1024]{1,0:T(8,128)S(1)}, f32[8,1024]{1,0:T(8,128)}, u32[]{:S(2)}) copy-start(f32[8,1024]{1,0:T(8,128)} %get-tuple-element.104) | copy-start | bytes 98308
  491.0 4.1 copy-start.13
  491.7 4.9 copy-start.19
  520.1 24.0 %copy-start.51 = (bf16[256,256]{0,1:T(8,128)(2,1)S(1)}, bf16[256,256]{0,1:T(8,128)(2,1)}, u32[]{:S(2)}) copy-start(bf16[256,256]{0,1:T(8,128)(2,1)} %copy-done.50) | copy-start | bytes 393220
  625.6 14.9 %copy-start.9 = (f32[256,256]{1,0:T(8,128)S(1)}, f32[256,256]{1,0:T(8,128)}, u32[]{:S(2)}) copy-start(f32[256,256]{1,0:T(8,128)} %get-tuple-element.99) | copy-start | bytes 786436
  625.6 15.7 %copy-start.49 = (f32[8,1024]{1,0:T(8,128)S(1)}, f32[8,1024]{1,0:T(8,128)}, u32[]{:S(2)}) copy-start(f32[8,1024]{1,0:T(8,128)} %get-tuple-element.102) | copy-start | bytes 98308
  625.6 17.4 %copy-start.28 = (f32[16,16,128]{2,1,0:T(8,128)S(1)}, f32[16,16,128]{2,1,0:T(8,128)}, u32[]{:S(2)}) copy-start(f32[16,16,128]{2,1,0:T(8,128)} %pad.18.clone) | copy-start | bytes 393220
  625.6 18.1 %copy-start.4 = (bf16[4,64,1024]{2,1,0:T(8,128)(2,1)S(1)}, bf16[4,64,1024]{2,1,0:T(8,128)(2,1)}, u32[]{:S(2)}) copy-start(bf16[4,64,1024]{2,1,0:T(8,128)(2,1)} %get-tuple-element.81) | copy-start | bytes 1572868
  625.7 18.1 %copy-start.43 = (bf16[256,4,64]{0,2,1:T(8,128)(2,1)S(1)}, bf16[256,4,64]{0,2,1:T(8,128)(2,1)}, u32[]{:S(2)}) copy-start(bf16[256,4,64]{0,2,1:T(8,128)(2,1)} %copy-done.42) | copy-start | bytes 393220
  625.7 18.5 %copy-start.2 = (bf16[4,64,1024]{2,1,0:T(8,128)(2,1)S(1)}, bf16[4,64,1024]{2,1,0:T(8,128)(2,1)}, u32[]{:S(2)}) copy-start(bf16[4,64,1024]{2,1,0:T(8,128)(2,1)} %get-tuple-element.69) | copy-start | bytes 1572868
  625.7 18.5 %copy-start.45 = (bf16[256,4,64]{0,2,1:T(8,128)(2,1)S(1)}, bf16[256,4,64]{0,2,1:T(8,128)(2,1)}, u32[]{:S(2)}) copy-start(bf16[256,4,64]{0,2,1:T(8,128)(2,1)} %copy-done.44) | copy-start | bytes 393220
  629.5 16.1 %copy-start.21 = (f32[256,256]{1,0:T(8,128)S(1)}, f32[256,256]{1,0:T(8,128)}, u32[]{:S(2)}) copy-start(f32[256,256]{1,0:T(8,128)} %get-tuple-element.90) | copy-start | bytes 786436
  646.0 4.3 copy-start.10
  646.0 4.3 copy-start.27
  647.4 3.3 copy-start.11
  647.4 3.3 copy-start.23
  648.8 3.3 copy-start.35
  648.8 3.3 copy-start.38
  650.3 2.6 copy-start.30
  650.3 2.6 copy-start.41
  653.7 2.4 copy-start.34
  653.7 3.1 copy-start.32
  653.7 3.1 copy-start.39
  657.6 2.4 copy-start.25
  657.6 2.4 copy-start.47
  657.6 3.0 copy-start.20
  657.6 3.0 copy-start.46
  (4 other events, 6.9 us)

commit v2 on v1

--- a/solution.py
+++ b/solution.py
@@ -12,7 +12,6 @@
 EPSILON = 1e-06
 MASKED_SCORE = -1e30
 RING = 4
-CHUNKS = 2
 VMEM_LIMIT = 56 * 1024 * 1024
 F32 = jnp.float32
 BF16 = jnp.bfloat16
@@ -56,6 +55,10 @@
     return back, jnp.sum(grad * normed, axis=0, keepdims=True), jnp.sum(grad, axis=0, keepdims=True)
 
 
+PLUS, FAR, MINUS = 1, 2, 3
+SUBS = 2
+
+
 def tensor_kernel(function, n_rows, n_vecs, n_out, n_sums, reduce, gather, with_seg, *refs):
     refs = list(refs)
     take = lambda count: [refs.pop(0) for _ in range(count)]
@@ -67,27 +70,26 @@
     sums_out = take(1)[0] if n_sums else None
     full = take(1)[0] if gather else None
     seg_out = take(1)[0] if with_seg else None
-    landing = take(1)[0] if reduce else None
+    passing, joined, from_minus, from_plus = take(4) if reduce else [None] * 4
     send, recv, local = take(3)
 
     me = lax.axis_index("tensor")
     barrier = pltpu.get_barrier_semaphore()
-    for k in range(1, RING):
+    for k in (PLUS, MINUS):
         pl.semaphore_signal(
             barrier, inc=1, device_id={"tensor": step(me, k)}, device_id_type=MESH
         )
-    pl.semaphore_wait(barrier, RING - 1)
-
-    total_rows = (rows_in[0] if rows_in else part).shape[-2]
-    chunk = total_rows // CHUNKS
+    pl.semaphore_wait(barrier, 2)
+
+    chunk = rows_in[0].shape[0] // (2 * SUBS)
     started = []
 
     def push(source, target, kind, index, k):
         copy = pltpu.make_async_remote_copy(
             src_ref=source,
             dst_ref=target,
-            send_sem=send.at[kind, index, k - 1],
-            recv_sem=recv.at[kind, index, k - 1],
+            send_sem=send.at[kind, index],
+            recv_sem=recv.at[kind, index],
             device_id={"tensor": step(me, k)},
             device_id_type=MESH,
         )
@@ -95,46 +97,71 @@
         started.append(copy)
         return copy
 
-    reduces = {}
+    chunks = range(2 * SUBS)
+    here = lambda c: pl.ds(c * chunk, chunk)
+    onward = lambda c: PLUS if c % 2 == 0 else MINUS
+    aside = lambda c: MINUS if c % 2 == 0 else PLUS
+    side_of = {PLUS: from_minus, MINUS: from_plus}
+    way, straight, summed = {}, {}, {}
     if reduce:
-        for c in range(CHUNKS):
-            here = pl.ds(c * chunk, chunk)
-            for k in range(1, RING):
-                reduces[c, k] = push(
-                    part.at[step(me, k), here], landing.at[k - 1, here], 0, c, k
-                )
+        for c in chunks:
+            way[c] = push(part.at[step(me, FAR), here(c)], passing.at[here(c)], 0, c, onward(c))
+        for c in chunks:
+            straight[c] = push(
+                part.at[step(me, aside(c)), here(c)], side_of[aside(c)].at[here(c)], 1, c, aside(c)
+            )
+        for c in chunks:
+            way[c].wait_recv()
+            joined[here(c)] = (
+                part[step(me, onward(c)), here(c)].astype(F32) + passing[here(c)].astype(F32)
+            ).astype(BF16)
+            summed[c] = push(joined.at[here(c)], side_of[onward(c)].at[here(c)], 2, c, onward(c))
     last = []
     if with_seg:
         own = pltpu.make_async_copy(seg_in, seg_out.at[me], local)
         own.start()
-        last += [push(seg_in, seg_out.at[me], 2, 0, k) for k in range(1, RING)]
+        seg_up = push(seg_in, seg_out.at[me], 6, 0, PLUS)
+        seg_down = push(seg_in, seg_out.at[me], 6, 1, MINUS)
+        last.append(seg_down)
     sums = [None] * n_sums
-    for c in range(CHUNKS):
-        here = pl.ds(c * chunk, chunk)
+    ups, downs = {}, {}
+    for c in chunks:
         total = None
         if reduce:
-            for k in range(1, RING):
-                reduces[c, k].wait_recv()
-            total = part[me, here].astype(F32)
-            for k in range(1, RING):
-                total = total + landing[k - 1, here].astype(F32)
+            straight[c].wait_recv()
+            summed[c].wait_recv()
+            total = (
+                part[me, here(c)].astype(F32)
+                + from_minus[here(c)].astype(F32)
+                + from_plus[here(c)].astype(F32)
+            )
         spread, outs, parts = function(
-            total, [ref[here].astype(F32) for ref in rows_in], vecs
+            total, [ref[here(c)].astype(F32) for ref in rows_in], vecs
         )
         if gather:
-            full[me, here] = spread.astype(BF16)
-            last += [push(full.at[me, here], full.at[me, here], 1, c, k) for k in range(1, RING)]
+            full[me, here(c)] = spread.astype(BF16)
+            ups[c] = push(full.at[me, here(c)], full.at[me, here(c)], 3, c, PLUS)
+            downs[c] = push(full.at[me, here(c)], full.at[me, here(c)], 4, c, MINUS)
         for ref, value in zip(rows_out, outs):
-            ref[here] = value.astype(ref.dtype)
+            ref[here(c)] = value.astype(ref.dtype)
         sums = [new if old is None else old + new for old, new in zip(sums, parts)]
+    if gather:
+        for c in chunks:
+            (ups if c % 2 == 0 else downs)[c].wait_recv()
+            came = full.at[step(me, aside(c)), here(c)]
+            last.append(push(came, came, 5, c, onward(c)))
+            last.append((downs if c % 2 == 0 else ups)[c])
     if n_sums:
         sums_out[...] = jnp.concatenate(
             sums + [jnp.zeros((8 - n_sums, sums[0].shape[1]), F32)], axis=0
-        ) if n_sums < 8 else jnp.concatenate(sums, axis=0)
+        )
+    if with_seg:
+        own.wait()
+        seg_up.wait_recv()
+        came = seg_out.at[step(me, MINUS)]
+        last.append(push(came, came, 6, 2, PLUS))
     for copy in last:
         copy.wait_recv()
-    if with_seg:
-        own.wait()
     for copy in started:
         copy.wait_send()
 
@@ -151,10 +178,10 @@
         shapes.append(jax.ShapeDtypeStruct((RING, height, width), BF16))
     if with_seg:
         shapes.append(jax.ShapeDtypeStruct((RING,) + seg.shape, seg.dtype))
-    scratch = [pltpu.VMEM((RING - 1, height, width), BF16)] if reduce else []
+    scratch = [pltpu.VMEM((height, width), BF16)] * 4 if reduce else []
     scratch += [
-        pltpu.SemaphoreType.DMA((3, CHUNKS, RING - 1)),
-        pltpu.SemaphoreType.DMA((3, CHUNKS, RING - 1)),
+        pltpu.SemaphoreType.DMA((7, 2 * SUBS)),
+        pltpu.SemaphoreType.DMA((7, 2 * SUBS)),
         pltpu.SemaphoreType.DMA,
     ]
     return pl.pallas_call(
@@ -242,10 +269,6 @@
     return None, [hidden_grad + part], [gain, shift]
 
 
-def place(lane_first, own, other):
-    return (other, own) if lane_first else (own, other)
-
-
 def dp_neighbour(y, z, along_z, k):
     if along_z:
         return {"dp": y * RING + step(z, k)}
@@ -256,7 +279,7 @@
     barrier = pltpu.get_barrier_semaphore()
     count = 0
     for along_z in (True, False):
-        for k in range(1, RING):
+        for k in (PLUS, MINUS):
             pl.semaphore_signal(
                 barrier, inc=1, device_id=dp_neighbour(y, z, along_z, k), device_id_type=MESH
             )
@@ -267,6 +290,23 @@
         )
         count += 1
     return barrier, count
+
+
+def pusher(send, recv, started):
+    def push(index, kind, k, source, target, device):
+        copy = pltpu.make_async_remote_copy(
+            src_ref=source,
+            dst_ref=target,
+            send_sem=send.at[index, kind, k],
+            recv_sem=recv.at[index, kind, k],
+            device_id=device,
+            device_id_type=MESH,
+        )
+        copy.start()
+        started.append(copy)
+        return copy
+
+    return push
 
 
 def gather_kernel(pieces, n_in, n_out, with_sibling, *refs):
@@ -278,58 +318,93 @@
     barrier, count = dp_barrier(y, z, section)
     pl.semaphore_wait(barrier, count)
     started = []
-
-    def push(index, stage, k, source, target, device):
-        copy = pltpu.make_async_remote_copy(
-            src_ref=source,
-            dst_ref=target,
-            send_sem=send.at[index, stage, k],
-            recv_sem=recv.at[index, stage, k],
-            device_id=device,
-            device_id_type=MESH,
-        )
-        copy.start()
-        started.append(copy)
-        return copy
-
-    def block(index, ys, zs):
-        number, pre, along_z = pieces[index]
+    push = pusher(send, recv, started)
+    every = range(len(pieces))
+
+    def block(i, along, across, rows=None):
+        number, pre, along_z = pieces[i]
         lead = ((section,) if with_sibling else ()) + pre
-        return outs[number].at[lead + (ys, zs)]
-
-    own, first, second, across = [], {}, {}, []
-    for index, (number, pre, along_z) in enumerate(pieces):
+        ys, zs = (across, along) if along_z else (along, across)
+        ys = ys if isinstance(ys, slice) else step(y, ys) if ys else y
+        zs = zs if isinstance(zs, slice) else step(z, zs) if zs else z
+        return outs[number].at[lead + (ys, zs) + (() if rows is None else (rows,))]
+
+    def first_way(i, k):
+        return dp_neighbour(y, z, pieces[i][2], k)
+
+    def second_way(i, k):
+        return dp_neighbour(y, z, not pieces[i][2], k)
+
+    def halves(i):
+        height = outs[pieces[i][0]].shape[-2]
+        if height < 32:
+            return {PLUS: None}
+        return {PLUS: pl.ds(0, height // 2), MINUS: pl.ds(height // 2, height // 2)}
+
+    own, first, onward, second, relayed = {}, {}, {}, {}, {}
+
+    def spread(i, offset, source):
+        for k in (PLUS, MINUS):
+            second[i, offset, k] = push(
+                i, 2 if k == PLUS else 3, offset, source, block(i, offset, 0), second_way(i, k)
+            )
+
+    for i in every:
+        number, pre, _ = pieces[i]
         source = ins[number].at[pre] if pre else ins[number]
-        copy = pltpu.make_async_copy(source, block(index, y, z), local.at[index])
-        copy.start()
-        own.append(copy)
-        for k in range(1, RING):
-            first[index, k] = push(
-                index, 0, k, source, block(index, y, z), dp_neighbour(y, z, along_z, k)
-            )
-
-    def line(index, k):
-        along_z = pieces[index][2]
-        return block(index, step(y, k), slice(None)) if along_z else block(index, slice(None), step(z, k))
-
-    for index, (number, pre, along_z) in enumerate(pieces):
-        own[index].wait()
-        for k in range(1, RING):
-            first[index, k].wait_recv()
-        for k in range(1, RING):
-            second[index, k] = push(
-                index, 1, k, line(index, 0), line(index, 0), dp_neighbour(y, z, not along_z, k)
-            )
+        for k in (PLUS, MINUS):
+            first[i, k] = push(i, 0, k, source, block(i, 0, 0), first_way(i, k))
+        spread(i, 0, source)
+        own[i] = pltpu.make_async_copy(source, block(i, 0, 0), local.at[i])
+        own[i].start()
+    for i in every:
+        split = halves(i)
+        for k in (PLUS, MINUS):
+            first[i, k].wait_recv()
+            came = RING - k
+            if k in split:
+                onward[i, k] = push(
+                    i, 1, k, block(i, came, 0, split[k]), block(i, came, 0, split[k]), first_way(i, k)
+                )
+            spread(i, came, block(i, came, 0))
+    ways = {0: PLUS, MINUS: MINUS, PLUS: PLUS, FAR: MINUS}
+
+    def relay(i, offset):
+        k = ways[offset]
+        second[i, offset, k].wait_recv()
+        came = block(i, offset, RING - k)
+        relayed[i, offset] = push(i, 4, offset, came, came, second_way(i, k))
+
+    for i in every:
+        relay(i, 0)
+    for i in every:
+        for k in halves(i):
+            onward[i, k].wait_recv()
+        spread(i, FAR, block(i, FAR, 0))
+    across = []
+
+    def pass_on(i, line):
+        came = block(i, slice(None), line)
+        across.append(push(i, 5, line, came, came, {"section": 1 - section}))
+
+    for i in every:
+        relay(i, MINUS)
+        relay(i, PLUS)
+        own[i].wait()
         if with_sibling:
-            across.append(
-                push(index, 2, 0, line(index, 0), line(index, 0), {"section": 1 - section})
-            )
-    for index in range(len(pieces)):
-        for k in range(1, RING):
-            second[index, k].wait_recv()
-            if with_sibling:
-                came = line(index, RING - k)
-                across.append(push(index, 2, k, came, came, {"section": 1 - section}))
+            pass_on(i, 0)
+    for i in every:
+        relay(i, FAR)
+        for offset, k in ways.items():
+            second[i, offset, RING - k].wait_recv()
+        if with_sibling:
+            pass_on(i, PLUS)
+            pass_on(i, MINUS)
+    for i in every:
+        for offset in range(RING):
+            relayed[i, offset].wait_recv()
+        if with_sibling:
+            pass_on(i, FAR)
     for copy in across:
         copy.wait_recv()
     for copy in started:
@@ -343,137 +418,189 @@
         in_specs=[vmem_spec()] * len(ins),
         out_specs=[any_spec()] * len(outs),
         scratch_shapes=[
-            pltpu.SemaphoreType.DMA((len(pieces), 3, RING)),
-            pltpu.SemaphoreType.DMA((len(pieces), 3, RING)),
+            pltpu.SemaphoreType.DMA((len(pieces), 6, RING)),
+            pltpu.SemaphoreType.DMA((len(pieces), 6, RING)),
             pltpu.SemaphoreType.DMA((len(pieces),)),
         ],
         compiler_params=comm_params(cid),
     )(*ins)
 
 
-def rows_loop(height, size, body):
-    if height <= size:
-        body(pl.ds(0, height))
-        return
-
-    def each(number, carry):
-        body(pl.ds(pl.multiple_of(number * size, size), size))
-        return carry
-
-    lax.fori_loop(0, height // size, each, 0)
-
-
-def scatter_first(index, along_z, source, landing, y, z, push):
-    copies = []
-    for k in range(1, RING):
-        line = (
-            source.at[:, step(z, k)] if along_z else source.at[step(y, k)]
-        )
-        copies.append(
-            push(index, 0, k, line, landing.at[k - 1], dp_neighbour(y, z, along_z, k))
-        )
-    return copies
-
-
-def scatter_second(index, along_z, source, landing, middle, arrivals, y, z, push, copies):
-    for copy in copies:
-        copy.wait_recv()
-    height, width = source.shape[-2:]
-    size = max(8, min(height, 65536 // width))
-    second = []
-    for k in list(range(1, RING)) + [0]:
-        at = step(y, k) if along_z else step(z, k)
-
-        def add(here):
-            value = (source[at, z, here] if along_z else source[y, at, here]).astype(F32)
-            for slot in range(RING - 1):
-                value = value + landing[slot, at, here].astype(F32)
-            middle[k, here] = value.astype(middle.dtype)
-
-        rows_loop(height, size, add)
-        if k:
-            second.append(
-                push(index, 1, k, middle.at[k], arrivals.at[k - 1], dp_neighbour(y, z, not along_z, k))
-            )
-    return second
-
-
-def scatter_last(middle, arrivals, out, copies):
-    for copy in copies:
-        copy.wait_recv()
-    height, width = middle.shape[-2:]
-    size = max(8, min(height, 65536 // width))
-
-    def add(here):
-        value = middle[0, here].astype(F32)
-        for slot in range(RING - 1):
-            value = value + arrivals[slot, here].astype(F32)
-        out[here] = value
-
-    rows_loop(height, size, add)
-
-
-def pusher(send, recv, started):
-    def push(index, stage, k, source, target, device):
-        copy = pltpu.make_async_remote_copy(
-            src_ref=source,
-            dst_ref=target,
-            send_sem=send.at[index, stage, k],
-            recv_sem=recv.at[index, stage, k],
-            device_id=device,
-            device_id_type=MESH,
-        )
-        copy.start()
-        started.append(copy)
-        return copy
-
-    return push
+class Scatter:
+    ORDER = (FAR, PLUS, MINUS, 0)
+    WAYS = {FAR: PLUS, 0: PLUS, PLUS: MINUS, MINUS: MINUS}
+
+    def __init__(self, index, along_z, source, buffers, y, z, push):
+        self.index, self.along_z, self.source = index, along_z, source
+        self.passing, self.joined, self.summed, self.straight, self.middle = buffers[:5]
+        self.far_two, self.joined_two, self.summed_two, self.straight_two = buffers[5:]
+        self.y, self.z, self.push = y, z, push
+        self.height, self.width = source.shape[-2:]
+
+    def at(self, along, across):
+        ys, zs = (across, along) if self.along_z else (along, across)
+        return step(self.y, ys), step(self.z, zs)
+
+    def way(self, first, k):
+        return dp_neighbour(self.y, self.z, self.along_z == first, k)
+
+    def add(self, target, terms, top=0, height=None):
+        height = self.height if height is None else height
+        size = max(8, min(height, 32768 // self.width))
+
+        def part(here):
+            value = terms[0](here).astype(F32)
+            for term in terms[1:]:
+                value = value + term(here).astype(F32)
+            target[here] = value.astype(target.dtype)
+
+        if height <= size:
+            part(pl.ds(top, height))
+            return
+
+        def each(number, carry):
+            part(pl.ds(pl.multiple_of(top + number * size, size), size))
+            return carry
+
+        lax.fori_loop(0, height // size, each, 0)
+
+    def begin(self):
+        self.via, self.direct, self.after = {}, {}, {}
+        for j in self.ORDER:
+            self.via[j] = self.push(
+                self.index, 0, j, self.source.at[self.at(FAR, j)], self.passing.at[j],
+                self.way(True, self.WAYS[j]),
+            )
+        for j in self.ORDER:
+            k = RING - self.WAYS[j]
+            self.direct[j] = self.push(
+                self.index, 1, j, self.source.at[self.at(k, j)], self.straight.at[j],
+                self.way(True, k),
+            )
+
+    def join(self):
+        for j in self.ORDER:
+            self.via[j].wait_recv()
+            k = self.WAYS[j]
+            at_y, at_z = self.at(k, j)
+            self.add(
+                self.joined.at[j],
+                [lambda h: self.source[at_y, at_z, h], lambda h: self.passing[j, h]],
+            )
+            self.after[j] = self.push(
+                self.index, 2, j, self.joined.at[j], self.summed.at[j], self.way(True, k)
+            )
+
+    def turn(self):
+        half = self.height // 2
+        low, high = pl.ds(0, half), pl.ds(half, half)
+        send = lambda kind, slot, source, target, k: self.push(
+            self.index, kind, slot, source, target, self.way(False, k)
+        )
+        for j in self.ORDER:
+            self.direct[j].wait_recv()
+            self.after[j].wait_recv()
+            at_y, at_z = self.at(0, j)
+            self.add(
+                self.middle.at[j],
+                [
+                    lambda h: self.source[at_y, at_z, h],
+                    lambda h: self.summed[j, h],
+                    lambda h: self.straight[j, h],
+                ],
+            )
+            if j == FAR:
+                self.via_two = [
+                    send(3, 0, self.middle.at[j, low], self.far_two.at[low], PLUS),
+                    send(3, 1, self.middle.at[j, high], self.far_two.at[high], MINUS),
+                ]
+            if j == PLUS:
+                high_copy = send(4, 1, self.middle.at[j, high], self.straight_two.at[high], PLUS)
+            if j == MINUS:
+                low_copy = send(4, 0, self.middle.at[j, low], self.straight_two.at[low], MINUS)
+        self.direct_two = [low_copy, high_copy]
+
+    def join_two(self):
+        half = self.height // 2
+        self.after_two = []
+        for number, (top, k) in enumerate(((0, PLUS), (half, MINUS))):
+            self.via_two[number].wait_recv()
+            self.add(
+                self.joined_two,
+                [lambda h: self.middle[k, h], lambda h: self.far_two[h]],
+                top,
+                half,
+            )
+            here = pl.ds(top, half)
+            self.after_two.append(
+                self.push(
+                    self.index, 5, number, self.joined_two.at[here], self.summed_two.at[here],
+                    self.way(False, k),
+                )
+            )
+
+    def finish(self, out):
+        for copy in self.direct_two + self.after_two:
+            copy.wait_recv()
+        self.add(
+            out,
+            [
+                lambda h: self.middle[0, h],
+                lambda h: self.summed_two[h],
+                lambda h: self.straight_two[h],
+            ],
+        )
+
+    @staticmethod
+    def scratch(block, dtype):
+        return [pltpu.VMEM((RING,) + block, dtype)] * 5 + [pltpu.VMEM(block, dtype)] * 4
+
+
+SCATTER_BUFFERS = 9
 
 
 def scatter_kernel(orders, *refs):
     n = len(orders)
     ins, outs = refs[:n], refs[n : 2 * n]
-    landings, middles, arrivals = refs[2 * n : 3 * n], refs[3 * n : 4 * n], refs[4 * n : 5 * n]
-    send, recv = refs[5 * n :]
+    buffers = refs[2 * n : 2 * n + n * SCATTER_BUFFERS]
+    send, recv = refs[2 * n + n * SCATTER_BUFFERS :]
     rank = lax.axis_index("dp")
     y, z = rank // RING, lax.rem(rank, RING)
     barrier, count = dp_barrier(y, z, None)
     pl.semaphore_wait(barrier, count)
     started = []
     push = pusher(send, recv, started)
-    first = [
-        scatter_first(i, orders[i], ins[i], landings[i], y, z, push) for i in range(n)
-    ]
-    second = [
-        scatter_second(i, orders[i], ins[i], landings[i], middles[i], arrivals[i], y, z, push, first[i])
+    parts = [
+        Scatter(
+            i, orders[i], ins[i], buffers[i * SCATTER_BUFFERS : (i + 1) * SCATTER_BUFFERS], y, z, push
+        )
         for i in range(n)
     ]
-    for i in range(n):
-        scatter_last(middles[i], arrivals[i], outs[i], second[i])
+    for part in parts:
+        part.begin()
+    for part in parts:
+        part.join()
+    for part in parts:
+        part.turn()
+    for part in parts:
+        part.join_two()
+    for part, out in zip(parts, outs):
+        part.finish(out)
     for copy in started:
         copy.wait_send()
 
 
-def scatter_scratch(block, dtype):
-    return (
-        pltpu.VMEM((RING - 1, RING) + block, dtype),
-        pltpu.VMEM((RING,) + block, dtype),
-        pltpu.VMEM((RING - 1,) + block, dtype),
-    )
-
-
 def scatter_call(cid, orders, ins):
     blocks = [value.shape[2:] for value in ins]
-    sets = [scatter_scratch(block, BF16) for block in blocks]
     return pl.pallas_call(
         functools.partial(scatter_kernel, orders),
         out_shape=[jax.ShapeDtypeStruct(block, F32) for block in blocks],
         in_specs=[vmem_spec()] * len(ins),
         out_specs=[vmem_spec()] * len(ins),
-        scratch_shapes=[group[i] for i in range(3) for group in sets]
+        scratch_shapes=[one for block in blocks for one in Scatter.scratch(block, BF16)]
         + [
-            pltpu.SemaphoreType.DMA((len(ins), 2, RING)),
-            pltpu.SemaphoreType.DMA((len(ins), 2, RING)),
+            pltpu.SemaphoreType.DMA((len(ins), 6, RING)),
+            pltpu.SemaphoreType.DMA((len(ins), 6, RING)),
         ],
         compiler_params=comm_params(cid),
     )(*ins)
@@ -485,7 +612,8 @@
     take = lambda count: [refs.pop(0) for _ in range(count)]
     ins, extras = take(n), take(n_extra)
     outs, extra_outs = take(n), take(n_extra)
-    siblings, owns, landings, middles, arrivals = take(n), take(n), take(n), take(n), take(n)
+    siblings, owns = take(n), take(n)
+    buffers = [take(SCATTER_BUFFERS) for _ in range(n)]
     vector_own, vector_parts = take(2)
     send, recv, local, extra_send, extra_recv = take(5)
     rank = lax.axis_index("dp")
@@ -503,7 +631,7 @@
     other = {"section": 1 - section}
     across, local_copies = [], []
     for i in range(n):
-        across.append(push(i, 2, 0, ins[i].at[1 - section], siblings[i], other))
+        across.append(push(i, 6, 0, ins[i].at[1 - section], siblings[i], other))
         copy = pltpu.make_async_copy(ins[i].at[section], owns[i], local.at[i])
         copy.start()
         local_copies.append(copy)
@@ -519,7 +647,7 @@
         )
         copy.start()
         extra_copies.append(copy)
-    first = []
+    parts = []
     for i in range(n):
         local_copies[i].wait()
         across[i].wait_recv()
@@ -533,21 +661,20 @@
             return carry
 
         lax.fori_loop(0, RING * RING, add, 0)
-        first.append(scatter_first(i, orders[i], own, landings[i], y, z, push))
-    second = [
-        scatter_second(i, orders[i], owns[i], landings[i], middles[i], arrivals[i], y, z, push, first[i])
-        for i in range(n)
-    ]
-    for i in range(n):
-        scatter_last(
-            middles[i], arrivals[i], vector_own if i == 0 else outs[i], second[i]
-        )
+        parts.append(Scatter(i, orders[i], own, buffers[i], y, z, push))
+        parts[i].begin()
+    for part in parts:
+        part.join()
+    for part in parts:
+        part.turn()
+    for part in parts:
+        part.join_two()
+    for i, part in enumerate(parts):
+        part.finish(vector_own if i == 0 else outs[i])
         if i == 0:
             vector_parts[me] = vector_own[...]
             vector_copies = [
-                push(
-                    0, 3, k, vector_own, vector_parts.at[me], {"tensor": step(me, k)}
-                )
+                push(0, 7, k, vector_own, vector_parts.at[me], {"tensor": step(me, k)})
                 for k in range(1, RING)
             ]
     for copy in vector_copies:
@@ -564,7 +691,6 @@
 
 def final_call(cid, orders, ins, extras):
     blocks = [value.shape[3:] for value in ins]
-    sets = [scatter_scratch(block, value.dtype) for block, value in zip(blocks, ins)]
     square = [
         pltpu.VMEM((RING, RING) + block, value.dtype) for block, value in zip(blocks, ins)
     ]
@@ -577,12 +703,12 @@
         out_specs=[vmem_spec()] * (count + extra),
         scratch_shapes=square
         + square
-        + [group[i] for i in range(3) for group in sets]
+        + [one for block, value in zip(blocks, ins) for one in Scatter.scratch(block, value.dtype)]
         + [
             pltpu.VMEM(blocks[0], F32),
             pltpu.VMEM((RING,) + blocks[0], F32),
-            pltpu.SemaphoreType.DMA((count, 4, RING)),
-            pltpu.SemaphoreType.DMA((count, 4, RING)),
+            pltpu.SemaphoreType.DMA((count, 8, RING)),
+            pltpu.SemaphoreType.DMA((count, 8, RING)),
             pltpu.SemaphoreType.DMA((count,)),
             pltpu.SemaphoreType.DMA((extra,)),
             pltpu.SemaphoreType.DMA((extra,)),
@@ -603,56 +729,155 @@
     return lax.dot_general(former, latter, (((0,), (0,)), ((), ())), preferred_element_type=F32)
 
 
-def attention_weights(queries, keys_full, seg_rows, seg_keys):
-    heads_here = queries.shape[1] // HEAD_DIM
-    query_heads = queries.reshape(queries.shape[0], heads_here, HEAD_DIM)
-    key_heads = keys_full.reshape(keys_full.shape[0], heads_here, HEAD_DIM)
-    raw_scores = jnp.einsum(
-        "rhd,shd->hrs", query_heads, key_heads, preferred_element_type=F32
-    ) * HEAD_DIM ** (-0.5)
-    allowed = seg_rows[:, None] == seg_keys[None, :]
-    masked = jnp.where(allowed[None], raw_scores, MASKED_SCORE)
-    highest = jnp.max(masked, axis=-1, keepdims=True)
-    exponent = jnp.exp(masked - highest)
-    total = jnp.sum(exponent, axis=-1, keepdims=True)
-    return exponent / total
-
-
-def attention_forward(queries, keys_full, values_full, seg_rows, seg_keys):
-    heads_here = queries.shape[1] // HEAD_DIM
-    soft = attention_weights(queries, keys_full, seg_rows, seg_keys)
-    mixed = jnp.einsum(
-        "hrs,shd->rhd",
-        soft.astype(BF16),
-        values_full.reshape(-1, heads_here, HEAD_DIM),
-        preferred_element_type=F32,
+KEY_BLOCK = 256
+
+
+def head_stack(values, scale):
+    column = lax.broadcasted_iota(jnp.int32, values.shape, 1) // HEAD_DIM
+    heads_here = values.shape[1] // HEAD_DIM
+    zero = jnp.zeros_like(values)
+    scaled = values * jnp.asarray(scale, values.dtype)
+    return jnp.concatenate(
+        [jnp.where(column == head, scaled, zero) for head in range(heads_here)], axis=0
     )
-    return mixed.reshape(queries.shape).astype(BF16)
-
-
-def attention_backward(queries, keys_full, values_full, mixed_grad, seg_rows, seg_keys):
-    local_width = queries.shape[1]
-    heads_here = local_width // HEAD_DIM
-    head_scale = HEAD_DIM ** (-0.5)
-    soft = attention_weights(queries, keys_full, seg_rows, seg_keys)
-    mixed_split = mixed_grad.reshape(-1, heads_here, HEAD_DIM)
-    value_heads = values_full.reshape(-1, heads_here, HEAD_DIM)
-    key_heads = keys_full.reshape(-1, heads_here, HEAD_DIM)
-    query_heads = queries.reshape(-1, heads_here, HEAD_DIM)
-    prob_grad = jnp.einsum("rhd,shd->hrs", mixed_split, value_heads, preferred_element_type=F32)
-    row_delta = jnp.sum(prob_grad * soft, axis=-1)
-    score_grad = soft * (prob_grad - row_delta[..., None])
-    score_low = (score_grad * head_scale).astype(BF16)
-    query_grad = jnp.einsum(
-        "hrs,shd->rhd", score_low, key_heads, preferred_element_type=F32
-    ).reshape(-1, local_width)
-    values_grad = jnp.einsum(
-        "hrs,rhd->shd", soft.astype(BF16), mixed_split, preferred_element_type=F32
-    ).reshape(-1, local_width)
-    keys_grad = jnp.einsum(
-        "hrs,rhd->shd", score_low, query_heads, preferred_element_type=F32
-    ).reshape(-1, local_width)
-    return query_grad, keys_grad.astype(BF16), values_grad.astype(BF16)
+
+
+def block_scores(key_block, stack, seg_column, seg_wide):
+    scores = flat_dot(key_block, stack)
+    return jnp.where(seg_column == seg_wide, scores, MASKED_SCORE)
+
+
+def attention_forward_kernel(q_ref, k_ref, v_ref, seg_q_ref, seg_k_ref, mixed_ref, wide_ref, lse_ref, stack, acc):
+    group, width = q_ref.shape
+    heads_here = width // HEAD_DIM
+    stack[...] = head_stack(q_ref[...], HEAD_DIM ** (-0.5))
+    acc[...] = jnp.zeros_like(acc)
+    seg_wide = jnp.concatenate([seg_q_ref[0:1, :]] * heads_here, axis=1)
+    seq = k_ref.shape[0]
+
+    def each(number, carry):
+        highest, total = carry
+        here = pl.ds(pl.multiple_of(number * KEY_BLOCK, KEY_BLOCK), KEY_BLOCK)
+        scores = block_scores(k_ref[here, :], stack[...], seg_k_ref[here, 0:1], seg_wide)
+        above = jnp.maximum(highest, jnp.max(scores, axis=0, keepdims=True))
+        weights = jnp.exp(scores - above)
+        fade = jnp.exp(highest - above)
+        total = total * fade + jnp.sum(weights, axis=0, keepdims=True)
+        low = weights.astype(BF16)
+        turned = v_ref[here, :].T
+        for head in range(heads_here):
+            rows = pl.ds(head * HEAD_DIM, HEAD_DIM)
+            lanes = slice(head * group, (head + 1) * group)
+            term = jnp.dot(
+                turned[head * HEAD_DIM : (head + 1) * HEAD_DIM], low[:, lanes],
+                preferred_element_type=F32,
+            )
+            acc[rows, :] = acc[rows, :] * fade[:, lanes] + term
+        return above, total
+
+    start = jnp.full((1, group * heads_here), MASKED_SCORE, F32)
+    highest, total = lax.fori_loop(
+        0, seq // KEY_BLOCK, each, (start, jnp.zeros_like(start))
+    )
+    inverse = 1.0 / total
+    for head in range(heads_here):
+        rows = pl.ds(head * HEAD_DIM, HEAD_DIM)
+        wide_ref[rows, :] = acc[rows, :] * inverse[:, head * group : (head + 1) * group]
+    mixed_ref[...] = wide_ref[...].T.astype(BF16)
+    lse_ref[...] = jnp.broadcast_to(highest + jnp.log(total), lse_ref.shape)
+
+
+def local_params():
+    return pltpu.CompilerParams(vmem_limit_bytes=VMEM_LIMIT)
+
+
+def attention_forward(queries, keys_full, values_full, seg_wide, seg_column):
+    group, width = queries.shape
+    heads_here = width // HEAD_DIM
+    return pl.pallas_call(
+        attention_forward_kernel,
+        out_shape=[
+            jax.ShapeDtypeStruct((group, width), BF16),
+            jax.ShapeDtypeStruct((width, group), F32),
+            jax.ShapeDtypeStruct((8, group * heads_here), F32),
+        ],
+        in_specs=[vmem_spec()] * 5,
+        out_specs=[vmem_spec()] * 3,
+        scratch_shapes=[
+            pltpu.VMEM((group * heads_here, width), BF16),
+            pltpu.VMEM((width, group), F32),
+        ],
+        compiler_params=local_params(),
+    )(queries, keys_full, values_full, seg_wide, seg_column)
+
+
+def attention_backward_kernel(
+    q_ref, k_ref, v_ref, grad_ref, wide_ref, lse_ref, seg_q_ref, seg_k_ref,
+    dq_ref, dk_ref, dv_ref,
+    stack, plain, grad_stack, grad_plain, acc,
+):
+    group, width = q_ref.shape
+    heads_here = width // HEAD_DIM
+    scale = HEAD_DIM ** (-0.5)
+    stack[...] = head_stack(q_ref[...], scale)
+    plain[...] = head_stack(q_ref[...], 1.0)
+    grad_stack[...] = head_stack(grad_ref[...], scale)
+    grad_plain[...] = head_stack(grad_ref[...], 1.0)
+    acc[...] = jnp.zeros_like(acc)
+    seg_wide = jnp.concatenate([seg_q_ref[0:1, :]] * heads_here, axis=1)
+    seq = k_ref.shape[0]
+    product = grad_ref[...].astype(F32).T * wide_ref[...]
+    delta = scale * jnp.concatenate(
+        [
+            jnp.sum(product[head * HEAD_DIM : (head + 1) * HEAD_DIM], axis=0, keepdims=True)
+            for head in range(heads_here)
+        ],
+        axis=1,
+    )
+    lse = lse_ref[0:1, :]
+
+    def each(number, carry):
+        here = pl.ds(pl.multiple_of(number * KEY_BLOCK, KEY_BLOCK), KEY_BLOCK)
+        key_block = k_ref[here, :]
+        scores = block_scores(key_block, stack[...], seg_k_ref[here, 0:1], seg_wide)
+        weights = jnp.exp(scores - lse)
+        dv_ref[here, :] = jnp.dot(
+            weights.astype(BF16), grad_plain[...], preferred_element_type=F32
+        ).astype(BF16)
+        prob_grad = flat_dot(v_ref[here, :], grad_stack[...])
+        low = (weights * (prob_grad - delta)).astype(BF16)
+        dk_ref[here, :] = jnp.dot(low, plain[...], preferred_element_type=F32).astype(BF16)
+        turned = key_block.T
+        for head in range(heads_here):
+            rows = pl.ds(head * HEAD_DIM, HEAD_DIM)
+            acc[rows, :] += jnp.dot(
+                turned[head * HEAD_DIM : (head + 1) * HEAD_DIM],
+                low[:, head * group : (head + 1) * group],
+                preferred_element_type=F32,
+            )
+        return carry
+
+    lax.fori_loop(0, seq // KEY_BLOCK, each, 0)
+    dq_ref[...] = acc[...].T
+
+
+def attention_backward(queries, keys_full, values_full, mixed_grad, wide, lse, seg_wide, seg_column):
+    group, width = queries.shape
+    heads_here = width // HEAD_DIM
+    seq = keys_full.shape[0]
+    return pl.pallas_call(
+        attention_backward_kernel,
+        out_shape=[
+            jax.ShapeDtypeStruct((group, width), F32),
+            jax.ShapeDtypeStruct((seq, width), BF16),
+            jax.ShapeDtypeStruct((seq, width), BF16),
+        ],
+        in_specs=[vmem_spec()] * 8,
+        out_specs=[vmem_spec()] * 3,
+        scratch_shapes=[pltpu.VMEM((group * heads_here, width), BF16)] * 4
+        + [pltpu.VMEM((width, group), F32)],
+        compiler_params=local_params(),
+    )(queries, keys_full, values_full, mixed_grad, wide, lse, seg_wide, seg_column)
 
 
 WEIGHT_PIECES = (
@@ -718,7 +943,6 @@
     seg_wide = jnp.broadcast_to(seg_rows[None], (8, group))
     inputs = my_tokens
     kept = []
-    seg_keys = None
     for layer in range(2):
         vec = small_rows[layer]
         normed = normed.reshape(group, width)
@@ -745,8 +969,10 @@
         keys_full = keys_full.reshape(-1, local_width)
         values_full = values_full.reshape(-1, local_width)
         if layer == 0:
-            seg_keys = seg_full[:, :, 0].reshape(-1)
-        mixed = attention_forward(queries, keys_full, values_full, seg_rows, seg_keys)
+            seg_column = jnp.broadcast_to(
+                seg_full[:, :, 0].reshape(-1)[:, None], (keys_full.shape[0], 128)
+            )
+        mixed, wide, lse = attention_forward(queries, keys_full, values_full, seg_wide, seg_column)
         part = flat_dot(mixed, full_out[layer]).astype(BF16).reshape(RING, rows, width)
         attn_out, hidden, normed_two = tensor_call(
             3, middle_rows, part, [inputs.astype(F32)], [vec], [F32, F32], 0, True
@@ -756,7 +982,7 @@
         activated = gelu_exact(pre_act).astype(BF16)
         part = flat_dot(activated, full_down[layer]).astype(BF16).reshape(RING, rows, width)
         step_kept = [inputs, normed, queries, keys_full, values_full, mixed, attn_out, hidden]
-        step_kept += [normed_two, pre_act, activated]
+        step_kept += [normed_two, pre_act, activated, wide, lse]
         if layer == 0:
             mlp_first, between, normed = tensor_call(
                 4, end_rows_first, part, [hidden], [vec, small_rows[1]], [F32, BF16], 0, True
@@ -774,7 +1000,7 @@
     for layer in (1, 0):
         vec = small_rows[layer]
         inputs, normed, queries, keys_full, values_full, mixed, attn_out, hidden = kept[layer][:8]
-        normed_two, pre_act, activated = kept[layer][8:]
+        normed_two, pre_act, activated, wide, lse = kept[layer][8:]
         mlp_rows = mlp_rows.reshape(group, width)
         act_grad = jnp.dot(mlp_rows, full_down[layer], preferred_element_type=F32)
         grad_down = rows_dot(mlp_rows, activated)
@@ -790,7 +1016,7 @@
         mixed_grad = jnp.dot(attn_rows, full_out[layer], preferred_element_type=F32).astype(BF16)
         grad_out = rows_dot(attn_rows, mixed)
         query_grad, keys_part, values_part = attention_backward(
-            queries, keys_full, values_full, mixed_grad, seg_rows, seg_keys
+            queries, keys_full, values_full, mixed_grad, wide, lse, seg_wide, seg_column
         )
         keys_grad, values_grad = scatter_call(
             7,

time: 747 us -> 542 us (0.73); the launches traced: 735 us -> 538 us
  matrix products: 222 us -> 56.1 us
  local copies, waits for them, and re-layouts: 90.4 us -> 25.4 us
  Pallas kernels: 394 us -> 430 us
    dot_general x10 -> x0, matrix products: 143 us -> none  [the longest x2 46.7 us: attention_backward(): jnp.einsum('hrs,rhd->shd', score_low, query_heads, preferred_element_type...]
    pallas_call x0 -> x4, Pallas kernels: none -> 68.6 us  [the longest x2 39.4 us: attention_backward(): pl.pallas_call(attention_backward_kernel, out_shape=[jax.ShapeDtypeStruct...]
    pallas_call x2, Pallas kernels: 78.8 us -> 45.2 us  [scatter_call(): pl.pallas_call(functools.partial(scatter_kernel, orders), out_shape=[jax....]
    pallas_call x3, Pallas kernels: 131 us -> 100 us  [gather_call(): pl.pallas_call(functools.partial(gather_kernel, pieces, len(ins), len(out...]
    convert_element_type x8 -> x0, local copies, waits for them, and re-layouts: 30.3 us -> none  [attention_backward(): return (query_grad, keys_grad.astype(BF16), values_grad.astype(BF16))]
    pallas_call x1, Pallas kernels: 61.3 us -> 84.6 us  [final_call(): pl.pallas_call(functools.partial(final_kernel, orders, extra), out_shape=...]
    sub x2 -> x0, matrix products: 21.4 us -> none  [attention_weights(): exponent = jnp.exp(masked - highest)]
    pallas_call x4 -> x0, local copies, waits for them, and re-layouts: 18.5 us -> none  [gather_call(): pl.pallas_call(functools.partial(gather_kernel, pieces, len(ins), len(out...]
where the time goes in v2:
time: 542 us; the launch traced here: 538 us
  Pallas kernels  430 us (79%)
  matrix products  56.1 us (10%)
  local copies, waits for them, and re-layouts  25.4 us (5%)
  other arithmetic  25 us (5%)
    pallas_call x9, Pallas kernels, tensor_call(): pl.pallas_call(functools.partial(tensor_kernel, function, len(rows), len(...  131 us
    pallas_call x3, Pallas kernels, gather_call(): pl.pallas_call(functools.partial(gather_kernel, pieces, len(ins), len(out...  100 us
    pallas_call x1, Pallas kernels, final_call(): pl.pallas_call(functools.partial(final_kernel, orders, extra), out_shape=...  84.6 us
    pallas_call x2, Pallas kernels, scatter_call(): pl.pallas_call(functools.partial(scatter_kernel, orders), out_shape=[jax....  45.2 us
    pallas_call x2, Pallas kernels, attention_backward(): pl.pallas_call(attention_backward_kernel, out_shape=[jax.ShapeDtypeStruct...  39.4 us
    pallas_call x2, Pallas kernels, attention_forward(): pl.pallas_call(attention_forward_kernel, out_shape=[jax.ShapeDtypeStruct(...  29.2 us
    dot_general x12, matrix products, flat_dot(): lax.dot_general(former, latter, (((1,), (1,)), ((), ())), preferred_eleme...  18.5 us
    dot_general x6, matrix products, shards(): jnp.dot(normed, full_qkv[layer, which], preferred_element_type=F32)  12.7 us

profile of v2, /device:TPU:1, one launch (start us, length us, event | category | flops | bytes accessed | tf_op | source)
XLA Modules:
  0.0 537.8 jit_solution(9579489954045605210)
XLA Ops:
  2.0 48.6 %shard_map.152 = (bf16[2,3,4,4,64,256]{5,4,3,2,1,0:T(8,128)(2,1)}, bf16[2,4,4,64,256]{4,3,2,1,0:T(8,128)(2,1)}, bf16[2,4,4,64,1024]{4,3,2,1,0:T(8,128)(2,1)}, bf...) custom-call(bf16[3,64,256]{2,1,0:T(8,128)(2,1)} %bitcast.264, bf16[64,256]{1,0:T(8,128)(2,1)} %bitcast.270, ...), custom_call_target="tpu_custom_call" | custom-call | tf_op jit(solution)/shard_map/pallas_call | solution.py:415
  51.7 2.0 fusion.44
  55.1 13.2 %shard_map.153 = (bf16[4,64,1024]{2,1,0:T(8,128)(2,1)}, s32[4,8,128]{2,1,0:T(8,128)}) custom-call(bf16[64,1024]{1,0:T(8,128)(2,1)} %get-tuple-element.201.refs_0_, f32[16,1024]{1,0:T(8,128)} %squeeze.43.refs_1_.refs_2_.refs_5_.refs_4_.refs_3_, s32[8,128]{1,0:T(8,128)} %scatter.4.refs_2_), custom_call_target="tpu_custom_call" | custom-call | tf_op jit(solution)/shard_map/pallas_call | solution.py:187
  68.4 2.2 fusion.2.q_ref
  70.6 2.2 convolution_convert_fusion.21.refs_0_
  72.7 2.0 fusion.3.refs_1_
  76.1 27.6 %shard_map.154 = (bf16[4,4,256,256]{3,2,1,0:T(8,128)(2,1)}, bf16[4,4,256,256]{3,2,1,0:T(8,128)(2,1)}, s32[4,4,8,256]{3,2,1,0:T(8,128)}) custom-call(bf16[256,256]{1,0:T(8,128)(2,1)} %convolution_convert_fusion.21.refs_0_, bf16[256,256]{1,0:T(8,128)(2,1)} %fusion.3.refs_1_, s32[8,256]{1,0:T(8,128)} %broadcast_in_dim.53.refs_2_.seg_q_ref), custom_call_target="tpu_custom_call" | custom-call | tf_op jit(solution)/shard_map/pallas_call | solution.py:415
  104.7 2.9 broadcast_in_dim.55.seg_k_ref
  107.6 14.7 %shard_map.155 = (bf16[256,256]{1,0:T(8,128)(2,1)}, f32[256,256]{1,0:T(8,128)}, f32[8,1024]{1,0:T(8,128)}) custom-call(bf16[256,256]{1,0:T(8,128)(2,1)} %fusion.2.q_ref, bf16[4096,256]{1,0:T(8,128)(2,1)} %bitcast.173, bf16[4096,256]{1,0:T(8,128)(2,1)} %bitcast.175, s32[8,256]{1,0:T(8,128)} %broadcast_in_dim.53.refs_2_.seg_q_ref, ...), custom_call_target="tpu_custom_call" | custom-call | tf_op jit(solution)/shard_map/pallas_call | solution.py:797
  124.3 14.7 %shard_map.156 = (f32[64,1024]{1,0:T(8,128)}, f32[64,1024]{1,0:T(8,128)}, bf16[4,64,1024]{2,1,0:T(8,128)(2,1)}) custom-call(bf16[4,64,1024]{2,1,0:T(8,128)(2,1)} %bitcast.222, f32[64,1024]{1,0:T(8,128)} %get-tuple-element.200.refs_1_.refs_2_, f32[16,1024]{1,0:T(8,128)} %squeeze.43.refs_1_.refs_2_.refs_5_.refs_4_.refs_3_), custom_call_target="tpu_custom_call" | custom-call | tf_op jit(solution)/shard_map/pallas_call | solution.py:187
  139.0 4.4 fusion.48
  143.5 4.1 multiply_convert_fusion.1
  147.5 1.5 convolution_convert_fusion.17
  149.8 16.4 %shard_map.157 = (f32[64,1024]{1,0:T(8,128)}, bf16[64,1024]{1,0:T(8,128)(2,1)}, bf16[4,64,1024]{2,1,0:T(8,128)(2,1)}) custom-call(bf16[4,64,1024]{2,1,0:T(8,128)(2,1)} %bitcast.241, f32[64,1024]{1,0:T(8,128)} %get-tuple-element.92.refs_1_.refs_2_, f32[16,1024]{1,0:T(8,128)} %squeeze.43.refs_1_.refs_2_.refs_5_.refs_4_.refs_3_, ...), custom_call_target="tpu_custom_call" | custom-call | tf_op jit(solution)/shard_map/pallas_call | solution.py:187
  166.2 2.2 fusion.4.q_ref
  168.4 2.2 convolution_convert_fusion.20.refs_0_
  170.5 2.0 fusion.5.refs_1_
  172.5 24.1 %shard_map.158 = (bf16[4,4,256,256]{3,2,1,0:T(8,128)(2,1)}, bf16[4,4,256,256]{3,2,1,0:T(8,128)(2,1)}, s32[4,4,8,256]{3,2,1,0:T(8,128)}) custom-call(bf16[256,256]{1,0:T(8,128)(2,1)} %convolution_convert_fusion.20.refs_0_, bf16[256,256]{1,0:T(8,128)(2,1)} %fusion.5.refs_1_, s32[8,256]{1,0:T(8,128)} %broadcast_in_dim.53.refs_2_.seg_q_ref), custom_call_target="tpu_custom_call" | custom-call | tf_op jit(solution)/shard_map/pallas_call | solution.py:415
  196.7 14.6 %shard_map.159 = (bf16[256,256]{1,0:T(8,128)(2,1)}, f32[256,256]{1,0:T(8,128)}, f32[8,1024]{1,0:T(8,128)}) custom-call(bf16[256,256]{1,0:T(8,128)(2,1)} %fusion.4.q_ref, bf16[4096,256]{1,0:T(8,128)(2,1)} %bitcast.177, bf16[4096,256]{1,0:T(8,128)(2,1)} %bitcast.179, s32[8,256]{1,0:T(8,128)} %broadcast_in_dim.53.refs_2_.seg_q_ref, ...), custom_call_target="tpu_custom_call" | custom-call | tf_op jit(solution)/shard_map/pallas_call | solution.py:797
  211.3 2.2 convolution_convert_fusion.12
  214.2 14.4 %shard_map.160 = (f32[64,1024]{1,0:T(8,128)}, f32[64,1024]{1,0:T(8,128)}, bf16[4,64,1024]{2,1,0:T(8,128)(2,1)}) custom-call(bf16[4,64,1024]{2,1,0:T(8,128)(2,1)} %bitcast.221, f32[64,1024]{1,0:T(8,128)} %convert_element_type.159.refs_1_.refs_2_, f32[16,1024]{1,0:T(8,128)} %squeeze.96.refs_3_.refs_2_.refs_4_), custom_call_target="tpu_custom_call" | custom-call | tf_op jit(solution)/shard_map/pallas_call | solution.py:187
  228.6 5.2 multiply_convert_fusion
  233.8 1.6 convolution_convert_fusion.16
  235.4 14.9 %shard_map.161 = (bf16[64,1024]{1,0:T(8,128)(2,1)}, f32[8,1024]{1,0:T(8,128)}, bf16[4,64,1024]{2,1,0:T(8,128)(2,1)}) custom-call(bf16[4,64,1024]{2,1,0:T(8,128)(2,1)} %bitcast.244, f32[64,1024]{1,0:T(8,128)} %get-tuple-element.99.refs_1_.refs_2_, bf16[64,1024]{1,0:T(8,128)(2,1)} %get-tuple-element.169.refs_2_, f32[16,1024]{1,0:T(8,128)} %squeeze.96.refs_3_.refs_2_.refs_4_), custom_call_target="tpu_custom_call" | custom-call | tf_op jit(solution)/shard_map/pallas_call | solution.py:187
  250.3 2.4 fusion.43
  252.8 1.5 convolution_convert_fusion.15
  254.3 15.1 %shard_map.162 = (f32[64,1024]{1,0:T(8,128)}, f32[8,1024]{1,0:T(8,128)}, bf16[4,64,1024]{2,1,0:T(8,128)(2,1)}) custom-call(bf16[4,64,1024]{2,1,0:T(8,128)(2,1)} %bitcast.242, f32[64,1024]{1,0:T(8,128)} %get-tuple-element.168.refs_1_, f32[64,1024]{1,0:T(8,128)} %get-tuple-element.99.refs_1_.refs_2_, f32[64,1024]{1,0:T(8,128)} %get-tuple-element.102.refs_3_, ...), custom_call_target="tpu_custom_call" | custom-call | tf_op jit(solution)/shard_map/pallas_call | solution.py:187
  269.5 2.0 convolution_convert_fusion.19.grad_ref
  271.5 19.6 %shard_map.163 = (f32[256,256]{1,0:T(8,128)}, bf16[4096,256]{1,0:T(8,128)(2,1)}, bf16[4096,256]{1,0:T(8,128)(2,1)}) custom-call(bf16[256,256]{1,0:T(8,128)(2,1)} %fusion.4.q_ref, bf16[4096,256]{1,0:T(8,128)(2,1)} %bitcast.178, bf16[4096,256]{1,0:T(8,128)(2,1)} %bitcast.180, bf16[256,256]{1,0:T(8,128)(2,1)} %convolution_convert_fusion.19.grad_ref, ...), custom_call_target="tpu_custom_call" | custom-call | tf_op jit(solution)/shard_map/pallas_call | solution.py:868
  291.1 1.5 fusion.19
  292.6 22.0 %shard_map.164 = (f32[256,256]{1,0:T(8,128)}, f32[256,256]{1,0:T(8,128)}) custom-call(bf16[4,4,256,256]{3,2,1,0:T(8,128)(2,1)} %bitcast.215, bf16[4,4,256,256]{3,2,1,0:T(8,128)(2,1)} %bitcast.216), custom_call_target="tpu_custom_call" | custom-call | tf_op jit(solution)/shard_map/pallas_call | solution.py:595
  314.6 1.5 convolution_add_fusion.3
  316.1 2.2 fusion
  318.3 15.7 %shard_map.165 = (f32[64,1024]{1,0:T(8,128)}, f32[8,1024]{1,0:T(8,128)}, bf16[4,64,1024]{2,1,0:T(8,128)(2,1)}) custom-call(bf16[4,64,1024]{2,1,0:T(8,128)(2,1)} %bitcast.232, f32[64,1024]{1,0:T(8,128)} %get-tuple-element.111.refs_1_, f32[64,1024]{1,0:T(8,128)} %convert_element_type.159.refs_1_.refs_2_, f32[64,1024]{1,0:T(8,128)} %get-tuple-element.112.refs_3_, ...), custom_call_target="tpu_custom_call" | custom-call | tf_op jit(solution)/shard_map/pallas_call | solution.py:187
  338.9 3.5 fusion.42
  342.4 1.6 convolution_convert_fusion.14
  344.8 16.2 %shard_map.166 = (f32[64,1024]{1,0:T(8,128)}, f32[8,1024]{1,0:T(8,128)}, bf16[4,64,1024]{2,1,0:T(8,128)(2,1)}) custom-call(bf16[4,64,1024]{2,1,0:T(8,128)(2,1)} %bitcast.243, f32[64,1024]{1,0:T(8,128)} %convert_convert_fusion.refs_1_, f32[64,1024]{1,0:T(8,128)} %get-tuple-element.92.refs_1_.refs_2_, f32[64,1024]{1,0:T(8,128)} %get-tuple-element.115.refs_3_, ...), custom_call_target="tpu_custom_call" | custom-call | tf_op jit(solution)/shard_map/pallas_call | solution.py:187
  360.9 2.0 convolution_convert_fusion.18.grad_ref
  362.9 19.8 %shard_map.167 = (f32[256,256]{1,0:T(8,128)}, bf16[4096,256]{1,0:T(8,128)(2,1)}, bf16[4096,256]{1,0:T(8,128)(2,1)}) custom-call(bf16[256,256]{1,0:T(8,128)(2,1)} %fusion.2.q_ref, bf16[4096,256]{1,0:T(8,128)(2,1)} %bitcast.174, bf16[4096,256]{1,0:T(8,128)(2,1)} %bitcast.176, bf16[256,256]{1,0:T(8,128)(2,1)} %convolution_convert_fusion.18.grad_ref, ...), custom_call_target="tpu_custom_call" | custom-call | tf_op jit(solution)/shard_map/pallas_call | solution.py:868
  384.0 23.2 %shard_map.168 = (f32[256,256]{1,0:T(8,128)}, f32[256,256]{1,0:T(8,128)}) custom-call(bf16[4,4,256,256]{3,2,1,0:T(8,128)(2,1)} %bitcast.213, bf16[4,4,256,256]{3,2,1,0:T(8,128)(2,1)} %bitcast.214), custom_call_target="tpu_custom_call" | custom-call | tf_op jit(solution)/shard_map/pallas_call | solution.py:595
  409.7 10.2 %shard_map.169 = (f32[64,1024]{1,0:T(8,128)}, f32[8,1024]{1,0:T(8,128)}) custom-call(bf16[4,64,1024]{2,1,0:T(8,128)(2,1)} %bitcast.223, f32[64,1024]{1,0:T(8,128)} %get-tuple-element.124.refs_1_, f32[64,1024]{1,0:T(8,128)} %get-tuple-element.200.refs_1_.refs_2_, f32[16,1024]{1,0:T(8,128)} %squeeze.43.refs_1_.refs_2_.refs_5_.refs_4_.refs_3_), custom_call_target="tpu_custom_call" | custom-call | tf_op jit(solution)/shard_map/pallas_call | solution.py:187
  434.2 2.3 pad_maximum_fusion.refs_5_
  438.5 2.4 pad_maximum_fusion.1.refs_6_
  442.3 84.6 %shard_map.170 = (f32[16,128]{1,0:T(8,128)}, f32[64,256]{1,0:T(8,128)}, f32[64,256]{1,0:T(8,128)}, f32[64,256]{1,0:T(8,128)}, f32[64,256]{1,0:T(8,128)}, /*index...) custom-call(f32[2,4,4,16,128]{4,3,2,1,0:T(8,128)} %pad_maximum_fusion.6.refs_0_, ...), custom_call_target="tpu_custom_call" | custom-call | tf_op jit(solution)/shard_map/pallas_call | solution.py:698
  526.9 1.8 maximum_select_fusion.1
  528.7 1.9 maximum_select_fusion
  530.6 1.6 maximum_bitcast_fusion
  534.7 1.5 copy.76
  (201 shorter events, 40.3 us)
Async XLA Ops:
  0.6 53.8 %copy-start.39 = (s32[2,64]{1,0:T(2,128)S(1)}, s32[2,64]{1,0:T(2,128)}, u32[]{:S(2)}) copy-start(s32[2,64]{1,0:T(2,128)} %param.12) | copy-start | bytes 1540
  68.3 4.4 copy-start
  107.6 14.7 %copy-start.15 = (bf16[2,4,4,64,256]{4,3,2,1,0:T(8,128)(2,1)S(1)}, bf16[2,4,4,64,256]{4,3,2,1,0:T(8,128)(2,1)}, u32[]{:S(2)}) copy-start(bf16[2,4,4,64,256]{4,3,2,1,0:T(8,128)(2,1)} %get-tuple-element.88) | copy-start | bytes 3145732
  107.6 31.4 %copy-start.2 = (bf16[2,4,4,64,1024]{4,3,2,1,0:T(8,128)(2,1)S(1)}, bf16[2,4,4,64,1024]{4,3,2,1,0:T(8,128)(2,1)}, u32[]{:S(2)}) copy-start(bf16[2,4,4,64,1024]{4,3,2,1,0:T(8,128)(2,1)} %get-tuple-element.90) | copy-start | bytes 12582916
  122.3 0.9 copy-start.19
  139.0 4.4 copy-start.22
  143.4 4.1 copy-start.10
  143.5 4.1 copy-start.12
  147.5 18.6 %copy-start.24 = (bf16[256,1024]{1,0:T(8,128)(2,1)}, bf16[256,1024]{1,0:T(8,128)(2,1)S(1)}, u32[]{:S(2)}) copy-start(bf16[256,1024]{1,0:T(8,128)(2,1)S(1)} %get-tuple-element.172) | copy-start | bytes 1572868
  166.2 4.4 copy-start.1
  196.7 16.8 %copy-start.20 = (bf16[64,1024]{1,0:T(8,128)(2,1)S(1)}, bf16[64,1024]{1,0:T(8,128)(2,1)}, u32[]{:S(2)}) copy-start(bf16[64,1024]{1,0:T(8,128)(2,1)} %get-tuple-element.93) | copy-start | bytes 393220
  211.3 17.3 %copy-start.13 = (bf16[1,4,4,64,1024]{4,3,2,1,0:T(8,128)(2,1)S(1)}, bf16[1,4,4,64,1024]{4,3,2,1,0:T(8,128)(2,1)}, u32[]{:S(2)}) copy-start(bf16[1,4,4,64,1024]{4,3,2,1,0:T(8,128)(2,1)} %get-tuple-element.197) | copy-start | bytes 6291460
  228.6 5.2 copy-start.14
  233.8 16.5 %copy-start.26 = (bf16[256,1024]{1,0:T(8,128)(2,1)}, bf16[256,1024]{1,0:T(8,128)(2,1)S(1)}, u32[]{:S(2)}) copy-start(bf16[256,1024]{1,0:T(8,128)(2,1)S(1)} %get-tuple-element.170) | copy-start | bytes 1572868
  252.8 16.7 %copy-start.30 = (bf16[256,1024]{1,0:T(8,128)(2,1)}, bf16[256,1024]{1,0:T(8,128)(2,1)S(1)}, u32[]{:S(2)}) copy-start(bf16[256,1024]{1,0:T(8,128)(2,1)S(1)} %get-tuple-element.167) | copy-start | bytes 1572868
  314.5 1.5 copy-start.4
  316.1 18.8 %copy-start.5 = (f32[256,256]{1,0:T(8,128)S(1)}, f32[256,256]{1,0:T(8,128)}, u32[]{:S(2)}) copy-start(f32[256,256]{1,0:T(8,128)} %get-tuple-element.106) | copy-start | bytes 786436
  316.1 21.0 %copy-start.38 = (f32[8,1024]{1,0:T(8,128)S(1)}, f32[8,1024]{1,0:T(8,128)}, u32[]{:S(2)}) copy-start(f32[8,1024]{1,0:T(8,128)} %get-tuple-element.128) | copy-start | bytes 98308
  338.9 3.5 copy-start.11
  342.4 1.6 copy-start.16
  362.9 19.8 %copy-start.3 = (bf16[2,3,4,4,64,256]{5,4,3,2,1,0:T(8,128)(2,1)S(1)}, bf16[2,3,4,4,64,256]{5,4,3,2,1,0:T(8,128)(2,1)}, u32[]{:S(2)}) copy-start(bf16[2,3,4,4,64,256]{5,4,3,2,1,0:T(8,128)(2,1)} %get-tuple-element.82) | copy-start | bytes 9437188
  407.2 1.4 copy-start.6
  408.6 12.2 %copy-start.7 = (f32[256,256]{1,0:T(8,128)S(1)}, f32[256,256]{1,0:T(8,128)}, u32[]{:S(2)}) copy-start(f32[256,256]{1,0:T(8,128)} %get-tuple-element.119) | copy-start | bytes 786436
  408.6 13.9 %copy-start.37 = (f32[8,1024]{1,0:T(8,128)S(1)}, f32[8,1024]{1,0:T(8,128)}, u32[]{:S(2)}) copy-start(f32[8,1024]{1,0:T(8,128)} %get-tuple-element.126) | copy-start | bytes 98308
  425.1 1.9 copy-start.17
  425.4 1.9 copy-start.18
  428.8 1.8 copy-start.8
  428.8 1.8 copy-start.21
  429.1 1.8 copy-start.9
  430.6 1.8 copy-start.28
  430.6 1.8 copy-start.31
  432.4 1.0 copy-start.23
  434.2 2.3 copy-start.27
  434.2 2.3 copy-start.29
  436.5 1.0 copy-start.25
  436.6 1.2 copy-start.32
  438.5 2.4 copy-start.36
  438.5 3.0 copy-start.35
  526.9 9.2 %copy-start.34 = (f32[64,1024]{1,0:T(8,128)S(1)}, f32[64,1024]{1,0:T(8,128)}, u32[]{:S(2)}) copy-start(f32[64,1024]{1,0:T(8,128)} %get-tuple-element.137) | copy-start | bytes 786436
  526.9 9.9 %copy-start.33 = (f32[64,1024]{1,0:T(8,128)S(1)}, f32[64,1024]{1,0:T(8,128)}, u32[]{:S(2)}) copy-start(f32[64,1024]{1,0:T(8,128)} %get-tuple-element.138) | copy-start | bytes 786436

commit v3 on v2

--- a/solution.py
+++ b/solution.py
@@ -309,102 +309,113 @@
     return push
 
 
+class Gather:
+    WAYS = {0: 1, 3: 1, 1: 1, 2: 3}
+
+    def __init__(self, pieces, outs, y, z, lead, push):
+        self.pieces, self.outs, self.y, self.z = pieces, outs, y, z
+        self.lead, self.push = lead, push
+        self.every = range(len(pieces))
+        self.first, self.onward, self.second, self.relayed = {}, {}, {}, {}
+
+    def block(self, i, along, across, rows=None):
+        number, pre, along_z = self.pieces[i]
+        ys, zs = (across, along) if along_z else (along, across)
+        ys = ys if isinstance(ys, slice) else step(self.y, ys) if ys else self.y
+        zs = zs if isinstance(zs, slice) else step(self.z, zs) if zs else self.z
+        return self.outs[number].at[self.lead + pre + (ys, zs) + (() if rows is None else (rows,))]
+
+    def way(self, i, first, k):
+        return dp_neighbour(self.y, self.z, self.pieces[i][2] == first, k)
+
+    def halves(self, i):
+        height = self.outs[self.pieces[i][0]].shape[-2]
+        if height < 32:
+            return {PLUS: None}
+        return {PLUS: pl.ds(0, height // 2), MINUS: pl.ds(height // 2, height // 2)}
+
+    def spread(self, i, offset, source):
+        for k in (PLUS, MINUS):
+            self.second[i, offset, k] = self.push(
+                i, 2 if k == PLUS else 3, offset, source, self.block(i, offset, 0), self.way(i, False, k)
+            )
+
+    def begin(self, i, source):
+        for k in (PLUS, MINUS):
+            self.first[i, k] = self.push(i, 0, k, source, self.block(i, 0, 0), self.way(i, True, k))
+        self.spread(i, 0, source)
+
+    def near(self):
+        for i in self.every:
+            split = self.halves(i)
+            for k in (PLUS, MINUS):
+                self.first[i, k].wait_recv()
+                came = RING - k
+                if k in split:
+                    self.onward[i, k] = self.push(
+                        i, 1, k, self.block(i, came, 0, split[k]), self.block(i, came, 0, split[k]),
+                        self.way(i, True, k),
+                    )
+                self.spread(i, came, self.block(i, came, 0))
+
+    def relay(self, i, offset):
+        k = self.WAYS[offset]
+        self.second[i, offset, k].wait_recv()
+        came = self.block(i, offset, RING - k)
+        self.relayed[i, offset] = self.push(i, 4, offset, came, came, self.way(i, False, k))
+
+    def other(self, i, offset):
+        self.second[i, offset, RING - self.WAYS[offset]].wait_recv()
+
+    def far(self, i):
+        for k in self.halves(i):
+            self.onward[i, k].wait_recv()
+        self.spread(i, FAR, self.block(i, FAR, 0))
+
+
 def gather_kernel(pieces, n_in, n_out, with_sibling, *refs):
     ins, outs = refs[:n_in], refs[n_in : n_in + n_out]
     send, recv, local = refs[n_in + n_out :]
     rank = lax.axis_index("dp")
     y, z = rank // RING, lax.rem(rank, RING)
-    section = lax.axis_index("section") if with_sibling else None
+    section = lax.axis_index("section")
     barrier, count = dp_barrier(y, z, section)
     pl.semaphore_wait(barrier, count)
     started = []
     push = pusher(send, recv, started)
-    every = range(len(pieces))
-
-    def block(i, along, across, rows=None):
-        number, pre, along_z = pieces[i]
-        lead = ((section,) if with_sibling else ()) + pre
-        ys, zs = (across, along) if along_z else (along, across)
-        ys = ys if isinstance(ys, slice) else step(y, ys) if ys else y
-        zs = zs if isinstance(zs, slice) else step(z, zs) if zs else z
-        return outs[number].at[lead + (ys, zs) + (() if rows is None else (rows,))]
-
-    def first_way(i, k):
-        return dp_neighbour(y, z, pieces[i][2], k)
-
-    def second_way(i, k):
-        return dp_neighbour(y, z, not pieces[i][2], k)
-
-    def halves(i):
-        height = outs[pieces[i][0]].shape[-2]
-        if height < 32:
-            return {PLUS: None}
-        return {PLUS: pl.ds(0, height // 2), MINUS: pl.ds(height // 2, height // 2)}
-
-    own, first, onward, second, relayed = {}, {}, {}, {}, {}
-
-    def spread(i, offset, source):
-        for k in (PLUS, MINUS):
-            second[i, offset, k] = push(
-                i, 2 if k == PLUS else 3, offset, source, block(i, offset, 0), second_way(i, k)
-            )
-
-    for i in every:
-        number, pre, _ = pieces[i]
+    ring = Gather(pieces, outs, y, z, (section,), push)
+    own = {}
+    for i, (number, pre, _) in enumerate(pieces):
         source = ins[number].at[pre] if pre else ins[number]
-        for k in (PLUS, MINUS):
-            first[i, k] = push(i, 0, k, source, block(i, 0, 0), first_way(i, k))
-        spread(i, 0, source)
-        own[i] = pltpu.make_async_copy(source, block(i, 0, 0), local.at[i])
+        ring.begin(i, source)
+        own[i] = pltpu.make_async_copy(source, ring.block(i, 0, 0), local.at[i])
         own[i].start()
-    for i in every:
-        split = halves(i)
-        for k in (PLUS, MINUS):
-            first[i, k].wait_recv()
-            came = RING - k
-            if k in split:
-                onward[i, k] = push(
-                    i, 1, k, block(i, came, 0, split[k]), block(i, came, 0, split[k]), first_way(i, k)
-                )
-            spread(i, came, block(i, came, 0))
-    ways = {0: PLUS, MINUS: MINUS, PLUS: PLUS, FAR: MINUS}
-
-    def relay(i, offset):
-        k = ways[offset]
-        second[i, offset, k].wait_recv()
-        came = block(i, offset, RING - k)
-        relayed[i, offset] = push(i, 4, offset, came, came, second_way(i, k))
-
-    for i in every:
-        relay(i, 0)
-    for i in every:
-        for k in halves(i):
-            onward[i, k].wait_recv()
-        spread(i, FAR, block(i, FAR, 0))
     across = []
 
     def pass_on(i, line):
-        came = block(i, slice(None), line)
+        came = ring.block(i, slice(None), line)
         across.append(push(i, 5, line, came, came, {"section": 1 - section}))
 
-    for i in every:
-        relay(i, MINUS)
-        relay(i, PLUS)
+    ring.near()
+    for i in ring.every:
+        ring.relay(i, 0)
+    for i in ring.every:
+        ring.far(i)
+    for i in ring.every:
+        ring.relay(i, MINUS)
+        ring.relay(i, PLUS)
         own[i].wait()
-        if with_sibling:
-            pass_on(i, 0)
-    for i in every:
-        relay(i, FAR)
-        for offset, k in ways.items():
-            second[i, offset, RING - k].wait_recv()
-        if with_sibling:
-            pass_on(i, PLUS)
-            pass_on(i, MINUS)
-    for i in every:
+        pass_on(i, 0)
+    for i in ring.every:
+        ring.relay(i, FAR)
         for offset in range(RING):
-            relayed[i, offset].wait_recv()
-        if with_sibling:
-            pass_on(i, FAR)
+            ring.other(i, offset)
+        pass_on(i, PLUS)
+        pass_on(i, MINUS)
+    for i in ring.every:
+        for offset in range(RING):
+            ring.relayed[i, offset].wait_recv()
+        pass_on(i, FAR)
     for copy in across:
         copy.wait_recv()
     for copy in started:
@@ -436,6 +447,7 @@
         self.far_two, self.joined_two, self.summed_two, self.straight_two = buffers[5:]
         self.y, self.z, self.push = y, z, push
         self.height, self.width = source.shape[-2:]
+        self.via, self.direct, self.after = {}, {}, {}
 
     def at(self, along, across):
         ys, zs = (across, along) if self.along_z else (along, across)
@@ -464,32 +476,39 @@
 
         lax.fori_loop(0, height // size, each, 0)
 
+    def send_via(self, j):
+        self.via[j] = self.push(
+            self.index, 0, j, self.source.at[self.at(FAR, j)], self.passing.at[j],
+            self.way(True, self.WAYS[j]),
+        )
+
+    def send_direct(self, j):
+        k = RING - self.WAYS[j]
+        self.direct[j] = self.push(
+            self.index, 1, j, self.source.at[self.at(k, j)], self.straight.at[j], self.way(True, k)
+        )
+
     def begin(self):
-        self.via, self.direct, self.after = {}, {}, {}
         for j in self.ORDER:
-            self.via[j] = self.push(
-                self.index, 0, j, self.source.at[self.at(FAR, j)], self.passing.at[j],
-                self.way(True, self.WAYS[j]),
-            )
+            self.send_via(j)
         for j in self.ORDER:
-            k = RING - self.WAYS[j]
-            self.direct[j] = self.push(
-                self.index, 1, j, self.source.at[self.at(k, j)], self.straight.at[j],
-                self.way(True, k),
-            )
+            self.send_direct(j)
+
+    def join_one(self, j):
+        self.via[j].wait_recv()
+        k = self.WAYS[j]
+        at_y, at_z = self.at(k, j)
+        self.add(
+            self.joined.at[j],
+            [lambda h: self.source[at_y, at_z, h], lambda h: self.passing[j, h]],
+        )
+        self.after[j] = self.push(
+            self.index, 2, j, self.joined.at[j], self.summed.at[j], self.way(True, k)
+        )
 
     def join(self):
         for j in self.ORDER:
-            self.via[j].wait_recv()
-            k = self.WAYS[j]
-            at_y, at_z = self.at(k, j)
-            self.add(
-                self.joined.at[j],
-                [lambda h: self.source[at_y, at_z, h], lambda h: self.passing[j, h]],
-            )
-            self.after[j] = self.push(
-                self.index, 2, j, self.joined.at[j], self.summed.at[j], self.way(True, k)
-            )
+            self.join_one(j)
 
     def turn(self):
         half = self.height // 2
@@ -557,53 +576,6 @@
 
 
 SCATTER_BUFFERS = 9
-
-
-def scatter_kernel(orders, *refs):
-    n = len(orders)
-    ins, outs = refs[:n], refs[n : 2 * n]
-    buffers = refs[2 * n : 2 * n + n * SCATTER_BUFFERS]
-    send, recv = refs[2 * n + n * SCATTER_BUFFERS :]
-    rank = lax.axis_index("dp")
-    y, z = rank // RING, lax.rem(rank, RING)
-    barrier, count = dp_barrier(y, z, None)
-    pl.semaphore_wait(barrier, count)
-    started = []
-    push = pusher(send, recv, started)
-    parts = [
-        Scatter(
-            i, orders[i], ins[i], buffers[i * SCATTER_BUFFERS : (i + 1) * SCATTER_BUFFERS], y, z, push
-        )
-        for i in range(n)
-    ]
-    for part in parts:
-        part.begin()
-    for part in parts:
-        part.join()
-    for part in parts:
-        part.turn()
-    for part in parts:
-        part.join_two()
-    for part, out in zip(parts, outs):
-        part.finish(out)
-    for copy in started:
-        copy.wait_send()
-
-
-def scatter_call(cid, orders, ins):
-    blocks = [value.shape[2:] for value in ins]
-    return pl.pallas_call(
-        functools.partial(scatter_kernel, orders),
-        out_shape=[jax.ShapeDtypeStruct(block, F32) for block in blocks],
-        in_specs=[vmem_spec()] * len(ins),
-        out_specs=[vmem_spec()] * len(ins),
-        scratch_shapes=[one for block in blocks for one in Scatter.scratch(block, BF16)]
-        + [
-            pltpu.SemaphoreType.DMA((len(ins), 6, RING)),
-            pltpu.SemaphoreType.DMA((len(ins), 6, RING)),
-        ],
-        compiler_params=comm_params(cid),
-    )(*ins)
 
 
 def final_kernel(orders, n_extra, *refs):
@@ -729,9 +701,6 @@
     return lax.dot_general(former, latter, (((0,), (0,)), ((), ())), preferred_element_type=F32)
 
 
-KEY_BLOCK = 256
-
-
 def head_stack(values, scale):
     column = lax.broadcasted_iota(jnp.int32, values.shape, 1) // HEAD_DIM
     heads_here = values.shape[1] // HEAD_DIM
@@ -747,24 +716,58 @@
     return jnp.where(seg_column == seg_wide, scores, MASKED_SCORE)
 
 
-def attention_forward_kernel(q_ref, k_ref, v_ref, seg_q_ref, seg_k_ref, mixed_ref, wide_ref, lse_ref, stack, acc):
+def attend_kernel(
+    layer, normed_ref, qkv_any, out_any, bias_ref, seg_q_ref, seg_k_ref,
+    q_ref, k_ref, v_ref, mixed_ref, wide_ref, lse_ref, part_ref,
+    qkv_ref, out_ref, stack, acc, top_ref, total_ref, send, recv, local,
+):
     group, width = q_ref.shape
     heads_here = width // HEAD_DIM
+    loads = [
+        pltpu.make_async_copy(qkv_any.at[layer, which], qkv_ref.at[which], local.at[which])
+        for which in range(3)
+    ]
+    loads.append(pltpu.make_async_copy(out_any.at[layer], out_ref, local.at[3]))
+    for which in (1, 2, 0, 3):
+        loads[which].start()
+    rank = lax.axis_index("dp")
+    y, z = rank // RING, lax.rem(rank, RING)
+    barrier, count = dp_barrier(y, z, None)
+    normed = normed_ref[...]
+    loads[1].wait()
+    k_ref[y, z] = jnp.dot(normed, qkv_ref[1], preferred_element_type=F32).astype(BF16)
+    pl.semaphore_wait(barrier, count)
+    started = []
+    ring = Gather(((0, (), True), (1, (), False)), (k_ref, v_ref), y, z, (), pusher(send, recv, started))
+    ring.begin(0, k_ref.at[y, z])
+    loads[2].wait()
+    v_ref[y, z] = (
+        jnp.dot(normed, qkv_ref[2], preferred_element_type=F32) + bias_ref[1:2, :]
+    ).astype(BF16)
+    ring.begin(1, v_ref.at[y, z])
+    loads[0].wait()
+    q_ref[...] = (
+        jnp.dot(normed, qkv_ref[0], preferred_element_type=F32) + bias_ref[0:1, :]
+    ).astype(BF16)
     stack[...] = head_stack(q_ref[...], HEAD_DIM ** (-0.5))
     acc[...] = jnp.zeros_like(acc)
+    top_ref[...] = jnp.full_like(top_ref, MASKED_SCORE)
+    total_ref[...] = jnp.zeros_like(total_ref)
     seg_wide = jnp.concatenate([seg_q_ref[0:1, :]] * heads_here, axis=1)
-    seq = k_ref.shape[0]
-
-    def each(number, carry):
-        highest, total = carry
-        here = pl.ds(pl.multiple_of(number * KEY_BLOCK, KEY_BLOCK), KEY_BLOCK)
-        scores = block_scores(k_ref[here, :], stack[...], seg_k_ref[here, 0:1], seg_wide)
+
+    def attend(offset_y, offset_z):
+        at_y, at_z = step(y, offset_y), step(z, offset_z)
+        highest = top_ref[0:1, :]
+        scores = block_scores(
+            k_ref[at_y, at_z], stack[...], seg_k_ref[at_y, at_z, :, 0:1], seg_wide
+        )
         above = jnp.maximum(highest, jnp.max(scores, axis=0, keepdims=True))
         weights = jnp.exp(scores - above)
         fade = jnp.exp(highest - above)
-        total = total * fade + jnp.sum(weights, axis=0, keepdims=True)
+        total_ref[0:1, :] = total_ref[0:1, :] * fade + jnp.sum(weights, axis=0, keepdims=True)
+        top_ref[0:1, :] = above
         low = weights.astype(BF16)
-        turned = v_ref[here, :].T
+        turned = v_ref[at_y, at_z].T
         for head in range(heads_here):
             rows = pl.ds(head * HEAD_DIM, HEAD_DIM)
             lanes = slice(head * group, (head + 1) * group)
@@ -773,80 +776,147 @@
                 preferred_element_type=F32,
             )
             acc[rows, :] = acc[rows, :] * fade[:, lanes] + term
-        return above, total
-
-    start = jnp.full((1, group * heads_here), MASKED_SCORE, F32)
-    highest, total = lax.fori_loop(
-        0, seq // KEY_BLOCK, each, (start, jnp.zeros_like(start))
+
+    def attend_all(count, offsets):
+        def each(number, carry):
+            attend(*offsets(number))
+            return carry
+
+        lax.fori_loop(0, count, each, 0)
+
+    side = lambda t: 1 + 2 * lax.rem(t, 2)
+    attend_all(1, lambda t: (t, t))
+    ring.near()
+    for i in ring.every:
+        ring.relay(i, 0)
+        ring.other(i, 0)
+    attend_all(2, lambda t: (t * 0, side(t)))
+    for i in ring.every:
+        ring.far(i)
+    attend_all(2, lambda t: (side(t), t * 0))
+    for i in ring.every:
+        ring.relay(i, MINUS)
+        ring.relay(i, PLUS)
+    for i in ring.every:
+        ring.other(i, MINUS)
+        ring.other(i, PLUS)
+    attend_all(4, lambda t: (side(t // 2), side(t)))
+    for i in ring.every:
+        ring.relay(i, FAR)
+        ring.relayed[i, 0].wait_recv()
+    attend_all(2, lambda t: (2 * t, 2 - 2 * t))
+    for i in ring.every:
+        ring.other(i, FAR)
+        ring.relayed[i, MINUS].wait_recv()
+        ring.relayed[i, PLUS].wait_recv()
+    attend_all(
+        4,
+        lambda t: (
+            2 * (t // 2) + side(t) * (1 - t // 2),
+            2 * (1 - t // 2) + side(t) * (t // 2),
+        ),
     )
+    for i in ring.every:
+        ring.relayed[i, FAR].wait_recv()
+    attend_all(1, lambda t: (t + FAR, t + FAR))
+
+    total = total_ref[0:1, :]
     inverse = 1.0 / total
     for head in range(heads_here):
         rows = pl.ds(head * HEAD_DIM, HEAD_DIM)
         wide_ref[rows, :] = acc[rows, :] * inverse[:, head * group : (head + 1) * group]
     mixed_ref[...] = wide_ref[...].T.astype(BF16)
-    lse_ref[...] = jnp.broadcast_to(highest + jnp.log(total), lse_ref.shape)
-
-
-def local_params():
-    return pltpu.CompilerParams(vmem_limit_bytes=VMEM_LIMIT)
-
-
-def attention_forward(queries, keys_full, values_full, seg_wide, seg_column):
-    group, width = queries.shape
+    lse_ref[...] = jnp.broadcast_to(top_ref[0:1, :] + jnp.log(total), lse_ref.shape)
+    loads[3].wait()
+    part = flat_dot(mixed_ref[...], out_ref[...]).astype(BF16)
+    part_ref[...] = part.reshape(part_ref.shape)
+    for copy in started:
+        copy.wait_send()
+
+
+def attend_call(cid, layer, normed, full_qkv, full_out, biases, seg_wide, seg_column):
+    group, model = normed.shape
+    width = full_out.shape[2]
     heads_here = width // HEAD_DIM
+    square = (RING, RING, group, width)
     return pl.pallas_call(
-        attention_forward_kernel,
+        functools.partial(attend_kernel, layer),
         out_shape=[
+            jax.ShapeDtypeStruct((group, width), BF16),
+            jax.ShapeDtypeStruct(square, BF16),
+            jax.ShapeDtypeStruct(square, BF16),
             jax.ShapeDtypeStruct((group, width), BF16),
             jax.ShapeDtypeStruct((width, group), F32),
             jax.ShapeDtypeStruct((8, group * heads_here), F32),
+            jax.ShapeDtypeStruct((RING, group // RING, model), BF16),
         ],
-        in_specs=[vmem_spec()] * 5,
-        out_specs=[vmem_spec()] * 3,
+        in_specs=[vmem_spec(), any_spec(), any_spec()] + [vmem_spec()] * 3,
+        out_specs=[vmem_spec()] * 7,
         scratch_shapes=[
+            pltpu.VMEM((3, model, width), BF16),
+            pltpu.VMEM((model, width), BF16),
             pltpu.VMEM((group * heads_here, width), BF16),
             pltpu.VMEM((width, group), F32),
+            pltpu.VMEM((8, group * heads_here), F32),
+            pltpu.VMEM((8, group * heads_here), F32),
+            pltpu.SemaphoreType.DMA((2, 5, RING)),
+            pltpu.SemaphoreType.DMA((2, 5, RING)),
+            pltpu.SemaphoreType.DMA((4,)),
         ],
-        compiler_params=local_params(),
-    )(queries, keys_full, values_full, seg_wide, seg_column)
-
-
-def attention_backward_kernel(
-    q_ref, k_ref, v_ref, grad_ref, wide_ref, lse_ref, seg_q_ref, seg_k_ref,
-    dq_ref, dk_ref, dv_ref,
-    stack, plain, grad_stack, grad_plain, acc,
+        compiler_params=comm_params(cid),
+    )(normed, full_qkv, full_out, biases, seg_wide, seg_column)
+
+
+def attend_back_kernel(
+    layer, rows_ref, qkv_any, out_any, q_ref, k_ref, v_ref, wide_ref, lse_ref, seg_q_ref, seg_k_ref,
+    triple_ref, sums_ref, part_ref, *scratch,
 ):
+    (
+        qkv_ref, out_ref, grad_ref, stack, plain, grad_stack, grad_plain, acc, delta_ref,
+        dk_ref, dv_ref, total_ref,
+    ) = scratch[:12]
+    buffers = scratch[12 : 12 + 2 * SCATTER_BUFFERS]
+    send, recv, local = scratch[12 + 2 * SCATTER_BUFFERS :]
     group, width = q_ref.shape
     heads_here = width // HEAD_DIM
     scale = HEAD_DIM ** (-0.5)
+    load_out = pltpu.make_async_copy(out_any.at[layer], out_ref, local.at[0])
+    load_qkv = pltpu.make_async_copy(qkv_any.at[layer], qkv_ref, local.at[1])
+    load_out.start()
+    load_qkv.start()
+    rank = lax.axis_index("dp")
+    y, z = rank // RING, lax.rem(rank, RING)
+    barrier, count = dp_barrier(y, z, None)
     stack[...] = head_stack(q_ref[...], scale)
     plain[...] = head_stack(q_ref[...], 1.0)
+    load_out.wait()
+    grad_ref[...] = jnp.dot(rows_ref[...], out_ref[...], preferred_element_type=F32).astype(BF16)
     grad_stack[...] = head_stack(grad_ref[...], scale)
     grad_plain[...] = head_stack(grad_ref[...], 1.0)
     acc[...] = jnp.zeros_like(acc)
     seg_wide = jnp.concatenate([seg_q_ref[0:1, :]] * heads_here, axis=1)
-    seq = k_ref.shape[0]
     product = grad_ref[...].astype(F32).T * wide_ref[...]
-    delta = scale * jnp.concatenate(
-        [
-            jnp.sum(product[head * HEAD_DIM : (head + 1) * HEAD_DIM], axis=0, keepdims=True)
-            for head in range(heads_here)
-        ],
-        axis=1,
-    )
-    lse = lse_ref[0:1, :]
-
-    def each(number, carry):
-        here = pl.ds(pl.multiple_of(number * KEY_BLOCK, KEY_BLOCK), KEY_BLOCK)
-        key_block = k_ref[here, :]
-        scores = block_scores(key_block, stack[...], seg_k_ref[here, 0:1], seg_wide)
-        weights = jnp.exp(scores - lse)
-        dv_ref[here, :] = jnp.dot(
+    for head in range(heads_here):
+        delta_ref[0:1, pl.ds(head * group, group)] = scale * jnp.sum(
+            product[head * HEAD_DIM : (head + 1) * HEAD_DIM], axis=0, keepdims=True
+        )
+    pl.semaphore_wait(barrier, count)
+    started = []
+    push = pusher(send, recv, started)
+    keys = Scatter(0, True, dk_ref, buffers[:SCATTER_BUFFERS], y, z, push)
+    values = Scatter(1, False, dv_ref, buffers[SCATTER_BUFFERS:], y, z, push)
+
+    def attend(offset_y, offset_z):
+        at_y, at_z = step(y, offset_y), step(z, offset_z)
+        key_block = k_ref[at_y, at_z]
+        scores = block_scores(key_block, stack[...], seg_k_ref[at_y, at_z, :, 0:1], seg_wide)
+        weights = jnp.exp(scores - lse_ref[0:1, :])
+        dv_ref[at_y, at_z] = jnp.dot(
             weights.astype(BF16), grad_plain[...], preferred_element_type=F32
         ).astype(BF16)
-        prob_grad = flat_dot(v_ref[here, :], grad_stack[...])
-        low = (weights * (prob_grad - delta)).astype(BF16)
-        dk_ref[here, :] = jnp.dot(low, plain[...], preferred_element_type=F32).astype(BF16)
+        prob_grad = flat_dot(v_ref[at_y, at_z], grad_stack[...])
+        low = (weights * (prob_grad - delta_ref[0:1, :])).astype(BF16)
+        dk_ref[at_y, at_z] = jnp.dot(low, plain[...], preferred_element_type=F32).astype(BF16)
         turned = key_block.T
         for head in range(heads_here):
             rows = pl.ds(head * HEAD_DIM, HEAD_DIM)
@@ -855,29 +925,95 @@
                 low[:, head * group : (head + 1) * group],
                 preferred_element_type=F32,
             )
-        return carry
-
-    lax.fori_loop(0, seq // KEY_BLOCK, each, 0)
-    dq_ref[...] = acc[...].T
-
-
-def attention_backward(queries, keys_full, values_full, mixed_grad, wide, lse, seg_wide, seg_column):
-    group, width = queries.shape
+
+    def attend_all(first, count, offsets):
+        def each(number, carry):
+            attend(*offsets(number))
+            return carry
+
+        lax.fori_loop(first, count, each, 0)
+
+    attend_all(0, 4, lambda t: (t * 0 + FAR, step(t, FAR)))
+    for j in Scatter.ORDER:
+        values.send_via(j)
+    keys.send_direct(FAR)
+    attend_all(1, 4, lambda t: (step(t, FAR), t * 0 + FAR))
+    for j in Scatter.ORDER:
+        keys.send_via(j)
+    values.send_direct(FAR)
+    attend_all(1, 4, lambda t: (t * 0 + PLUS, step(t, FAR)))
+    keys.send_direct(PLUS)
+    values.send_direct(PLUS)
+    values.send_direct(MINUS)
+    attend_all(1, 4, lambda t: (t * 0 + MINUS, step(t, FAR)))
+    keys.send_direct(MINUS)
+    values.send_direct(0)
+    values.join()
+    for j in (FAR, PLUS, MINUS):
+        keys.join_one(j)
+    attend_all(1, 4, lambda t: (t * 0, step(t, FAR)))
+    keys.send_direct(0)
+    keys.join_one(0)
+    values.turn()
+    keys.turn()
+    values.join_two()
+    keys.join_two()
+    sums_ref[...] = jnp.zeros_like(sums_ref)
+    query_grad = acc[...].T
+    sums_ref[0:1, :] = jnp.sum(query_grad, axis=0, keepdims=True)
+    triple_ref[0] = query_grad.astype(BF16)
+    load_qkv.wait()
+    part = flat_dot(triple_ref[0], qkv_ref[0])
+    values.finish(total_ref)
+    triple_ref[2] = total_ref[...].astype(BF16)
+    sums_ref[1:2, :] = jnp.sum(total_ref[...], axis=0, keepdims=True)
+    part = part + flat_dot(triple_ref[2], qkv_ref[2])
+    keys.finish(total_ref)
+    triple_ref[1] = total_ref[...].astype(BF16)
+    part = part + flat_dot(triple_ref[1], qkv_ref[1])
+    part_ref[...] = part.astype(BF16).reshape(part_ref.shape)
+    for copy in started:
+        copy.wait_send()
+
+
+def attend_back_call(cid, layer, attn_rows, full_qkv, full_out, queries, keys, values, wide, lse, seg_wide, seg_column):
+    group, model = attn_rows.shape
+    width = queries.shape[1]
     heads_here = width // HEAD_DIM
-    seq = keys_full.shape[0]
+    block = (group, width)
+    stacked = pltpu.VMEM((group * heads_here, width), BF16)
     return pl.pallas_call(
-        attention_backward_kernel,
+        functools.partial(attend_back_kernel, layer),
         out_shape=[
-            jax.ShapeDtypeStruct((group, width), F32),
-            jax.ShapeDtypeStruct((seq, width), BF16),
-            jax.ShapeDtypeStruct((seq, width), BF16),
+            jax.ShapeDtypeStruct((3, group, width), BF16),
+            jax.ShapeDtypeStruct((8, width), F32),
+            jax.ShapeDtypeStruct((RING, group // RING, model), BF16),
         ],
-        in_specs=[vmem_spec()] * 8,
+        in_specs=[vmem_spec(), any_spec(), any_spec()] + [vmem_spec()] * 7,
         out_specs=[vmem_spec()] * 3,
-        scratch_shapes=[pltpu.VMEM((group * heads_here, width), BF16)] * 4
-        + [pltpu.VMEM((width, group), F32)],
-        compiler_params=local_params(),
-    )(queries, keys_full, values_full, mixed_grad, wide, lse, seg_wide, seg_column)
+        scratch_shapes=[
+            pltpu.VMEM((3, model, width), BF16),
+            pltpu.VMEM((model, width), BF16),
+            pltpu.VMEM(block, BF16),
+            stacked,
+            stacked,
+            stacked,
+            stacked,
+            pltpu.VMEM((width, group), F32),
+            pltpu.VMEM((8, group * heads_here), F32),
+            pltpu.VMEM((RING, RING) + block, BF16),
+            pltpu.VMEM((RING, RING) + block, BF16),
+            pltpu.VMEM(block, F32),
+        ]
+        + Scatter.scratch(block, BF16)
+        + Scatter.scratch(block, BF16)
+        + [
+            pltpu.SemaphoreType.DMA((2, 6, RING)),
+            pltpu.SemaphoreType.DMA((2, 6, RING)),
+            pltpu.SemaphoreType.DMA((2,)),
+        ],
+        compiler_params=comm_params(cid),
+    )(attn_rows, full_qkv, full_out, queries, keys, values, wide, lse, seg_wide, seg_column)
 
 
 WEIGHT_PIECES = (
@@ -886,6 +1022,7 @@
     (0, (2,), True),
     (1, (), False),
     (4, (), True),
+    (5, (), False),
     (2, (), True),
     (3, (), False),
 )
@@ -908,16 +1045,19 @@
         ((0, 2), (0, 128 - depth)),
     )
     shape = lambda *dims: jax.ShapeDtypeStruct(dims, BF16)
-    full_qkv, full_out, full_up, full_down, full_small = gather_call(
+    my_segments = own(segment_ids)
+    seg_block = jnp.zeros((8, 128), jnp.int32).at[0, :rows].set(my_segments)
+    full_qkv, full_out, full_up, full_down, full_small, full_seg = gather_call(
         0,
         WEIGHT_PIECES,
-        [w_qkv[0], w_out[0], w_up[0], w_down[0], small],
+        [w_qkv[0], w_out[0], w_up[0], w_down[0], small, seg_block],
         [
             shape(2, 3, *square, depth, local_width),
             shape(2, *square, depth, local_width),
             shape(2, *square, depth, local_hidden),
             shape(2, *square, depth, local_hidden),
             shape(2, *square, 16, 128),
+            jax.ShapeDtypeStruct((2,) + square + (8, 128), jnp.int32),
         ],
         True,
     )
@@ -934,13 +1074,14 @@
 
     my_tokens = own(tokens)
     my_cotangent = own(cotangent)
-    my_segments = own(segment_ids)
-    seg_block = jnp.zeros((8, 128), jnp.int32).at[0, :rows].set(my_segments)
+    seg_mine = own(full_seg)[:, :, 0, :rows].reshape(8, 128)
     normed, seg_group = tensor_call(
-        1, first_rows, None, [my_tokens], [small_rows[0]], [], 0, True, seg_block
+        1, first_rows, None, [my_tokens], [small_rows[0]], [], 0, True, seg_mine
     )
-    seg_rows = seg_group[:, 0, :rows].reshape(group)
+    seg_all = seg_group.reshape(RING, RING * RING, rows).transpose(1, 0, 2).reshape(-1, group)
+    seg_rows = lax.dynamic_index_in_dim(seg_all, lax.axis_index("dp"), 0, keepdims=False)
     seg_wide = jnp.broadcast_to(seg_rows[None], (8, group))
+    seg_column = jnp.broadcast_to(seg_all.reshape(*square, group)[..., None], square + (group, 128))
     inputs = my_tokens
     kept = []
     for layer in range(2):
@@ -951,29 +1092,10 @@
         up_bias = lax.dynamic_slice_in_dim(
             vec[9:13].reshape(-1), tensor_rank * local_hidden, local_hidden
         )
-        project = lambda which: jnp.dot(normed, full_qkv[layer, which], preferred_element_type=F32)
-        queries = (project(0) + query_bias).astype(BF16)
-        keys = project(1).astype(BF16)
-        values = (project(2) + value_bias).astype(BF16)
-        keys_full, values_full, seg_full = gather_call(
-            2,
-            ((2, (), True), (0, (), True), (1, (), False)),
-            [keys, values, seg_wide],
-            [
-                shape(*square, group, local_width),
-                shape(*square, group, local_width),
-                jax.ShapeDtypeStruct(square + (8, group), jnp.int32),
-            ],
-            False,
-        )
-        keys_full = keys_full.reshape(-1, local_width)
-        values_full = values_full.reshape(-1, local_width)
-        if layer == 0:
-            seg_column = jnp.broadcast_to(
-                seg_full[:, :, 0].reshape(-1)[:, None], (keys_full.shape[0], 128)
-            )
-        mixed, wide, lse = attention_forward(queries, keys_full, values_full, seg_wide, seg_column)
-        part = flat_dot(mixed, full_out[layer]).astype(BF16).reshape(RING, rows, width)
+        biases = jnp.zeros((8, local_width), F32).at[0].set(query_bias).at[1].set(value_bias)
+        queries, keys_full, values_full, mixed, wide, lse, part = attend_call(
+            2 + 12 * layer, layer, normed, full_qkv, full_out, biases, seg_wide, seg_column
+        )
         attn_out, hidden, normed_two = tensor_call(
             3, middle_rows, part, [inputs.astype(F32)], [vec], [F32, F32], 0, True
         )
@@ -1013,25 +1135,13 @@
             6, back_middle_rows, part, [upstream, hidden, attn_out], [vec], [F32], 4, True
         )
         attn_rows = attn_rows.reshape(group, width)
-        mixed_grad = jnp.dot(attn_rows, full_out[layer], preferred_element_type=F32).astype(BF16)
         grad_out = rows_dot(attn_rows, mixed)
-        query_grad, keys_part, values_part = attention_backward(
-            queries, keys_full, values_full, mixed_grad, wide, lse, seg_wide, seg_column
-        )
-        keys_grad, values_grad = scatter_call(
-            7,
-            (True, False),
-            [
-                keys_part.reshape(*square, group, local_width),
-                values_part.reshape(*square, group, local_width),
-            ],
-        )
-        query_bias_grad = jnp.sum(query_grad, axis=0)
-        value_bias_grad = jnp.sum(values_grad, axis=0)
-        triple = [value.astype(BF16) for value in (query_grad, keys_grad, values_grad)]
-        grad_qkv = [rows_dot(normed, value) for value in triple]
-        part = sum(flat_dot(triple[which], full_qkv[layer, which]) for which in range(3))
-        part = part.astype(BF16).reshape(RING, rows, width)
+        triple, sums_attend, part = attend_back_call(
+            7 + 12 * layer, layer, attn_rows, full_qkv, full_out, queries, keys_full, values_full,
+            wide, lse, seg_wide, seg_column,
+        )
+        query_bias_grad, value_bias_grad = sums_attend[0], sums_attend[1]
+        grad_qkv = [rows_dot(normed, triple[which]) for which in range(3)]
         if layer == 1:
             input_grad, sums_last, mlp_rows = tensor_call(
                 8,

time: 542 us -> 480 us (0.89)
  Pallas kernels: 430 us -> 394 us
  matrix products: 56.1 us -> 28.4 us
    pallas_call x3 -> x1, Pallas kernels: 100 us -> 53 us  [gather_call(): pl.pallas_call(functools.partial(gather_kernel, pieces, len(ins), len(out...]
    dot_general x8 -> x0, matrix products: 16.7 us -> none  [the longest x6 12.7 us: shards(): jnp.dot(normed, full_qkv[layer, which], preferred_element_type=F32)]
    pallas_call x6 -> x4, Pallas kernels: 114 us -> 128 us  [the longest x2 64.9 us: attend_call(): pl.pallas_call(functools.partial(attend_kernel, layer), out_shape=[jax.Sh...]
    dot_general x12 -> x4, matrix products: 18.5 us -> 6.22 us  [flat_dot(): lax.dot_general(former, latter, (((1,), (1,)), ((), ())), preferred_eleme...]
where the time goes in v3:
time: 480 us; the launch traced here: 475 us
  Pallas kernels  394 us (82%)
  matrix products  28.4 us (6%)
  local copies, waits for them, and re-layouts  28.1 us (6%)
  other arithmetic  23.5 us (5%)
    pallas_call x9, Pallas kernels, tensor_call(): pl.pallas_call(functools.partial(tensor_kernel, function, len(rows), len(...  130 us
    pallas_call x1, Pallas kernels, final_call(): pl.pallas_call(functools.partial(final_kernel, orders, extra), out_shape=...  83.4 us
    pallas_call x2, Pallas kernels, attend_call(): pl.pallas_call(functools.partial(attend_kernel, layer), out_shape=[jax.Sh...  64.9 us
    pallas_call x2, Pallas kernels, attend_back_call(): pl.pallas_call(functools.partial(attend_back_kernel, layer), out_shape=[j...  62.7 us
    pallas_call x1, Pallas kernels, gather_call(): pl.pallas_call(functools.partial(gather_kernel, pieces, len(ins), len(out...  53 us
    dot_general x2, matrix products, shards(): jnp.dot(normed_two, full_up[layer], preferred_element_type=F32) + up_bias  10.4 us
    another operation x7, other arithmetic, shards(): stacked = [jnp.stack(pair) for pair in zip(*grads)]  9.78 us

profile of v3, /device:TPU:1, one launch (start us, length us, event | category | flops | bytes accessed | tf_op | source)
XLA Modules:
  0.0 475.4 jit_solution(17932005501570950136)
XLA Ops:
  0.6 1.3 fusion.33.refs_4_
  1.9 0.8 broadcast_select_fusion.2
  3.3 53.0 %shard_map.152 = (bf16[2,3,4,4,64,256]{5,4,3,2,1,0:T(8,128)(2,1)}, bf16[2,4,4,64,256]{4,3,2,1,0:T(8,128)(2,1)}, bf16[2,4,4,64,1024]{4,3,2,1,0:T(8,128)(2,1)}, bf...) custom-call(bf16[3,64,256]{2,1,0:T(8,128)(2,1)} %bitcast.210, ...), custom_call_target="tpu_custom_call" | custom-call | tf_op jit(solution)/shard_map/pallas_call | solution.py:426
  56.3 5.9 %fusion.44 = (bf16[1,4,4,64,1024]{4,3,2,1,0:T(8,128)(2,1)}, bf16[1,4,4,64,1024]{4,3,2,1,0:T(8,128)(2,1)}, bf16[1,4,4,64,1024]{4,3,2,1,0:T(8,128)(2,1)}, bf16[1,4,4,64,1024]{4,3,2,1,0:T(8,128)(2,1)S(1)}) fusion(bf16[2,4,4,64,1024]{4,3,2,1,0:T(8,128)(2,1)} %get-tuple-element.137, bf16[2,4,4,64,1024]{4,3,2,1,0:T(8,128)(2,1)} %get-tuple-element.136), kind=kLoop, calls=%fused_computation.148 | loop fusion | bytes 16777216 | tf_op jit(solution)/shard_map/slice | solution.py:1105
  62.4 0.9 fusion.40
  64.8 12.7 %shard_map.153 = (bf16[4,64,1024]{2,1,0:T(8,128)(2,1)}, s32[4,8,128]{2,1,0:T(8,128)}) custom-call(bf16[64,1024]{1,0:T(8,128)(2,1)} %get-tuple-element.243.refs_0_, f32[16,1024]{1,0:T(8,128)} %squeeze.41.refs_1_.refs_2_.refs_5_.refs_4_.refs_3_, s32[8,128]{1,0:T(8,128)} %reshape_squeeze.3.refs_2_), custom_call_target="tpu_custom_call" | custom-call | tf_op jit(solution)/shard_map/pallas_call | solution.py:187
  78.1 0.8 reshape.407
  79.7 1.7 broadcast_in_dim.44.seg_k_ref
  81.4 34.9 %shard_map.154 = (bf16[256,256]{1,0:T(8,128)(2,1)}, bf16[4,4,256,256]{3,2,1,0:T(8,128)(2,1)}, bf16[4,4,256,256]{3,2,1,0:T(8,128)(2,1)}, bf16[256,256]{1,0:T(8,12...) custom-call(bf16[256,1024]{1,0:T(8,128)(2,1)} %bitcast.157, ...), custom_call_target="tpu_custom_call" | custom-call | tf_op jit(solution)/shard_map/pallas_call | solution.py:842
  116.3 14.3 %shard_map.155 = (f32[64,1024]{1,0:T(8,128)}, f32[64,1024]{1,0:T(8,128)}, bf16[4,64,1024]{2,1,0:T(8,128)(2,1)}) custom-call(bf16[4,64,1024]{2,1,0:T(8,128)(2,1)} %get-tuple-element.134.refs_0_, f32[64,1024]{1,0:T(8,128)} %get-tuple-element.242.refs_1_.refs_2_, f32[16,1024]{1,0:T(8,128)} %squeeze.41.refs_1_.refs_2_.refs_5_.refs_4_.refs_3_), custom_call_target="tpu_custom_call" | custom-call | tf_op jit(solution)/shard_map/pallas_call | solution.py:187
  130.6 5.2 %multiply_convert_fusion.1 = (bf16[256,1024]{1,0:T(8,128)(2,1)S(1)}, f32[256,1024]{1,0:T(8,128)}, f32[256,1024]{1,0:T(8,128)}) fusion(f32[1024]{0:T(1024)S(1)} %dynamic_slice.25, bf16[256,1024]{1,0:T(8,128)(2,1)} %bitcast.191, bf16[1024,1024]{1,0:T(8,128)(2,1)S(1)} %bitcast.177), kind=kOutput, calls=%fused_computation.43 | convolution fusion | flops 554172416 | bytes 5246976 | tf_op jit(solution)/shard_map/dot_general | solution.py:1103
  135.8 1.6 convolution_convert_fusion.15
  138.1 17.2 %shard_map.156 = (f32[64,1024]{1,0:T(8,128)}, bf16[64,1024]{1,0:T(8,128)(2,1)}, bf16[4,64,1024]{2,1,0:T(8,128)(2,1)}) custom-call(bf16[4,64,1024]{2,1,0:T(8,128)(2,1)} %bitcast.185, f32[64,1024]{1,0:T(8,128)} %get-tuple-element.138.refs_1_.refs_2_, f32[16,1024]{1,0:T(8,128)} %squeeze.41.refs_1_.refs_2_.refs_5_.refs_4_.refs_3_, ...), custom_call_target="tpu_custom_call" | custom-call | tf_op jit(solution)/shard_map/pallas_call | solution.py:187
  156.0 30.0 %shard_map.157 = (bf16[256,256]{1,0:T(8,128)(2,1)}, bf16[4,4,256,256]{3,2,1,0:T(8,128)(2,1)}, bf16[4,4,256,256]{3,2,1,0:T(8,128)(2,1)}, bf16[256,256]{1,0:T(8,12...) custom-call(bf16[256,1024]{1,0:T(8,128)(2,1)} %bitcast.161, ...), custom_call_target="tpu_custom_call" | custom-call | tf_op jit(solution)/shard_map/pallas_call | solution.py:842
  186.7 14.1 %shard_map.158 = (f32[64,1024]{1,0:T(8,128)}, f32[64,1024]{1,0:T(8,128)}, bf16[4,64,1024]{2,1,0:T(8,128)(2,1)}) custom-call(bf16[4,64,1024]{2,1,0:T(8,128)(2,1)} %get-tuple-element.141.refs_0_, f32[64,1024]{1,0:T(8,128)} %convert_element_type.97.refs_1_.refs_2_, f32[16,1024]{1,0:T(8,128)} %squeeze.86.refs_3_.refs_2_.refs_4_), custom_call_target="tpu_custom_call" | custom-call | tf_op jit(solution)/shard_map/pallas_call | solution.py:187
  200.9 5.2 %multiply_convert_fusion = (bf16[256,1024]{1,0:T(8,128)(2,1)S(1)}, f32[256,1024]{1,0:T(8,128)}, f32[256,1024]{1,0:T(8,128)}) fusion(f32[1024]{0:T(1024)S(1)} %dynamic_slice.28, bf16[256,1024]{1,0:T(8,128)(2,1)} %bitcast.193, bf16[1024,1024]{1,0:T(8,128)(2,1)S(1)} %bitcast.181), kind=kOutput, calls=%fused_computation.30 | convolution fusion | flops 554172416 | bytes 5246976 | tf_op jit(solution)/shard_map/dot_general | solution.py:1103
  206.1 1.5 convolution_convert_fusion.14
  207.6 14.9 %shard_map.159 = (bf16[64,1024]{1,0:T(8,128)(2,1)}, f32[8,1024]{1,0:T(8,128)}, bf16[4,64,1024]{2,1,0:T(8,128)(2,1)}) custom-call(bf16[4,64,1024]{2,1,0:T(8,128)(2,1)} %bitcast.188, f32[64,1024]{1,0:T(8,128)} %get-tuple-element.143.refs_1_.refs_2_, bf16[64,1024]{1,0:T(8,128)(2,1)} %get-tuple-element.217.refs_2_, f32[16,1024]{1,0:T(8,128)} %squeeze.86.refs_3_.refs_2_.refs_4_), custom_call_target="tpu_custom_call" | custom-call | tf_op jit(solution)/shard_map/pallas_call | solution.py:187
  222.6 2.7 fusion.39
  225.3 1.5 convolution_convert_fusion.13
  226.8 14.9 %shard_map.160 = (f32[64,1024]{1,0:T(8,128)}, f32[8,1024]{1,0:T(8,128)}, bf16[4,64,1024]{2,1,0:T(8,128)(2,1)}) custom-call(bf16[4,64,1024]{2,1,0:T(8,128)(2,1)} %bitcast.186, f32[64,1024]{1,0:T(8,128)} %get-tuple-element.216.refs_1_, f32[64,1024]{1,0:T(8,128)} %get-tuple-element.143.refs_1_.refs_2_, f32[64,1024]{1,0:T(8,128)} %get-tuple-element.146.refs_3_, ...), custom_call_target="tpu_custom_call" | custom-call | tf_op jit(solution)/shard_map/pallas_call | solution.py:187
  241.8 30.4 %shard_map.161 = (bf16[3,256,256]{2,1,0:T(8,128)(2,1)}, f32[8,256]{1,0:T(8,128)}, bf16[4,64,1024]{2,1,0:T(8,128)(2,1)}) custom-call(bf16[256,1024]{1,0:T(8,128)(2,1)} %bitcast.165, bf16[2,3,1024,256]{3,2,1,0:T(8,128)(2,1)} %bitcast.147, bf16[2,1024,256]{2,1,0:T(8,128)(2,1)} %bitcast.151, bf16[256,256]{1,0:T(8,128)(2,1)} %get-tuple-element.148.q_ref, ...), custom_call_target="tpu_custom_call" | custom-call | tf_op jit(solution)/shard_map/pallas_call | solution.py:985
  272.3 16.1 %shard_map.162 = (f32[64,1024]{1,0:T(8,128)}, f32[8,1024]{1,0:T(8,128)}, bf16[4,64,1024]{2,1,0:T(8,128)(2,1)}) custom-call(bf16[4,64,1024]{2,1,0:T(8,128)(2,1)} %get-tuple-element.153.refs_0_, f32[64,1024]{1,0:T(8,128)} %get-tuple-element.154.refs_1_, f32[64,1024]{1,0:T(8,128)} %convert_element_type.97.refs_1_.refs_2_, ...), custom_call_target="tpu_custom_call" | custom-call | tf_op jit(solution)/shard_map/pallas_call | solution.py:187
  288.4 0.8 slice.269
  292.9 0.9 slice_reduce_fusion.2
  294.4 3.3 fusion.38
  297.7 1.5 convolution_convert_fusion.12
  300.0 15.9 %shard_map.163 = (f32[64,1024]{1,0:T(8,128)}, f32[8,1024]{1,0:T(8,128)}, bf16[4,64,1024]{2,1,0:T(8,128)(2,1)}) custom-call(bf16[4,64,1024]{2,1,0:T(8,128)(2,1)} %bitcast.187, f32[64,1024]{1,0:T(8,128)} %convert_convert_fusion.refs_1_, f32[64,1024]{1,0:T(8,128)} %get-tuple-element.138.refs_1_.refs_2_, f32[64,1024]{1,0:T(8,128)} %get-tuple-element.158.refs_3_, ...), custom_call_target="tpu_custom_call" | custom-call | tf_op jit(solution)/shard_map/pallas_call | solution.py:187
  315.9 32.2 %shard_map.164 = (bf16[3,256,256]{2,1,0:T(8,128)(2,1)}, f32[8,256]{1,0:T(8,128)}, bf16[4,64,1024]{2,1,0:T(8,128)(2,1)}) custom-call(bf16[256,1024]{1,0:T(8,128)(2,1)} %bitcast.167, bf16[2,3,1024,256]{3,2,1,0:T(8,128)(2,1)} %bitcast.148, bf16[2,1024,256]{2,1,0:T(8,128)(2,1)} %bitcast.152, bf16[256,256]{1,0:T(8,128)(2,1)} %get-tuple-element.160.q_ref, ...), custom_call_target="tpu_custom_call" | custom-call | tf_op jit(solution)/shard_map/pallas_call | solution.py:985
  348.2 9.6 %shard_map.165 = (f32[64,1024]{1,0:T(8,128)}, f32[8,1024]{1,0:T(8,128)}) custom-call(bf16[4,64,1024]{2,1,0:T(8,128)(2,1)} %get-tuple-element.165.refs_0_, f32[64,1024]{1,0:T(8,128)} %get-tuple-element.166.refs_1_, f32[64,1024]{1,0:T(8,128)} %get-tuple-element.242.refs_1_.refs_2_, f32[16,1024]{1,0:T(8,128)} %squeeze.41.refs_1_.refs_2_.refs_5_.refs_4_.refs_3_), custom_call_target="tpu_custom_call" | custom-call | tf_op jit(solution)/shard_map/pallas_call | solution.py:187
  357.8 0.8 slice.261
  361.7 0.9 slice_reduce_fusion.6
  364.7 1.1 pad_maximum_fusion.2.refs_1_
  366.6 1.1 pad_maximum_fusion.3.refs_2_
  368.4 1.1 pad_maximum_fusion.4.refs_3_
  370.2 1.1 pad_maximum_fusion.5.refs_4_
  371.3 0.7 convolution_convert_fusion.2
  373.3 2.3 pad_maximum_fusion.refs_5_
  375.6 0.7 convolution_convert_fusion
  376.6 0.7 convolution_convert_fusion.1
  377.4 2.4 pad_maximum_fusion.1.refs_6_
  380.4 0.7 select_bitcast_fusion
  381.2 83.4 %shard_map.166 = (f32[16,128]{1,0:T(8,128)}, f32[64,256]{1,0:T(8,128)}, f32[64,256]{1,0:T(8,128)}, f32[64,256]{1,0:T(8,128)}, f32[64,256]{1,0:T(8,128)}, /*index...) custom-call(f32[2,4,4,16,128]{4,3,2,1,0:T(8,128)} %pad_maximum_fusion.6.refs_0_, ...), custom_call_target="tpu_custom_call" | custom-call | tf_op jit(solution)/shard_map/pallas_call | solution.py:670
  464.6 1.8 maximum_select_fusion.1
  466.4 1.9 maximum_select_fusion
  468.3 1.6 maximum_bitcast_fusion
  471.2 1.2 slice.284
  472.4 1.5 copy.80
  (175 shorter events, 23.0 us)
Async XLA Ops:
  56.3 5.9 %copy-start.29 = (bf16[2,4,4,16,128]{4,3,2,1,0:T(8,128)(2,1)S(1)}, bf16[2,4,4,16,128]{4,3,2,1,0:T(8,128)(2,1)}, u32[]{:S(2)}) copy-start(bf16[2,4,4,16,128]{4,3,2,1,0:T(8,128)(2,1)} %get-tuple-element.128) | copy-start | bytes 393220
  56.3 6.1 %copy-start.21 = (bf16[2,64,1024]{2,1,0:T(8,128)(2,1)S(1)}, bf16[2,64,1024]{2,1,0:T(8,128)(2,1)}, u32[]{:S(2)}) copy-start(bf16[2,64,1024]{2,1,0:T(8,128)(2,1)} %param.27) | copy-start | bytes 786436
  56.3 6.1 %copy-start.22 = (bf16[2,64,1024]{2,1,0:T(8,128)(2,1)S(1)}, bf16[2,64,1024]{2,1,0:T(8,128)(2,1)}, u32[]{:S(2)}) copy-start(bf16[2,64,1024]{2,1,0:T(8,128)(2,1)} %param.19) | copy-start | bytes 786436
  62.2 1.9 copy-start.30
  78.1 3.3 copy-start.32
  130.6 5.2 %copy-start.4 = (bf16[1,4,4,64,1024]{4,3,2,1,0:T(8,128)(2,1)S(1)}, bf16[1,4,4,64,1024]{4,3,2,1,0:T(8,128)(2,1)}, u32[]{:S(2)}) copy-start(bf16[1,4,4,64,1024]{4,3,2,1,0:T(8,128)(2,1)} %get-tuple-element.225) | copy-start | bytes 6291460
  155.4 0.6 copy-start.31
  156.0 30.0 %copy-start.8 = (bf16[64,1024]{1,0:T(8,128)(2,1)S(1)}, bf16[64,1024]{1,0:T(8,128)(2,1)}, u32[]{:S(2)}) copy-start(bf16[64,1024]{1,0:T(8,128)(2,1)} %get-tuple-element.139) | copy-start | bytes 393220
  156.0 44.9 %copy-start.5 = (bf16[1,4,4,64,1024]{4,3,2,1,0:T(8,128)(2,1)S(1)}, bf16[1,4,4,64,1024]{4,3,2,1,0:T(8,128)(2,1)}, u32[]{:S(2)}) copy-start(bf16[1,4,4,64,1024]{4,3,2,1,0:T(8,128)(2,1)} %get-tuple-element.244) | copy-start | bytes 6291460
  200.9 5.2 %copy-start.6 = (bf16[1,4,4,64,1024]{4,3,2,1,0:T(8,128)(2,1)S(1)}, bf16[1,4,4,64,1024]{4,3,2,1,0:T(8,128)(2,1)}, u32[]{:S(2)}) copy-start(bf16[1,4,4,64,1024]{4,3,2,1,0:T(8,128)(2,1)} %get-tuple-element.224) | copy-start | bytes 6291460
  206.1 16.5 %copy-start.10 = (bf16[256,1024]{1,0:T(8,128)(2,1)}, bf16[256,1024]{1,0:T(8,128)(2,1)S(1)}, u32[]{:S(2)}) copy-start(bf16[256,1024]{1,0:T(8,128)(2,1)S(1)} %get-tuple-element.218) | copy-start | bytes 1572868
  225.3 1.6 copy-start.14
  241.8 50.9 %copy-start.34 = (f32[8,1024]{1,0:T(8,128)S(1)}, f32[8,1024]{1,0:T(8,128)}, u32[]{:S(2)}) copy-start(f32[8,1024]{1,0:T(8,128)} %get-tuple-element.172) | copy-start | bytes 98308
  297.7 1.6 copy-start.17
  297.7 1.6 copy-start.7
  315.9 45.6 %copy-start.33 = (f32[8,1024]{1,0:T(8,128)S(1)}, f32[8,1024]{1,0:T(8,128)}, u32[]{:S(2)}) copy-start(f32[8,1024]{1,0:T(8,128)} %get-tuple-element.169) | copy-start | bytes 98308
  348.1 15.8 %copy-start.1 = (bf16[4,64,1024]{2,1,0:T(8,128)(2,1)S(1)}, bf16[4,64,1024]{2,1,0:T(8,128)(2,1)}, u32[]{:S(2)}) copy-start(bf16[4,64,1024]{2,1,0:T(8,128)(2,1)} %get-tuple-element.140) | copy-start | bytes 1572868
  348.2 15.8 %copy-start.19 = (bf16[3,256,256]{2,1,0:T(8,128)(2,1)S(1)}, bf16[3,256,256]{2,1,0:T(8,128)(2,1)}, u32[]{:S(2)}) copy-start(bf16[3,256,256]{2,1,0:T(8,128)(2,1)} %get-tuple-element.175) | copy-start | bytes 1179652
  348.2 16.1 %copy-start = (bf16[4,64,1024]{2,1,0:T(8,128)(2,1)S(1)}, bf16[4,64,1024]{2,1,0:T(8,128)(2,1)}, u32[]{:S(2)}) copy-start(bf16[4,64,1024]{2,1,0:T(8,128)(2,1)} %get-tuple-element.130) | copy-start | bytes 1572868
  363.1 1.2 copy-start.20
  367.7 1.8 copy-start.2
  367.7 1.8 copy-start.28
  368.0 1.8 copy-start.3
  368.0 1.8 copy-start.26
  369.5 1.8 copy-start.12
  369.5 1.8 copy-start.15
  371.3 1.0 copy-start.9
  371.3 1.2 copy-start.18
  373.3 2.3 copy-start.11
  373.3 2.3 copy-start.13
  375.6 1.0 copy-start.16
  377.4 2.4 copy-start.27
  377.4 3.1 copy-start.25
  464.6 9.2 %copy-start.24 = (f32[64,1024]{1,0:T(8,128)S(1)}, f32[64,1024]{1,0:T(8,128)}, u32[]{:S(2)}) copy-start(f32[64,1024]{1,0:T(8,128)} %get-tuple-element.185) | copy-start | bytes 786436
  464.6 9.9 %copy-start.23 = (f32[64,1024]{1,0:T(8,128)S(1)}, f32[64,1024]{1,0:T(8,128)}, u32[]{:S(2)}) copy-start(f32[64,1024]{1,0:T(8,128)} %get-tuple-element.186) | copy-start | bytes 786436

commit v4 on v3

--- a/solution.py
+++ b/solution.py
@@ -56,40 +56,60 @@
 
 
 PLUS, FAR, MINUS = 1, 2, 3
-SUBS = 2
-
-
-def tensor_kernel(function, n_rows, n_vecs, n_out, n_sums, reduce, gather, with_seg, *refs):
+CHUNKS = 2
+
+
+class Rider:
+    def __init__(self, build, ins, in_specs, outs, out_specs, scratch):
+        self.build, self.ins, self.in_specs = build, ins, in_specs
+        self.outs, self.out_specs, self.scratch = outs, out_specs, scratch
+
+
+def tensor_barrier(me):
+    barrier = pltpu.get_barrier_semaphore()
+    for k in range(1, RING):
+        pl.semaphore_signal(
+            barrier, inc=1, device_id={"tensor": step(me, k)}, device_id_type=MESH
+        )
+    return barrier, RING - 1
+
+
+def tensor_kernel(function, n_rows, n_vecs, n_out, n_sums, reduce, gather, with_seg, rider, *refs):
     refs = list(refs)
     take = lambda count: [refs.pop(0) for _ in range(count)]
     part = take(1)[0] if reduce else None
     rows_in = take(n_rows)
     vecs = take(n_vecs)
     seg_in = take(1)[0] if with_seg else None
+    rider_ins = take(len(rider.ins)) if rider else []
     rows_out = take(n_out)
     sums_out = take(1)[0] if n_sums else None
     full = take(1)[0] if gather else None
     seg_out = take(1)[0] if with_seg else None
-    passing, joined, from_minus, from_plus = take(4) if reduce else [None] * 4
+    rider_outs = take(len(rider.outs)) if rider else []
+    landing = take(1)[0] if reduce else None
     send, recv, local = take(3)
 
     me = lax.axis_index("tensor")
-    barrier = pltpu.get_barrier_semaphore()
-    for k in (PLUS, MINUS):
-        pl.semaphore_signal(
-            barrier, inc=1, device_id={"tensor": step(me, k)}, device_id_type=MESH
-        )
-    pl.semaphore_wait(barrier, 2)
-
-    chunk = rows_in[0].shape[0] // (2 * SUBS)
+    barrier, count = tensor_barrier(me)
+    stages = []
+    if rider:
+        rank = lax.axis_index("dp")
+        y, z = rank // RING, lax.rem(rank, RING)
+        section = lax.axis_index("section")
+        count += dp_barrier(y, z, section)[1]
+        stages = rider.build(y, z, section, rider_ins, rider_outs, refs)
+    pl.semaphore_wait(barrier, count)
+
+    chunk = rows_in[0].shape[0] // CHUNKS
     started = []
 
     def push(source, target, kind, index, k):
         copy = pltpu.make_async_remote_copy(
             src_ref=source,
             dst_ref=target,
-            send_sem=send.at[kind, index],
-            recv_sem=recv.at[kind, index],
+            send_sem=send.at[kind, index, k - 1],
+            recv_sem=recv.at[kind, index, k - 1],
             device_id={"tensor": step(me, k)},
             device_id_type=MESH,
         )
@@ -97,76 +117,59 @@
         started.append(copy)
         return copy
 
-    chunks = range(2 * SUBS)
-    here = lambda c: pl.ds(c * chunk, chunk)
-    onward = lambda c: PLUS if c % 2 == 0 else MINUS
-    aside = lambda c: MINUS if c % 2 == 0 else PLUS
-    side_of = {PLUS: from_minus, MINUS: from_plus}
-    way, straight, summed = {}, {}, {}
+    def ride():
+        if stages:
+            stages.pop(0)()
+
+    reduces = {}
     if reduce:
-        for c in chunks:
-            way[c] = push(part.at[step(me, FAR), here(c)], passing.at[here(c)], 0, c, onward(c))
-        for c in chunks:
-            straight[c] = push(
-                part.at[step(me, aside(c)), here(c)], side_of[aside(c)].at[here(c)], 1, c, aside(c)
-            )
-        for c in chunks:
-            way[c].wait_recv()
-            joined[here(c)] = (
-                part[step(me, onward(c)), here(c)].astype(F32) + passing[here(c)].astype(F32)
-            ).astype(BF16)
-            summed[c] = push(joined.at[here(c)], side_of[onward(c)].at[here(c)], 2, c, onward(c))
+        for c in range(CHUNKS):
+            here = pl.ds(c * chunk, chunk)
+            for k in range(1, RING):
+                reduces[c, k] = push(
+                    part.at[step(me, k), here], landing.at[k - 1, here], 0, c, k
+                )
     last = []
     if with_seg:
         own = pltpu.make_async_copy(seg_in, seg_out.at[me], local)
         own.start()
-        seg_up = push(seg_in, seg_out.at[me], 6, 0, PLUS)
-        seg_down = push(seg_in, seg_out.at[me], 6, 1, MINUS)
-        last.append(seg_down)
+        last += [push(seg_in, seg_out.at[me], 2, 0, k) for k in range(1, RING)]
+    ride()
     sums = [None] * n_sums
-    ups, downs = {}, {}
-    for c in chunks:
+    for c in range(CHUNKS):
+        here = pl.ds(c * chunk, chunk)
         total = None
         if reduce:
-            straight[c].wait_recv()
-            summed[c].wait_recv()
-            total = (
-                part[me, here(c)].astype(F32)
-                + from_minus[here(c)].astype(F32)
-                + from_plus[here(c)].astype(F32)
-            )
+            for k in range(1, RING):
+                reduces[c, k].wait_recv()
+            total = part[me, here].astype(F32)
+            for k in range(1, RING):
+                total = total + landing[k - 1, here].astype(F32)
         spread, outs, parts = function(
-            total, [ref[here(c)].astype(F32) for ref in rows_in], vecs
+            total, [ref[here].astype(F32) for ref in rows_in], vecs
         )
         if gather:
-            full[me, here(c)] = spread.astype(BF16)
-            ups[c] = push(full.at[me, here(c)], full.at[me, here(c)], 3, c, PLUS)
-            downs[c] = push(full.at[me, here(c)], full.at[me, here(c)], 4, c, MINUS)
+            full[me, here] = spread.astype(BF16)
+            last += [push(full.at[me, here], full.at[me, here], 1, c, k) for k in range(1, RING)]
         for ref, value in zip(rows_out, outs):
-            ref[here(c)] = value.astype(ref.dtype)
+            ref[here] = value.astype(ref.dtype)
         sums = [new if old is None else old + new for old, new in zip(sums, parts)]
-    if gather:
-        for c in chunks:
-            (ups if c % 2 == 0 else downs)[c].wait_recv()
-            came = full.at[step(me, aside(c)), here(c)]
-            last.append(push(came, came, 5, c, onward(c)))
-            last.append((downs if c % 2 == 0 else ups)[c])
+        ride()
     if n_sums:
         sums_out[...] = jnp.concatenate(
             sums + [jnp.zeros((8 - n_sums, sums[0].shape[1]), F32)], axis=0
         )
+    while stages:
+        ride()
+    for copy in last:
+        copy.wait_recv()
     if with_seg:
         own.wait()
-        seg_up.wait_recv()
-        came = seg_out.at[step(me, MINUS)]
-        last.append(push(came, came, 6, 2, PLUS))
-    for copy in last:
-        copy.wait_recv()
     for copy in started:
         copy.wait_send()
 
 
-def tensor_call(cid, function, part, rows, vecs, outs, n_sums, gather, seg=None):
+def tensor_call(cid, function, part, rows, vecs, outs, n_sums, gather, seg=None, rider=None):
     height, width = rows[0].shape
     reduce = part is not None
     with_seg = seg is not None
@@ -178,19 +181,25 @@
         shapes.append(jax.ShapeDtypeStruct((RING, height, width), BF16))
     if with_seg:
         shapes.append(jax.ShapeDtypeStruct((RING,) + seg.shape, seg.dtype))
-    scratch = [pltpu.VMEM((height, width), BF16)] * 4 if reduce else []
+    in_specs, out_specs = [vmem_spec()] * len(args), [vmem_spec()] * len(shapes)
+    scratch = [pltpu.VMEM((RING - 1, height, width), BF16)] if reduce else []
     scratch += [
-        pltpu.SemaphoreType.DMA((7, 2 * SUBS)),
-        pltpu.SemaphoreType.DMA((7, 2 * SUBS)),
+        pltpu.SemaphoreType.DMA((3, CHUNKS, RING - 1)),
+        pltpu.SemaphoreType.DMA((3, CHUNKS, RING - 1)),
         pltpu.SemaphoreType.DMA,
     ]
+    if rider:
+        args, in_specs = args + rider.ins, in_specs + rider.in_specs
+        shapes, out_specs = shapes + rider.outs, out_specs + rider.out_specs
+        scratch = scratch + rider.scratch
     return pl.pallas_call(
         functools.partial(
-            tensor_kernel, function, len(rows), len(vecs), len(outs), n_sums, reduce, gather, with_seg
+            tensor_kernel, function, len(rows), len(vecs), len(outs), n_sums, reduce, gather, with_seg,
+            rider,
         ),
         out_shape=shapes,
-        in_specs=[vmem_spec()] * len(args),
-        out_specs=[vmem_spec()] * len(shapes),
+        in_specs=in_specs,
+        out_specs=out_specs,
         scratch_shapes=scratch,
         compiler_params=comm_params(cid),
     )(*args)
@@ -373,68 +382,195 @@
         self.spread(i, FAR, self.block(i, FAR, 0))
 
 
-def gather_kernel(pieces, n_in, n_out, with_sibling, *refs):
-    ins, outs = refs[:n_in], refs[n_in : n_in + n_out]
-    send, recv, local = refs[n_in + n_out :]
+def half_of(section, height):
+    return pl.ds(pl.multiple_of(section * height, height), height)
+
+
+def spread_stages(ring, sources, local, section, push):
+    own, across = {}, []
+
+    def pass_on(i, line):
+        came = ring.block(i, slice(None), line)
+        across.append(push(i, 5, line, came, came, {"section": 1 - section}))
+
+    def begin():
+        for i in ring.every:
+            ring.begin(i, sources[i])
+            own[i] = pltpu.make_async_copy(sources[i], ring.block(i, 0, 0), local.at[i])
+            own[i].start()
+
+    def near():
+        ring.near()
+        for i in ring.every:
+            ring.relay(i, 0)
+
+    def middle():
+        for i in ring.every:
+            ring.far(i)
+        for i in ring.every:
+            ring.relay(i, MINUS)
+            ring.relay(i, PLUS)
+            own[i].wait()
+            pass_on(i, 0)
+
+    def end():
+        for i in ring.every:
+            ring.relay(i, FAR)
+            for offset in range(RING):
+                ring.other(i, offset)
+            pass_on(i, PLUS)
+            pass_on(i, MINUS)
+        for i in ring.every:
+            for offset in range(RING):
+                ring.relayed[i, offset].wait_recv()
+            pass_on(i, FAR)
+        for copy in across:
+            copy.wait_recv()
+
+    return [begin, near, middle, end]
+
+
+def out_views(ref, rows):
+    if len(ref.shape) == 5:
+        return [ref.at[which, :, :, rows] for which in range(ref.shape[0])]
+    return [ref.at[:, :, rows]]
+
+
+def in_views(ref):
+    if len(ref.shape) == 3:
+        return [ref.at[which] for which in range(ref.shape[0])]
+    return [ref]
+
+
+def weight_pieces(count):
+    return tuple((i, (), i % 2 == 0) for i in range(count))
+
+
+def weight_rider(halves):
+    count = sum(3 if value.ndim == 3 else 1 for value in halves)
+    height = halves[0].shape[-2]
+
+    def build(y, z, section, ins, outs, scratch):
+        send, recv, local = scratch
+        started = []
+        push = pusher(send, recv, started)
+        rows = half_of(section, height)
+        views = [view for ref in outs for view in out_views(ref, rows)]
+        sources = [view for ref in ins for view in in_views(ref)]
+        ring = Gather(weight_pieces(count), views, y, z, (), push)
+
+        def finish():
+            for copy in started:
+                copy.wait_send()
+
+        return spread_stages(ring, sources, local, section, push) + [finish]
+
+    outs = [
+        jax.ShapeDtypeStruct(
+            value.shape[:-2] + (RING, RING, 2 * height, value.shape[-1]), value.dtype
+        )
+        for value in halves
+    ]
+    return Rider(
+        build,
+        list(halves),
+        [vmem_spec()] * len(halves),
+        outs,
+        [any_spec()] * len(outs),
+        [
+            pltpu.SemaphoreType.DMA((count, 6, RING)),
+            pltpu.SemaphoreType.DMA((count, 6, RING)),
+            pltpu.SemaphoreType.DMA((count,)),
+        ],
+    )
+
+
+def first_kernel(
+    qkv_in, out_in, up_in, down_in, small_in, seg_in,
+    qkv_half, out_half, up_half, down_half, qkv_out, out_out, rows_out, seg_out,
+    small_all, send, recv, local, swap_send, swap_recv, swap_local,
+):
     rank = lax.axis_index("dp")
     y, z = rank // RING, lax.rem(rank, RING)
     section = lax.axis_index("section")
     barrier, count = dp_barrier(y, z, section)
+    height = out_half.shape[-2]
+    mine, other = half_of(section, height), half_of(1 - section, height)
+    lead = lambda ref: (slice(None),) * (len(ref.shape) - 2)
     pl.semaphore_wait(barrier, count)
-    started = []
+    started, swaps = [], []
+    for i, (source, target) in enumerate(
+        ((qkv_in, qkv_half), (out_in, out_half), (up_in, up_half), (down_in, down_half))
+    ):
+        copy = pltpu.make_async_remote_copy(
+            src_ref=source.at[lead(source) + (other,)],
+            dst_ref=target.at[section],
+            send_sem=swap_send.at[i],
+            recv_sem=swap_recv.at[i],
+            device_id={"section": 1 - section},
+            device_id_type=MESH,
+        )
+        copy.start()
+        started.append(copy)
+        kept = pltpu.make_async_copy(
+            source.at[lead(source) + (mine,)], target.at[section], swap_local.at[i]
+        )
+        kept.start()
+        swaps.append((copy, kept))
     push = pusher(send, recv, started)
-    ring = Gather(pieces, outs, y, z, (section,), push)
-    own = {}
-    for i, (number, pre, _) in enumerate(pieces):
-        source = ins[number].at[pre] if pre else ins[number]
-        ring.begin(i, source)
-        own[i] = pltpu.make_async_copy(source, ring.block(i, 0, 0), local.at[i])
-        own[i].start()
-    across = []
-
-    def pass_on(i, line):
-        came = ring.block(i, slice(None), line)
-        across.append(push(i, 5, line, came, came, {"section": 1 - section}))
-
-    ring.near()
-    for i in ring.every:
-        ring.relay(i, 0)
-    for i in ring.every:
-        ring.far(i)
-    for i in ring.every:
-        ring.relay(i, MINUS)
-        ring.relay(i, PLUS)
-        own[i].wait()
-        pass_on(i, 0)
-    for i in ring.every:
-        ring.relay(i, FAR)
-        for offset in range(RING):
-            ring.other(i, offset)
-        pass_on(i, PLUS)
-        pass_on(i, MINUS)
-    for i in ring.every:
-        for offset in range(RING):
-            ring.relayed[i, offset].wait_recv()
-        pass_on(i, FAR)
-    for copy in across:
+    views = [small_all.at[section], seg_out.at[section]]
+    views += [qkv_out.at[which, :, :, mine] for which in range(3)] + [out_out.at[:, :, mine]]
+    sources = [small_in, seg_in]
+    sources += [qkv_half.at[0, which] for which in range(3)] + [out_half.at[0]]
+    ring = Gather(weight_pieces(6), views, y, z, (), push)
+    stages = spread_stages(ring, sources, local, section, push)
+    for copy, kept in swaps[:2]:
         copy.wait_recv()
+        kept.wait()
+    for stage in stages:
+        stage()
+    depth = rows_out.shape[-1] // (RING * RING)
+    for layer in range(2):
+        for number in range(RING * RING):
+            block = small_all[layer, number // RING, number % RING]
+            rows_out[layer, :, number * depth : (number + 1) * depth] = block[:, :depth].astype(F32)
+    for copy, kept in swaps[2:]:
+        copy.wait_recv()
+        kept.wait()
     for copy in started:
         copy.wait_send()
 
 
-def gather_call(cid, pieces, ins, outs, with_sibling):
+def first_call(cid, w_qkv, w_out, w_up, w_down, small, seg):
+    depth, width = w_out.shape
+    hidden = w_up.shape[1]
+    half = depth // 2
+    shape = lambda *dims: jax.ShapeDtypeStruct(dims, BF16)
     return pl.pallas_call(
-        functools.partial(gather_kernel, pieces, len(ins), len(outs), with_sibling),
-        out_shape=outs,
-        in_specs=[vmem_spec()] * len(ins),
-        out_specs=[any_spec()] * len(outs),
+        first_kernel,
+        out_shape=[
+            shape(2, 3, half, width),
+            shape(2, half, width),
+            shape(2, half, hidden),
+            shape(2, half, hidden),
+            shape(3, RING, RING, depth, width),
+            shape(RING, RING, depth, width),
+            jax.ShapeDtypeStruct((2, 16, RING * RING * depth), F32),
+            jax.ShapeDtypeStruct((2, RING, RING) + seg.shape, seg.dtype),
+        ],
+        in_specs=[vmem_spec()] * 6,
+        out_specs=[vmem_spec()] * 4 + [any_spec()] * 2 + [vmem_spec()] * 2,
         scratch_shapes=[
-            pltpu.SemaphoreType.DMA((len(pieces), 6, RING)),
-            pltpu.SemaphoreType.DMA((len(pieces), 6, RING)),
-            pltpu.SemaphoreType.DMA((len(pieces),)),
+            pltpu.VMEM((2, RING, RING) + small.shape, BF16),
+            pltpu.SemaphoreType.DMA((6, 6, RING)),
+            pltpu.SemaphoreType.DMA((6, 6, RING)),
+            pltpu.SemaphoreType.DMA((6,)),
+            pltpu.SemaphoreType.DMA((4,)),
+            pltpu.SemaphoreType.DMA((4,)),
+            pltpu.SemaphoreType.DMA((4,)),
         ],
         compiler_params=comm_params(cid),
-    )(*ins)
+    )(w_qkv, w_out, w_up, w_down, small, seg)
 
 
 class Scatter:
@@ -578,35 +714,147 @@
 SCATTER_BUFFERS = 9
 
 
-def final_kernel(orders, n_extra, *refs):
-    n = len(orders)
+def gradient_scratch(values):
+    scratch = []
+    for value in values:
+        block = (value.shape[2] // 2, value.shape[3])
+        square = pltpu.VMEM((RING, RING) + block, value.dtype)
+        scratch += [square, square] + Scatter.scratch(block, value.dtype)
+    return scratch + [
+        pltpu.SemaphoreType.DMA((len(values), 8, RING)),
+        pltpu.SemaphoreType.DMA((len(values), 8, RING)),
+    ]
+
+
+def gradient_stages(y, z, section, ins, outs, scratch, shared):
+    count = len(ins)
+    size = 2 + SCATTER_BUFFERS
+    send, recv = scratch[count * size :]
+    started = []
+    push = pusher(send, recv, started)
+    other = {"section": 1 - section}
+    siblings = [scratch[i * size] for i in range(count)]
+    owns = [scratch[i * size + 1] for i in range(count)]
+    parts = [
+        Scatter(
+            i, i % 2 == 0, owns[i], scratch[i * size + 2 : (i + 1) * size], y, z, push
+        )
+        for i in range(count)
+    ]
+    across, results = [], []
+
+    def swap():
+        for i in range(count):
+            height = owns[i].shape[2]
+            across.append(
+                push(i, 6, 0, ins[i].at[:, :, half_of(1 - section, height)], siblings[i], other)
+            )
+
+    def begin():
+        for i in range(count):
+            across[i].wait_recv()
+            mine = half_of(section, owns[i].shape[2])
+
+            def add(number, carry):
+                at_y, at_z = number // RING, lax.rem(number, RING)
+                owns[i][at_y, at_z] = (
+                    ins[i][at_y, at_z, mine].astype(F32) + siblings[i][at_y, at_z].astype(F32)
+                ).astype(owns[i].dtype)
+                return carry
+
+            lax.fori_loop(0, RING * RING, add, 0)
+            parts[i].begin()
+
+    def join():
+        for part in parts:
+            part.join()
+
+    def turn():
+        for part in parts:
+            part.turn()
+
+    def join_two():
+        for part in parts:
+            part.join_two()
+
+    def finish():
+        for i in range(count):
+            height = owns[i].shape[2]
+            if shared[i]:
+                mine = outs[i].at[half_of(section, height)]
+                parts[i].finish(mine)
+                results.append(push(i, 7, 0, mine, mine, other))
+            else:
+                parts[i].finish(outs[i])
+
+    def end():
+        for copy in results:
+            copy.wait_recv()
+        for copy in started:
+            copy.wait_send()
+
+    return [swap, begin, join, turn, join_two, finish, end]
+
+
+def gradient_rider(values):
+    def build(y, z, section, ins, outs, scratch):
+        return gradient_stages(y, z, section, ins, outs, scratch, [True] * len(ins))
+
+    return Rider(
+        build,
+        list(values),
+        [vmem_spec()] * len(values),
+        [jax.ShapeDtypeStruct(value.shape[2:], F32) for value in values],
+        [vmem_spec()] * len(values),
+        gradient_scratch(values),
+    )
+
+
+def final_kernel(n_extra, n_grad, *refs):
     refs = list(refs)
     take = lambda count: [refs.pop(0) for _ in range(count)]
-    ins, extras = take(n), take(n_extra)
-    outs, extra_outs = take(n), take(n_extra)
-    siblings, owns = take(n), take(n)
-    buffers = [take(SCATTER_BUFFERS) for _ in range(n)]
-    vector_own, vector_parts = take(2)
-    send, recv, local, extra_send, extra_recv = take(5)
+    sums = [take(5), take(5)]
+    ins, extras = take(n_grad), take(n_extra)
+    small_out = take(1)[0]
+    outs, extra_outs = take(n_grad), take(n_extra)
+    small_in, small_rows, vector_own, vector_parts = take(4)
+    vector_send, vector_recv, extra_send, extra_recv = take(4)
     rank = lax.axis_index("dp")
     y, z = rank // RING, lax.rem(rank, RING)
     section = lax.axis_index("section")
     me = lax.axis_index("tensor")
-    barrier, count = dp_barrier(y, z, section)
-    for k in range(1, RING):
-        pl.semaphore_signal(
-            barrier, inc=1, device_id={"tensor": step(me, k)}, device_id_type=MESH
-        )
-    pl.semaphore_wait(barrier, count + RING - 1)
-    started = []
-    push = pusher(send, recv, started)
-    other = {"section": 1 - section}
-    across, local_copies = [], []
-    for i in range(n):
-        across.append(push(i, 6, 0, ins[i].at[1 - section], siblings[i], other))
-        copy = pltpu.make_async_copy(ins[i].at[section], owns[i], local.at[i])
-        copy.start()
-        local_copies.append(copy)
+    barrier, count = tensor_barrier(me)
+    count += dp_barrier(y, z, section)[1]
+    small_rows[...] = jnp.zeros_like(small_rows)
+    width = small_rows.shape[1]
+    for layer in range(2):
+        first, middle, end, attend, up = sums[layer]
+        top = 16 * layer
+        part = attend.shape[1]
+        lanes = pl.ds(pl.multiple_of(me * part, part), part)
+        small_rows[top : top + 2, :] = first[0:2, :]
+        small_rows[top + 2 : top + 3, lanes] = attend[0:1, :]
+        small_rows[top + 3 : top + 4, lanes] = attend[1:2, :]
+        small_rows[top + 4 : top + 5, :] = middle[2:3, :]
+        small_rows[top + 5 : top + 7, :] = middle[0:2, :]
+        small_rows[top + 7 : top + 8, :] = end[1:2, :]
+        small_rows[top + 8 : top + 9, :] = end[0:1, :]
+        for rank_of in range(RING):
+            small_rows[top + 9 + rank_of : top + 10 + rank_of, :] = jnp.where(
+                me == rank_of, up[0:1, :], 0.0
+            )
+        small_rows[top + 13 : top + 14, :] = middle[3:4, :]
+    small_in[...] = jnp.zeros_like(small_in)
+    depth = width // (RING * RING)
+    for number in range(RING * RING):
+        small_in[number // RING, number % RING, :, 0:depth] = small_rows[
+            :, number * depth : (number + 1) * depth
+        ]
+    pl.semaphore_wait(barrier, count)
+    stages = gradient_stages(
+        y, z, section, [small_in] + ins, [vector_own] + outs, refs, [False] + [True] * n_grad
+    )
+    stages[0]()
     extra_copies = []
     for i in range(n_extra):
         copy = pltpu.make_async_remote_copy(
@@ -614,79 +862,62 @@
             dst_ref=extra_outs[i],
             send_sem=extra_send.at[i],
             recv_sem=extra_recv.at[i],
-            device_id=other,
+            device_id={"section": 1 - section},
             device_id_type=MESH,
         )
         copy.start()
         extra_copies.append(copy)
-    parts = []
-    for i in range(n):
-        local_copies[i].wait()
-        across[i].wait_recv()
-        own, sibling = owns[i], siblings[i]
-
-        def add(number, carry):
-            at_y, at_z = number // RING, lax.rem(number, RING)
-            own[at_y, at_z] = (
-                own[at_y, at_z].astype(F32) + sibling[at_y, at_z].astype(F32)
-            ).astype(own.dtype)
-            return carry
-
-        lax.fori_loop(0, RING * RING, add, 0)
-        parts.append(Scatter(i, orders[i], own, buffers[i], y, z, push))
-        parts[i].begin()
-    for part in parts:
-        part.join()
-    for part in parts:
-        part.turn()
-    for part in parts:
-        part.join_two()
-    for i, part in enumerate(parts):
-        part.finish(vector_own if i == 0 else outs[i])
-        if i == 0:
-            vector_parts[me] = vector_own[...]
-            vector_copies = [
-                push(0, 7, k, vector_own, vector_parts.at[me], {"tensor": step(me, k)})
-                for k in range(1, RING)
-            ]
+    for stage in stages[1:6]:
+        stage()
+    vector_parts[me] = vector_own[...]
+    vector_copies = []
+    for k in range(1, RING):
+        copy = pltpu.make_async_remote_copy(
+            src_ref=vector_own,
+            dst_ref=vector_parts.at[me],
+            send_sem=vector_send.at[k],
+            recv_sem=vector_recv.at[k],
+            device_id={"tensor": step(me, k)},
+            device_id_type=MESH,
+        )
+        copy.start()
+        vector_copies.append(copy)
+    stages[6]()
     for copy in vector_copies:
-        copy.wait_recv()
+        copy.wait()
     total = vector_parts[0]
     for k in range(1, RING):
         total = total + vector_parts[k]
-    outs[0][...] = total
+    small_out[...] = total
     for copy in extra_copies:
         copy.wait()
-    for copy in started:
-        copy.wait_send()
-
-
-def final_call(cid, orders, ins, extras):
-    blocks = [value.shape[3:] for value in ins]
-    square = [
-        pltpu.VMEM((RING, RING) + block, value.dtype) for block, value in zip(blocks, ins)
-    ]
-    count, extra = len(ins), len(extras)
+
+
+def final_call(cid, sums, grads, extras):
+    extra = len(extras)
+    width = sums[0].shape[1]
+    small = jax.ShapeDtypeStruct((RING, RING, 32, 128), F32)
+    args = list(sums) + list(grads) + list(extras)
     return pl.pallas_call(
-        functools.partial(final_kernel, orders, extra),
-        out_shape=[jax.ShapeDtypeStruct(block, F32) for block in blocks]
+        functools.partial(final_kernel, extra, len(grads)),
+        out_shape=[jax.ShapeDtypeStruct((16, 128), F32)]
+        + [jax.ShapeDtypeStruct(value.shape[2:], F32) for value in grads]
         + [jax.ShapeDtypeStruct(value.shape, value.dtype) for value in extras],
-        in_specs=[any_spec()] * count + [vmem_spec()] * extra,
-        out_specs=[vmem_spec()] * (count + extra),
-        scratch_shapes=square
-        + square
-        + [one for block, value in zip(blocks, ins) for one in Scatter.scratch(block, value.dtype)]
-        + [
-            pltpu.VMEM(blocks[0], F32),
-            pltpu.VMEM((RING,) + blocks[0], F32),
-            pltpu.SemaphoreType.DMA((count, 8, RING)),
-            pltpu.SemaphoreType.DMA((count, 8, RING)),
-            pltpu.SemaphoreType.DMA((count,)),
+        in_specs=[vmem_spec()] * len(args),
+        out_specs=[vmem_spec()] * (1 + len(grads) + extra),
+        scratch_shapes=[
+            pltpu.VMEM(small.shape, F32),
+            pltpu.VMEM((32, width), F32),
+            pltpu.VMEM((16, 128), F32),
+            pltpu.VMEM((RING, 16, 128), F32),
+            pltpu.SemaphoreType.DMA((RING,)),
+            pltpu.SemaphoreType.DMA((RING,)),
             pltpu.SemaphoreType.DMA((extra,)),
             pltpu.SemaphoreType.DMA((extra,)),
-        ],
+        ]
+        + gradient_scratch([small] + list(grads)),
         compiler_params=comm_params(cid),
-    )(*ins, *extras)
+    )(*args)
 
 
 def gelu_exact(values):
@@ -717,17 +948,17 @@
 
 
 def attend_kernel(
-    layer, normed_ref, qkv_any, out_any, bias_ref, seg_q_ref, seg_k_ref,
+    normed_ref, qkv_any, out_any, bias_ref, seg_q_ref, seg_k_ref,
     q_ref, k_ref, v_ref, mixed_ref, wide_ref, lse_ref, part_ref,
     qkv_ref, out_ref, stack, acc, top_ref, total_ref, send, recv, local,
 ):
     group, width = q_ref.shape
     heads_here = width // HEAD_DIM
     loads = [
-        pltpu.make_async_copy(qkv_any.at[layer, which], qkv_ref.at[which], local.at[which])
+        pltpu.make_async_copy(qkv_any.at[which], qkv_ref.at[which], local.at[which])
         for which in range(3)
     ]
-    loads.append(pltpu.make_async_copy(out_any.at[layer], out_ref, local.at[3]))
+    loads.append(pltpu.make_async_copy(out_any, out_ref, local.at[3]))
     for which in (1, 2, 0, 3):
         loads[which].start()
     rank = lax.axis_index("dp")
@@ -834,13 +1065,13 @@
         copy.wait_send()
 
 
-def attend_call(cid, layer, normed, full_qkv, full_out, biases, seg_wide, seg_column):
+def attend_call(cid, normed, full_qkv, full_out, biases, seg_wide, seg_column):
     group, model = normed.shape
-    width = full_out.shape[2]
+    width = full_out.shape[1]
     heads_here = width // HEAD_DIM
     square = (RING, RING, group, width)
     return pl.pallas_call(
-        functools.partial(attend_kernel, layer),
+        attend_kernel,
         out_shape=[
             jax.ShapeDtypeStruct((group, width), BF16),
             jax.ShapeDtypeStruct(square, BF16),
@@ -868,7 +1099,7 @@
 
 
 def attend_back_kernel(
-    layer, rows_ref, qkv_any, out_any, q_ref, k_ref, v_ref, wide_ref, lse_ref, seg_q_ref, seg_k_ref,
+    rows_ref, qkv_any, out_any, q_ref, k_ref, v_ref, wide_ref, lse_ref, seg_q_ref, seg_k_ref,
     triple_ref, sums_ref, part_ref, *scratch,
 ):
     (
@@ -880,8 +1111,8 @@
     group, width = q_ref.shape
     heads_here = width // HEAD_DIM
     scale = HEAD_DIM ** (-0.5)
-    load_out = pltpu.make_async_copy(out_any.at[layer], out_ref, local.at[0])
-    load_qkv = pltpu.make_async_copy(qkv_any.at[layer], qkv_ref, local.at[1])
+    load_out = pltpu.make_async_copy(out_any, out_ref, local.at[0])
+    load_qkv = pltpu.make_async_copy(qkv_any, qkv_ref, local.at[1])
     load_out.start()
     load_qkv.start()
     rank = lax.axis_index("dp")
@@ -976,14 +1207,14 @@
         copy.wait_send()
 
 
-def attend_back_call(cid, layer, attn_rows, full_qkv, full_out, queries, keys, values, wide, lse, seg_wide, seg_column):
+def attend_back_call(cid, attn_rows, full_qkv, full_out, queries, keys, values, wide, lse, seg_wide, seg_column):
     group, model = attn_rows.shape
     width = queries.shape[1]
     heads_here = width // HEAD_DIM
     block = (group, width)
     stacked = pltpu.VMEM((group * heads_here, width), BF16)
     return pl.pallas_call(
-        functools.partial(attend_back_kernel, layer),
+        attend_back_kernel,
         out_shape=[
             jax.ShapeDtypeStruct((3, group, width), BF16),
             jax.ShapeDtypeStruct((8, width), F32),
@@ -1016,18 +1247,6 @@
     )(attn_rows, full_qkv, full_out, queries, keys, values, wide, lse, seg_wide, seg_column)
 
 
-WEIGHT_PIECES = (
-    (0, (0,), True),
-    (0, (1,), False),
-    (0, (2,), True),
-    (1, (), False),
-    (4, (), True),
-    (5, (), False),
-    (2, (), True),
-    (3, (), False),
-)
-
-
 def shards(tokens, segment_ids, w_qkv, w_out, w_up, w_down, vectors, out_bias, cotangent):
     section = lax.axis_index("section")
     tensor_rank = lax.axis_index("tensor")
@@ -1044,40 +1263,23 @@
         jnp.concatenate([vectors[0], out_bias], axis=0),
         ((0, 2), (0, 128 - depth)),
     )
-    shape = lambda *dims: jax.ShapeDtypeStruct(dims, BF16)
     my_segments = own(segment_ids)
-    seg_block = jnp.zeros((8, 128), jnp.int32).at[0, :rows].set(my_segments)
-    full_qkv, full_out, full_up, full_down, full_small, full_seg = gather_call(
-        0,
-        WEIGHT_PIECES,
-        [w_qkv[0], w_out[0], w_up[0], w_down[0], small, seg_block],
-        [
-            shape(2, 3, *square, depth, local_width),
-            shape(2, *square, depth, local_width),
-            shape(2, *square, depth, local_hidden),
-            shape(2, *square, depth, local_hidden),
-            shape(2, *square, 16, 128),
-            jax.ShapeDtypeStruct((2,) + square + (8, 128), jnp.int32),
-        ],
-        True,
+    seg_block = jnp.pad(my_segments[None], ((0, 7), (0, 128 - rows)))
+    qkv_half, out_half, up_half, down_half, qkv_first, out_first, small_rows, full_seg = first_call(
+        0, w_qkv[0], w_out[0], w_up[0], w_down[0], small, seg_block
     )
-    full_qkv = full_qkv.reshape(2, 3, width, local_width)
-    full_out = full_out.reshape(2, width, local_width)
-    full_up = full_up.reshape(2, width, local_hidden)
-    full_down = full_down.reshape(2, width, local_hidden)
-    small_rows = (
-        full_small.reshape(2, RING * RING, 16, 128)[..., :depth]
-        .transpose(0, 2, 1, 3)
-        .reshape(2, 16, width)
-        .astype(F32)
-    )
+    joined_qkv = lambda value: value.reshape(3, width, local_width)
+    joined = lambda value: value.reshape(width, value.shape[-1])
 
     my_tokens = own(tokens)
     my_cotangent = own(cotangent)
     seg_mine = own(full_seg)[:, :, 0, :rows].reshape(8, 128)
-    normed, seg_group = tensor_call(
-        1, first_rows, None, [my_tokens], [small_rows[0]], [], 0, True, seg_mine
+    normed, seg_group, up_first, down_first = tensor_call(
+        1, first_rows, None, [my_tokens], [small_rows[0]], [], 0, True, seg_mine,
+        weight_rider([up_half[0], down_half[0]]),
     )
+    full_qkv, full_out = [joined_qkv(qkv_first), None], [joined(out_first), None]
+    full_up, full_down = [joined(up_first), None], [joined(down_first), None]
     seg_all = seg_group.reshape(RING, RING * RING, rows).transpose(1, 0, 2).reshape(-1, group)
     seg_rows = lax.dynamic_index_in_dim(seg_all, lax.axis_index("dp"), 0, keepdims=False)
     seg_wide = jnp.broadcast_to(seg_rows[None], (8, group))
@@ -1092,13 +1294,18 @@
         up_bias = lax.dynamic_slice_in_dim(
             vec[9:13].reshape(-1), tensor_rank * local_hidden, local_hidden
         )
-        biases = jnp.zeros((8, local_width), F32).at[0].set(query_bias).at[1].set(value_bias)
+        biases = jnp.pad(jnp.stack([query_bias, value_bias]), ((0, 6), (0, 0)))
         queries, keys_full, values_full, mixed, wide, lse, part = attend_call(
-            2 + 12 * layer, layer, normed, full_qkv, full_out, biases, seg_wide, seg_column
-        )
-        attn_out, hidden, normed_two = tensor_call(
-            3, middle_rows, part, [inputs.astype(F32)], [vec], [F32, F32], 0, True
-        )
+            2 + 12 * layer, normed, full_qkv[layer], full_out[layer], biases, seg_wide, seg_column
+        )
+        rider = weight_rider([qkv_half[1], out_half[1]]) if layer == 0 else None
+        results = tensor_call(
+            3 + 12 * layer, middle_rows, part, [inputs.astype(F32)], [vec], [F32, F32], 0, True,
+            None, rider,
+        )
+        attn_out, hidden, normed_two = results[:3]
+        if layer == 0:
+            full_qkv[1], full_out[1] = joined_qkv(results[3]), joined(results[4])
         normed_two = normed_two.reshape(group, width)
         pre_act = jnp.dot(normed_two, full_up[layer], preferred_element_type=F32) + up_bias
         activated = gelu_exact(pre_act).astype(BF16)
@@ -1106,9 +1313,11 @@
         step_kept = [inputs, normed, queries, keys_full, values_full, mixed, attn_out, hidden]
         step_kept += [normed_two, pre_act, activated, wide, lse]
         if layer == 0:
-            mlp_first, between, normed = tensor_call(
-                4, end_rows_first, part, [hidden], [vec, small_rows[1]], [F32, BF16], 0, True
+            mlp_first, between, normed, up_second, down_second = tensor_call(
+                4, end_rows_first, part, [hidden], [vec, small_rows[1]], [F32, BF16], 0, True,
+                None, weight_rider([up_half[1], down_half[1]]),
             )
+            full_up[1], full_down[1] = joined(up_second), joined(down_second)
             inputs = between
         else:
             outputs, sums_end, mlp_rows = tensor_call(
@@ -1117,33 +1326,37 @@
         kept.append(step_kept)
 
     upstream = my_cotangent.astype(F32)
-    grads = [None, None]
-    scale_two, down_bias = sums_end[0], sums_end[1]
+    blocks = lambda value: value.astype(BF16).reshape(*square, depth, value.shape[-1])
+    sums, waiting, summed = [None, None], None, [None, None]
     for layer in (1, 0):
         vec = small_rows[layer]
         inputs, normed, queries, keys_full, values_full, mixed, attn_out, hidden = kept[layer][:8]
         normed_two, pre_act, activated, wide, lse = kept[layer][8:]
         mlp_rows = mlp_rows.reshape(group, width)
         act_grad = jnp.dot(mlp_rows, full_down[layer], preferred_element_type=F32)
-        grad_down = rows_dot(mlp_rows, activated)
+        grad_down = blocks(rows_dot(mlp_rows, activated))
         pre_grad = jax.vjp(gelu_exact, pre_act)[1](act_grad)[0]
-        up_bias_grad = jnp.sum(pre_grad, axis=0)
+        up_bias_grad = jnp.broadcast_to(jnp.sum(pre_grad, axis=0)[None], (8, local_hidden))
         pre_low = pre_grad.astype(BF16)
-        grad_up = rows_dot(normed_two, pre_low)
+        grad_up = blocks(rows_dot(normed_two, pre_low))
         part = flat_dot(pre_low, full_up[layer]).astype(BF16).reshape(RING, rows, width)
-        hidden_grad, sums_middle, attn_rows = tensor_call(
-            6, back_middle_rows, part, [upstream, hidden, attn_out], [vec], [F32], 4, True
-        )
+        results = tensor_call(
+            6 + 12 * layer, back_middle_rows, part, [upstream, hidden, attn_out], [vec], [F32], 4, True,
+            None, gradient_rider(waiting) if layer == 0 else None,
+        )
+        hidden_grad, sums_middle, attn_rows = results[:3]
+        if layer == 0:
+            summed[1] = results[3:] + summed[1]
         attn_rows = attn_rows.reshape(group, width)
-        grad_out = rows_dot(attn_rows, mixed)
+        grad_out = blocks(rows_dot(attn_rows, mixed))
         triple, sums_attend, part = attend_back_call(
-            7 + 12 * layer, layer, attn_rows, full_qkv, full_out, queries, keys_full, values_full,
+            7 + 12 * layer, attn_rows, full_qkv[layer], full_out[layer], queries, keys_full, values_full,
             wide, lse, seg_wide, seg_column,
         )
-        query_bias_grad, value_bias_grad = sums_attend[0], sums_attend[1]
-        grad_qkv = [rows_dot(normed, triple[which]) for which in range(3)]
+        waiting = [blocks(rows_dot(normed, triple[which])) for which in range(3)]
+        rider = gradient_rider([grad_up, grad_down, grad_out])
         if layer == 1:
-            input_grad, sums_last, mlp_rows = tensor_call(
+            results = tensor_call(
                 8,
                 back_end_rows_last,
                 part,
@@ -1152,64 +1365,45 @@
                 [F32],
                 4,
                 True,
+                None,
+                rider,
             )
+            input_grad, sums_last, mlp_rows = results[:3]
+            summed[1] = results[3:]
         else:
-            input_grad, sums_last = tensor_call(
-                9, back_end_rows_first, part, [hidden_grad, inputs.astype(F32)], [vec], [F32], 2, False
+            results = tensor_call(
+                9, back_end_rows_first, part, [hidden_grad, inputs.astype(F32)], [vec], [F32], 2, False,
+                None, rider,
             )
-
-        def placed(values, length):
-            empty = jnp.zeros((length,), F32)
-            return lax.dynamic_update_slice(empty, values, (tensor_rank * values.shape[0],))
-
-        vector_rows = jnp.concatenate(
-            [
-                sums_last[0:2],
-                placed(query_bias_grad, width)[None],
-                placed(value_bias_grad, width)[None],
-                sums_middle[2:3],
-                sums_middle[0:2],
-                down_bias[None],
-                scale_two[None],
-                placed(up_bias_grad, local_hidden * RING).reshape(-1, width),
-                sums_middle[3:4],
-                jnp.zeros((2, width), F32),
-            ],
-            axis=0,
-        )
-        vector_rows = jnp.pad(
-            vector_rows.reshape(16, RING * RING, depth).transpose(1, 0, 2),
-            ((0, 0), (0, 0), (0, 128 - depth)),
-        ).reshape(*square, 16, 128)
-        grads[layer] = [vector_rows] + [
-            value.astype(BF16).reshape(*square, depth, value.shape[-1])
-            for value in grad_qkv + [grad_out, grad_up, grad_down]
-        ]
+            input_grad, sums_last = results[:2]
+            summed[0] = results[2:]
+        sums[layer] = [sums_last, sums_middle, sums_end, sums_attend, up_bias_grad]
         if layer == 1:
             last_grad = input_grad
             upstream = input_grad.astype(BF16).astype(F32)
-            scale_two, down_bias = sums_last[2], sums_last[3]
+            sums_end = sums_last[2:]
     first_grad = input_grad
 
-    stacked = [jnp.stack(pair) for pair in zip(*grads)]
     extras = [
         jnp.where(section == 0, outputs, between),
         jnp.where(section == 0, last_grad, first_grad),
     ]
-    results = final_call(10, (True, True, False, True, False, True, False), stacked, extras)
-    small_sum, grad_q, grad_k, grad_v, grad_out, grad_up, grad_down, came_out, came_grad = results
+    results = final_call(10, sums[0] + sums[1], waiting, extras)
+    small_sum, came_out, came_grad = results[0], results[4], results[5]
+    summed[0] = results[1:4] + summed[0]
     mine_out = jnp.where(section == 0, between, outputs)
     mine_grad = jnp.where(section == 0, first_grad, last_grad)
     pair = lambda mine, came: jnp.where(
         section == 0, jnp.stack([mine, came]), jnp.stack([came, mine])
     )[None]
+    pick = lambda which: jnp.where(section == 0, summed[0][which], summed[1][which])
     return (
         pair(mine_out, came_out),
         pair(mine_grad, came_grad),
-        jnp.stack([grad_q, grad_k, grad_v])[None],
-        grad_out[None],
-        grad_up[None],
-        grad_down[None],
+        jnp.stack([pick(0), pick(1), pick(2)])[None],
+        pick(5)[None],
+        pick(3)[None],
+        pick(4)[None],
         small_sum[:13, :depth][None],
         small_sum[13:14, :depth],
     )

time: 480 us -> 517 us (1.077)
  the two profiles are of different devices: /device:TPU:1 before, /device:TPU:0 now
where the time goes in v4:
time: 517 us; the launch traced here: 508 us
  Pallas kernels  427 us (83%)
  matrix products  41.2 us (8%)
  other arithmetic  21 us (4%)
  local copies, waits for them, and re-layouts  16.7 us (3%)
    pallas_call x9, Pallas kernels, tensor_call(): pl.pallas_call(functools.partial(tensor_kernel, function, len(rows), len(...  225 us
    pallas_call x2, Pallas kernels, attend_call(): pl.pallas_call(attend_kernel, out_shape=[jax.ShapeDtypeStruct((group, wid...  78 us
    pallas_call x2, Pallas kernels, attend_back_call(): pl.pallas_call(attend_back_kernel, out_shape=[jax.ShapeDtypeStruct((3, gr...  73.8 us
    pallas_call x1, Pallas kernels, first_call(): pl.pallas_call(first_kernel, out_shape=[shape(2, 3, half, width), shape(2...  25.7 us
    pallas_call x1, Pallas kernels, final_call(): pl.pallas_call(functools.partial(final_kernel, extra, len(grads)), out_sh...  24.7 us
    dot_general x12, matrix products, rows_dot(): lax.dot_general(former, latter, (((0,), (0,)), ((), ())), preferred_eleme...  19.5 us
    dot_general x2, matrix products, shards(): jnp.dot(normed_two, full_up[layer], preferred_element_type=F32) + up_bias  10.7 us

profile of v4, /device:TPU:0, one launch (start us, length us, event | category | flops | bytes accessed | tf_op | source)
XLA Modules:
  0.0 508.0 jit_solution(6584603521945885003)
XLA Ops:
  2.0 1.3 fusion.33.small_in
  3.3 1.7 fusion.43
  5.0 1.7 fusion.40
  6.8 25.7 %shard_map.152 = (bf16[2,3,32,256]{3,2,1,0:T(8,128)(2,1)}, bf16[2,32,256]{2,1,0:T(8,128)(2,1)}, bf16[2,32,1024]{2,1,0:T(8,128)(2,1)}, bf16[2,32,1024]{2,1,0:T(8,...) custom-call(bf16[3,64,256]{2,1,0:T(8,128)(2,1)} %bitcast.207, ...), custom_call_target="tpu_custom_call" | custom-call | tf_op jit(solution)/shard_map/pallas_call | solution.py:549
  34.1 1.3 slice_bitcast_fusion.9.refs_4_
  38.4 1.5 slice_bitcast_fusion.2
  39.9 1.4 slice_bitcast_fusion.6.refs_3_
  41.3 1.5 slice_bitcast_fusion.1
  42.8 1.5 slice_bitcast_fusion
  44.4 26.0 %shard_map.153 = (bf16[4,64,1024]{2,1,0:T(8,128)(2,1)}, s32[4,8,128]{2,1,0:T(8,128)}, bf16[4,4,64,1024]{3,2,1,0:T(8,128)(2,1)}, bf16[4,4,64,1024]{3,2,1,0:T(8,128)(2,1)}) custom-call(bf16[64,1024]{1,0:T(8,128)(2,1)} %get-tuple-element.183.refs_0_, f32[16,1024]{1,0:T(8,128)} %get-tuple-element.199.refs_1_.refs_2_.refs_5_.refs_4_.refs_3_, ...), custom_call_target="tpu_custom_call" | custom-call | tf_op jit(solution)/shard_map/pallas_call | solution.py:195
  72.0 1.7 broadcast_in_dim.50.seg_k_ref
  73.6 39.5 %shard_map.154 = (bf16[256,256]{1,0:T(8,128)(2,1)}, bf16[4,4,256,256]{3,2,1,0:T(8,128)(2,1)}, bf16[4,4,256,256]{3,2,1,0:T(8,128)(2,1)}, bf16[256,256]{1,0:T(8,12...) custom-call(bf16[256,1024]{1,0:T(8,128)(2,1)} %bitcast.159, ...), custom_call_target="tpu_custom_call" | custom-call | tf_op jit(solution)/shard_map/pallas_call | solution.py:1073
  113.1 25.3 %shard_map.155 = (f32[64,1024]{1,0:T(8,128)}, f32[64,1024]{1,0:T(8,128)}, bf16[4,64,1024]{2,1,0:T(8,128)(2,1)}, bf16[3,4,4,64,256]{4,3,2,1,0:T(8,128)(2,1)}, bf16[4,4,64,256]{3,2,1,0:T(8,128)(2,1)}) custom-call(bf16[4,64,1024]{2,1,0:T(8,128)(2,1)} %get-tuple-element.90.refs_0_, f32[64,1024]{1,0:T(8,128)} %get-tuple-element.182.refs_1_.refs_2_, ...), custom_call_target="tpu_custom_call" | custom-call | tf_op jit(solution)/shard_map/pallas_call | solution.py:195
  138.5 5.5 %multiply_convert_fusion.1 = (bf16[256,1024]{1,0:T(8,128)(2,1)S(1)}, f32[256,1024]{1,0:T(8,128)S(1)}, f32[256,1024]{1,0:T(8,128)}) fusion(f32[1024]{0:T(1024)S(1)} %dynamic_slice.25, bf16[256,1024]{1,0:T(8,128)(2,1)} %bitcast.192, bf16[1024,1024]{1,0:T(8,128)(2,1)S(1)} %bitcast.213), kind=kOutput, calls=%fused_computation.37 | convolution fusion | flops 554172416 | bytes 5246976 | tf_op jit(solution)/shard_map/dot_general | solution.py:1310
  144.0 1.6 convolution_convert_fusion.15
  145.6 27.5 %shard_map.156 = (f32[64,1024]{1,0:T(8,128)}, bf16[64,1024]{1,0:T(8,128)(2,1)}, bf16[4,64,1024]{2,1,0:T(8,128)(2,1)}, bf16[4,4,64,1024]{3,2,1,0:T(8,128)(2,1)}, bf16[4,4,64,1024]{3,2,1,0:T(8,128)(2,1)}) custom-call(bf16[4,64,1024]{2,1,0:T(8,128)(2,1)} %bitcast.190, f32[64,1024]{1,0:T(8,128)} %get-tuple-element.96.refs_1_.refs_2_, ...), custom_call_target="tpu_custom_call" | custom-call | tf_op jit(solution)/shard_map/pallas_call | solution.py:195
  173.1 1.6 convert_element_type.85.refs_1_.refs_2_
  174.8 38.5 %shard_map.157 = (bf16[256,256]{1,0:T(8,128)(2,1)}, bf16[4,4,256,256]{3,2,1,0:T(8,128)(2,1)}, bf16[4,4,256,256]{3,2,1,0:T(8,128)(2,1)}, bf16[256,256]{1,0:T(8,12...) custom-call(bf16[256,1024]{1,0:T(8,128)(2,1)} %bitcast.163, ...), custom_call_target="tpu_custom_call" | custom-call | tf_op jit(solution)/shard_map/pallas_call | solution.py:1073
  213.3 18.3 %shard_map.158 = (f32[64,1024]{1,0:T(8,128)}, f32[64,1024]{1,0:T(8,128)}, bf16[4,64,1024]{2,1,0:T(8,128)(2,1)}) custom-call(bf16[4,64,1024]{2,1,0:T(8,128)(2,1)} %get-tuple-element.101.refs_0_, f32[64,1024]{1,0:T(8,128)} %convert_element_type.85.refs_1_.refs_2_, f32[16,1024]{1,0:T(8,128)} %get-tuple-element.198.refs_3_.refs_2_.refs_4_), custom_call_target="tpu_custom_call" | custom-call | tf_op jit(solution)/shard_map/pallas_call | solution.py:195
  231.6 5.2 %multiply_convert_fusion = (bf16[256,1024]{1,0:T(8,128)(2,1)S(1)}, f32[256,1024]{1,0:T(8,128)S(1)}, f32[256,1024]{1,0:T(8,128)}) fusion(f32[1024]{0:T(1024)S(1)} %dynamic_slice.28, bf16[256,1024]{1,0:T(8,128)(2,1)} %bitcast.194, bf16[1024,1024]{1,0:T(8,128)(2,1)S(1)} %bitcast.217), kind=kOutput, calls=%fused_computation.24 | convolution fusion | flops 554172416 | bytes 5246976 | tf_op jit(solution)/shard_map/dot_general | solution.py:1310
  236.9 1.6 convolution_convert_fusion.14
  238.5 17.2 %shard_map.159 = (bf16[64,1024]{1,0:T(8,128)(2,1)}, f32[8,1024]{1,0:T(8,128)}, bf16[4,64,1024]{2,1,0:T(8,128)(2,1)}) custom-call(bf16[4,64,1024]{2,1,0:T(8,128)(2,1)} %bitcast.191, f32[64,1024]{1,0:T(8,128)} %get-tuple-element.105.refs_1_.refs_2_, bf16[64,1024]{1,0:T(8,128)(2,1)} %get-tuple-element.177.refs_2_, ...), custom_call_target="tpu_custom_call" | custom-call | tf_op jit(solution)/shard_map/pallas_call | solution.py:195
  255.7 2.6 fusion.38
  258.3 1.6 convolution_convert_fusion.13
  259.9 17.5 %shard_map.160 = (f32[64,1024]{1,0:T(8,128)}, f32[8,1024]{1,0:T(8,128)}, bf16[4,64,1024]{2,1,0:T(8,128)(2,1)}) custom-call(bf16[4,64,1024]{2,1,0:T(8,128)(2,1)} %bitcast.189, f32[64,1024]{1,0:T(8,128)} %get-tuple-element.176.refs_1_, f32[64,1024]{1,0:T(8,128)} %get-tuple-element.105.refs_1_.refs_2_, f32[64,1024]{1,0:T(8,128)} %get-tuple-element.108.refs_3_, ...), custom_call_target="tpu_custom_call" | custom-call | tf_op jit(solution)/shard_map/pallas_call | solution.py:195
  277.4 34.9 %shard_map.161 = (bf16[3,256,256]{2,1,0:T(8,128)(2,1)}, f32[8,256]{1,0:T(8,128)}, bf16[4,64,1024]{2,1,0:T(8,128)(2,1)}) custom-call(bf16[256,1024]{1,0:T(8,128)(2,1)} %bitcast.187, bf16[3,1024,256]{2,1,0:T(8,128)(2,1)} %bitcast.172, bf16[1024,256]{1,0:T(8,128)(2,1)} %bitcast.184, bf16[256,256]{1,0:T(8,128)(2,1)} %get-tuple-element.110.q_ref, ...), custom_call_target="tpu_custom_call" | custom-call | tf_op jit(solution)/shard_map/pallas_call | solution.py:1216
  312.4 1.2 convolution_convert_fusion.11
  314.8 2.0 convolution_convert_fusion.8
  318.0 1.2 convolution_convert_fusion.10
  319.2 2.1 convolution_convert_fusion.2
  321.3 2.2 convolution_convert_fusion.3
  323.5 33.2 %shard_map.162 = (f32[64,1024]{1,0:T(8,128)}, f32[8,1024]{1,0:T(8,128)}, bf16[4,64,1024]{2,1,0:T(8,128)(2,1)}, f32[64,1024]{1,0:T(8,128)}, f32[64,1024]{1,0:T(8,128)}, /*index=5*/f32[64,256]{1,0:T(8,128)}) custom-call(bf16[4,64,1024]{2,1,0:T(8,128)(2,1)} %get-tuple-element.115.refs_0_, f32[64,1024]{1,0:T(8,128)} %get-tuple-element.116.refs_1_, ...), custom_call_target="tpu_custom_call" | custom-call | tf_op jit(solution)/shard_map/pallas_call | solution.py:195
  356.7 2.0 fusion.39
  358.7 1.5 convolution_convert_fusion.12
  362.2 28.3 %shard_map.163 = (f32[64,1024]{1,0:T(8,128)}, f32[8,1024]{1,0:T(8,128)}, bf16[4,64,1024]{2,1,0:T(8,128)(2,1)}, f32[64,256]{1,0:T(8,128)}, f32[64,256]{1,0:T(8,128)}, /*index=5*/f32[64,256]{1,0:T(8,128)}) custom-call(bf16[4,64,1024]{2,1,0:T(8,128)(2,1)} %bitcast.200, f32[64,1024]{1,0:T(8,128)} %convert_convert_fusion.refs_1_, ...), custom_call_target="tpu_custom_call" | custom-call | tf_op jit(solution)/shard_map/pallas_call | solution.py:195
  390.6 38.9 %shard_map.164 = (bf16[3,256,256]{2,1,0:T(8,128)(2,1)}, f32[8,256]{1,0:T(8,128)}, bf16[4,64,1024]{2,1,0:T(8,128)(2,1)}) custom-call(bf16[256,1024]{1,0:T(8,128)(2,1)} %bitcast.185, bf16[3,1024,256]{2,1,0:T(8,128)(2,1)} %bitcast.170, bf16[1024,256]{1,0:T(8,128)(2,1)} %bitcast.182, bf16[256,256]{1,0:T(8,128)(2,1)} %get-tuple-element.124.q_ref, ...), custom_call_target="tpu_custom_call" | custom-call | tf_op jit(solution)/shard_map/pallas_call | solution.py:1216
  430.7 2.1 convolution_convert_fusion.4
  432.8 1.2 convolution_convert_fusion.5
  433.9 1.2 convolution_convert_fusion.6
  435.1 2.1 convolution_convert_fusion
  437.2 2.1 convolution_convert_fusion.1
  439.3 32.0 %shard_map.165 = (f32[64,1024]{1,0:T(8,128)}, f32[8,1024]{1,0:T(8,128)}, f32[64,1024]{1,0:T(8,128)}, f32[64,1024]{1,0:T(8,128)}, f32[64,256]{1,0:T(8,128)}) custom-call(bf16[4,64,1024]{2,1,0:T(8,128)(2,1)} %get-tuple-element.129.refs_0_, f32[64,1024]{1,0:T(8,128)} %get-tuple-element.130.refs_1_, f32[64,1024]{1,0:T(8,128)} %get-tuple-element.182.refs_1_.refs_2_, ...), custom_call_target="tpu_custom_call" | custom-call | tf_op jit(solution)/shard_map/pallas_call | solution.py:195
  471.4 1.9 select_bitcast_fusion
  473.3 1.7 select_bitcast_fusion.2
  475.1 24.7 %shard_map.166 = (f32[16,128]{1,0:T(8,128)}, f32[64,256]{1,0:T(8,128)}, f32[64,256]{1,0:T(8,128)}, f32[64,256]{1,0:T(8,128)}, bf16[64,1024]{1,0:T(8,128)(2,1)}, /*index=5*/f32[64,1024]{1,0:T(8,128)}) custom-call(f32[8,1024]{1,0:T(8,128)} %get-tuple-element.132.refs_0_, f32[8,1024]{1,0:T(8,128)} %get-tuple-element.133.refs_1_, f32[6,1024]{1,0:T(8,128)} %slice.139.refs_2_, ...), custom_call_target="tpu_custom_call" | custom-call | tf_op jit(solution)/shard_map/pallas_call | solution.py:901
  499.8 1.5 select_bitcast_fusion.6
  501.3 1.7 maximum_select_fusion.1
  503.0 1.9 maximum_select_fusion
  (99 shorter events, 15.8 us)
Async XLA Ops:
  73.6 64.8 %copy-start.24 = (bf16[4,4,64,1024]{3,2,1,0:T(8,128)(2,1)S(1)}, bf16[4,4,64,1024]{3,2,1,0:T(8,128)(2,1)}, u32[]{:S(2)}) copy-start(bf16[4,4,64,1024]{3,2,1,0:T(8,128)(2,1)} %get-tuple-element.94) | copy-start | bytes 6291460
  138.5 5.5 %copy-start.25 = (bf16[4,4,64,1024]{3,2,1,0:T(8,128)(2,1)S(1)}, bf16[4,4,64,1024]{3,2,1,0:T(8,128)(2,1)}, u32[]{:S(2)}) copy-start(bf16[4,4,64,1024]{3,2,1,0:T(8,128)(2,1)} %get-tuple-element.95) | copy-start | bytes 6291460
  174.8 56.8 %copy-start.27 = (bf16[4,4,64,1024]{3,2,1,0:T(8,128)(2,1)S(1)}, bf16[4,4,64,1024]{3,2,1,0:T(8,128)(2,1)}, u32[]{:S(2)}) copy-start(bf16[4,4,64,1024]{3,2,1,0:T(8,128)(2,1)} %get-tuple-element.103) | copy-start | bytes 6291460
  231.6 5.3 %copy-start.29 = (bf16[4,4,64,1024]{3,2,1,0:T(8,128)(2,1)S(1)}, bf16[4,4,64,1024]{3,2,1,0:T(8,128)(2,1)}, u32[]{:S(2)}) copy-start(bf16[4,4,64,1024]{3,2,1,0:T(8,128)(2,1)} %get-tuple-element.104) | copy-start | bytes 6291460
  236.9 18.8 %copy-start.30 = (bf16[4,4,64,1024]{3,2,1,0:T(8,128)(2,1)S(1)}, bf16[4,4,64,1024]{3,2,1,0:T(8,128)(2,1)}, u32[]{:S(2)}) copy-start(bf16[4,4,64,1024]{3,2,1,0:T(8,128)(2,1)} %get-tuple-element.104) | copy-start | bytes 6291460
  255.7 2.6 copy-start.28
  277.4 35.0 %copy-start.3 = (bf16[4,64,1024]{2,1,0:T(8,128)(2,1)S(1)}, bf16[4,64,1024]{2,1,0:T(8,128)(2,1)}, u32[]{:S(2)}) copy-start(bf16[4,64,1024]{2,1,0:T(8,128)(2,1)} %get-tuple-element.109) | copy-start | bytes 1572868
  277.4 35.0 %copy-start.16 = (bf16[256,256]{1,0:T(8,128)(2,1)S(1)}, bf16[256,256]{1,0:T(8,128)(2,1)}, u32[]{:S(2)}) copy-start(bf16[256,256]{1,0:T(8,128)(2,1)} %get-tuple-element.118) | copy-start | bytes 393220
  277.4 36.1 %copy-start.5 = (bf16[64,1024]{1,0:T(8,128)(2,1)S(1)}, bf16[64,1024]{1,0:T(8,128)(2,1)}, u32[]{:S(2)}) copy-start(bf16[64,1024]{1,0:T(8,128)(2,1)} %get-tuple-element.97) | copy-start | bytes 393220
  277.4 36.1 %copy-start.17 = (bf16[64,1024]{1,0:T(8,128)(2,1)S(1)}, bf16[64,1024]{1,0:T(8,128)(2,1)}, u32[]{:S(2)}) copy-start(bf16[64,1024]{1,0:T(8,128)(2,1)} %get-tuple-element.106) | copy-start | bytes 393220
  277.4 37.4 %copy-start.1 = (bf16[4,64,1024]{2,1,0:T(8,128)(2,1)S(1)}, bf16[4,64,1024]{2,1,0:T(8,128)(2,1)}, u32[]{:S(2)}) copy-start(bf16[4,64,1024]{2,1,0:T(8,128)(2,1)} %get-tuple-element.98) | copy-start | bytes 1572868
  312.4 4.5 copy-start.10
  313.5 5.7 %copy-start.9 = (bf16[4,64,1024]{2,1,0:T(8,128)(2,1)S(1)}, bf16[4,64,1024]{2,1,0:T(8,128)(2,1)}, u32[]{:S(2)}) copy-start(bf16[4,64,1024]{2,1,0:T(8,128)(2,1)} %get-tuple-element.107) | copy-start | bytes 1572868
  318.0 3.3 copy-start.7
  323.5 33.2 %copy-start.26 = (bf16[4,4,64,1024]{3,2,1,0:T(8,128)(2,1)S(1)}, bf16[4,4,64,1024]{3,2,1,0:T(8,128)(2,1)}, u32[]{:S(2)}) copy-start(bf16[4,4,64,1024]{3,2,1,0:T(8,128)(2,1)} %get-tuple-element.95) | copy-start | bytes 6291460
  323.5 33.2 %copy-start.31 = (f32[256,1024]{1,0:T(8,128)S(1)}, f32[256,1024]{1,0:T(8,128)}, u32[]{:S(2)}) copy-start(f32[256,1024]{1,0:T(8,128)} %get-tuple-element.200) | copy-start | bytes 3145732
  358.7 2.2 copy-start.14
  358.7 2.8 copy-start.4
  390.5 39.0 %copy-start.2 = (bf16[4,64,1024]{2,1,0:T(8,128)(2,1)S(1)}, bf16[4,64,1024]{2,1,0:T(8,128)(2,1)}, u32[]{:S(2)}) copy-start(bf16[4,64,1024]{2,1,0:T(8,128)(2,1)} %get-tuple-element.123) | copy-start | bytes 1572868
  390.6 39.0 %copy-start.15 = (bf16[256,256]{1,0:T(8,128)(2,1)S(1)}, bf16[256,256]{1,0:T(8,128)(2,1)}, u32[]{:S(2)}) copy-start(bf16[256,256]{1,0:T(8,128)(2,1)} %get-tuple-element.131) | copy-start | bytes 393220
  390.6 40.1 %copy-start = (bf16[4,64,1024]{2,1,0:T(8,128)(2,1)S(1)}, bf16[4,64,1024]{2,1,0:T(8,128)(2,1)}, u32[]{:S(2)}) copy-start(bf16[4,64,1024]{2,1,0:T(8,128)(2,1)} %get-tuple-element.86) | copy-start | bytes 1572868
  429.5 3.2 copy-start.11
  429.5 5.6 %copy-start.8 = (bf16[4,64,1024]{2,1,0:T(8,128)(2,1)S(1)}, bf16[4,64,1024]{2,1,0:T(8,128)(2,1)}, u32[]{:S(2)}) copy-start(bf16[4,64,1024]{2,1,0:T(8,128)(2,1)} %get-tuple-element.119) | copy-start | bytes 1572868
  433.9 3.3 copy-start.6
  439.3 32.1 %copy-start.12 = (f32[64,1024]{1,0:T(8,128)S(1)}, f32[64,1024]{1,0:T(8,128)}, u32[]{:S(2)}) copy-start(f32[64,1024]{1,0:T(8,128)} %get-tuple-element.152) | copy-start | bytes 786436
  439.3 32.1 %copy-start.13 = (f32[64,1024]{1,0:T(8,128)S(1)}, f32[64,1024]{1,0:T(8,128)}, u32[]{:S(2)}) copy-start(f32[64,1024]{1,0:T(8,128)} %get-tuple-element.154) | copy-start | bytes 786436
  471.4 28.4 %copy-start.18 = (f32[64,256]{1,0:T(8,128)S(1)}, f32[64,256]{1,0:T(8,128)}, u32[]{:S(2)}) copy-start(f32[64,256]{1,0:T(8,128)} %get-tuple-element.150) | copy-start | bytes 196612
  471.4 28.4 %copy-start.21 = (f32[64,256]{1,0:T(8,128)S(1)}, f32[64,256]{1,0:T(8,128)}, u32[]{:S(2)}) copy-start(f32[64,256]{1,0:T(8,128)} %get-tuple-element.148) | copy-start | bytes 196612
  471.4 28.4 %copy-start.22 = (f32[64,256]{1,0:T(8,128)S(1)}, f32[64,256]{1,0:T(8,128)}, u32[]{:S(2)}) copy-start(f32[64,256]{1,0:T(8,128)} %get-tuple-element.149) | copy-start | bytes 196612
  475.0 29.8 %copy-start.19 = (f32[64,256]{1,0:T(8,128)S(1)}, f32[64,256]{1,0:T(8,128)}, u32[]{:S(2)}) copy-start(f32[64,256]{1,0:T(8,128)} %get-tuple-element.144) | copy-start | bytes 196612
  475.0 29.8 %copy-start.20 = (f32[64,256]{1,0:T(8,128)S(1)}, f32[64,256]{1,0:T(8,128)}, u32[]{:S(2)}) copy-start(f32[64,256]{1,0:T(8,128)} %get-tuple-element.146) | copy-start | bytes 196612
  499.7 6.7 %copy-start.23 = (f32[16,128]{1,0:T(8,128)S(1)}, f32[16,128]{1,0:T(8,128)}, u32[]{:S(2)}) copy-start(f32[16,128]{1,0:T(8,128)} %get-tuple-element.155) | copy-start | bytes 24580

commit v5 on v4

--- a/solution.py
+++ b/solution.py
@@ -59,12 +59,6 @@
 CHUNKS = 2
 
 
-class Rider:
-    def __init__(self, build, ins, in_specs, outs, out_specs, scratch):
-        self.build, self.ins, self.in_specs = build, ins, in_specs
-        self.outs, self.out_specs, self.scratch = outs, out_specs, scratch
-
-
 def tensor_barrier(me):
     barrier = pltpu.get_barrier_semaphore()
     for k in range(1, RING):
@@ -74,31 +68,22 @@
     return barrier, RING - 1
 
 
-def tensor_kernel(function, n_rows, n_vecs, n_out, n_sums, reduce, gather, with_seg, rider, *refs):
+def tensor_kernel(function, n_rows, n_vecs, n_out, n_sums, reduce, gather, with_seg, *refs):
     refs = list(refs)
     take = lambda count: [refs.pop(0) for _ in range(count)]
     part = take(1)[0] if reduce else None
     rows_in = take(n_rows)
     vecs = take(n_vecs)
     seg_in = take(1)[0] if with_seg else None
-    rider_ins = take(len(rider.ins)) if rider else []
     rows_out = take(n_out)
     sums_out = take(1)[0] if n_sums else None
     full = take(1)[0] if gather else None
     seg_out = take(1)[0] if with_seg else None
-    rider_outs = take(len(rider.outs)) if rider else []
     landing = take(1)[0] if reduce else None
     send, recv, local = take(3)
 
     me = lax.axis_index("tensor")
     barrier, count = tensor_barrier(me)
-    stages = []
-    if rider:
-        rank = lax.axis_index("dp")
-        y, z = rank // RING, lax.rem(rank, RING)
-        section = lax.axis_index("section")
-        count += dp_barrier(y, z, section)[1]
-        stages = rider.build(y, z, section, rider_ins, rider_outs, refs)
     pl.semaphore_wait(barrier, count)
 
     chunk = rows_in[0].shape[0] // CHUNKS
@@ -116,10 +101,6 @@
         copy.start()
         started.append(copy)
         return copy
-
-    def ride():
-        if stages:
-            stages.pop(0)()
 
     reduces = {}
     if reduce:
@@ -134,7 +115,6 @@
         own = pltpu.make_async_copy(seg_in, seg_out.at[me], local)
         own.start()
         last += [push(seg_in, seg_out.at[me], 2, 0, k) for k in range(1, RING)]
-    ride()
     sums = [None] * n_sums
     for c in range(CHUNKS):
         here = pl.ds(c * chunk, chunk)
@@ -154,13 +134,10 @@
         for ref, value in zip(rows_out, outs):
             ref[here] = value.astype(ref.dtype)
         sums = [new if old is None else old + new for old, new in zip(sums, parts)]
-        ride()
     if n_sums:
         sums_out[...] = jnp.concatenate(
             sums + [jnp.zeros((8 - n_sums, sums[0].shape[1]), F32)], axis=0
         )
-    while stages:
-        ride()
     for copy in last:
         copy.wait_recv()
     if with_seg:
@@ -169,7 +146,7 @@
         copy.wait_send()
 
 
-def tensor_call(cid, function, part, rows, vecs, outs, n_sums, gather, seg=None, rider=None):
+def tensor_call(cid, function, part, rows, vecs, outs, n_sums, gather, seg=None):
     height, width = rows[0].shape
     reduce = part is not None
     with_seg = seg is not None
@@ -188,14 +165,9 @@
         pltpu.SemaphoreType.DMA((3, CHUNKS, RING - 1)),
         pltpu.SemaphoreType.DMA,
     ]
-    if rider:
-        args, in_specs = args + rider.ins, in_specs + rider.in_specs
-        shapes, out_specs = shapes + rider.outs, out_specs + rider.out_specs
-        scratch = scratch + rider.scratch
     return pl.pallas_call(
         functools.partial(
             tensor_kernel, function, len(rows), len(vecs), len(outs), n_sums, reduce, gather, with_seg,
-            rider,
         ),
         out_shape=shapes,
         in_specs=in_specs,
@@ -341,7 +313,8 @@
         height = self.outs[self.pieces[i][0]].shape[-2]
         if height < 32:
             return {PLUS: None}
-        return {PLUS: pl.ds(0, height // 2), MINUS: pl.ds(height // 2, height // 2)}
+        half = height // 32 * 16
+        return {PLUS: pl.ds(0, half), MINUS: pl.ds(half, height - half)}
 
     def spread(self, i, offset, source):
         for k in (PLUS, MINUS):
@@ -430,147 +403,80 @@
     return [begin, near, middle, end]
 
 
-def out_views(ref, rows):
-    if len(ref.shape) == 5:
-        return [ref.at[which, :, :, rows] for which in range(ref.shape[0])]
-    return [ref.at[:, :, rows]]
-
-
-def in_views(ref):
-    if len(ref.shape) == 3:
-        return [ref.at[which] for which in range(ref.shape[0])]
-    return [ref]
-
-
-def weight_pieces(count):
-    return tuple((i, (), i % 2 == 0) for i in range(count))
-
-
-def weight_rider(halves):
-    count = sum(3 if value.ndim == 3 else 1 for value in halves)
-    height = halves[0].shape[-2]
-
-    def build(y, z, section, ins, outs, scratch):
-        send, recv, local = scratch
-        started = []
-        push = pusher(send, recv, started)
-        rows = half_of(section, height)
-        views = [view for ref in outs for view in out_views(ref, rows)]
-        sources = [view for ref in ins for view in in_views(ref)]
-        ring = Gather(weight_pieces(count), views, y, z, (), push)
-
-        def finish():
-            for copy in started:
-                copy.wait_send()
-
-        return spread_stages(ring, sources, local, section, push) + [finish]
-
-    outs = [
-        jax.ShapeDtypeStruct(
-            value.shape[:-2] + (RING, RING, 2 * height, value.shape[-1]), value.dtype
-        )
-        for value in halves
-    ]
-    return Rider(
-        build,
-        list(halves),
-        [vmem_spec()] * len(halves),
-        outs,
-        [any_spec()] * len(outs),
-        [
-            pltpu.SemaphoreType.DMA((count, 6, RING)),
-            pltpu.SemaphoreType.DMA((count, 6, RING)),
-            pltpu.SemaphoreType.DMA((count,)),
-        ],
-    )
+PACKED = 192
+SMALL = 16
 
 
 def first_kernel(
-    qkv_in, out_in, up_in, down_in, small_in, seg_in,
-    qkv_half, out_half, up_half, down_half, qkv_out, out_out, rows_out, seg_out,
-    small_all, send, recv, local, swap_send, swap_recv, swap_local,
+    qkv_in, out_in, up_in, down_in, small_in, packed_out, small_all, rows_out,
+    block, send, recv, local, pack_local, last_local,
 ):
     rank = lax.axis_index("dp")
     y, z = rank // RING, lax.rem(rank, RING)
     section = lax.axis_index("section")
     barrier, count = dp_barrier(y, z, section)
-    height = out_half.shape[-2]
-    mine, other = half_of(section, height), half_of(1 - section, height)
-    lead = lambda ref: (slice(None),) * (len(ref.shape) - 2)
+    depth, width = out_in.shape
+    packs = [
+        (qkv_in.at[which], block.at[0:depth, which * width : (which + 1) * width]) for which in range(3)
+    ]
+    packs += [
+        (out_in, block.at[0:depth, 3 * width : 4 * width]),
+        (up_in, block.at[depth : 2 * depth]),
+        (down_in, block.at[2 * depth : 3 * depth]),
+        (small_in, block.at[PACKED : PACKED + SMALL, 0 : small_in.shape[1]]),
+    ]
+    block[PACKED : PACKED + SMALL] = jnp.zeros((SMALL, block.shape[1]), BF16)
+    copies = [
+        pltpu.make_async_copy(source, target, pack_local.at[i])
+        for i, (source, target) in enumerate(packs)
+    ]
+    for copy in copies:
+        copy.start()
+    for copy in copies:
+        copy.wait()
     pl.semaphore_wait(barrier, count)
-    started, swaps = [], []
-    for i, (source, target) in enumerate(
-        ((qkv_in, qkv_half), (out_in, out_half), (up_in, up_half), (down_in, down_half))
-    ):
-        copy = pltpu.make_async_remote_copy(
-            src_ref=source.at[lead(source) + (other,)],
-            dst_ref=target.at[section],
-            send_sem=swap_send.at[i],
-            recv_sem=swap_recv.at[i],
-            device_id={"section": 1 - section},
-            device_id_type=MESH,
-        )
-        copy.start()
-        started.append(copy)
-        kept = pltpu.make_async_copy(
-            source.at[lead(source) + (mine,)], target.at[section], swap_local.at[i]
-        )
-        kept.start()
-        swaps.append((copy, kept))
+    started = []
     push = pusher(send, recv, started)
-    views = [small_all.at[section], seg_out.at[section]]
-    views += [qkv_out.at[which, :, :, mine] for which in range(3)] + [out_out.at[:, :, mine]]
-    sources = [small_in, seg_in]
-    sources += [qkv_half.at[0, which] for which in range(3)] + [out_half.at[0]]
-    ring = Gather(weight_pieces(6), views, y, z, (), push)
-    stages = spread_stages(ring, sources, local, section, push)
-    for copy, kept in swaps[:2]:
-        copy.wait_recv()
-        kept.wait()
-    for stage in stages:
+    low, high = pl.ds(0, PACKED // 2), pl.ds(PACKED // 2, PACKED // 2 + SMALL)
+    views = [packed_out.at[section, :, :, low], packed_out.at[section, :, :, high]]
+    ring = Gather(((0, (), True), (1, (), False)), views, y, z, (), push)
+    for stage in spread_stages(ring, [block.at[low], block.at[high]], local, section, push):
         stage()
-    depth = rows_out.shape[-1] // (RING * RING)
+    last = pltpu.make_async_copy(
+        packed_out.at[:, :, :, pl.ds(PACKED, SMALL), pl.ds(0, small_in.shape[1])], small_all, last_local
+    )
+    last.start()
+    last.wait()
     for layer in range(2):
         for number in range(RING * RING):
-            block = small_all[layer, number // RING, number % RING]
-            rows_out[layer, :, number * depth : (number + 1) * depth] = block[:, :depth].astype(F32)
-    for copy, kept in swaps[2:]:
-        copy.wait_recv()
-        kept.wait()
+            part = small_all[layer, number // RING, number % RING]
+            rows_out[layer, :, number * depth : (number + 1) * depth] = part[:, :depth].astype(F32)
     for copy in started:
         copy.wait_send()
 
 
-def first_call(cid, w_qkv, w_out, w_up, w_down, small, seg):
-    depth, width = w_out.shape
+def first_call(cid, w_qkv, w_out, w_up, w_down, small):
+    depth = w_out.shape[0]
     hidden = w_up.shape[1]
-    half = depth // 2
-    shape = lambda *dims: jax.ShapeDtypeStruct(dims, BF16)
     return pl.pallas_call(
         first_kernel,
         out_shape=[
-            shape(2, 3, half, width),
-            shape(2, half, width),
-            shape(2, half, hidden),
-            shape(2, half, hidden),
-            shape(3, RING, RING, depth, width),
-            shape(RING, RING, depth, width),
-            jax.ShapeDtypeStruct((2, 16, RING * RING * depth), F32),
-            jax.ShapeDtypeStruct((2, RING, RING) + seg.shape, seg.dtype),
+            jax.ShapeDtypeStruct((2, RING, RING, PACKED + SMALL, hidden), BF16),
+            jax.ShapeDtypeStruct((2, RING, RING) + small.shape, BF16),
+            jax.ShapeDtypeStruct((2, SMALL, RING * RING * depth), F32),
         ],
-        in_specs=[vmem_spec()] * 6,
-        out_specs=[vmem_spec()] * 4 + [any_spec()] * 2 + [vmem_spec()] * 2,
+        in_specs=[vmem_spec()] * 5,
+        out_specs=[any_spec(), vmem_spec(), vmem_spec()],
         scratch_shapes=[
-            pltpu.VMEM((2, RING, RING) + small.shape, BF16),
-            pltpu.SemaphoreType.DMA((6, 6, RING)),
-            pltpu.SemaphoreType.DMA((6, 6, RING)),
-            pltpu.SemaphoreType.DMA((6,)),
-            pltpu.SemaphoreType.DMA((4,)),
-            pltpu.SemaphoreType.DMA((4,)),
-            pltpu.SemaphoreType.DMA((4,)),
+            pltpu.VMEM((PACKED + SMALL, hidden), BF16),
+            pltpu.SemaphoreType.DMA((2, 6, RING)),
+            pltpu.SemaphoreType.DMA((2, 6, RING)),
+            pltpu.SemaphoreType.DMA((2,)),
+            pltpu.SemaphoreType.DMA((7,)),
+            pltpu.SemaphoreType.DMA,
         ],
         compiler_params=comm_params(cid),
-    )(w_qkv, w_out, w_up, w_down, small, seg)
+    )(w_qkv, w_out, w_up, w_down, small)
 
 
 class Scatter:
@@ -594,7 +500,9 @@
 
     def add(self, target, terms, top=0, height=None):
         height = self.height if height is None else height
-        size = max(8, min(height, 32768 // self.width))
+        size = max(8, min(height, 65536 // self.width))
+        while height % size:
+            size -= 16
 
         def part(here):
             value = terms[0](here).astype(F32)
@@ -714,122 +622,52 @@
 SCATTER_BUFFERS = 9
 
 
-def gradient_scratch(values):
-    scratch = []
-    for value in values:
-        block = (value.shape[2] // 2, value.shape[3])
-        square = pltpu.VMEM((RING, RING) + block, value.dtype)
-        scratch += [square, square] + Scatter.scratch(block, value.dtype)
-    return scratch + [
-        pltpu.SemaphoreType.DMA((len(values), 8, RING)),
-        pltpu.SemaphoreType.DMA((len(values), 8, RING)),
-    ]
-
-
-def gradient_stages(y, z, section, ins, outs, scratch, shared):
-    count = len(ins)
-    size = 2 + SCATTER_BUFFERS
-    send, recv = scratch[count * size :]
-    started = []
-    push = pusher(send, recv, started)
-    other = {"section": 1 - section}
-    siblings = [scratch[i * size] for i in range(count)]
-    owns = [scratch[i * size + 1] for i in range(count)]
-    parts = [
-        Scatter(
-            i, i % 2 == 0, owns[i], scratch[i * size + 2 : (i + 1) * size], y, z, push
-        )
-        for i in range(count)
-    ]
-    across, results = [], []
-
-    def swap():
-        for i in range(count):
-            height = owns[i].shape[2]
-            across.append(
-                push(i, 6, 0, ins[i].at[:, :, half_of(1 - section, height)], siblings[i], other)
-            )
-
-    def begin():
-        for i in range(count):
-            across[i].wait_recv()
-            mine = half_of(section, owns[i].shape[2])
-
-            def add(number, carry):
-                at_y, at_z = number // RING, lax.rem(number, RING)
-                owns[i][at_y, at_z] = (
-                    ins[i][at_y, at_z, mine].astype(F32) + siblings[i][at_y, at_z].astype(F32)
-                ).astype(owns[i].dtype)
-                return carry
-
-            lax.fori_loop(0, RING * RING, add, 0)
-            parts[i].begin()
-
-    def join():
-        for part in parts:
-            part.join()
-
-    def turn():
-        for part in parts:
-            part.turn()
-
-    def join_two():
-        for part in parts:
-            part.join_two()
-
-    def finish():
-        for i in range(count):
-            height = owns[i].shape[2]
-            if shared[i]:
-                mine = outs[i].at[half_of(section, height)]
-                parts[i].finish(mine)
-                results.append(push(i, 7, 0, mine, mine, other))
-            else:
-                parts[i].finish(outs[i])
-
-    def end():
-        for copy in results:
-            copy.wait_recv()
-        for copy in started:
-            copy.wait_send()
-
-    return [swap, begin, join, turn, join_two, finish, end]
-
-
-def gradient_rider(values):
-    def build(y, z, section, ins, outs, scratch):
-        return gradient_stages(y, z, section, ins, outs, scratch, [True] * len(ins))
-
-    return Rider(
-        build,
-        list(values),
-        [vmem_spec()] * len(values),
-        [jax.ShapeDtypeStruct(value.shape[2:], F32) for value in values],
-        [vmem_spec()] * len(values),
-        gradient_scratch(values),
-    )
-
-
-def final_kernel(n_extra, n_grad, *refs):
+def scatter_buffers(block, dtype):
+    square = pltpu.VMEM((RING, RING) + block, dtype)
+    return [square, square] + Scatter.scratch(block, dtype)
+
+
+def final_kernel(n_extra, *refs):
     refs = list(refs)
     take = lambda count: [refs.pop(0) for _ in range(count)]
     sums = [take(5), take(5)]
-    ins, extras = take(n_grad), take(n_extra)
-    small_out = take(1)[0]
-    outs, extra_outs = take(n_grad), take(n_extra)
-    small_in, small_rows, vector_own, vector_parts = take(4)
-    vector_send, vector_recv, extra_send, extra_recv = take(4)
+    grads = [take(6), take(6)]
+    extras = take(n_extra)
+    small_out, packed_out = take(2)
+    extra_outs = take(n_extra)
+    small_in, small_rows, vector_own, vector_parts, summed = take(5)
+    buffers = [take(2 + SCATTER_BUFFERS) for _ in range(3)]
+    send, recv, swap_send, swap_recv, keep_local = take(5)
+    vector_send, vector_recv, extra_send, extra_recv, result_send, result_recv, result_local = take(7)
     rank = lax.axis_index("dp")
     y, z = rank // RING, lax.rem(rank, RING)
     section = lax.axis_index("section")
     me = lax.axis_index("tensor")
+    other = {"section": 1 - section}
     barrier, count = tensor_barrier(me)
     count += dp_barrier(y, z, section)[1]
+
+    depth, width = grads[0][0].shape[2:]
+    hidden = grads[0][5].shape[3]
+    half = depth // 2
+    mine, others = half_of(section, half), half_of(1 - section, half)
+    places = [(0, which * width, width) for which in range(4)]
+    places += [(half, 0, hidden), (2 * half, 0, hidden)]
+    keeps, swaps = [], []
+    for layer in range(2):
+        for i, (row, column, columns) in enumerate(places):
+            region = (slice(None), slice(None), pl.ds(row, half), pl.ds(column, columns))
+            copy = pltpu.make_async_copy(
+                grads[layer][i].at[:, :, mine], buffers[layer][0].at[region], keep_local.at[layer, i]
+            )
+            copy.start()
+            keeps.append(copy)
+
     small_rows[...] = jnp.zeros_like(small_rows)
-    width = small_rows.shape[1]
+    model = small_rows.shape[1]
     for layer in range(2):
         first, middle, end, attend, up = sums[layer]
-        top = 16 * layer
+        top = SMALL * layer
         part = attend.shape[1]
         lanes = pl.ds(pl.multiple_of(me * part, part), part)
         small_rows[top : top + 2, :] = first[0:2, :]
@@ -845,16 +683,28 @@
             )
         small_rows[top + 13 : top + 14, :] = middle[3:4, :]
     small_in[...] = jnp.zeros_like(small_in)
-    depth = width // (RING * RING)
     for number in range(RING * RING):
         small_in[number // RING, number % RING, :, 0:depth] = small_rows[
             :, number * depth : (number + 1) * depth
         ]
     pl.semaphore_wait(barrier, count)
-    stages = gradient_stages(
-        y, z, section, [small_in] + ins, [vector_own] + outs, refs, [False] + [True] * n_grad
-    )
-    stages[0]()
+    started = []
+    push = pusher(send, recv, started)
+    for layer in range(2):
+        for i, (row, column, columns) in enumerate(places):
+            region = (slice(None), slice(None), pl.ds(row, half), pl.ds(column, columns))
+            copy = pltpu.make_async_remote_copy(
+                src_ref=grads[layer][i].at[:, :, others],
+                dst_ref=buffers[layer][1].at[region],
+                send_sem=swap_send.at[layer, i],
+                recv_sem=swap_recv.at[layer, i],
+                device_id=other,
+                device_id_type=MESH,
+            )
+            copy.start()
+            swaps.append(copy)
+    started += swaps
+    small_swap = push(2, 6, 0, small_in.at[:, :, half_of(1 - section, SMALL)], buffers[2][1], other)
     extra_copies = []
     for i in range(n_extra):
         copy = pltpu.make_async_remote_copy(
@@ -862,13 +712,42 @@
             dst_ref=extra_outs[i],
             send_sem=extra_send.at[i],
             recv_sem=extra_recv.at[i],
-            device_id={"section": 1 - section},
+            device_id=other,
             device_id_type=MESH,
         )
         copy.start()
         extra_copies.append(copy)
-    for stage in stages[1:6]:
-        stage()
+
+    parts = []
+    for piece in range(3):
+        own, sibling = buffers[piece][:2]
+        if piece == 2:
+            small_swap.wait_recv()
+            kept = small_in.at[:, :, half_of(section, SMALL)]
+        else:
+            for i in range(len(places)):
+                keeps[piece * len(places) + i].wait()
+                swaps[piece * len(places) + i].wait_recv()
+            kept = own
+
+        def add(number, carry):
+            at_y, at_z = number // RING, lax.rem(number, RING)
+            own[at_y, at_z] = (
+                kept[at_y, at_z].astype(F32) + sibling[at_y, at_z].astype(F32)
+            ).astype(own.dtype)
+            return carry
+
+        lax.fori_loop(0, RING * RING, add, 0)
+        parts.append(Scatter(piece, piece != 1, own, buffers[piece][2:], y, z, push))
+        parts[piece].begin()
+    for part in parts:
+        part.join()
+    order = (parts[2], parts[0], parts[1])
+    for part in order:
+        part.turn()
+    for part in order:
+        part.join_two()
+    parts[2].finish(vector_own)
     vector_parts[me] = vector_own[...]
     vector_copies = []
     for k in range(1, RING):
@@ -882,7 +761,21 @@
         )
         copy.start()
         vector_copies.append(copy)
-    stages[6]()
+    for layer in range(2):
+        parts[layer].finish(summed.at[layer])
+    result = pltpu.make_async_remote_copy(
+        src_ref=summed.at[1 - section],
+        dst_ref=packed_out.at[section],
+        send_sem=result_send,
+        recv_sem=result_recv,
+        device_id=other,
+        device_id_type=MESH,
+    )
+    result.start()
+    own_result = pltpu.make_async_copy(summed.at[section], packed_out.at[section], result_local)
+    own_result.start()
+    own_result.wait()
+    result.wait()
     for copy in vector_copies:
         copy.wait()
     total = vector_parts[0]
@@ -891,31 +784,49 @@
     small_out[...] = total
     for copy in extra_copies:
         copy.wait()
+    for copy in started:
+        copy.wait_send()
 
 
 def final_call(cid, sums, grads, extras):
     extra = len(extras)
     width = sums[0].shape[1]
-    small = jax.ShapeDtypeStruct((RING, RING, 32, 128), F32)
+    hidden = grads[-1].shape[3]
     args = list(sums) + list(grads) + list(extras)
+    block = (PACKED // 2, hidden)
     return pl.pallas_call(
-        functools.partial(final_kernel, extra, len(grads)),
-        out_shape=[jax.ShapeDtypeStruct((16, 128), F32)]
-        + [jax.ShapeDtypeStruct(value.shape[2:], F32) for value in grads]
+        functools.partial(final_kernel, extra),
+        out_shape=[
+            jax.ShapeDtypeStruct((SMALL, 128), F32),
+            jax.ShapeDtypeStruct((2, PACKED // 2, hidden), F32),
+        ]
         + [jax.ShapeDtypeStruct(value.shape, value.dtype) for value in extras],
-        in_specs=[vmem_spec()] * len(args),
-        out_specs=[vmem_spec()] * (1 + len(grads) + extra),
+        in_specs=[vmem_spec()] * len(sums) + [any_spec()] * len(grads) + [vmem_spec()] * extra,
+        out_specs=[vmem_spec()] * (2 + extra),
         scratch_shapes=[
-            pltpu.VMEM(small.shape, F32),
-            pltpu.VMEM((32, width), F32),
-            pltpu.VMEM((16, 128), F32),
-            pltpu.VMEM((RING, 16, 128), F32),
+            pltpu.VMEM((RING, RING, 2 * SMALL, 128), F32),
+            pltpu.VMEM((2 * SMALL, width), F32),
+            pltpu.VMEM((SMALL, 128), F32),
+            pltpu.VMEM((RING, SMALL, 128), F32),
+            pltpu.VMEM((2,) + block, F32),
+        ]
+        + scatter_buffers(block, BF16)
+        + scatter_buffers(block, BF16)
+        + scatter_buffers((SMALL, 128), F32)
+        + [
+            pltpu.SemaphoreType.DMA((3, 7, RING)),
+            pltpu.SemaphoreType.DMA((3, 7, RING)),
+            pltpu.SemaphoreType.DMA((2, 6)),
+            pltpu.SemaphoreType.DMA((2, 6)),
+            pltpu.SemaphoreType.DMA((2, 6)),
             pltpu.SemaphoreType.DMA((RING,)),
             pltpu.SemaphoreType.DMA((RING,)),
             pltpu.SemaphoreType.DMA((extra,)),
             pltpu.SemaphoreType.DMA((extra,)),
-        ]
-        + gradient_scratch([small] + list(grads)),
+            pltpu.SemaphoreType.DMA,
+            pltpu.SemaphoreType.DMA,
+            pltpu.SemaphoreType.DMA,
+        ],
         compiler_params=comm_params(cid),
     )(*args)
 
@@ -948,37 +859,32 @@
 
 
 def attend_kernel(
-    normed_ref, qkv_any, out_any, bias_ref, seg_q_ref, seg_k_ref,
+    layer, normed_ref, packed_any, bias_ref, seg_q_ref, seg_k_ref,
     q_ref, k_ref, v_ref, mixed_ref, wide_ref, lse_ref, part_ref,
-    qkv_ref, out_ref, stack, acc, top_ref, total_ref, send, recv, local,
+    pack_ref, stack, acc, top_ref, total_ref, send, recv, local,
 ):
     group, width = q_ref.shape
     heads_here = width // HEAD_DIM
-    loads = [
-        pltpu.make_async_copy(qkv_any.at[which], qkv_ref.at[which], local.at[which])
-        for which in range(3)
-    ]
-    loads.append(pltpu.make_async_copy(out_any, out_ref, local.at[3]))
-    for which in (1, 2, 0, 3):
-        loads[which].start()
+    depth = group // RING
+    load = pltpu.make_async_copy(packed_any.at[layer, :, :, pl.ds(0, depth)], pack_ref, local)
+    load.start()
+    matrix = lambda which: pack_ref[:, :, :, which * width : (which + 1) * width].reshape(-1, width)
     rank = lax.axis_index("dp")
     y, z = rank // RING, lax.rem(rank, RING)
     barrier, count = dp_barrier(y, z, None)
     normed = normed_ref[...]
-    loads[1].wait()
-    k_ref[y, z] = jnp.dot(normed, qkv_ref[1], preferred_element_type=F32).astype(BF16)
+    load.wait()
+    k_ref[y, z] = jnp.dot(normed, matrix(1), preferred_element_type=F32).astype(BF16)
     pl.semaphore_wait(barrier, count)
     started = []
     ring = Gather(((0, (), True), (1, (), False)), (k_ref, v_ref), y, z, (), pusher(send, recv, started))
     ring.begin(0, k_ref.at[y, z])
-    loads[2].wait()
     v_ref[y, z] = (
-        jnp.dot(normed, qkv_ref[2], preferred_element_type=F32) + bias_ref[1:2, :]
+        jnp.dot(normed, matrix(2), preferred_element_type=F32) + bias_ref[1:2, :]
     ).astype(BF16)
     ring.begin(1, v_ref.at[y, z])
-    loads[0].wait()
     q_ref[...] = (
-        jnp.dot(normed, qkv_ref[0], preferred_element_type=F32) + bias_ref[0:1, :]
+        jnp.dot(normed, matrix(0), preferred_element_type=F32) + bias_ref[0:1, :]
     ).astype(BF16)
     stack[...] = head_stack(q_ref[...], HEAD_DIM ** (-0.5))
     acc[...] = jnp.zeros_like(acc)
@@ -1058,20 +964,19 @@
         wide_ref[rows, :] = acc[rows, :] * inverse[:, head * group : (head + 1) * group]
     mixed_ref[...] = wide_ref[...].T.astype(BF16)
     lse_ref[...] = jnp.broadcast_to(top_ref[0:1, :] + jnp.log(total), lse_ref.shape)
-    loads[3].wait()
-    part = flat_dot(mixed_ref[...], out_ref[...]).astype(BF16)
+    part = flat_dot(mixed_ref[...], matrix(3)).astype(BF16)
     part_ref[...] = part.reshape(part_ref.shape)
     for copy in started:
         copy.wait_send()
 
 
-def attend_call(cid, normed, full_qkv, full_out, biases, seg_wide, seg_column):
+def attend_call(cid, layer, normed, packed, biases, seg_wide, seg_column):
     group, model = normed.shape
-    width = full_out.shape[1]
+    width = biases.shape[1]
     heads_here = width // HEAD_DIM
     square = (RING, RING, group, width)
     return pl.pallas_call(
-        attend_kernel,
+        functools.partial(attend_kernel, layer),
         out_shape=[
             jax.ShapeDtypeStruct((group, width), BF16),
             jax.ShapeDtypeStruct(square, BF16),
@@ -1081,47 +986,46 @@
             jax.ShapeDtypeStruct((8, group * heads_here), F32),
             jax.ShapeDtypeStruct((RING, group // RING, model), BF16),
         ],
-        in_specs=[vmem_spec(), any_spec(), any_spec()] + [vmem_spec()] * 3,
+        in_specs=[vmem_spec(), any_spec()] + [vmem_spec()] * 3,
         out_specs=[vmem_spec()] * 7,
         scratch_shapes=[
-            pltpu.VMEM((3, model, width), BF16),
-            pltpu.VMEM((model, width), BF16),
+            pltpu.VMEM((RING, RING, group // RING, model), BF16),
             pltpu.VMEM((group * heads_here, width), BF16),
             pltpu.VMEM((width, group), F32),
             pltpu.VMEM((8, group * heads_here), F32),
             pltpu.VMEM((8, group * heads_here), F32),
             pltpu.SemaphoreType.DMA((2, 5, RING)),
             pltpu.SemaphoreType.DMA((2, 5, RING)),
-            pltpu.SemaphoreType.DMA((4,)),
+            pltpu.SemaphoreType.DMA,
         ],
         compiler_params=comm_params(cid),
-    )(normed, full_qkv, full_out, biases, seg_wide, seg_column)
+    )(normed, packed, biases, seg_wide, seg_column)
 
 
 def attend_back_kernel(
-    rows_ref, qkv_any, out_any, q_ref, k_ref, v_ref, wide_ref, lse_ref, seg_q_ref, seg_k_ref,
+    layer, rows_ref, packed_any, q_ref, k_ref, v_ref, wide_ref, lse_ref, seg_q_ref, seg_k_ref,
     triple_ref, sums_ref, part_ref, *scratch,
 ):
     (
-        qkv_ref, out_ref, grad_ref, stack, plain, grad_stack, grad_plain, acc, delta_ref,
+        pack_ref, grad_ref, stack, plain, grad_stack, grad_plain, acc, delta_ref,
         dk_ref, dv_ref, total_ref,
-    ) = scratch[:12]
-    buffers = scratch[12 : 12 + 2 * SCATTER_BUFFERS]
-    send, recv, local = scratch[12 + 2 * SCATTER_BUFFERS :]
+    ) = scratch[:11]
+    buffers = scratch[11 : 11 + 2 * SCATTER_BUFFERS]
+    send, recv, local = scratch[11 + 2 * SCATTER_BUFFERS :]
     group, width = q_ref.shape
     heads_here = width // HEAD_DIM
     scale = HEAD_DIM ** (-0.5)
-    load_out = pltpu.make_async_copy(out_any, out_ref, local.at[0])
-    load_qkv = pltpu.make_async_copy(qkv_any, qkv_ref, local.at[1])
-    load_out.start()
-    load_qkv.start()
+    depth = group // RING
+    load = pltpu.make_async_copy(packed_any.at[layer, :, :, pl.ds(0, depth)], pack_ref, local)
+    load.start()
+    matrix = lambda which: pack_ref[:, :, :, which * width : (which + 1) * width].reshape(-1, width)
     rank = lax.axis_index("dp")
     y, z = rank // RING, lax.rem(rank, RING)
     barrier, count = dp_barrier(y, z, None)
     stack[...] = head_stack(q_ref[...], scale)
     plain[...] = head_stack(q_ref[...], 1.0)
-    load_out.wait()
-    grad_ref[...] = jnp.dot(rows_ref[...], out_ref[...], preferred_element_type=F32).astype(BF16)
+    load.wait()
+    grad_ref[...] = jnp.dot(rows_ref[...], matrix(3), preferred_element_type=F32).astype(BF16)
     grad_stack[...] = head_stack(grad_ref[...], scale)
     grad_plain[...] = head_stack(grad_ref[...], 1.0)
     acc[...] = jnp.zeros_like(acc)
@@ -1193,38 +1097,36 @@
     query_grad = acc[...].T
     sums_ref[0:1, :] = jnp.sum(query_grad, axis=0, keepdims=True)
     triple_ref[0] = query_grad.astype(BF16)
-    load_qkv.wait()
-    part = flat_dot(triple_ref[0], qkv_ref[0])
+    part = flat_dot(triple_ref[0], matrix(0))
     values.finish(total_ref)
     triple_ref[2] = total_ref[...].astype(BF16)
     sums_ref[1:2, :] = jnp.sum(total_ref[...], axis=0, keepdims=True)
-    part = part + flat_dot(triple_ref[2], qkv_ref[2])
+    part = part + flat_dot(triple_ref[2], matrix(2))
     keys.finish(total_ref)
     triple_ref[1] = total_ref[...].astype(BF16)
-    part = part + flat_dot(triple_ref[1], qkv_ref[1])
+    part = part + flat_dot(triple_ref[1], matrix(1))
     part_ref[...] = part.astype(BF16).reshape(part_ref.shape)
     for copy in started:
         copy.wait_send()
 
 
-def attend_back_call(cid, attn_rows, full_qkv, full_out, queries, keys, values, wide, lse, seg_wide, seg_column):
+def attend_back_call(cid, layer, attn_rows, packed, queries, keys, values, wide, lse, seg_wide, seg_column):
     group, model = attn_rows.shape
     width = queries.shape[1]
     heads_here = width // HEAD_DIM
     block = (group, width)
     stacked = pltpu.VMEM((group * heads_here, width), BF16)
     return pl.pallas_call(
-        attend_back_kernel,
+        functools.partial(attend_back_kernel, layer),
         out_shape=[
             jax.ShapeDtypeStruct((3, group, width), BF16),
             jax.ShapeDtypeStruct((8, width), F32),
             jax.ShapeDtypeStruct((RING, group // RING, model), BF16),
         ],
-        in_specs=[vmem_spec(), any_spec(), any_spec()] + [vmem_spec()] * 7,
+        in_specs=[vmem_spec(), any_spec()] + [vmem_spec()] * 7,
         out_specs=[vmem_spec()] * 3,
         scratch_shapes=[
-            pltpu.VMEM((3, model, width), BF16),
-            pltpu.VMEM((model, width), BF16),
+            pltpu.VMEM((RING, RING, group // RING, model), BF16),
             pltpu.VMEM(block, BF16),
             stacked,
             stacked,
@@ -1241,10 +1143,10 @@
         + [
             pltpu.SemaphoreType.DMA((2, 6, RING)),
             pltpu.SemaphoreType.DMA((2, 6, RING)),
-            pltpu.SemaphoreType.DMA((2,)),
+            pltpu.SemaphoreType.DMA,
         ],
         compiler_params=comm_params(cid),
-    )(attn_rows, full_qkv, full_out, queries, keys, values, wide, lse, seg_wide, seg_column)
+    )(attn_rows, packed, queries, keys, values, wide, lse, seg_wide, seg_column)
 
 
 def shards(tokens, segment_ids, w_qkv, w_out, w_up, w_down, vectors, out_bias, cotangent):
@@ -1259,27 +1161,25 @@
     local_hidden = w_up.shape[2]
 
     depth = w_out.shape[1]
+    my_segments = own(segment_ids)
+    wide_segments = jnp.pad(my_segments, (0, depth - rows)).astype(BF16)[None]
     small = jnp.pad(
-        jnp.concatenate([vectors[0], out_bias], axis=0),
-        ((0, 2), (0, 128 - depth)),
+        jnp.concatenate([vectors[0], out_bias, wide_segments], axis=0),
+        ((0, 1), (0, 128 - depth)),
     )
-    my_segments = own(segment_ids)
-    seg_block = jnp.pad(my_segments[None], ((0, 7), (0, 128 - rows)))
-    qkv_half, out_half, up_half, down_half, qkv_first, out_first, small_rows, full_seg = first_call(
-        0, w_qkv[0], w_out[0], w_up[0], w_down[0], small, seg_block
-    )
-    joined_qkv = lambda value: value.reshape(3, width, local_width)
-    joined = lambda value: value.reshape(width, value.shape[-1])
+    packed, small_all, small_rows = first_call(0, w_qkv[0], w_out[0], w_up[0], w_down[0], small)
+    matrix = lambda layer, number: packed[
+        layer, :, :, number * depth : (number + 1) * depth
+    ].reshape(width, local_hidden)
+    full_up = [matrix(layer, 1) for layer in range(2)]
+    full_down = [matrix(layer, 2) for layer in range(2)]
 
     my_tokens = own(tokens)
     my_cotangent = own(cotangent)
-    seg_mine = own(full_seg)[:, :, 0, :rows].reshape(8, 128)
-    normed, seg_group, up_first, down_first = tensor_call(
-        1, first_rows, None, [my_tokens], [small_rows[0]], [], 0, True, seg_mine,
-        weight_rider([up_half[0], down_half[0]]),
+    seg_mine = own(small_all)[:, :, 14, :rows].astype(jnp.int32).reshape(8, 128)
+    normed, seg_group = tensor_call(
+        1, first_rows, None, [my_tokens], [small_rows[0]], [], 0, True, seg_mine
     )
-    full_qkv, full_out = [joined_qkv(qkv_first), None], [joined(out_first), None]
-    full_up, full_down = [joined(up_first), None], [joined(down_first), None]
     seg_all = seg_group.reshape(RING, RING * RING, rows).transpose(1, 0, 2).reshape(-1, group)
     seg_rows = lax.dynamic_index_in_dim(seg_all, lax.axis_index("dp"), 0, keepdims=False)
     seg_wide = jnp.broadcast_to(seg_rows[None], (8, group))
@@ -1296,16 +1196,11 @@
         )
         biases = jnp.pad(jnp.stack([query_bias, value_bias]), ((0, 6), (0, 0)))
         queries, keys_full, values_full, mixed, wide, lse, part = attend_call(
-            2 + 12 * layer, normed, full_qkv[layer], full_out[layer], biases, seg_wide, seg_column
-        )
-        rider = weight_rider([qkv_half[1], out_half[1]]) if layer == 0 else None
-        results = tensor_call(
-            3 + 12 * layer, middle_rows, part, [inputs.astype(F32)], [vec], [F32, F32], 0, True,
-            None, rider,
-        )
-        attn_out, hidden, normed_two = results[:3]
-        if layer == 0:
-            full_qkv[1], full_out[1] = joined_qkv(results[3]), joined(results[4])
+            2 + 12 * layer, layer, normed, packed, biases, seg_wide, seg_column
+        )
+        attn_out, hidden, normed_two = tensor_call(
+            3, middle_rows, part, [inputs.astype(F32)], [vec], [F32, F32], 0, True
+        )
         normed_two = normed_two.reshape(group, width)
         pre_act = jnp.dot(normed_two, full_up[layer], preferred_element_type=F32) + up_bias
         activated = gelu_exact(pre_act).astype(BF16)
@@ -1313,11 +1208,9 @@
         step_kept = [inputs, normed, queries, keys_full, values_full, mixed, attn_out, hidden]
         step_kept += [normed_two, pre_act, activated, wide, lse]
         if layer == 0:
-            mlp_first, between, normed, up_second, down_second = tensor_call(
-                4, end_rows_first, part, [hidden], [vec, small_rows[1]], [F32, BF16], 0, True,
-                None, weight_rider([up_half[1], down_half[1]]),
+            mlp_first, between, normed = tensor_call(
+                4, end_rows_first, part, [hidden], [vec, small_rows[1]], [F32, BF16], 0, True
             )
-            full_up[1], full_down[1] = joined(up_second), joined(down_second)
             inputs = between
         else:
             outputs, sums_end, mlp_rows = tensor_call(
@@ -1327,7 +1220,7 @@
 
     upstream = my_cotangent.astype(F32)
     blocks = lambda value: value.astype(BF16).reshape(*square, depth, value.shape[-1])
-    sums, waiting, summed = [None, None], None, [None, None]
+    sums, grads = [None, None], [None, None]
     for layer in (1, 0):
         vec = small_rows[layer]
         inputs, normed, queries, keys_full, values_full, mixed, attn_out, hidden = kept[layer][:8]
@@ -1340,23 +1233,19 @@
         pre_low = pre_grad.astype(BF16)
         grad_up = blocks(rows_dot(normed_two, pre_low))
         part = flat_dot(pre_low, full_up[layer]).astype(BF16).reshape(RING, rows, width)
-        results = tensor_call(
-            6 + 12 * layer, back_middle_rows, part, [upstream, hidden, attn_out], [vec], [F32], 4, True,
-            None, gradient_rider(waiting) if layer == 0 else None,
-        )
-        hidden_grad, sums_middle, attn_rows = results[:3]
-        if layer == 0:
-            summed[1] = results[3:] + summed[1]
+        hidden_grad, sums_middle, attn_rows = tensor_call(
+            6, back_middle_rows, part, [upstream, hidden, attn_out], [vec], [F32], 4, True
+        )
         attn_rows = attn_rows.reshape(group, width)
         grad_out = blocks(rows_dot(attn_rows, mixed))
         triple, sums_attend, part = attend_back_call(
-            7 + 12 * layer, attn_rows, full_qkv[layer], full_out[layer], queries, keys_full, values_full,
+            7 + 12 * layer, layer, attn_rows, packed, queries, keys_full, values_full,
             wide, lse, seg_wide, seg_column,
         )
-        waiting = [blocks(rows_dot(normed, triple[which])) for which in range(3)]
-        rider = gradient_rider([grad_up, grad_down, grad_out])
+        grads[layer] = [blocks(rows_dot(normed, triple[which])) for which in range(3)]
+        grads[layer] += [grad_out, grad_up, grad_down]
         if layer == 1:
-            results = tensor_call(
+            input_grad, sums_last, mlp_rows = tensor_call(
                 8,
                 back_end_rows_last,
                 part,
@@ -1365,18 +1254,11 @@
                 [F32],
                 4,
                 True,
-                None,
-                rider,
             )
-            input_grad, sums_last, mlp_rows = results[:3]
-            summed[1] = results[3:]
         else:
-            results = tensor_call(
-                9, back_end_rows_first, part, [hidden_grad, inputs.astype(F32)], [vec], [F32], 2, False,
-                None, rider,
+            input_grad, sums_last = tensor_call(
+                9, back_end_rows_first, part, [hidden_grad, inputs.astype(F32)], [vec], [F32], 2, False
             )
-            input_grad, sums_last = results[:2]
-            summed[0] = results[2:]
         sums[layer] = [sums_last, sums_middle, sums_end, sums_attend, up_bias_grad]
         if layer == 1:
             last_grad = input_grad
@@ -1388,22 +1270,25 @@
         jnp.where(section == 0, outputs, between),
         jnp.where(section == 0, last_grad, first_grad),
     ]
-    results = final_call(10, sums[0] + sums[1], waiting, extras)
-    small_sum, came_out, came_grad = results[0], results[4], results[5]
-    summed[0] = results[1:4] + summed[0]
+    small_sum, packed_sum, came_out, came_grad = final_call(
+        10, sums[0] + sums[1], grads[0] + grads[1], extras
+    )
     mine_out = jnp.where(section == 0, between, outputs)
     mine_grad = jnp.where(section == 0, first_grad, last_grad)
     pair = lambda mine, came: jnp.where(
         section == 0, jnp.stack([mine, came]), jnp.stack([came, mine])
     )[None]
-    pick = lambda which: jnp.where(section == 0, summed[0][which], summed[1][which])
+    half = depth // 2
+    columns = lambda which: packed_sum[
+        :, :half, which * local_width : (which + 1) * local_width
+    ].reshape(depth, local_width)
     return (
         pair(mine_out, came_out),
         pair(mine_grad, came_grad),
-        jnp.stack([pick(0), pick(1), pick(2)])[None],
-        pick(5)[None],
-        pick(3)[None],
-        pick(4)[None],
+        jnp.stack([columns(0), columns(1), columns(2)])[None],
+        columns(3)[None],
+        packed_sum[:, half : 2 * half].reshape(1, depth, local_hidden),
+        packed_sum[:, 2 * half :].reshape(1, depth, local_hidden),
         small_sum[:13, :depth][None],
         small_sum[13:14, :depth],
     )

time: 517 us -> 469 us (0.907)
  the two profiles are of different devices: /device:TPU:0 before, /device:TPU:1 now
where the time goes in v5:
time: 469 us; the launch traced here: 461 us
  Pallas kernels  385 us (82%)
  matrix products  39.5 us (8%)
  local copies, waits for them, and re-layouts  19.1 us (4%)
  other arithmetic  15.4 us (3%)
    pallas_call x9, Pallas kernels, tensor_call(): pl.pallas_call(functools.partial(tensor_kernel, function, len(rows), len(...  122 us
    pallas_call x1, Pallas kernels, final_call(): pl.pallas_call(functools.partial(final_kernel, extra), out_shape=[jax.Sha...  75.2 us
    pallas_call x2, Pallas kernels, attend_call(): pl.pallas_call(functools.partial(attend_kernel, layer), out_shape=[jax.Sh...  68.3 us
    pallas_call x2, Pallas kernels, attend_back_call(): pl.pallas_call(functools.partial(attend_back_kernel, layer), out_shape=[j...  63.9 us
    pallas_call x1, Pallas kernels, first_call(): pl.pallas_call(first_kernel, out_shape=[jax.ShapeDtypeStruct((2, RING, RI...  55.8 us
    dot_general x12, matrix products, rows_dot(): lax.dot_general(former, latter, (((0,), (0,)), ((), ())), preferred_eleme...  17.7 us
    dot_general x2, matrix products, shards(): jnp.dot(normed_two, full_up[layer], preferred_element_type=F32) + up_bias  9.83 us

profile of v5, /device:TPU:1, one launch (start us, length us, event | category | flops | bytes accessed | tf_op | source)
XLA Modules:
  0.0 460.6 jit_solution(7211636287719352873)
XLA Ops:
  1.4 1.3 fusion.37.small_in
  2.7 2.0 fusion.45
  4.7 55.8 %shard_map.152 = (bf16[2,4,4,208,1024]{4,3,2,1,0:T(8,128)(2,1)}, bf16[2,4,4,16,128]{4,3,2,1,0:T(8,128)(2,1)}, f32[2,16,1024]{2,1,0:T(8,128)}) custom-call(bf16[3,64,256]{2,1,0:T(8,128)(2,1)} %bitcast.188, bf16[64,256]{1,0:T(8,128)(2,1)} %bitcast.190, bf16[64,1024]{1,0:T(8,128)(2,1)} %bitcast.185, bf16[64,1024]{1,0:T(8,128)(2,1)} %bitcast.186, ...), custom_call_target="tpu_custom_call" | custom-call | tf_op jit(solution)/shard_map/pallas_call | solution.py:461
  60.6 0.9 select_bitcast_fusion.4
  62.2 0.9 fusion.52
  65.1 1.5 slice_bitcast_fusion
  66.6 12.1 %shard_map.153 = (bf16[4,64,1024]{2,1,0:T(8,128)(2,1)}, s32[4,8,128]{2,1,0:T(8,128)}) custom-call(bf16[64,1024]{1,0:T(8,128)(2,1)} %get-tuple-element.165.refs_0_, f32[16,1024]{1,0:T(8,128)} %get-tuple-element.161.refs_1_.refs_2_.refs_5_.refs_4_.refs_3_, s32[8,128]{1,0:T(8,128)} %reshape.289.refs_2_), custom_call_target="tpu_custom_call" | custom-call | tf_op jit(solution)/shard_map/pallas_call | solution.py:168
  80.4 1.7 broadcast_in_dim.19.seg_k_ref
  82.0 36.0 %shard_map.154 = (bf16[256,256]{1,0:T(8,128)(2,1)}, bf16[4,4,256,256]{3,2,1,0:T(8,128)(2,1)}, bf16[4,4,256,256]{3,2,1,0:T(8,128)(2,1)}, bf16[256,256]{1,0:T(8,12...) custom-call(bf16[256,1024]{1,0:T(8,128)(2,1)} %bitcast.137, ...), custom_call_target="tpu_custom_call" | custom-call | tf_op jit(solution)/shard_map/pallas_call | solution.py:978
  118.1 15.8 %shard_map.155 = (f32[64,1024]{1,0:T(8,128)}, f32[64,1024]{1,0:T(8,128)}, bf16[4,64,1024]{2,1,0:T(8,128)(2,1)}) custom-call(bf16[4,64,1024]{2,1,0:T(8,128)(2,1)} %get-tuple-element.65.refs_0_, f32[64,1024]{1,0:T(8,128)} %get-tuple-element.164.refs_1_.refs_2_, f32[16,1024]{1,0:T(8,128)} %get-tuple-element.161.refs_1_.refs_2_.refs_5_.refs_4_.refs_3_), custom_call_target="tpu_custom_call" | custom-call | tf_op jit(solution)/shard_map/pallas_call | solution.py:168
  133.9 5.1 %fusion.49 = (bf16[1,4,4,64,1024]{4,3,2,1,0:T(8,128)(2,1)}, bf16[1,4,4,64,1024]{4,3,2,1,0:T(8,128)(2,1)S(1)}, bf16[1,4,4,64,1024]{4,3,2,1,0:T(8,128)(2,1)S(1)}, bf16[1,4,4,64,1024]{4,3,2,1,0:T(8,128)(2,1)S(1)}) fusion(bf16[2,4,4,208,1024]{4,3,2,1,0:T(8,128)(2,1)} %get-tuple-element.63.packed_any), kind=kLoop, calls=%fused_computation.118 | loop fusion | bytes 16777216 | tf_op jit(solution)/shard_map/slice | solution.py:1171
  139.0 4.2 multiply_convert_fusion.1
  143.2 1.5 convolution_convert_fusion.15
  144.8 16.9 %shard_map.156 = (f32[64,1024]{1,0:T(8,128)}, bf16[64,1024]{1,0:T(8,128)(2,1)}, bf16[4,64,1024]{2,1,0:T(8,128)(2,1)}) custom-call(bf16[4,64,1024]{2,1,0:T(8,128)(2,1)} %bitcast.165, f32[64,1024]{1,0:T(8,128)} %get-tuple-element.67.refs_1_.refs_2_, f32[16,1024]{1,0:T(8,128)} %get-tuple-element.161.refs_1_.refs_2_.refs_5_.refs_4_.refs_3_, ...), custom_call_target="tpu_custom_call" | custom-call | tf_op jit(solution)/shard_map/pallas_call | solution.py:168
  161.7 1.6 convert_element_type.99.refs_1_.refs_2_
  163.3 32.3 %shard_map.157 = (bf16[256,256]{1,0:T(8,128)(2,1)}, bf16[4,4,256,256]{3,2,1,0:T(8,128)(2,1)}, bf16[4,4,256,256]{3,2,1,0:T(8,128)(2,1)}, bf16[256,256]{1,0:T(8,12...) custom-call(bf16[256,1024]{1,0:T(8,128)(2,1)} %bitcast.141, ...), custom_call_target="tpu_custom_call" | custom-call | tf_op jit(solution)/shard_map/pallas_call | solution.py:978
  195.6 12.9 %shard_map.158 = (f32[64,1024]{1,0:T(8,128)}, f32[64,1024]{1,0:T(8,128)}, bf16[4,64,1024]{2,1,0:T(8,128)(2,1)}) custom-call(bf16[4,64,1024]{2,1,0:T(8,128)(2,1)} %get-tuple-element.70.refs_0_, f32[64,1024]{1,0:T(8,128)} %convert_element_type.99.refs_1_.refs_2_, f32[16,1024]{1,0:T(8,128)} %get-tuple-element.160.refs_3_.refs_2_.refs_4_), custom_call_target="tpu_custom_call" | custom-call | tf_op jit(solution)/shard_map/pallas_call | solution.py:168
  208.6 5.6 %multiply_convert_fusion = (bf16[256,1024]{1,0:T(8,128)(2,1)S(1)}, f32[256,1024]{1,0:T(8,128)}, f32[256,1024]{1,0:T(8,128)}) fusion(f32[1024]{0:T(1024)S(1)} %dynamic_slice.28, bf16[256,1024]{1,0:T(8,128)(2,1)} %bitcast.171, bf16[1024,1024]{1,0:T(8,128)(2,1)S(1)} %bitcast.161), kind=kOutput, calls=%fused_computation.24 | convolution fusion | flops 554172416 | bytes 5246976 | tf_op jit(solution)/shard_map/dot_general | solution.py:1205
  214.2 1.6 convolution_convert_fusion.14
  215.8 13.7 %shard_map.159 = (bf16[64,1024]{1,0:T(8,128)(2,1)}, f32[8,1024]{1,0:T(8,128)}, bf16[4,64,1024]{2,1,0:T(8,128)(2,1)}) custom-call(bf16[4,64,1024]{2,1,0:T(8,128)(2,1)} %bitcast.168, f32[64,1024]{1,0:T(8,128)} %get-tuple-element.72.refs_1_.refs_2_, bf16[64,1024]{1,0:T(8,128)(2,1)} %get-tuple-element.133.refs_2_, ...), custom_call_target="tpu_custom_call" | custom-call | tf_op jit(solution)/shard_map/pallas_call | solution.py:168
  229.5 3.3 fusion.43
  232.9 1.5 convolution_convert_fusion.13
  234.4 12.9 %shard_map.160 = (f32[64,1024]{1,0:T(8,128)}, f32[8,1024]{1,0:T(8,128)}, bf16[4,64,1024]{2,1,0:T(8,128)(2,1)}) custom-call(bf16[4,64,1024]{2,1,0:T(8,128)(2,1)} %bitcast.167, f32[64,1024]{1,0:T(8,128)} %get-tuple-element.132.refs_1_, f32[64,1024]{1,0:T(8,128)} %get-tuple-element.72.refs_1_.refs_2_, f32[64,1024]{1,0:T(8,128)} %get-tuple-element.75.refs_3_, ...), custom_call_target="tpu_custom_call" | custom-call | tf_op jit(solution)/shard_map/pallas_call | solution.py:168
  247.3 31.9 %shard_map.161 = (bf16[3,256,256]{2,1,0:T(8,128)(2,1)}, f32[8,256]{1,0:T(8,128)}, bf16[4,64,1024]{2,1,0:T(8,128)(2,1)}) custom-call(bf16[256,1024]{1,0:T(8,128)(2,1)} %bitcast.155, bf16[2,4,4,208,1024]{4,3,2,1,0:T(8,128)(2,1)} %get-tuple-element.63.packed_any, bf16[256,256]{1,0:T(8,128)(2,1)} %get-tuple-element.77.q_ref, ...), custom_call_target="tpu_custom_call" | custom-call | tf_op jit(solution)/shard_map/pallas_call | solution.py:1119
  279.3 1.2 convolution_convert_fusion.4
  280.5 15.1 %shard_map.162 = (f32[64,1024]{1,0:T(8,128)}, f32[8,1024]{1,0:T(8,128)}, bf16[4,64,1024]{2,1,0:T(8,128)(2,1)}) custom-call(bf16[4,64,1024]{2,1,0:T(8,128)(2,1)} %get-tuple-element.82.refs_0_, f32[64,1024]{1,0:T(8,128)} %get-tuple-element.83.refs_1_, f32[64,1024]{1,0:T(8,128)} %convert_element_type.99.refs_1_.refs_2_, f32[64,1024]{1,0:T(8,128)} %get-tuple-element.84.refs_3_, ...), custom_call_target="tpu_custom_call" | custom-call | tf_op jit(solution)/shard_map/pallas_call | solution.py:168
  295.6 2.4 fusion.44
  298.1 1.5 convolution_convert_fusion.12
  302.9 13.4 %shard_map.163 = (f32[64,1024]{1,0:T(8,128)}, f32[8,1024]{1,0:T(8,128)}, bf16[4,64,1024]{2,1,0:T(8,128)(2,1)}) custom-call(bf16[4,64,1024]{2,1,0:T(8,128)(2,1)} %bitcast.166, f32[64,1024]{1,0:T(8,128)} %convert_convert_fusion.refs_1_, f32[64,1024]{1,0:T(8,128)} %get-tuple-element.67.refs_1_.refs_2_, f32[64,1024]{1,0:T(8,128)} %get-tuple-element.87.refs_3_, ...), custom_call_target="tpu_custom_call" | custom-call | tf_op jit(solution)/shard_map/pallas_call | solution.py:168
  316.3 31.9 %shard_map.164 = (bf16[3,256,256]{2,1,0:T(8,128)(2,1)}, f32[8,256]{1,0:T(8,128)}, bf16[4,64,1024]{2,1,0:T(8,128)(2,1)}) custom-call(bf16[256,1024]{1,0:T(8,128)(2,1)} %bitcast.153, bf16[2,4,4,208,1024]{4,3,2,1,0:T(8,128)(2,1)} %get-tuple-element.63.packed_any, bf16[256,256]{1,0:T(8,128)(2,1)} %get-tuple-element.89.q_ref, ...), custom_call_target="tpu_custom_call" | custom-call | tf_op jit(solution)/shard_map/pallas_call | solution.py:1119
  348.3 1.2 convolution_convert_fusion.8
  349.4 9.3 %shard_map.165 = (f32[64,1024]{1,0:T(8,128)}, f32[8,1024]{1,0:T(8,128)}) custom-call(bf16[4,64,1024]{2,1,0:T(8,128)(2,1)} %get-tuple-element.94.refs_0_, f32[64,1024]{1,0:T(8,128)} %get-tuple-element.95.refs_1_, f32[64,1024]{1,0:T(8,128)} %get-tuple-element.164.refs_1_.refs_2_, f32[16,1024]{1,0:T(8,128)} %get-tuple-element.161.refs_1_.refs_2_.refs_5_.refs_4_.refs_3_), custom_call_target="tpu_custom_call" | custom-call | tf_op jit(solution)/shard_map/pallas_call | solution.py:168
  358.7 1.8 select_bitcast_fusion
  360.5 1.2 convolution_convert_fusion.9
  361.7 1.1 convolution_convert_fusion.10
  362.8 1.1 convolution_convert_fusion.11
  364.0 1.2 convolution_convert_fusion.5
  365.1 1.2 convolution_convert_fusion.6
  366.3 1.1 convolution_convert_fusion.7
  367.4 2.1 convolution_convert_fusion.2
  369.5 2.1 convolution_convert_fusion
  371.7 2.1 convolution_convert_fusion.3
  373.8 2.2 convolution_convert_fusion.1
  375.9 75.2 %shard_map.166 = (f32[16,128]{1,0:T(8,128)}, f32[2,96,1024]{2,1,0:T(8,128)}, bf16[64,1024]{1,0:T(8,128)(2,1)}, f32[64,1024]{1,0:T(8,128)}) custom-call(f32[8,1024]{1,0:T(8,128)} %get-tuple-element.96.refs_0_, f32[8,1024]{1,0:T(8,128)} %get-tuple-element.97.refs_1_, f32[6,1024]{1,0:T(8,128)} %slice.146.refs_2_, f32[8,256]{1,0:T(8,128)} %get-tuple-element.99.refs_3_, ...), custom_call_target="tpu_custom_call" | custom-call | tf_op jit(solution)/shard_map/pallas_call | solution.py:797
  451.2 1.8 maximum_select_fusion.1
  452.9 1.9 maximum_select_fusion
  454.8 1.2 slice.160
  457.3 1.6 fusion.51
  (68 shorter events, 11.3 us)
Async XLA Ops:
  133.9 5.1 %copy-start.8 = (bf16[4,64,1024]{2,1,0:T(8,128)(2,1)S(1)}, bf16[4,64,1024]{2,1,0:T(8,128)(2,1)}, u32[]{:S(2)}) copy-start(bf16[4,64,1024]{2,1,0:T(8,128)(2,1)} %get-tuple-element.66) | copy-start | bytes 1572868
  208.5 5.6 %copy-start.4 = (bf16[1,4,4,64,1024]{4,3,2,1,0:T(8,128)(2,1)S(1)}, bf16[1,4,4,64,1024]{4,3,2,1,0:T(8,128)(2,1)}, u32[]{:S(2)}) copy-start(bf16[1,4,4,64,1024]{4,3,2,1,0:T(8,128)(2,1)} %get-tuple-element.140) | copy-start | bytes 6291460
  232.9 1.6 copy-start.11
  247.3 32.0 %copy-start.3 = (bf16[4,64,1024]{2,1,0:T(8,128)(2,1)S(1)}, bf16[4,64,1024]{2,1,0:T(8,128)(2,1)}, u32[]{:S(2)}) copy-start(bf16[4,64,1024]{2,1,0:T(8,128)(2,1)} %get-tuple-element.76) | copy-start | bytes 1572868
  247.3 32.0 %copy-start.19 = (bf16[256,256]{1,0:T(8,128)(2,1)S(1)}, bf16[256,256]{1,0:T(8,128)(2,1)}, u32[]{:S(2)}) copy-start(bf16[256,256]{1,0:T(8,128)(2,1)} %get-tuple-element.106) | copy-start | bytes 393220
  279.3 16.3 %copy-start.20 = (f32[256,1024]{1,0:T(8,128)S(1)}, f32[256,1024]{1,0:T(8,128)}, u32[]{:S(2)}) copy-start(f32[256,1024]{1,0:T(8,128)} %get-tuple-element.137) | copy-start | bytes 3145732
  298.0 1.6 copy-start.7
  298.0 1.6 copy-start.18
  298.0 3.5 copy-start.16
  298.1 4.1 copy-start.5
  316.3 31.9 %copy-start.2 = (bf16[4,64,1024]{2,1,0:T(8,128)(2,1)S(1)}, bf16[4,64,1024]{2,1,0:T(8,128)(2,1)}, u32[]{:S(2)}) copy-start(bf16[4,64,1024]{2,1,0:T(8,128)(2,1)} %get-tuple-element.88) | copy-start | bytes 1572868
  316.3 31.9 %copy-start.17 = (bf16[256,256]{1,0:T(8,128)(2,1)S(1)}, bf16[256,256]{1,0:T(8,128)(2,1)}, u32[]{:S(2)}) copy-start(bf16[256,256]{1,0:T(8,128)(2,1)} %get-tuple-element.104) | copy-start | bytes 393220
  348.2 12.3 %copy-start = (bf16[4,64,1024]{2,1,0:T(8,128)(2,1)S(1)}, bf16[4,64,1024]{2,1,0:T(8,128)(2,1)}, u32[]{:S(2)}) copy-start(bf16[4,64,1024]{2,1,0:T(8,128)(2,1)} %get-tuple-element.62) | copy-start | bytes 1572868
  348.3 12.3 %copy-start.15 = (bf16[3,256,256]{2,1,0:T(8,128)(2,1)S(1)}, bf16[3,256,256]{2,1,0:T(8,128)(2,1)}, u32[]{:S(2)}) copy-start(bf16[3,256,256]{2,1,0:T(8,128)(2,1)} %get-tuple-element.103) | copy-start | bytes 1179652
  358.7 5.3 %copy-start.1 = (bf16[4,64,1024]{2,1,0:T(8,128)(2,1)S(1)}, bf16[4,64,1024]{2,1,0:T(8,128)(2,1)}, u32[]{:S(2)}) copy-start(bf16[4,64,1024]{2,1,0:T(8,128)(2,1)} %get-tuple-element.69) | copy-start | bytes 1572868
  358.7 5.3 %copy-start.14 = (bf16[3,256,256]{2,1,0:T(8,128)(2,1)S(1)}, bf16[3,256,256]{2,1,0:T(8,128)(2,1)}, u32[]{:S(2)}) copy-start(bf16[3,256,256]{2,1,0:T(8,128)(2,1)} %get-tuple-element.105) | copy-start | bytes 1179652
  362.8 4.6 %copy-start.13 = (bf16[4,64,1024]{2,1,0:T(8,128)(2,1)S(1)}, bf16[4,64,1024]{2,1,0:T(8,128)(2,1)}, u32[]{:S(2)}) copy-start(bf16[4,64,1024]{2,1,0:T(8,128)(2,1)} %get-tuple-element.85) | copy-start | bytes 1572868
  366.3 3.3 copy-start.10
  371.7 2.1 copy-start.9
  371.7 2.1 copy-start.12
  451.1 7.7 %copy-start.6 = (f32[2,96,1024]{2,1,0:T(8,128)S(1)}, f32[2,96,1024]{2,1,0:T(8,128)}, u32[]{:S(2)}) copy-start(f32[2,96,1024]{2,1,0:T(8,128)} %get-tuple-element.110) | copy-start | bytes 2359300

commit v6 on v5

--- a/solution.py
+++ b/solution.py
@@ -1,4 +1,5 @@
 import functools
+from types import SimpleNamespace
 
 import jax
 import jax.numpy as jnp
@@ -393,6 +394,8 @@
                 ring.other(i, offset)
             pass_on(i, PLUS)
             pass_on(i, MINUS)
+
+    def last():
         for i in ring.every:
             for offset in range(RING):
                 ring.relayed[i, offset].wait_recv()
@@ -400,50 +403,72 @@
         for copy in across:
             copy.wait_recv()
 
-    return [begin, near, middle, end]
-
-
-PACKED = 192
+    return [begin, near, middle, end, last]
+
+
+HALF_ROWS = 96
 SMALL = 16
 
 
+def half_places(half, width, hidden):
+    return [(0, which * width, width) for which in range(4)] + [
+        (half, 0, hidden),
+        (2 * half, 0, hidden),
+    ]
+
+
 def first_kernel(
-    qkv_in, out_in, up_in, down_in, small_in, packed_out, small_all, rows_out,
-    block, send, recv, local, pack_local, last_local,
+    qkv_in, out_in, up_in, down_in, small_in, packed_out, stage, small_all, rows_out,
+    send, recv, local, swap_send, swap_recv, swap_local, last_local,
 ):
     rank = lax.axis_index("dp")
     y, z = rank // RING, lax.rem(rank, RING)
     section = lax.axis_index("section")
     barrier, count = dp_barrier(y, z, section)
     depth, width = out_in.shape
-    packs = [
-        (qkv_in.at[which], block.at[0:depth, which * width : (which + 1) * width]) for which in range(3)
+    half = depth // 2
+    mine, others = half_of(section, half), half_of(1 - section, half)
+    sources = [qkv_in.at[which] for which in range(3)] + [out_in, up_in, down_in]
+    places = half_places(half, width, stage.shape[2])
+    tail = pl.ds(HALF_ROWS, SMALL)
+    stage[0, tail] = jnp.zeros((SMALL, stage.shape[2]), BF16)
+    stage[1, tail] = jnp.zeros((SMALL, stage.shape[2]), BF16)
+    kept = [
+        pltpu.make_async_copy(
+            small_in, stage.at[0, tail, pl.ds(0, small_in.shape[1])], swap_local.at[len(places)]
+        )
     ]
-    packs += [
-        (out_in, block.at[0:depth, 3 * width : 4 * width]),
-        (up_in, block.at[depth : 2 * depth]),
-        (down_in, block.at[2 * depth : 3 * depth]),
-        (small_in, block.at[PACKED : PACKED + SMALL, 0 : small_in.shape[1]]),
-    ]
-    block[PACKED : PACKED + SMALL] = jnp.zeros((SMALL, block.shape[1]), BF16)
-    copies = [
-        pltpu.make_async_copy(source, target, pack_local.at[i])
-        for i, (source, target) in enumerate(packs)
-    ]
-    for copy in copies:
-        copy.start()
-    for copy in copies:
-        copy.wait()
+    kept[0].start()
     pl.semaphore_wait(barrier, count)
     started = []
     push = pusher(send, recv, started)
-    low, high = pl.ds(0, PACKED // 2), pl.ds(PACKED // 2, PACKED // 2 + SMALL)
+    swaps = []
+    for i, (source, (row, column, columns)) in enumerate(zip(sources, places)):
+        target = stage.at[section, pl.ds(row, half), pl.ds(column, columns)]
+        copy = pltpu.make_async_remote_copy(
+            src_ref=source.at[others],
+            dst_ref=target,
+            send_sem=swap_send.at[i],
+            recv_sem=swap_recv.at[i],
+            device_id={"section": 1 - section},
+            device_id_type=MESH,
+        )
+        copy.start()
+        swaps.append(copy)
+        copy = pltpu.make_async_copy(source.at[mine], target, swap_local.at[i])
+        copy.start()
+        kept.append(copy)
+    for copy in kept:
+        copy.wait()
+    for copy in swaps:
+        copy.wait_recv()
+    low, high = pl.ds(0, HALF_ROWS // 2), pl.ds(HALF_ROWS // 2, HALF_ROWS // 2 + SMALL)
     views = [packed_out.at[section, :, :, low], packed_out.at[section, :, :, high]]
     ring = Gather(((0, (), True), (1, (), False)), views, y, z, (), push)
-    for stage in spread_stages(ring, [block.at[low], block.at[high]], local, section, push):
-        stage()
+    for each in spread_stages(ring, [stage.at[0, low], stage.at[0, high]], local, section, push):
+        each()
     last = pltpu.make_async_copy(
-        packed_out.at[:, :, :, pl.ds(PACKED, SMALL), pl.ds(0, small_in.shape[1])], small_all, last_local
+        packed_out.at[:, :, :, tail, pl.ds(0, small_in.shape[1])], small_all, last_local
     )
     last.start()
     last.wait()
@@ -451,8 +476,16 @@
         for number in range(RING * RING):
             part = small_all[layer, number // RING, number % RING]
             rows_out[layer, :, number * depth : (number + 1) * depth] = part[:, :depth].astype(F32)
-    for copy in started:
+    for copy in started + swaps:
         copy.wait_send()
+
+
+def gather_scratch():
+    return [
+        pltpu.SemaphoreType.DMA((2, 6, RING)),
+        pltpu.SemaphoreType.DMA((2, 6, RING)),
+        pltpu.SemaphoreType.DMA((2,)),
+    ]
 
 
 def first_call(cid, w_qkv, w_out, w_up, w_down, small):
@@ -461,17 +494,17 @@
     return pl.pallas_call(
         first_kernel,
         out_shape=[
-            jax.ShapeDtypeStruct((2, RING, RING, PACKED + SMALL, hidden), BF16),
+            jax.ShapeDtypeStruct((2, RING, RING, HALF_ROWS + SMALL, hidden), BF16),
+            jax.ShapeDtypeStruct((2, HALF_ROWS + SMALL, hidden), BF16),
             jax.ShapeDtypeStruct((2, RING, RING) + small.shape, BF16),
             jax.ShapeDtypeStruct((2, SMALL, RING * RING * depth), F32),
         ],
         in_specs=[vmem_spec()] * 5,
-        out_specs=[any_spec(), vmem_spec(), vmem_spec()],
-        scratch_shapes=[
-            pltpu.VMEM((PACKED + SMALL, hidden), BF16),
-            pltpu.SemaphoreType.DMA((2, 6, RING)),
-            pltpu.SemaphoreType.DMA((2, 6, RING)),
-            pltpu.SemaphoreType.DMA((2,)),
+        out_specs=[any_spec(), vmem_spec(), vmem_spec(), vmem_spec()],
+        scratch_shapes=gather_scratch()
+        + [
+            pltpu.SemaphoreType.DMA((6,)),
+            pltpu.SemaphoreType.DMA((6,)),
             pltpu.SemaphoreType.DMA((7,)),
             pltpu.SemaphoreType.DMA,
         ],
@@ -627,18 +660,125 @@
     return [square, square] + Scatter.scratch(block, dtype)
 
 
+class LayerGradients:
+    def __init__(self, grads, buffers, semaphores, y, z, section, push):
+        self.grads, self.buffers, self.y, self.z = grads, buffers, y, z
+        self.section, self.push = section, push
+        self.swap_send, self.swap_recv, self.keep_local = semaphores
+        depth, width = grads[0].shape[2:]
+        hidden = grads[5].shape[3]
+        self.half = depth // 2
+        self.places = [(0, 0, which * width, width) for which in range(4)]
+        self.places += [(1, 0, 0, hidden), (1, self.half, 0, hidden)]
+
+    def region(self, which, place):
+        piece, row, column, columns = place
+        return self.buffers[piece][which].at[:, :, pl.ds(row, self.half), pl.ds(column, columns)]
+
+    def keep(self):
+        mine = half_of(self.section, self.half)
+        self.keeps = []
+        for i, place in enumerate(self.places):
+            copy = pltpu.make_async_copy(
+                self.grads[i].at[:, :, mine], self.region(0, place), self.keep_local.at[i]
+            )
+            copy.start()
+            self.keeps.append(copy)
+
+    def swap(self):
+        others = half_of(1 - self.section, self.half)
+        self.swaps = []
+        for i, place in enumerate(self.places):
+            copy = pltpu.make_async_remote_copy(
+                src_ref=self.grads[i].at[:, :, others],
+                dst_ref=self.region(1, place),
+                send_sem=self.swap_send.at[i],
+                recv_sem=self.swap_recv.at[i],
+                device_id={"section": 1 - self.section},
+                device_id_type=MESH,
+            )
+            copy.start()
+            self.swaps.append(copy)
+
+    def begin(self):
+        self.parts = []
+        for piece in range(2):
+            for i, place in enumerate(self.places):
+                if place[0] == piece:
+                    self.keeps[i].wait()
+                    self.swaps[i].wait_recv()
+            own, sibling = self.buffers[piece][:2]
+            add_blocks(own, own, sibling)
+            self.parts.append(
+                Scatter(piece, piece == 0, own, self.buffers[piece][2:], self.y, self.z, self.push)
+            )
+            self.parts[piece].begin()
+
+    def join(self):
+        for part in self.parts:
+            part.join()
+
+    def turn(self):
+        for part in self.parts:
+            part.turn()
+
+    def join_two(self):
+        for part in self.parts:
+            part.join_two()
+
+    def finish(self, out):
+        self.parts[0].finish(out.at[pl.ds(0, self.half)])
+        self.parts[1].finish(out.at[pl.ds(self.half, 2 * self.half)])
+
+    def end(self):
+        for copy in self.swaps:
+            copy.wait_send()
+
+    @staticmethod
+    def scratch(half, hidden):
+        return (
+            scatter_buffers((half, hidden), BF16)
+            + scatter_buffers((2 * half, hidden), BF16)
+            + [pltpu.SemaphoreType.DMA((6,))] * 3
+            + [pltpu.SemaphoreType.DMA((3, 7, RING))] * 2
+        )
+
+
+LAYER_SCRATCH = 2 * (2 + SCATTER_BUFFERS) + 5
+
+
+def layer_gradients(grads, scratch, y, z, section, started):
+    size = 2 + SCATTER_BUFFERS
+    push = pusher(scratch[-2], scratch[-1], started)
+    return LayerGradients(
+        grads, [scratch[:size], scratch[size : 2 * size]], scratch[2 * size : 2 * size + 3],
+        y, z, section, push,
+    )
+
+
+def add_blocks(out, former, latter):
+    def add(number, carry):
+        at_y, at_z = number // RING, lax.rem(number, RING)
+        out[at_y, at_z] = (
+            former[at_y, at_z].astype(F32) + latter[at_y, at_z].astype(F32)
+        ).astype(out.dtype)
+        return carry
+
+    lax.fori_loop(0, RING * RING, add, 0)
+
+
 def final_kernel(n_extra, *refs):
     refs = list(refs)
     take = lambda count: [refs.pop(0) for _ in range(count)]
     sums = [take(5), take(5)]
-    grads = [take(6), take(6)]
+    grads, summed_last = take(6), take(1)[0]
     extras = take(n_extra)
     small_out, packed_out = take(2)
     extra_outs = take(n_extra)
     small_in, small_rows, vector_own, vector_parts, summed = take(5)
-    buffers = [take(2 + SCATTER_BUFFERS) for _ in range(3)]
-    send, recv, swap_send, swap_recv, keep_local = take(5)
-    vector_send, vector_recv, extra_send, extra_recv, result_send, result_recv, result_local = take(7)
+    small_buffers = take(2 + SCATTER_BUFFERS)
+    layer_scratch = take(LAYER_SCRATCH)
+    vector_send, vector_recv, extra_send, extra_recv, result_send, result_recv, result_local, hand_local = take(8)
     rank = lax.axis_index("dp")
     y, z = rank // RING, lax.rem(rank, RING)
     section = lax.axis_index("section")
@@ -647,21 +787,13 @@
     barrier, count = tensor_barrier(me)
     count += dp_barrier(y, z, section)[1]
 
-    depth, width = grads[0][0].shape[2:]
-    hidden = grads[0][5].shape[3]
-    half = depth // 2
-    mine, others = half_of(section, half), half_of(1 - section, half)
-    places = [(0, which * width, width) for which in range(4)]
-    places += [(half, 0, hidden), (2 * half, 0, hidden)]
-    keeps, swaps = [], []
-    for layer in range(2):
-        for i, (row, column, columns) in enumerate(places):
-            region = (slice(None), slice(None), pl.ds(row, half), pl.ds(column, columns))
-            copy = pltpu.make_async_copy(
-                grads[layer][i].at[:, :, mine], buffers[layer][0].at[region], keep_local.at[layer, i]
-            )
-            copy.start()
-            keeps.append(copy)
+    started = []
+    first_layer = layer_gradients(grads, layer_scratch, y, z, section, started)
+    push = first_layer.push
+    first_layer.keep()
+    handed = pltpu.make_async_copy(summed_last, summed.at[1], hand_local)
+    handed.start()
+    depth = grads[0].shape[2]
 
     small_rows[...] = jnp.zeros_like(small_rows)
     model = small_rows.shape[1]
@@ -688,23 +820,8 @@
             :, number * depth : (number + 1) * depth
         ]
     pl.semaphore_wait(barrier, count)
-    started = []
-    push = pusher(send, recv, started)
-    for layer in range(2):
-        for i, (row, column, columns) in enumerate(places):
-            region = (slice(None), slice(None), pl.ds(row, half), pl.ds(column, columns))
-            copy = pltpu.make_async_remote_copy(
-                src_ref=grads[layer][i].at[:, :, others],
-                dst_ref=buffers[layer][1].at[region],
-                send_sem=swap_send.at[layer, i],
-                recv_sem=swap_recv.at[layer, i],
-                device_id=other,
-                device_id_type=MESH,
-            )
-            copy.start()
-            swaps.append(copy)
-    started += swaps
-    small_swap = push(2, 6, 0, small_in.at[:, :, half_of(1 - section, SMALL)], buffers[2][1], other)
+    first_layer.swap()
+    small_swap = push(2, 6, 0, small_in.at[:, :, half_of(1 - section, SMALL)], small_buffers[1], other)
     extra_copies = []
     for i in range(n_extra):
         copy = pltpu.make_async_remote_copy(
@@ -718,36 +835,18 @@
         copy.start()
         extra_copies.append(copy)
 
-    parts = []
-    for piece in range(3):
-        own, sibling = buffers[piece][:2]
-        if piece == 2:
-            small_swap.wait_recv()
-            kept = small_in.at[:, :, half_of(section, SMALL)]
-        else:
-            for i in range(len(places)):
-                keeps[piece * len(places) + i].wait()
-                swaps[piece * len(places) + i].wait_recv()
-            kept = own
-
-        def add(number, carry):
-            at_y, at_z = number // RING, lax.rem(number, RING)
-            own[at_y, at_z] = (
-                kept[at_y, at_z].astype(F32) + sibling[at_y, at_z].astype(F32)
-            ).astype(own.dtype)
-            return carry
-
-        lax.fori_loop(0, RING * RING, add, 0)
-        parts.append(Scatter(piece, piece != 1, own, buffers[piece][2:], y, z, push))
-        parts[piece].begin()
-    for part in parts:
-        part.join()
-    order = (parts[2], parts[0], parts[1])
-    for part in order:
-        part.turn()
-    for part in order:
-        part.join_two()
-    parts[2].finish(vector_own)
+    first_layer.begin()
+    small_swap.wait_recv()
+    add_blocks(small_buffers[0], small_in.at[:, :, half_of(section, SMALL)], small_buffers[1])
+    small_part = Scatter(2, True, small_buffers[0], small_buffers[2:], y, z, push)
+    small_part.begin()
+    first_layer.join()
+    small_part.join()
+    first_layer.turn()
+    small_part.turn()
+    first_layer.join_two()
+    small_part.join_two()
+    small_part.finish(vector_own)
     vector_parts[me] = vector_own[...]
     vector_copies = []
     for k in range(1, RING):
@@ -761,8 +860,8 @@
         )
         copy.start()
         vector_copies.append(copy)
-    for layer in range(2):
-        parts[layer].finish(summed.at[layer])
+    first_layer.finish(summed.at[0])
+    handed.wait()
     result = pltpu.make_async_remote_copy(
         src_ref=summed.at[1 - section],
         dst_ref=packed_out.at[section],
@@ -784,24 +883,25 @@
     small_out[...] = total
     for copy in extra_copies:
         copy.wait()
+    first_layer.end()
     for copy in started:
         copy.wait_send()
 
 
-def final_call(cid, sums, grads, extras):
+def final_call(cid, sums, grads, summed_last, extras):
     extra = len(extras)
     width = sums[0].shape[1]
     hidden = grads[-1].shape[3]
-    args = list(sums) + list(grads) + list(extras)
-    block = (PACKED // 2, hidden)
+    args = list(sums) + list(grads) + [summed_last] + list(extras)
+    block = (HALF_ROWS, hidden)
     return pl.pallas_call(
         functools.partial(final_kernel, extra),
         out_shape=[
             jax.ShapeDtypeStruct((SMALL, 128), F32),
-            jax.ShapeDtypeStruct((2, PACKED // 2, hidden), F32),
+            jax.ShapeDtypeStruct((2, HALF_ROWS, hidden), F32),
         ]
         + [jax.ShapeDtypeStruct(value.shape, value.dtype) for value in extras],
-        in_specs=[vmem_spec()] * len(sums) + [any_spec()] * len(grads) + [vmem_spec()] * extra,
+        in_specs=[vmem_spec()] * len(sums) + [any_spec()] * (len(grads) + 1) + [vmem_spec()] * extra,
         out_specs=[vmem_spec()] * (2 + extra),
         scratch_shapes=[
             pltpu.VMEM((RING, RING, 2 * SMALL, 128), F32),
@@ -810,15 +910,9 @@
             pltpu.VMEM((RING, SMALL, 128), F32),
             pltpu.VMEM((2,) + block, F32),
         ]
-        + scatter_buffers(block, BF16)
-        + scatter_buffers(block, BF16)
         + scatter_buffers((SMALL, 128), F32)
+        + LayerGradients.scratch(HALF_ROWS // 3, hidden)
         + [
-            pltpu.SemaphoreType.DMA((3, 7, RING)),
-            pltpu.SemaphoreType.DMA((3, 7, RING)),
-            pltpu.SemaphoreType.DMA((2, 6)),
-            pltpu.SemaphoreType.DMA((2, 6)),
-            pltpu.SemaphoreType.DMA((2, 6)),
             pltpu.SemaphoreType.DMA((RING,)),
             pltpu.SemaphoreType.DMA((RING,)),
             pltpu.SemaphoreType.DMA((extra,)),
@@ -826,13 +920,10 @@
             pltpu.SemaphoreType.DMA,
             pltpu.SemaphoreType.DMA,
             pltpu.SemaphoreType.DMA,
+            pltpu.SemaphoreType.DMA,
         ],
         compiler_params=comm_params(cid),
     )(*args)
-
-
-def gelu_exact(values):
-    return jax.nn.gelu(values, approximate=False)
 
 
 def flat_dot(former, latter):
@@ -858,22 +949,35 @@
     return jnp.where(seg_column == seg_wide, scores, MASKED_SCORE)
 
 
+def load_matrix(packed_any, target, number, half, semaphores):
+    copies = []
+    for which in range(2):
+        copy = pltpu.make_async_copy(
+            packed_any.at[which, :, :, pl.ds(number * half, half)],
+            target.at[:, :, pl.ds(which * half, half)],
+            semaphores.at[which],
+        )
+        copy.start()
+        copies.append(copy)
+    return copies
+
+
 def attend_kernel(
-    layer, normed_ref, packed_any, bias_ref, seg_q_ref, seg_k_ref,
+    normed_ref, packed_any, bias_ref, seg_q_ref, seg_k_ref,
     q_ref, k_ref, v_ref, mixed_ref, wide_ref, lse_ref, part_ref,
     pack_ref, stack, acc, top_ref, total_ref, send, recv, local,
 ):
     group, width = q_ref.shape
     heads_here = width // HEAD_DIM
     depth = group // RING
-    load = pltpu.make_async_copy(packed_any.at[layer, :, :, pl.ds(0, depth)], pack_ref, local)
-    load.start()
+    loads = load_matrix(packed_any, pack_ref, 0, depth // 2, local)
     matrix = lambda which: pack_ref[:, :, :, which * width : (which + 1) * width].reshape(-1, width)
     rank = lax.axis_index("dp")
     y, z = rank // RING, lax.rem(rank, RING)
     barrier, count = dp_barrier(y, z, None)
     normed = normed_ref[...]
-    load.wait()
+    for load in loads:
+        load.wait()
     k_ref[y, z] = jnp.dot(normed, matrix(1), preferred_element_type=F32).astype(BF16)
     pl.semaphore_wait(barrier, count)
     started = []
@@ -970,13 +1074,13 @@
         copy.wait_send()
 
 
-def attend_call(cid, layer, normed, packed, biases, seg_wide, seg_column):
+def attend_call(cid, normed, packed, biases, seg_wide, seg_column):
     group, model = normed.shape
     width = biases.shape[1]
     heads_here = width // HEAD_DIM
     square = (RING, RING, group, width)
     return pl.pallas_call(
-        functools.partial(attend_kernel, layer),
+        attend_kernel,
         out_shape=[
             jax.ShapeDtypeStruct((group, width), BF16),
             jax.ShapeDtypeStruct(square, BF16),
@@ -996,14 +1100,14 @@
             pltpu.VMEM((8, group * heads_here), F32),
             pltpu.SemaphoreType.DMA((2, 5, RING)),
             pltpu.SemaphoreType.DMA((2, 5, RING)),
-            pltpu.SemaphoreType.DMA,
+            pltpu.SemaphoreType.DMA((2,)),
         ],
         compiler_params=comm_params(cid),
     )(normed, packed, biases, seg_wide, seg_column)
 
 
 def attend_back_kernel(
-    layer, rows_ref, packed_any, q_ref, k_ref, v_ref, wide_ref, lse_ref, seg_q_ref, seg_k_ref,
+    rows_ref, packed_any, q_ref, k_ref, v_ref, wide_ref, lse_ref, seg_q_ref, seg_k_ref,
     triple_ref, sums_ref, part_ref, *scratch,
 ):
     (
@@ -1016,15 +1120,15 @@
     heads_here = width // HEAD_DIM
     scale = HEAD_DIM ** (-0.5)
     depth = group // RING
-    load = pltpu.make_async_copy(packed_any.at[layer, :, :, pl.ds(0, depth)], pack_ref, local)
-    load.start()
+    loads = load_matrix(packed_any, pack_ref, 0, depth // 2, local)
     matrix = lambda which: pack_ref[:, :, :, which * width : (which + 1) * width].reshape(-1, width)
     rank = lax.axis_index("dp")
     y, z = rank // RING, lax.rem(rank, RING)
     barrier, count = dp_barrier(y, z, None)
     stack[...] = head_stack(q_ref[...], scale)
     plain[...] = head_stack(q_ref[...], 1.0)
-    load.wait()
+    for load in loads:
+        load.wait()
     grad_ref[...] = jnp.dot(rows_ref[...], matrix(3), preferred_element_type=F32).astype(BF16)
     grad_stack[...] = head_stack(grad_ref[...], scale)
     grad_plain[...] = head_stack(grad_ref[...], 1.0)
@@ -1110,14 +1214,14 @@
         copy.wait_send()
 
 
-def attend_back_call(cid, layer, attn_rows, packed, queries, keys, values, wide, lse, seg_wide, seg_column):
+def attend_back_call(cid, attn_rows, packed, queries, keys, values, wide, lse, seg_wide, seg_column):
     group, model = attn_rows.shape
     width = queries.shape[1]
     heads_here = width // HEAD_DIM
     block = (group, width)
     stacked = pltpu.VMEM((group * heads_here, width), BF16)
     return pl.pallas_call(
-        functools.partial(attend_back_kernel, layer),
+        attend_back_kernel,
         out_shape=[
             jax.ShapeDtypeStruct((3, group, width), BF16),
             jax.ShapeDtypeStruct((8, width), F32),
@@ -1143,10 +1247,314 @@
         + [
             pltpu.SemaphoreType.DMA((2, 6, RING)),
             pltpu.SemaphoreType.DMA((2, 6, RING)),
-            pltpu.SemaphoreType.DMA,
+            pltpu.SemaphoreType.DMA((2,)),
         ],
         compiler_params=comm_params(cid),
     )(attn_rows, packed, queries, keys, values, wide, lse, seg_wide, seg_column)
+
+
+class Exchange:
+    def __init__(self, me, send, recv, landing, started):
+        self.me, self.send, self.recv, self.landing, self.started = me, send, recv, landing, started
+        self.reduces = {}
+
+    def push(self, source, target, kind, index, k):
+        copy = pltpu.make_async_remote_copy(
+            src_ref=source,
+            dst_ref=target,
+            send_sem=self.send.at[kind, index, k - 1],
+            recv_sem=self.recv.at[kind, index, k - 1],
+            device_id={"tensor": step(self.me, k)},
+            device_id_type=MESH,
+        )
+        copy.start()
+        self.started.append(copy)
+        return copy
+
+    def reduce(self, part, peers=(1, 2, 3)):
+        chunk = part.shape[-2] // CHUNKS
+        for c in range(CHUNKS):
+            here = pl.ds(c * chunk, chunk)
+            for k in peers:
+                self.reduces[c, k] = self.push(
+                    part.at[step(self.me, k), here], self.landing.at[k - 1, here], 0, c, k
+                )
+
+    def run(self, part, function, rows_in, vecs, rows_out, sums_out, full, side=()):
+        side = list(side)
+        me = self.me
+        chunk = part.shape[-2] // CHUNKS
+        if side:
+            side.pop(0)()
+        sums, last = None, []
+        for c in range(CHUNKS):
+            here = pl.ds(c * chunk, chunk)
+            for k in range(1, RING):
+                self.reduces[c, k].wait_recv()
+            total = part[me, here].astype(F32)
+            for k in range(1, RING):
+                total = total + self.landing[k - 1, here].astype(F32)
+            spread, outs, parts = function(total, [ref[here].astype(F32) for ref in rows_in], vecs)
+            if full is not None:
+                full[me, here] = spread.astype(BF16)
+                last += [
+                    self.push(full.at[me, here], full.at[me, here], 1, c, k) for k in range(1, RING)
+                ]
+            for ref, value in zip(rows_out, outs):
+                ref[here] = value.astype(ref.dtype)
+            sums = parts if sums is None else [old + new for old, new in zip(sums, parts)]
+        if sums_out is not None:
+            sums_out[...] = jnp.concatenate(
+                sums + [jnp.zeros((8 - len(sums), sums[0].shape[1]), F32)], axis=0
+            )
+        for work in side:
+            work()
+        for copy in last:
+            copy.wait_recv()
+
+
+TILES = ((2, 1), (3, 0))
+
+
+def rows_of(ref, me, tile):
+    return jnp.concatenate([ref[step(me, k)] for k in tile], axis=0)
+
+
+def put_rows(ref, me, tile, value):
+    rows = ref.shape[1]
+    for i, k in enumerate(tile):
+        ref[step(me, k)] = value[i * rows : (i + 1) * rows].astype(ref.dtype)
+
+
+def wide_of(pack_ref):
+    return pack_ref[...].reshape(-1, pack_ref.shape[-1])
+
+
+def mlp_forward(me, full, up_ref, down_ref, bias_ref, act_ref, slope_ref, part_ref, exchange):
+    for tile in TILES:
+        value = jnp.dot(rows_of(full, me, tile), wide_of(up_ref), preferred_element_type=F32)
+        value = value + bias_ref[0:1, :]
+        phi = 0.5 * (1.0 + lax.erf(value * (0.5**0.5)))
+        act = (value * phi).astype(BF16)
+        density = jnp.exp(-0.5 * value * value) * 0.3989422804014327
+        put_rows(act_ref, me, tile, act)
+        put_rows(slope_ref, me, tile, phi + value * density)
+        put_rows(part_ref, me, tile, flat_dot(act, wide_of(down_ref)))
+        exchange.reduce(part_ref, [k for k in tile if k])
+
+
+def mlp_backward(me, full, up_ref, down_ref, slope_ref, pre_ref, bias_out, part_ref, exchange):
+    total = None
+    for tile in TILES:
+        value = jnp.dot(rows_of(full, me, tile), wide_of(down_ref), preferred_element_type=F32)
+        value = value * rows_of(slope_ref, me, tile)
+        part = jnp.sum(value, axis=0, keepdims=True)
+        total = part if total is None else total + part
+        low = value.astype(BF16)
+        put_rows(pre_ref, me, tile, low)
+        put_rows(part_ref, me, tile, flat_dot(low, wide_of(up_ref)))
+        exchange.reduce(part_ref, [k for k in tile if k])
+    bias_out[...] = jnp.broadcast_to(total, bias_out.shape)
+
+
+def product(former_ref, latter_ref, out_ref):
+    def work():
+        tokens = lambda ref: ref[...].reshape(-1, ref.shape[-1])
+        size = 256
+
+        def each(number, carry):
+            columns = pl.ds(pl.multiple_of(number * size, size), size)
+            left = former_ref[..., columns].reshape(-1, size)
+            value = jnp.dot(left.T, tokens(latter_ref), preferred_element_type=F32)
+            out_ref[number] = value.astype(BF16).reshape(out_ref.shape[1:])
+            return carry
+
+        lax.fori_loop(0, RING, each, 0)
+
+    return work
+
+
+def chain_call(cid, body, exchanges, packed_array, ins, outs, inside, any_names=(), extra=None):
+    names = list(ins) + list(outs) + list(inside)
+    rows, model = 64, 1024
+    count = len(names)
+    load_packed = packed_array is not None
+
+    def kernel(*refs):
+        refs = list(refs)
+        packed = refs.pop(0) if load_packed else None
+        env = SimpleNamespace(**dict(zip(names, refs[:count])))
+        refs = refs[count:]
+        me = lax.axis_index("tensor")
+        barrier, peers = tensor_barrier(me)
+        started = []
+        loads = []
+        if load_packed:
+            env.up, env.down, local = refs[:3]
+            refs = refs[3:]
+            half = env.up.shape[2] // 2
+            for i, matrix in enumerate((env.up, env.down)):
+                loads += load_matrix(packed, matrix, i + 1, half, local.at[i])
+        if extra is not None:
+            env.extra = refs[3 * exchanges :]
+            rank = lax.axis_index("dp")
+            env.place = (rank // RING, lax.rem(rank, RING), lax.axis_index("section"))
+            peers += dp_barrier(*env.place)[1]
+        pl.semaphore_wait(barrier, peers)
+        env.started = started
+        rings = [
+            Exchange(me, refs[3 * i + 1], refs[3 * i + 2], refs[3 * i], started)
+            for i in range(exchanges)
+        ]
+        body(me, env, rings, loads)
+        for copy in started:
+            copy.wait_send()
+
+    scratch = [pltpu.VMEM(shape, dtype) for shape, dtype in inside.values()]
+    spec_of = lambda name: any_spec() if name in any_names else vmem_spec()
+    args, in_specs = list(ins.values()), [spec_of(name) for name in ins]
+    if load_packed:
+        args, in_specs = [packed_array] + args, [any_spec()] + in_specs
+        matrix = pltpu.VMEM((RING, RING, rows, model), BF16)
+        scratch += [matrix, matrix, pltpu.SemaphoreType.DMA((2, 2))]
+    for _ in range(exchanges):
+        scratch += [
+            pltpu.VMEM((RING - 1, rows, model), BF16),
+            pltpu.SemaphoreType.DMA((2, CHUNKS, RING - 1)),
+            pltpu.SemaphoreType.DMA((2, CHUNKS, RING - 1)),
+        ]
+    scratch += extra or []
+    results = pl.pallas_call(
+        kernel,
+        out_shape=[jax.ShapeDtypeStruct(shape, dtype) for shape, dtype in outs.values()],
+        in_specs=in_specs,
+        out_specs=[spec_of(name) for name in outs],
+        scratch_shapes=scratch,
+        compiler_params=comm_params(cid),
+    )(*args)
+    return SimpleNamespace(**dict(zip(outs, results)))
+
+
+def first_mlp_body(me, env, rings, loads):
+    y, z, section = env.place
+    send, recv, local = env.extra
+    push = pusher(send, recv, env.started)
+    halves = [pl.ds(0, HALF_ROWS // 2), pl.ds(HALF_ROWS // 2, HALF_ROWS // 2)]
+    ring = Gather(
+        ((0, (), True), (1, (), False)),
+        [env.packed_next.at[section, :, :, half] for half in halves], y, z, (), push,
+    )
+    begin, near, middle, end, final = spread_stages(
+        ring, [env.stage.at[1, half] for half in halves], local, section, push
+    )
+    rings[0].reduce(env.part)
+    rings[0].run(
+        env.part, middle_rows, [env.inputs], [env.vec],
+        [env.attn_out, env.hidden], None, env.normed, [begin, near],
+    )
+    middle()
+    for copy in loads:
+        copy.wait()
+    mlp_forward(
+        me, env.normed, env.up, env.down, env.bias, env.act, env.slope, env.sent, rings[1],
+    )
+    end()
+    rings[1].run(
+        env.sent, end_rows_first, [env.hidden], [env.vec, env.after],
+        [env.mlp_out, env.outputs], None, env.next, [lambda: None, final],
+    )
+
+
+def last_mlp_body(me, env, rings, loads):
+    rings[0].reduce(env.part)
+    rings[0].run(
+        env.part, middle_rows, [env.inputs], [env.vec],
+        [env.attn_out, env.hidden], None, env.normed,
+    )
+    for copy in loads:
+        copy.wait()
+    mlp_forward(
+        me, env.normed, env.up, env.down, env.bias, env.act, env.slope,
+        env.sent, rings[1],
+    )
+    rings[1].run(
+        env.sent, end_rows_last, [env.hidden, env.upstream], [env.vec],
+        [env.outputs], env.sums_end, env.mlp_rows,
+    )
+    mlp_backward(
+        me, env.mlp_rows, env.up, env.down, env.slope, env.pre, env.bias_grad,
+        env.sent_two, rings[2],
+    )
+    rings[2].run(
+        env.sent_two, back_middle_rows, [env.upstream, env.hidden, env.attn_out],
+        [env.vec], [env.hidden_grad], env.sums_middle, env.attn_rows,
+        [
+            product(env.mlp_rows, env.act, env.grad_down),
+            product(env.normed, env.pre, env.grad_up),
+        ],
+    )
+
+
+def attention_products(env):
+    return [
+        product(env.attn_rows_in, env.mixed, env.grad_out)
+    ] + [
+        product(env.normed_in, env.triple.at[which], env.grad_qkv.at[which])
+        for which in range(3)
+    ]
+
+
+def between_body(me, env, rings, loads):
+    y, z, section = env.place
+    grads = [env.grad_qkv.at[which] for which in range(3)]
+    grads += [env.grad_out, env.last_up, env.last_down]
+    layer = layer_gradients(grads, env.extra, y, z, section, env.started)
+
+    def swap():
+        for work in attention_products(env):
+            work()
+        layer.keep()
+        layer.swap()
+
+    rings[0].reduce(env.part)
+    rings[0].run(
+        env.part, back_end_rows_last, [env.hidden_grad_in, env.inputs, env.mlp_out],
+        [env.vec_last, env.vec], [env.input_grad], env.sums_last, env.mlp_rows,
+        [swap, layer.begin],
+    )
+    for copy in loads:
+        copy.wait()
+    mlp_backward(
+        me, env.mlp_rows, env.up, env.down, env.slope, env.pre, env.bias_grad, env.sent, rings[1],
+    )
+    layer.join()
+
+    def products():
+        product(env.mlp_rows, env.act, env.grad_down)()
+        product(env.normed, env.pre, env.grad_up)()
+
+    def rest():
+        layer.turn()
+        layer.join_two()
+        layer.finish(env.summed)
+        layer.end()
+
+    rings[1].run(
+        env.sent, back_middle_rows_low, [env.input_grad, env.hidden, env.attn_out],
+        [env.vec], [env.hidden_grad], env.sums_middle, env.attn_rows, [products, rest],
+    )
+
+
+def back_middle_rows_low(total, rows, vecs):
+    return back_middle_rows(total, [rows[0].astype(BF16).astype(F32)] + rows[1:], vecs)
+
+
+def close_body(me, env, rings, loads):
+    rings[0].reduce(env.part)
+    rings[0].run(
+        env.part, back_end_rows_first, [env.hidden_grad_in, env.inputs],
+        [env.vec], [env.input_grad], env.sums_last, None, attention_products(env),
+    )
 
 
 def shards(tokens, segment_ids, w_qkv, w_out, w_up, w_down, vectors, out_bias, cotangent):
@@ -1167,13 +1575,7 @@
         jnp.concatenate([vectors[0], out_bias, wide_segments], axis=0),
         ((0, 1), (0, 128 - depth)),
     )
-    packed, small_all, small_rows = first_call(0, w_qkv[0], w_out[0], w_up[0], w_down[0], small)
-    matrix = lambda layer, number: packed[
-        layer, :, :, number * depth : (number + 1) * depth
-    ].reshape(width, local_hidden)
-    full_up = [matrix(layer, 1) for layer in range(2)]
-    full_down = [matrix(layer, 2) for layer in range(2)]
-
+    packed_first, stage, small_all, small_rows = first_call(0, w_qkv[0], w_out[0], w_up[0], w_down[0], small)
     my_tokens = own(tokens)
     my_cotangent = own(cotangent)
     seg_mine = own(small_all)[:, :, 14, :rows].astype(jnp.int32).reshape(8, 128)
@@ -1184,86 +1586,123 @@
     seg_rows = lax.dynamic_index_in_dim(seg_all, lax.axis_index("dp"), 0, keepdims=False)
     seg_wide = jnp.broadcast_to(seg_rows[None], (8, group))
     seg_column = jnp.broadcast_to(seg_all.reshape(*square, group)[..., None], square + (group, 128))
-    inputs = my_tokens
-    kept = []
-    for layer in range(2):
+    whole = (RING, rows, width)
+    blocks = lambda columns: square + (depth, columns)
+    spread = (RING, rows, local_hidden)
+    row_shape = (rows, width)
+    inputs = my_tokens.astype(F32)
+    up_biases = [
+        jnp.broadcast_to(
+            lax.dynamic_slice_in_dim(
+                small_rows[layer, 9:13].reshape(-1), tensor_rank * local_hidden, local_hidden
+            )[None],
+            (8, local_hidden),
+        )
+        for layer in range(2)
+    ]
+
+    def attend_layer(layer, normed, packed):
         vec = small_rows[layer]
-        normed = normed.reshape(group, width)
         query_bias = lax.dynamic_slice_in_dim(vec[2], tensor_rank * local_width, local_width)
         value_bias = lax.dynamic_slice_in_dim(vec[3], tensor_rank * local_width, local_width)
-        up_bias = lax.dynamic_slice_in_dim(
-            vec[9:13].reshape(-1), tensor_rank * local_hidden, local_hidden
-        )
         biases = jnp.pad(jnp.stack([query_bias, value_bias]), ((0, 6), (0, 0)))
-        queries, keys_full, values_full, mixed, wide, lse, part = attend_call(
-            2 + 12 * layer, layer, normed, packed, biases, seg_wide, seg_column
-        )
-        attn_out, hidden, normed_two = tensor_call(
-            3, middle_rows, part, [inputs.astype(F32)], [vec], [F32, F32], 0, True
-        )
-        normed_two = normed_two.reshape(group, width)
-        pre_act = jnp.dot(normed_two, full_up[layer], preferred_element_type=F32) + up_bias
-        activated = gelu_exact(pre_act).astype(BF16)
-        part = flat_dot(activated, full_down[layer]).astype(BF16).reshape(RING, rows, width)
-        step_kept = [inputs, normed, queries, keys_full, values_full, mixed, attn_out, hidden]
-        step_kept += [normed_two, pre_act, activated, wide, lse]
-        if layer == 0:
-            mlp_first, between, normed = tensor_call(
-                4, end_rows_first, part, [hidden], [vec, small_rows[1]], [F32, BF16], 0, True
-            )
-            inputs = between
-        else:
-            outputs, sums_end, mlp_rows = tensor_call(
-                5, end_rows_last, part, [hidden, my_cotangent], [vec], [BF16], 2, True
-            )
-        kept.append(step_kept)
-
-    upstream = my_cotangent.astype(F32)
-    blocks = lambda value: value.astype(BF16).reshape(*square, depth, value.shape[-1])
-    sums, grads = [None, None], [None, None]
-    for layer in (1, 0):
-        vec = small_rows[layer]
-        inputs, normed, queries, keys_full, values_full, mixed, attn_out, hidden = kept[layer][:8]
-        normed_two, pre_act, activated, wide, lse = kept[layer][8:]
-        mlp_rows = mlp_rows.reshape(group, width)
-        act_grad = jnp.dot(mlp_rows, full_down[layer], preferred_element_type=F32)
-        grad_down = blocks(rows_dot(mlp_rows, activated))
-        pre_grad = jax.vjp(gelu_exact, pre_act)[1](act_grad)[0]
-        up_bias_grad = jnp.broadcast_to(jnp.sum(pre_grad, axis=0)[None], (8, local_hidden))
-        pre_low = pre_grad.astype(BF16)
-        grad_up = blocks(rows_dot(normed_two, pre_low))
-        part = flat_dot(pre_low, full_up[layer]).astype(BF16).reshape(RING, rows, width)
-        hidden_grad, sums_middle, attn_rows = tensor_call(
-            6, back_middle_rows, part, [upstream, hidden, attn_out], [vec], [F32], 4, True
-        )
-        attn_rows = attn_rows.reshape(group, width)
-        grad_out = blocks(rows_dot(attn_rows, mixed))
-        triple, sums_attend, part = attend_back_call(
-            7 + 12 * layer, layer, attn_rows, packed, queries, keys_full, values_full,
-            wide, lse, seg_wide, seg_column,
-        )
-        grads[layer] = [blocks(rows_dot(normed, triple[which])) for which in range(3)]
-        grads[layer] += [grad_out, grad_up, grad_down]
-        if layer == 1:
-            input_grad, sums_last, mlp_rows = tensor_call(
-                8,
-                back_end_rows_last,
-                part,
-                [hidden_grad, inputs.astype(F32), mlp_first],
-                [vec, small_rows[0]],
-                [F32],
-                4,
-                True,
-            )
-        else:
-            input_grad, sums_last = tensor_call(
-                9, back_end_rows_first, part, [hidden_grad, inputs.astype(F32)], [vec], [F32], 2, False
-            )
-        sums[layer] = [sums_last, sums_middle, sums_end, sums_attend, up_bias_grad]
-        if layer == 1:
-            last_grad = input_grad
-            upstream = input_grad.astype(BF16).astype(F32)
-            sums_end = sums_last[2:]
+        return attend_call(
+            2 + 12 * layer, normed.reshape(group, width), packed, biases, seg_wide, seg_column
+        )
+
+    normed_first = normed
+    *kept_first, part = attend_layer(0, normed_first, packed_first)
+    first = chain_call(
+        3, first_mlp_body, 2, packed_first,
+        dict(
+            part=part, inputs=inputs, vec=small_rows[0], after=small_rows[1],
+            bias=up_biases[0], stage=stage,
+        ),
+        dict(
+            attn_out=(row_shape, F32), hidden=(row_shape, F32), normed=(whole, BF16),
+            act=(spread, BF16), slope=(spread, F32), mlp_out=(row_shape, F32),
+            outputs=(row_shape, BF16), next=(whole, BF16),
+            packed_next=((2,) + square + (HALF_ROWS, local_hidden), BF16),
+        ),
+        dict(sent=(whole, BF16)),
+        ("packed_next",),
+        gather_scratch(),
+    )
+    between = first.outputs
+    packed_last = first.packed_next
+    *kept_last, part = attend_layer(1, first.next, packed_last)
+    last = chain_call(
+        5, last_mlp_body, 3, packed_last,
+        dict(
+            part=part, inputs=between.astype(F32), vec=small_rows[1],
+            bias=up_biases[1], upstream=my_cotangent.astype(F32),
+        ),
+        dict(
+            outputs=(row_shape, BF16), sums_end=((8, width), F32),
+            hidden_grad=(row_shape, F32), sums_middle=((8, width), F32),
+            attn_rows=(whole, BF16), bias_grad=((8, local_hidden), F32),
+            grad_up=(blocks(local_hidden), BF16), grad_down=(blocks(local_hidden), BF16),
+        ),
+        dict(
+            attn_out=(row_shape, F32), hidden=(row_shape, F32), normed=(whole, BF16),
+            act=(spread, BF16), slope=(spread, F32), pre=(spread, BF16),
+            mlp_rows=(whole, BF16), sent=(whole, BF16), sent_two=(whole, BF16),
+        ),
+    )
+    outputs = last.outputs
+
+    def attend_back_layer(layer, attn_rows, kept, packed):
+        queries, keys_full, values_full, mixed, wide, lse = kept
+        return attend_back_call(
+            7 + 12 * layer, attn_rows.reshape(group, width), packed, queries, keys_full,
+            values_full, wide, lse, seg_wide, seg_column,
+        )
+
+    attention_grads = dict(
+        grad_out=(blocks(local_width), BF16), grad_qkv=((3,) + blocks(local_width), BF16),
+    )
+    triple, attend_last, part = attend_back_layer(1, last.attn_rows, kept_last, packed_last)
+    middle = chain_call(
+        8, between_body, 2, packed_first,
+        dict(
+            part=part, hidden_grad_in=last.hidden_grad, inputs=between.astype(F32),
+            mlp_out=first.mlp_out, vec_last=small_rows[1], vec=small_rows[0],
+            slope=first.slope, act=first.act, normed=first.normed,
+            hidden=first.hidden, attn_out=first.attn_out,
+            attn_rows_in=last.attn_rows, mixed=kept_last[3], normed_in=first.next,
+            triple=triple, last_up=last.grad_up, last_down=last.grad_down,
+        ),
+        dict(
+            summed=((HALF_ROWS, local_hidden), F32),
+            input_grad=(row_shape, F32), sums_last=((8, width), F32),
+            hidden_grad=(row_shape, F32), sums_middle=((8, width), F32),
+            attn_rows=(whole, BF16), bias_grad=((8, local_hidden), F32),
+            grad_up=(blocks(local_hidden), BF16), grad_down=(blocks(local_hidden), BF16),
+            **attention_grads,
+        ),
+        dict(pre=(spread, BF16), mlp_rows=(whole, BF16), sent=(whole, BF16)),
+        ("last_up", "last_down"),
+        LayerGradients.scratch(HALF_ROWS // 3, local_hidden),
+    )
+    last_grad = middle.input_grad
+    triple, attend_first, part = attend_back_layer(0, middle.attn_rows, kept_first, packed_first)
+    close = chain_call(
+        9, close_body, 1, None,
+        dict(
+            part=part, hidden_grad_in=middle.hidden_grad, inputs=inputs,
+            vec=small_rows[0], attn_rows_in=middle.attn_rows, mixed=kept_first[3],
+            normed_in=normed_first, triple=triple,
+        ),
+        dict(input_grad=(row_shape, F32), sums_last=((8, width), F32), **attention_grads),
+        dict(),
+    )
+    input_grad = close.input_grad
+    sums = [
+        [close.sums_last, middle.sums_middle, middle.sums_last[2:], attend_first, middle.bias_grad],
+        [middle.sums_last, last.sums_middle, last.sums_end, attend_last, last.bias_grad],
+    ]
+    grads = [close.grad_qkv[which] for which in range(3)]
+    grads += [close.grad_out, middle.grad_up, middle.grad_down]
     first_grad = input_grad
 
     extras = [
@@ -1271,7 +1710,7 @@
         jnp.where(section == 0, last_grad, first_grad),
     ]
     small_sum, packed_sum, came_out, came_grad = final_call(
-        10, sums[0] + sums[1], grads[0] + grads[1], extras
+        10, sums[0] + sums[1], grads, middle.summed, extras
     )
     mine_out = jnp.where(section == 0, between, outputs)
     mine_grad = jnp.where(section == 0, first_grad, last_grad)

time: 469 us -> 424 us (0.904)
  matrix products: 39.5 us -> 0 us
    pallas_call x4 -> x8, Pallas kernels: 132 us -> 290 us  [the longest x4 146 us: chain_call(): pl.pallas_call(kernel, out_shape=[jax.ShapeDtypeStruct(shape, dtype) for...]
    pallas_call x9 -> x1, Pallas kernels: 122 us -> 12.9 us  [tensor_call(): pl.pallas_call(functools.partial(tensor_kernel, function, len(rows), len(...]
    dot_general x20 -> x0, matrix products: 39.5 us -> none  [the longest x12 17.7 us: rows_dot(): lax.dot_general(former, latter, (((0,), (0,)), ((), ())), preferred_eleme...]
    pallas_call x1, Pallas kernels: 75.2 us -> 42.2 us  [final_call(): pl.pallas_call(functools.partial(final_kernel, extra), out_shape=[jax.Sha...]
    pallas_call x1, Pallas kernels: 55.8 us -> 40.5 us  [first_call(): pl.pallas_call(first_kernel, out_shape=[jax.ShapeDtypeStruct((2, RING, RI...]
    slice x3 -> x2, local copies, waits for them, and re-layouts: 6.57 us -> 1.47 us  [the longest x1 0.85 us: attend_layer(): vec[2]]
where the time goes in v6:
time: 424 us; the launch traced here: 418 us
  Pallas kernels  386 us (91%)
  local copies, waits for them, and re-layouts  16.5 us (4%)
  other arithmetic  14.5 us (3%)
    pallas_call x4, Pallas kernels, chain_call(): pl.pallas_call(kernel, out_shape=[jax.ShapeDtypeStruct(shape, dtype) for...  146 us
    pallas_call x2, Pallas kernels, attend_back_call(): pl.pallas_call(attend_back_kernel, out_shape=[jax.ShapeDtypeStruct((3, gr...  72.9 us
    pallas_call x2, Pallas kernels, attend_call(): pl.pallas_call(attend_kernel, out_shape=[jax.ShapeDtypeStruct((group, wid...  71.1 us
    pallas_call x1, Pallas kernels, final_call(): pl.pallas_call(functools.partial(final_kernel, extra), out_shape=[jax.Sha...  42.2 us
    pallas_call x1, Pallas kernels, first_call(): pl.pallas_call(first_kernel, out_shape=[jax.ShapeDtypeStruct((2, RING, RI...  40.5 us
    pallas_call x1, Pallas kernels, tensor_call(): pl.pallas_call(functools.partial(tensor_kernel, function, len(rows), len(...  12.9 us

profile of v6, /device:TPU:1, one launch (start us, length us, event | category | flops | bytes accessed | tf_op | source)
XLA Modules:
  0.0 418.1 jit_solution(12160638687978566706)
XLA Ops:
  0.6 0.8 fusion.14
  1.4 1.3 fusion.9.small_in
  2.7 2.0 fusion.15
  4.7 40.5 %shard_map.152 = (bf16[2,4,4,112,1024]{4,3,2,1,0:T(8,128)(2,1)}, bf16[2,112,1024]{2,1,0:T(8,128)(2,1)}, bf16[2,4,4,16,128]{4,3,2,1,0:T(8,128)(2,1)}, f32[2,16,1024]{2,1,0:T(8,128)}) custom-call(bf16[3,64,256]{2,1,0:T(8,128)(2,1)} %bitcast.78, bf16[64,256]{1,0:T(8,128)(2,1)} %bitcast.80, bf16[64,1024]{1,0:T(8,128)(2,1)} %bitcast.75, ...), custom_call_target="tpu_custom_call" | custom-call | tf_op jit(solution)/shard_map/pallas_call | solution.py:494
  45.2 0.9 select_bitcast_fusion.3
  46.1 0.7 reshape.197.refs_2_
  46.8 0.9 fusion.18
  47.7 0.6 select_maximum_fusion.bias_ref
  48.3 0.6 select_maximum_fusion.1.bias_ref
  48.9 0.8 slice_bitcast_fusion.5
  49.7 1.5 slice_bitcast_fusion.3
  51.3 0.6 broadcast_in_dim.40.refs_5_
  51.9 0.6 broadcast_in_dim.41.refs_4_
  52.5 12.9 %shard_map.153 = (bf16[4,64,1024]{2,1,0:T(8,128)(2,1)}, s32[4,8,128]{2,1,0:T(8,128)}) custom-call(bf16[64,1024]{1,0:T(8,128)(2,1)} %get-tuple-element.145.refs_0_, f32[16,1024]{1,0:T(8,128)} %get-tuple-element.166.refs_1_.refs_3_.refs_6_, s32[8,128]{1,0:T(8,128)} %reshape.197.refs_2_), custom_call_target="tpu_custom_call" | custom-call | tf_op jit(solution)/shard_map/pallas_call | solution.py:169
  65.4 0.8 reshape.190
  66.2 0.1 broadcast_in_dim.18
  66.3 0.1 reshape.191
  66.4 0.6 broadcast_in_dim.17.seg_q_ref
  67.0 1.7 broadcast_in_dim.19.seg_k_ref
  68.6 35.9 %shard_map.154 = (bf16[256,256]{1,0:T(8,128)(2,1)}, bf16[4,4,256,256]{3,2,1,0:T(8,128)(2,1)}, bf16[4,4,256,256]{3,2,1,0:T(8,128)(2,1)}, bf16[256,256]{1,0:T(8,12...) custom-call(bf16[256,1024]{1,0:T(8,128)(2,1)} %bitcast.65, ...), custom_call_target="tpu_custom_call" | custom-call | tf_op jit(solution)/shard_map/pallas_call | solution.py:1082
  104.6 36.4 %shard_map.155 = (f32[64,1024]{1,0:T(8,128)}, f32[64,1024]{1,0:T(8,128)}, bf16[4,64,1024]{2,1,0:T(8,128)(2,1)}, bf16[4,64,1024]{2,1,0:T(8,128)(2,1)}, f32[4,64,1...) custom-call(bf16[2,4,4,112,1024]{4,3,2,1,0:T(8,128)(2,1)} %get-tuple, ...), custom_call_target="tpu_custom_call" | custom-call | tf_op jit(solution)/shard_map/pallas_call | solution.py:1427
  141.0 1.6 convert_element_type.32.refs_2_.refs_3_
  142.6 35.2 %shard_map.156 = (bf16[256,256]{1,0:T(8,128)(2,1)}, bf16[4,4,256,256]{3,2,1,0:T(8,128)(2,1)}, bf16[4,4,256,256]{3,2,1,0:T(8,128)(2,1)}, bf16[256,256]{1,0:T(8,12...) custom-call(bf16[256,1024]{1,0:T(8,128)(2,1)} %bitcast.63, ...), custom_call_target="tpu_custom_call" | custom-call | tf_op jit(solution)/shard_map/pallas_call | solution.py:1082
  177.8 44.6 %shard_map.157 = (bf16[64,1024]{1,0:T(8,128)(2,1)}, f32[8,1024]{1,0:T(8,128)}, f32[64,1024]{1,0:T(8,128)}, f32[8,1024]{1,0:T(8,128)}, bf16[4,64,1024]{2,1,0:T(8,...) custom-call(bf16[2,4,4,96,1024]{4,3,2,1,0:T(8,128)(2,1)} %get-tuple-element.76.pack, ...), custom_call_target="tpu_custom_call" | custom-call | tf_op jit(solution)/shard_map/pallas_call | solution.py:1427
  222.5 0.0 copy-start.1
  222.5 0.0 copy-start.4
  222.5 35.3 %shard_map.158 = (bf16[3,256,256]{2,1,0:T(8,128)(2,1)}, f32[8,256]{1,0:T(8,128)}, bf16[4,64,1024]{2,1,0:T(8,128)(2,1)}) custom-call(bf16[256,1024]{1,0:T(8,128)(2,1)} %bitcast.64, bf16[2,4,4,96,1024]{4,3,2,1,0:T(8,128)(2,1)} %get-tuple-element.76.packed_any.refs_0_, bf16[256,256]{1,0:T(8,128)(2,1)} %get-tuple-element.81.q_ref, ...), custom_call_target="tpu_custom_call" | custom-call | tf_op jit(solution)/shard_map/pallas_call | solution.py:1223
  257.8 0.0 copy-done.1
  257.8 0.0 copy-done.4
  257.8 0.7 select_bitcast_fusion.1
  258.5 51.7 %shard_map.159 = (f32[96,1024]{1,0:T(8,128)}, f32[64,1024]{1,0:T(8,128)}, f32[8,1024]{1,0:T(8,128)}, f32[64,1024]{1,0:T(8,128)}, f32[8,1024]{1,0:T(8,128)}, /*in...) custom-call(bf16[2,4,4,112,1024]{4,3,2,1,0:T(8,128)(2,1)} %get-tuple, ...), custom_call_target="tpu_custom_call" | custom-call | tf_op jit(solution)/shard_map/pallas_call | solution.py:1427
  310.2 37.7 %shard_map.160 = (bf16[3,256,256]{2,1,0:T(8,128)(2,1)}, f32[8,256]{1,0:T(8,128)}, bf16[4,64,1024]{2,1,0:T(8,128)(2,1)}) custom-call(bf16[256,1024]{1,0:T(8,128)(2,1)} %bitcast.66, bf16[2,4,4,112,1024]{4,3,2,1,0:T(8,128)(2,1)} %get-tuple-element.68.packed_any.refs_0_, bf16[256,256]{1,0:T(8,128)(2,1)} %get-tuple-element.99.q_ref, ...), custom_call_target="tpu_custom_call" | custom-call | tf_op jit(solution)/shard_map/pallas_call | solution.py:1223
  347.9 0.0 copy-start.3
  347.9 0.0 copy-start.2
  347.9 13.3 %shard_map.161 = (f32[64,1024]{1,0:T(8,128)}, f32[8,1024]{1,0:T(8,128)}, bf16[4,4,64,256]{3,2,1,0:T(8,128)(2,1)}, bf16[3,4,4,64,256]{4,3,2,1,0:T(8,128)(2,1)}) custom-call(bf16[4,64,1024]{2,1,0:T(8,128)(2,1)} %get-tuple-element.104.refs_0_, f32[64,1024]{1,0:T(8,128)} %get-tuple-element.105.refs_1_, f32[64,1024]{1,0:T(8,128)} %get-tuple-element.144.refs_2_, ...), custom_call_target="tpu_custom_call" | custom-call | tf_op jit(solution)/shard_map/pallas_call | solution.py:1427
  361.2 0.0 copy-done.3
  361.2 0.6 slice.119.refs_2_
  361.8 1.7 select_bitcast_fusion
  363.5 2.5 slice_bitcast_fusion
  366.1 42.2 %shard_map.162 = (f32[16,128]{1,0:T(8,128)}, f32[2,96,1024]{2,1,0:T(8,128)}, bf16[64,1024]{1,0:T(8,128)(2,1)}, f32[64,1024]{1,0:T(8,128)}) custom-call(f32[8,1024]{1,0:T(8,128)} %get-tuple-element.108.refs_0_, f32[8,1024]{1,0:T(8,128)} %get-tuple-element.109.refs_1_, f32[6,1024]{1,0:T(8,128)} %slice.119.refs_2_, f32[8,256]{1,0:T(8,128)} %get-tuple-element.111.refs_3_, ...), custom_call_target="tpu_custom_call" | custom-call | tf_op jit(solution)/shard_map/pallas_call | solution.py:897
  408.3 1.8 maximum_select_fusion.1
  410.1 1.9 maximum_select_fusion
  412.0 1.2 slice.130
  413.2 0.7 slice_bitcast_fusion.7
  413.9 0.6 copy.20
  414.5 1.6 fusion.17
  416.1 0.8 fusion.16
  416.9 0.7 maximum_bitcast_fusion
  (11 shorter events, 0.1 us)
Async XLA Ops:
  222.5 35.3 %copy-start.1 = (bf16[64,1024]{1,0:T(8,128)(2,1)S(1)}, bf16[64,1024]{1,0:T(8,128)(2,1)}, u32[]{:S(2)}) copy-start(bf16[64,1024]{1,0:T(8,128)(2,1)} %get-tuple-element.75) | copy-start | bytes 393220
  222.5 35.3 %copy-start.4 = (bf16[64,1024]{1,0:T(8,128)(2,1)S(1)}, bf16[64,1024]{1,0:T(8,128)(2,1)}, u32[]{:S(2)}) copy-start(bf16[64,1024]{1,0:T(8,128)(2,1)} %get-tuple-element.79) | copy-start | bytes 393220
  347.9 13.3 %copy-start.3 = (f32[8,1024]{1,0:T(8,128)S(1)}, f32[8,1024]{1,0:T(8,128)}, u32[]{:S(2)}) copy-start(f32[8,1024]{1,0:T(8,128)} %get-tuple-element.110.refs_5_) | copy-start | bytes 98308
  347.9 13.9 %copy-start.2 = (f32[64,1024]{1,0:T(8,128)S(1)}, f32[64,1024]{1,0:T(8,128)}, u32[]{:S(2)}) copy-start(f32[64,1024]{1,0:T(8,128)} %get-tuple-element.122) | copy-start | bytes 786436
  408.3 7.8 %copy-start = (f32[2,96,1024]{2,1,0:T(8,128)S(1)}, f32[2,96,1024]{2,1,0:T(8,128)}, u32[]{:S(2)}) copy-start(f32[2,96,1024]{2,1,0:T(8,128)} %get-tuple-element.126) | copy-start | bytes 2359300

commit v7 on v6

--- a/solution.py
+++ b/solution.py
@@ -69,121 +69,8 @@
     return barrier, RING - 1
 
 
-def tensor_kernel(function, n_rows, n_vecs, n_out, n_sums, reduce, gather, with_seg, *refs):
-    refs = list(refs)
-    take = lambda count: [refs.pop(0) for _ in range(count)]
-    part = take(1)[0] if reduce else None
-    rows_in = take(n_rows)
-    vecs = take(n_vecs)
-    seg_in = take(1)[0] if with_seg else None
-    rows_out = take(n_out)
-    sums_out = take(1)[0] if n_sums else None
-    full = take(1)[0] if gather else None
-    seg_out = take(1)[0] if with_seg else None
-    landing = take(1)[0] if reduce else None
-    send, recv, local = take(3)
-
-    me = lax.axis_index("tensor")
-    barrier, count = tensor_barrier(me)
-    pl.semaphore_wait(barrier, count)
-
-    chunk = rows_in[0].shape[0] // CHUNKS
-    started = []
-
-    def push(source, target, kind, index, k):
-        copy = pltpu.make_async_remote_copy(
-            src_ref=source,
-            dst_ref=target,
-            send_sem=send.at[kind, index, k - 1],
-            recv_sem=recv.at[kind, index, k - 1],
-            device_id={"tensor": step(me, k)},
-            device_id_type=MESH,
-        )
-        copy.start()
-        started.append(copy)
-        return copy
-
-    reduces = {}
-    if reduce:
-        for c in range(CHUNKS):
-            here = pl.ds(c * chunk, chunk)
-            for k in range(1, RING):
-                reduces[c, k] = push(
-                    part.at[step(me, k), here], landing.at[k - 1, here], 0, c, k
-                )
-    last = []
-    if with_seg:
-        own = pltpu.make_async_copy(seg_in, seg_out.at[me], local)
-        own.start()
-        last += [push(seg_in, seg_out.at[me], 2, 0, k) for k in range(1, RING)]
-    sums = [None] * n_sums
-    for c in range(CHUNKS):
-        here = pl.ds(c * chunk, chunk)
-        total = None
-        if reduce:
-            for k in range(1, RING):
-                reduces[c, k].wait_recv()
-            total = part[me, here].astype(F32)
-            for k in range(1, RING):
-                total = total + landing[k - 1, here].astype(F32)
-        spread, outs, parts = function(
-            total, [ref[here].astype(F32) for ref in rows_in], vecs
-        )
-        if gather:
-            full[me, here] = spread.astype(BF16)
-            last += [push(full.at[me, here], full.at[me, here], 1, c, k) for k in range(1, RING)]
-        for ref, value in zip(rows_out, outs):
-            ref[here] = value.astype(ref.dtype)
-        sums = [new if old is None else old + new for old, new in zip(sums, parts)]
-    if n_sums:
-        sums_out[...] = jnp.concatenate(
-            sums + [jnp.zeros((8 - n_sums, sums[0].shape[1]), F32)], axis=0
-        )
-    for copy in last:
-        copy.wait_recv()
-    if with_seg:
-        own.wait()
-    for copy in started:
-        copy.wait_send()
-
-
-def tensor_call(cid, function, part, rows, vecs, outs, n_sums, gather, seg=None):
-    height, width = rows[0].shape
-    reduce = part is not None
-    with_seg = seg is not None
-    args = ([part] if reduce else []) + list(rows) + list(vecs) + ([seg] if with_seg else [])
-    shapes = [jax.ShapeDtypeStruct((height, width), dtype) for dtype in outs]
-    if n_sums:
-        shapes.append(jax.ShapeDtypeStruct((8, width), F32))
-    if gather:
-        shapes.append(jax.ShapeDtypeStruct((RING, height, width), BF16))
-    if with_seg:
-        shapes.append(jax.ShapeDtypeStruct((RING,) + seg.shape, seg.dtype))
-    in_specs, out_specs = [vmem_spec()] * len(args), [vmem_spec()] * len(shapes)
-    scratch = [pltpu.VMEM((RING - 1, height, width), BF16)] if reduce else []
-    scratch += [
-        pltpu.SemaphoreType.DMA((3, CHUNKS, RING - 1)),
-        pltpu.SemaphoreType.DMA((3, CHUNKS, RING - 1)),
-        pltpu.SemaphoreType.DMA,
-    ]
-    return pl.pallas_call(
-        functools.partial(
-            tensor_kernel, function, len(rows), len(vecs), len(outs), n_sums, reduce, gather, with_seg,
-        ),
-        out_shape=shapes,
-        in_specs=in_specs,
-        out_specs=out_specs,
-        scratch_shapes=scratch,
-        compiler_params=comm_params(cid),
-    )(*args)
-
-
 def row(ref, index):
     return ref[pl.ds(index, 1), :]
-
-
-def first_rows(total, rows, vecs):
-    return layer_norm(rows[0], row(vecs[0], 0), row(vecs[0], 1)), [], []
 
 
 def middle_rows(total, rows, vecs):
@@ -418,31 +305,30 @@
 
 
 def first_kernel(
-    qkv_in, out_in, up_in, down_in, small_in, packed_out, stage, small_all, rows_out,
-    send, recv, local, swap_send, swap_recv, swap_local, last_local,
+    tokens_in, cotangent_in, qkv_in, out_in, up_in, down_in, small_in,
+    packed_out, stage, rows_out, full, tokens_out, cotangent_out, seg_wide, seg_column,
+    small_all, seg_parts, seg_rows,
+    send, recv, local, small_send, small_recv, small_local,
+    swap_send, swap_recv, swap_local, tensor_send, tensor_recv,
 ):
     rank = lax.axis_index("dp")
     y, z = rank // RING, lax.rem(rank, RING)
     section = lax.axis_index("section")
+    me = lax.axis_index("tensor")
     barrier, count = dp_barrier(y, z, section)
+    count += tensor_barrier(me)[1]
     depth, width = out_in.shape
     half = depth // 2
     mine, others = half_of(section, half), half_of(1 - section, half)
     sources = [qkv_in.at[which] for which in range(3)] + [out_in, up_in, down_in]
     places = half_places(half, width, stage.shape[2])
-    tail = pl.ds(HALF_ROWS, SMALL)
-    stage[0, tail] = jnp.zeros((SMALL, stage.shape[2]), BF16)
-    stage[1, tail] = jnp.zeros((SMALL, stage.shape[2]), BF16)
-    kept = [
-        pltpu.make_async_copy(
-            small_in, stage.at[0, tail, pl.ds(0, small_in.shape[1])], swap_local.at[len(places)]
-        )
-    ]
-    kept[0].start()
+    tokens_out[...] = jnp.where(section == 0, tokens_in[0], tokens_in[1])
+    cotangent_out[...] = jnp.where(section == 0, cotangent_in[0], cotangent_in[1])
+    seg_parts[me] = jnp.zeros(seg_parts.shape[1:], jnp.int32)
     pl.semaphore_wait(barrier, count)
     started = []
     push = pusher(send, recv, started)
-    swaps = []
+    swaps, kept = [], []
     for i, (source, (row, column, columns)) in enumerate(zip(sources, places)):
         target = stage.at[section, pl.ds(row, half), pl.ds(column, columns)]
         copy = pltpu.make_async_remote_copy(
@@ -458,25 +344,63 @@
         copy = pltpu.make_async_copy(source.at[mine], target, swap_local.at[i])
         copy.start()
         kept.append(copy)
+    small_push = pusher(small_send, small_recv, started)
+    small_ring = Gather(((0, (), True),), [small_all.at[section]], y, z, (), small_push)
+    small_stages = spread_stages(small_ring, [small_in], small_local, section, small_push)
+    small_stages[0]()
     for copy in kept:
         copy.wait()
     for copy in swaps:
         copy.wait_recv()
-    low, high = pl.ds(0, HALF_ROWS // 2), pl.ds(HALF_ROWS // 2, HALF_ROWS // 2 + SMALL)
-    views = [packed_out.at[section, :, :, low], packed_out.at[section, :, :, high]]
+    halves = [pl.ds(0, HALF_ROWS // 2), pl.ds(HALF_ROWS // 2, HALF_ROWS // 2)]
+    views = [packed_out.at[section, :, :, rows] for rows in halves]
     ring = Gather(((0, (), True), (1, (), False)), views, y, z, (), push)
-    for each in spread_stages(ring, [stage.at[0, low], stage.at[0, high]], local, section, push):
-        each()
-    last = pltpu.make_async_copy(
-        packed_out.at[:, :, :, tail, pl.ds(0, small_in.shape[1])], small_all, last_local
-    )
-    last.start()
-    last.wait()
+    stages = spread_stages(ring, [stage.at[0, rows] for rows in halves], local, section, push)
+    stages[0]()
+    small_stages[1]()
+    small_stages[2]()
+    stages[1]()
+    small_stages[3]()
+    small_stages[4]()
     for layer in range(2):
         for number in range(RING * RING):
             part = small_all[layer, number // RING, number % RING]
             rows_out[layer, :, number * depth : (number + 1) * depth] = part[:, :depth].astype(F32)
-    for copy in started + swaps:
+    for number in range(RING * RING):
+        part = small_all[section, number // RING, number % RING]
+        seg_parts[me, number : number + 1, 0:depth] = (
+            part[14:15, :depth].astype(F32).astype(jnp.int32)
+        )
+    full[me] = layer_norm(
+        tokens_out[...].astype(F32), rows_out[0, 0:1, :], rows_out[0, 1:2, :]
+    ).astype(BF16)
+    tensor_copies = []
+    for i, ref in enumerate((seg_parts, full)):
+        for k in range(1, RING):
+            copy = pltpu.make_async_remote_copy(
+                src_ref=ref.at[me],
+                dst_ref=ref.at[me],
+                send_sem=tensor_send.at[i, k],
+                recv_sem=tensor_recv.at[i, k],
+                device_id={"tensor": step(me, k)},
+                device_id_type=MESH,
+            )
+            copy.start()
+            tensor_copies.append(copy)
+    stages[2]()
+    stages[3]()
+    for copy in tensor_copies:
+        copy.wait_recv()
+    for number in range(RING):
+        seg_rows[:, number * depth : (number + 1) * depth] = seg_parts[number][:, :depth]
+    seg_wide[...] = jnp.broadcast_to(seg_rows[pl.ds(rank, 1), :], seg_wide.shape)
+    turned = seg_rows[...].astype(F32).T
+    for number in range(RING * RING):
+        seg_column[number // RING, number % RING] = jnp.broadcast_to(
+            turned[:, number : number + 1], seg_column.shape[2:]
+        ).astype(jnp.int32)
+    stages[4]()
+    for copy in started + swaps + tensor_copies:
         copy.wait_send()
 
 
@@ -488,28 +412,41 @@
     ]
 
 
-def first_call(cid, w_qkv, w_out, w_up, w_down, small):
+def first_call(cid, tokens, cotangent, w_qkv, w_out, w_up, w_down, small):
     depth = w_out.shape[0]
     hidden = w_up.shape[1]
+    rows, width = tokens.shape[1:]
+    group = RING * rows
     return pl.pallas_call(
         first_kernel,
         out_shape=[
-            jax.ShapeDtypeStruct((2, RING, RING, HALF_ROWS + SMALL, hidden), BF16),
-            jax.ShapeDtypeStruct((2, HALF_ROWS + SMALL, hidden), BF16),
-            jax.ShapeDtypeStruct((2, RING, RING) + small.shape, BF16),
-            jax.ShapeDtypeStruct((2, SMALL, RING * RING * depth), F32),
+            jax.ShapeDtypeStruct((2, RING, RING, HALF_ROWS, hidden), BF16),
+            jax.ShapeDtypeStruct((2, HALF_ROWS, hidden), BF16),
+            jax.ShapeDtypeStruct((2, SMALL, width), F32),
+            jax.ShapeDtypeStruct((RING, rows, width), BF16),
+            jax.ShapeDtypeStruct((rows, width), BF16),
+            jax.ShapeDtypeStruct((rows, width), BF16),
+            jax.ShapeDtypeStruct((8, group), jnp.int32),
+            jax.ShapeDtypeStruct((RING, RING, group, 128), jnp.int32),
         ],
-        in_specs=[vmem_spec()] * 5,
-        out_specs=[any_spec(), vmem_spec(), vmem_spec(), vmem_spec()],
-        scratch_shapes=gather_scratch()
+        in_specs=[vmem_spec()] * 7,
+        out_specs=[any_spec()] + [vmem_spec()] * 7,
+        scratch_shapes=[
+            pltpu.VMEM((2, RING, RING) + small.shape, BF16),
+            pltpu.VMEM((RING, RING * RING, 128), jnp.int32),
+            pltpu.VMEM((RING * RING, group), jnp.int32),
+        ]
+        + gather_scratch()
+        + gather_scratch()
         + [
             pltpu.SemaphoreType.DMA((6,)),
             pltpu.SemaphoreType.DMA((6,)),
-            pltpu.SemaphoreType.DMA((7,)),
-            pltpu.SemaphoreType.DMA,
+            pltpu.SemaphoreType.DMA((6,)),
+            pltpu.SemaphoreType.DMA((2, RING)),
+            pltpu.SemaphoreType.DMA((2, RING)),
         ],
         compiler_params=comm_params(cid),
-    )(w_qkv, w_out, w_up, w_down, small)
+    )(tokens, cotangent, w_qkv, w_out, w_up, w_down, small)
 
 
 class Scatter:
@@ -767,15 +704,16 @@
     lax.fori_loop(0, RING * RING, add, 0)
 
 
-def final_kernel(n_extra, *refs):
+def final_kernel(*refs):
     refs = list(refs)
     take = lambda count: [refs.pop(0) for _ in range(count)]
     sums = [take(5), take(5)]
     grads, summed_last = take(6), take(1)[0]
-    extras = take(n_extra)
+    extras = take(4)
     small_out, packed_out = take(2)
-    extra_outs = take(n_extra)
+    extra_outs = take(2)
     small_in, small_rows, vector_own, vector_parts, summed = take(5)
+    extra_sends = take(2)
     small_buffers = take(2 + SCATTER_BUFFERS)
     layer_scratch = take(LAYER_SCRATCH)
     vector_send, vector_recv, extra_send, extra_recv, result_send, result_recv, result_local, hand_local = take(8)
@@ -794,6 +732,10 @@
     handed = pltpu.make_async_copy(summed_last, summed.at[1], hand_local)
     handed.start()
     depth = grads[0].shape[2]
+    for i in range(2):
+        last_value, first_value = extras[2 * i][...], extras[2 * i + 1][...]
+        extra_outs[i][section] = jnp.where(section == 0, first_value, last_value)
+        extra_sends[i][...] = jnp.where(section == 0, last_value, first_value)
 
     small_rows[...] = jnp.zeros_like(small_rows)
     model = small_rows.shape[1]
@@ -823,10 +765,10 @@
     first_layer.swap()
     small_swap = push(2, 6, 0, small_in.at[:, :, half_of(1 - section, SMALL)], small_buffers[1], other)
     extra_copies = []
-    for i in range(n_extra):
+    for i in range(2):
         copy = pltpu.make_async_remote_copy(
-            src_ref=extras[i],
-            dst_ref=extra_outs[i],
+            src_ref=extra_sends[i],
+            dst_ref=extra_outs[i].at[section],
             send_sem=extra_send.at[i],
             recv_sem=extra_recv.at[i],
             device_id=other,
@@ -895,14 +837,14 @@
     args = list(sums) + list(grads) + [summed_last] + list(extras)
     block = (HALF_ROWS, hidden)
     return pl.pallas_call(
-        functools.partial(final_kernel, extra),
+        final_kernel,
         out_shape=[
             jax.ShapeDtypeStruct((SMALL, 128), F32),
             jax.ShapeDtypeStruct((2, HALF_ROWS, hidden), F32),
         ]
-        + [jax.ShapeDtypeStruct(value.shape, value.dtype) for value in extras],
+        + [jax.ShapeDtypeStruct((2,) + value.shape, value.dtype) for value in extras[::2]],
         in_specs=[vmem_spec()] * len(sums) + [any_spec()] * (len(grads) + 1) + [vmem_spec()] * extra,
-        out_specs=[vmem_spec()] * (2 + extra),
+        out_specs=[vmem_spec()] * 4,
         scratch_shapes=[
             pltpu.VMEM((RING, RING, 2 * SMALL, 128), F32),
             pltpu.VMEM((2 * SMALL, width), F32),
@@ -910,6 +852,7 @@
             pltpu.VMEM((RING, SMALL, 128), F32),
             pltpu.VMEM((2,) + block, F32),
         ]
+        + [pltpu.VMEM(value.shape, value.dtype) for value in extras[::2]]
         + scatter_buffers((SMALL, 128), F32)
         + LayerGradients.scratch(HALF_ROWS // 3, hidden)
         + [
@@ -963,7 +906,7 @@
 
 
 def attend_kernel(
-    normed_ref, packed_any, bias_ref, seg_q_ref, seg_k_ref,
+    layer, normed_ref, packed_any, vec_ref, seg_q_ref, seg_k_ref,
     q_ref, k_ref, v_ref, mixed_ref, wide_ref, lse_ref, part_ref,
     pack_ref, stack, acc, top_ref, total_ref, send, recv, local,
 ):
@@ -976,6 +919,9 @@
     y, z = rank // RING, lax.rem(rank, RING)
     barrier, count = dp_barrier(y, z, None)
     normed = normed_ref[...]
+    start = pl.multiple_of(lax.axis_index("tensor") * width, width)
+    query_bias = vec_ref[layer, 2:3, pl.ds(start, width)]
+    value_bias = vec_ref[layer, 3:4, pl.ds(start, width)]
     for load in loads:
         load.wait()
     k_ref[y, z] = jnp.dot(normed, matrix(1), preferred_element_type=F32).astype(BF16)
@@ -984,11 +930,11 @@
     ring = Gather(((0, (), True), (1, (), False)), (k_ref, v_ref), y, z, (), pusher(send, recv, started))
     ring.begin(0, k_ref.at[y, z])
     v_ref[y, z] = (
-        jnp.dot(normed, matrix(2), preferred_element_type=F32) + bias_ref[1:2, :]
+        jnp.dot(normed, matrix(2), preferred_element_type=F32) + value_bias
     ).astype(BF16)
     ring.begin(1, v_ref.at[y, z])
     q_ref[...] = (
-        jnp.dot(normed, matrix(0), preferred_element_type=F32) + bias_ref[0:1, :]
+        jnp.dot(normed, matrix(0), preferred_element_type=F32) + query_bias
     ).astype(BF16)
     stack[...] = head_stack(q_ref[...], HEAD_DIM ** (-0.5))
     acc[...] = jnp.zeros_like(acc)
@@ -1074,13 +1020,13 @@
         copy.wait_send()
 
 
-def attend_call(cid, normed, packed, biases, seg_wide, seg_column):
+def attend_call(cid, layer, normed, packed, vectors, seg_wide, seg_column):
     group, model = normed.shape
-    width = biases.shape[1]
+    width = model // RING
     heads_here = width // HEAD_DIM
     square = (RING, RING, group, width)
     return pl.pallas_call(
-        attend_kernel,
+        functools.partial(attend_kernel, layer),
         out_shape=[
             jax.ShapeDtypeStruct((group, width), BF16),
             jax.ShapeDtypeStruct(square, BF16),
@@ -1103,7 +1049,7 @@
             pltpu.SemaphoreType.DMA((2,)),
         ],
         compiler_params=comm_params(cid),
-    )(normed, packed, biases, seg_wide, seg_column)
+    )(normed, packed, vectors, seg_wide, seg_column)
 
 
 def attend_back_kernel(
@@ -1330,10 +1276,10 @@
     return pack_ref[...].reshape(-1, pack_ref.shape[-1])
 
 
-def mlp_forward(me, full, up_ref, down_ref, bias_ref, act_ref, slope_ref, part_ref, exchange):
+def mlp_forward(me, full, up_ref, down_ref, bias, act_ref, slope_ref, part_ref, exchange):
     for tile in TILES:
         value = jnp.dot(rows_of(full, me, tile), wide_of(up_ref), preferred_element_type=F32)
-        value = value + bias_ref[0:1, :]
+        value = value + bias
         phi = 0.5 * (1.0 + lax.erf(value * (0.5**0.5)))
         act = (value * phi).astype(BF16)
         density = jnp.exp(-0.5 * value * value) * 0.3989422804014327
@@ -1449,18 +1395,18 @@
     )
     rings[0].reduce(env.part)
     rings[0].run(
-        env.part, middle_rows, [env.inputs], [env.vec],
+        env.part, middle_rows, [env.inputs], [env.vectors.at[0]],
         [env.attn_out, env.hidden], None, env.normed, [begin, near],
     )
     middle()
     for copy in loads:
         copy.wait()
     mlp_forward(
-        me, env.normed, env.up, env.down, env.bias, env.act, env.slope, env.sent, rings[1],
+        me, env.normed, env.up, env.down, env.vectors[0, pl.ds(9 + me, 1), :], env.act, env.slope, env.sent, rings[1],
     )
     end()
     rings[1].run(
-        env.sent, end_rows_first, [env.hidden], [env.vec, env.after],
+        env.sent, end_rows_first, [env.hidden], [env.vectors.at[0], env.vectors.at[1]],
         [env.mlp_out, env.outputs], None, env.next, [lambda: None, final],
     )
 
@@ -1468,17 +1414,17 @@
 def last_mlp_body(me, env, rings, loads):
     rings[0].reduce(env.part)
     rings[0].run(
-        env.part, middle_rows, [env.inputs], [env.vec],
+        env.part, middle_rows, [env.inputs], [env.vectors.at[1]],
         [env.attn_out, env.hidden], None, env.normed,
     )
     for copy in loads:
         copy.wait()
     mlp_forward(
-        me, env.normed, env.up, env.down, env.bias, env.act, env.slope,
+        me, env.normed, env.up, env.down, env.vectors[1, pl.ds(9 + me, 1), :], env.act, env.slope,
         env.sent, rings[1],
     )
     rings[1].run(
-        env.sent, end_rows_last, [env.hidden, env.upstream], [env.vec],
+        env.sent, end_rows_last, [env.hidden, env.upstream], [env.vectors.at[1]],
         [env.outputs], env.sums_end, env.mlp_rows,
     )
     mlp_backward(
@@ -1487,7 +1433,7 @@
     )
     rings[2].run(
         env.sent_two, back_middle_rows, [env.upstream, env.hidden, env.attn_out],
-        [env.vec], [env.hidden_grad], env.sums_middle, env.attn_rows,
+        [env.vectors.at[1]], [env.hidden_grad], env.sums_middle, env.attn_rows,
         [
             product(env.mlp_rows, env.act, env.grad_down),
             product(env.normed, env.pre, env.grad_up),
@@ -1519,7 +1465,7 @@
     rings[0].reduce(env.part)
     rings[0].run(
         env.part, back_end_rows_last, [env.hidden_grad_in, env.inputs, env.mlp_out],
-        [env.vec_last, env.vec], [env.input_grad], env.sums_last, env.mlp_rows,
+        [env.vectors.at[1], env.vectors.at[0]], [env.input_grad], env.sums_last, env.mlp_rows,
         [swap, layer.begin],
     )
     for copy in loads:
@@ -1541,7 +1487,7 @@
 
     rings[1].run(
         env.sent, back_middle_rows_low, [env.input_grad, env.hidden, env.attn_out],
-        [env.vec], [env.hidden_grad], env.sums_middle, env.attn_rows, [products, rest],
+        [env.vectors.at[0]], [env.hidden_grad], env.sums_middle, env.attn_rows, [products, rest],
     )
 
 
@@ -1553,7 +1499,7 @@
     rings[0].reduce(env.part)
     rings[0].run(
         env.part, back_end_rows_first, [env.hidden_grad_in, env.inputs],
-        [env.vec], [env.input_grad], env.sums_last, None, attention_products(env),
+        [env.vectors.at[0]], [env.input_grad], env.sums_last, None, attention_products(env),
     )
 
 
@@ -1575,39 +1521,17 @@
         jnp.concatenate([vectors[0], out_bias, wide_segments], axis=0),
         ((0, 1), (0, 128 - depth)),
     )
-    packed_first, stage, small_all, small_rows = first_call(0, w_qkv[0], w_out[0], w_up[0], w_down[0], small)
-    my_tokens = own(tokens)
-    my_cotangent = own(cotangent)
-    seg_mine = own(small_all)[:, :, 14, :rows].astype(jnp.int32).reshape(8, 128)
-    normed, seg_group = tensor_call(
-        1, first_rows, None, [my_tokens], [small_rows[0]], [], 0, True, seg_mine
-    )
-    seg_all = seg_group.reshape(RING, RING * RING, rows).transpose(1, 0, 2).reshape(-1, group)
-    seg_rows = lax.dynamic_index_in_dim(seg_all, lax.axis_index("dp"), 0, keepdims=False)
-    seg_wide = jnp.broadcast_to(seg_rows[None], (8, group))
-    seg_column = jnp.broadcast_to(seg_all.reshape(*square, group)[..., None], square + (group, 128))
+    packed_first, stage, small_rows, normed, inputs, my_cotangent, seg_wide, seg_column = first_call(
+        0, tokens, cotangent, w_qkv[0], w_out[0], w_up[0], w_down[0], small
+    )
+
     whole = (RING, rows, width)
     blocks = lambda columns: square + (depth, columns)
     spread = (RING, rows, local_hidden)
     row_shape = (rows, width)
-    inputs = my_tokens.astype(F32)
-    up_biases = [
-        jnp.broadcast_to(
-            lax.dynamic_slice_in_dim(
-                small_rows[layer, 9:13].reshape(-1), tensor_rank * local_hidden, local_hidden
-            )[None],
-            (8, local_hidden),
-        )
-        for layer in range(2)
-    ]
-
     def attend_layer(layer, normed, packed):
-        vec = small_rows[layer]
-        query_bias = lax.dynamic_slice_in_dim(vec[2], tensor_rank * local_width, local_width)
-        value_bias = lax.dynamic_slice_in_dim(vec[3], tensor_rank * local_width, local_width)
-        biases = jnp.pad(jnp.stack([query_bias, value_bias]), ((0, 6), (0, 0)))
         return attend_call(
-            2 + 12 * layer, normed.reshape(group, width), packed, biases, seg_wide, seg_column
+            2 + 12 * layer, layer, normed.reshape(group, width), packed, small_rows, seg_wide, seg_column
         )
 
     normed_first = normed
@@ -1615,8 +1539,7 @@
     first = chain_call(
         3, first_mlp_body, 2, packed_first,
         dict(
-            part=part, inputs=inputs, vec=small_rows[0], after=small_rows[1],
-            bias=up_biases[0], stage=stage,
+            part=part, inputs=inputs, vectors=small_rows, stage=stage,
         ),
         dict(
             attn_out=(row_shape, F32), hidden=(row_shape, F32), normed=(whole, BF16),
@@ -1634,8 +1557,7 @@
     last = chain_call(
         5, last_mlp_body, 3, packed_last,
         dict(
-            part=part, inputs=between.astype(F32), vec=small_rows[1],
-            bias=up_biases[1], upstream=my_cotangent.astype(F32),
+            part=part, inputs=between, vectors=small_rows, upstream=my_cotangent,
         ),
         dict(
             outputs=(row_shape, BF16), sums_end=((8, width), F32),
@@ -1665,8 +1587,8 @@
     middle = chain_call(
         8, between_body, 2, packed_first,
         dict(
-            part=part, hidden_grad_in=last.hidden_grad, inputs=between.astype(F32),
-            mlp_out=first.mlp_out, vec_last=small_rows[1], vec=small_rows[0],
+            part=part, hidden_grad_in=last.hidden_grad, inputs=between,
+            mlp_out=first.mlp_out, vectors=small_rows,
             slope=first.slope, act=first.act, normed=first.normed,
             hidden=first.hidden, attn_out=first.attn_out,
             attn_rows_in=last.attn_rows, mixed=kept_last[3], normed_in=first.next,
@@ -1690,7 +1612,7 @@
         9, close_body, 1, None,
         dict(
             part=part, hidden_grad_in=middle.hidden_grad, inputs=inputs,
-            vec=small_rows[0], attn_rows_in=middle.attn_rows, mixed=kept_first[3],
+            vectors=small_rows, attn_rows_in=middle.attn_rows, mixed=kept_first[3],
             normed_in=normed_first, triple=triple,
         ),
         dict(input_grad=(row_shape, F32), sums_last=((8, width), F32), **attention_grads),
@@ -1705,25 +1627,16 @@
     grads += [close.grad_out, middle.grad_up, middle.grad_down]
     first_grad = input_grad
 
-    extras = [
-        jnp.where(section == 0, outputs, between),
-        jnp.where(section == 0, last_grad, first_grad),
-    ]
-    small_sum, packed_sum, came_out, came_grad = final_call(
-        10, sums[0] + sums[1], grads, middle.summed, extras
-    )
-    mine_out = jnp.where(section == 0, between, outputs)
-    mine_grad = jnp.where(section == 0, first_grad, last_grad)
-    pair = lambda mine, came: jnp.where(
-        section == 0, jnp.stack([mine, came]), jnp.stack([came, mine])
-    )[None]
+    small_sum, packed_sum, out_pair, grad_pair = final_call(
+        10, sums[0] + sums[1], grads, middle.summed, [outputs, between, last_grad, first_grad]
+    )
     half = depth // 2
     columns = lambda which: packed_sum[
         :, :half, which * local_width : (which + 1) * local_width
     ].reshape(depth, local_width)
     return (
-        pair(mine_out, came_out),
-        pair(mine_grad, came_grad),
+        out_pair[None],
+        grad_pair[None],
         jnp.stack([columns(0), columns(1), columns(2)])[None],
         columns(3)[None],
         packed_sum[:, half : 2 * half].reshape(1, depth, local_hidden),

time: 424 us -> 398 us (0.939)
  other arithmetic: 14.5 us -> 2.76 us
  Pallas kernels: 386 us -> 378 us
  local copies, waits for them, and re-layouts: 16.5 us -> 10.7 us
    pallas_call x4 -> x3, Pallas kernels: 126 us -> 117 us  [the longest x2 74 us: attend_call(): pl.pallas_call(functools.partial(attend_kernel, layer), out_shape=[jax.Sh...]
    select_n x3 -> x0, other arithmetic: 4.54 us -> none  [the longest x2 3.66 us: shards(): jnp.where(section == 0, jnp.stack([mine, came]), jnp.stack([came, mine]))]
where the time goes in v7:
time: 398 us; the launch traced here: 392 us
  Pallas kernels  378 us (95%)
  local copies, waits for them, and re-layouts  10.7 us (3%)
    pallas_call x4, Pallas kernels, chain_call(): pl.pallas_call(kernel, out_shape=[jax.ShapeDtypeStruct(shape, dtype) for...  146 us
    pallas_call x2, Pallas kernels, attend_call(): pl.pallas_call(functools.partial(attend_kernel, layer), out_shape=[jax.Sh...  74 us
    pallas_call x2, Pallas kernels, attend_back_call(): pl.pallas_call(attend_back_kernel, out_shape=[jax.ShapeDtypeStruct((3, gr...  73.1 us
    pallas_call x1, Pallas kernels, final_call(): pl.pallas_call(final_kernel, out_shape=[jax.ShapeDtypeStruct((SMALL, 128)...  43.2 us
    pallas_call x1, Pallas kernels, first_call(): pl.pallas_call(first_kernel, out_shape=[jax.ShapeDtypeStruct((2, RING, RI...  41.5 us

profile of v7, /device:TPU:1, one launch (start us, length us, event | category | flops | bytes accessed | tf_op | source)
XLA Modules:
  0.0 392.3 jit_solution(6704822145559440126)
XLA Ops:
  0.6 0.8 fusion.9
  1.4 1.3 fusion.8.small_in
  2.7 41.5 %shard_map.152 = (bf16[2,4,4,96,1024]{4,3,2,1,0:T(8,128)(2,1)}, bf16[2,96,1024]{2,1,0:T(8,128)(2,1)}, f32[2,16,1024]{2,1,0:T(8,128)}, bf16[4,64,1024]{2,1,0:T(8,...) custom-call(bf16[2,64,1024]{2,1,0:T(8,128)(2,1)} %tokens_in.1, ...), custom_call_target="tpu_custom_call" | custom-call | tf_op jit(solution)/shard_map/pallas_call | solution.py:420
  44.2 38.8 %shard_map.153 = (bf16[256,256]{1,0:T(8,128)(2,1)}, bf16[4,4,256,256]{3,2,1,0:T(8,128)(2,1)}, bf16[4,4,256,256]{3,2,1,0:T(8,128)(2,1)}, bf16[256,256]{1,0:T(8,12...) custom-call(bf16[256,1024]{1,0:T(8,128)(2,1)} %bitcast.27, ...), custom_call_target="tpu_custom_call" | custom-call | tf_op jit(solution)/shard_map/pallas_call | solution.py:1028
  82.9 35.7 %shard_map.154 = (f32[64,1024]{1,0:T(8,128)}, f32[64,1024]{1,0:T(8,128)}, bf16[4,64,1024]{2,1,0:T(8,128)(2,1)}, bf16[4,64,1024]{2,1,0:T(8,128)(2,1)}, f32[4,64,1...) custom-call(bf16[2,4,4,96,1024]{4,3,2,1,0:T(8,128)(2,1)} %get-tuple-, ...), custom_call_target="tpu_custom_call" | custom-call | tf_op jit(solution)/shard_map/pallas_call | solution.py:1373
  118.7 35.2 %shard_map.155 = (bf16[256,256]{1,0:T(8,128)(2,1)}, bf16[4,4,256,256]{3,2,1,0:T(8,128)(2,1)}, bf16[4,4,256,256]{3,2,1,0:T(8,128)(2,1)}, bf16[256,256]{1,0:T(8,12...) custom-call(bf16[256,1024]{1,0:T(8,128)(2,1)} %bitcast.28, ...), custom_call_target="tpu_custom_call" | custom-call | tf_op jit(solution)/shard_map/pallas_call | solution.py:1028
  153.9 45.2 %shard_map.156 = (bf16[64,1024]{1,0:T(8,128)(2,1)}, f32[8,1024]{1,0:T(8,128)}, f32[64,1024]{1,0:T(8,128)}, f32[8,1024]{1,0:T(8,128)}, bf16[4,64,1024]{2,1,0:T(8,...) custom-call(bf16[2,4,4,96,1024]{4,3,2,1,0:T(8,128)(2,1)} %get-tuple-element.78.pack, ...), custom_call_target="tpu_custom_call" | custom-call | tf_op jit(solution)/shard_map/pallas_call | solution.py:1373
  199.2 36.3 %shard_map.157 = (bf16[3,256,256]{2,1,0:T(8,128)(2,1)}, f32[8,256]{1,0:T(8,128)}, bf16[4,64,1024]{2,1,0:T(8,128)(2,1)}) custom-call(bf16[256,1024]{1,0:T(8,128)(2,1)} %bitcast.30, bf16[2,4,4,96,1024]{4,3,2,1,0:T(8,128)(2,1)} %get-tuple-element.78.packed_any.refs_0_, bf16[256,256]{1,0:T(8,128)(2,1)} %get-tuple-element.84.q_ref, ...), custom_call_target="tpu_custom_call" | custom-call | tf_op jit(solution)/shard_map/pallas_call | solution.py:1169
  235.5 51.3 %shard_map.158 = (f32[96,1024]{1,0:T(8,128)}, f32[64,1024]{1,0:T(8,128)}, f32[8,1024]{1,0:T(8,128)}, f32[64,1024]{1,0:T(8,128)}, f32[8,1024]{1,0:T(8,128)}, /*in...) custom-call(bf16[2,4,4,96,1024]{4,3,2,1,0:T(8,128)(2,1)} %get-tuple-, ...), custom_call_target="tpu_custom_call" | custom-call | tf_op jit(solution)/shard_map/pallas_call | solution.py:1373
  286.8 36.8 %shard_map.159 = (bf16[3,256,256]{2,1,0:T(8,128)(2,1)}, f32[8,256]{1,0:T(8,128)}, bf16[4,64,1024]{2,1,0:T(8,128)(2,1)}) custom-call(bf16[256,1024]{1,0:T(8,128)(2,1)} %bitcast.29, bf16[2,4,4,96,1024]{4,3,2,1,0:T(8,128)(2,1)} %get-tuple-element.70.packed_any.refs_0_, bf16[256,256]{1,0:T(8,128)(2,1)} %get-tuple-element.102.q_ref, ...), custom_call_target="tpu_custom_call" | custom-call | tf_op jit(solution)/shard_map/pallas_call | solution.py:1169
  323.6 0.0 copy-start.2
  323.6 13.5 %shard_map.160 = (f32[64,1024]{1,0:T(8,128)}, f32[8,1024]{1,0:T(8,128)}, bf16[4,4,64,256]{3,2,1,0:T(8,128)(2,1)}, bf16[3,4,4,64,256]{4,3,2,1,0:T(8,128)(2,1)}) custom-call(bf16[4,64,1024]{2,1,0:T(8,128)(2,1)} %get-tuple-element.107.refs_0_, f32[64,1024]{1,0:T(8,128)} %get-tuple-element.108.refs_1_, bf16[64,1024]{1,0:T(8,128)(2,1)} %get-tuple-element.76.refs_2_, ...), custom_call_target="tpu_custom_call" | custom-call | tf_op jit(solution)/shard_map/pallas_call | solution.py:1373
  337.2 0.0 copy-done.2
  337.2 0.6 slice.44.refs_2_
  337.8 2.6 slice_bitcast_fusion
  340.3 43.2 %shard_map.161 = (f32[16,128]{1,0:T(8,128)}, f32[2,96,1024]{2,1,0:T(8,128)}, bf16[2,64,1024]{2,1,0:T(8,128)(2,1)}, f32[2,64,1024]{2,1,0:T(8,128)}) custom-call(f32[8,1024]{1,0:T(8,128)} %get-tuple-element.111.refs_0_, f32[8,1024]{1,0:T(8,128)} %get-tuple-element.112.refs_1_, f32[6,1024]{1,0:T(8,128)} %slice.44.refs_2_, f32[8,256]{1,0:T(8,128)} %get-tuple-element.114.refs_3_, ...), custom_call_target="tpu_custom_call" | custom-call | tf_op jit(solution)/shard_map/pallas_call | solution.py:839
  383.5 0.0 copy-start.1
  383.5 0.0 copy-start
  383.6 1.3 slice.55
  384.8 0.7 slice_bitcast_fusion.3
  385.5 0.6 copy.17
  386.1 1.6 fusion.11
  387.7 1.9 fusion.10
  389.6 0.7 maximum_bitcast_fusion
  390.3 0.0 copy-done.1
  390.3 0.7 copy.20
  391.0 0.0 copy-done
  391.0 0.8 copy.21
Async XLA Ops:
  323.6 13.5 %copy-start.2 = (f32[8,1024]{1,0:T(8,128)S(1)}, f32[8,1024]{1,0:T(8,128)}, u32[]{:S(2)}) copy-start(f32[8,1024]{1,0:T(8,128)} %get-tuple-element.113.refs_5_) | copy-start | bytes 98308
  383.5 6.7 %copy-start.1 = (bf16[2,64,1024]{2,1,0:T(8,128)(2,1)S(1)}, bf16[2,64,1024]{2,1,0:T(8,128)(2,1)}, u32[]{:S(2)}) copy-start(bf16[2,64,1024]{2,1,0:T(8,128)(2,1)} %get-tuple-element.128) | copy-start | bytes 786436
  383.5 7.4 %copy-start = (f32[2,64,1024]{2,1,0:T(8,128)S(1)}, f32[2,64,1024]{2,1,0:T(8,128)}, u32[]{:S(2)}) copy-start(f32[2,64,1024]{2,1,0:T(8,128)} %get-tuple-element.129) | copy-start | bytes 1572868

commit v8 on v7

--- a/solution.py
+++ b/solution.py
@@ -708,9 +708,12 @@
     refs = list(refs)
     take = lambda count: [refs.pop(0) for _ in range(count)]
     sums = [take(5), take(5)]
-    grads, summed_last = take(6), take(1)[0]
+    grad_qkv, *grads = take(4)
+    grads = [grad_qkv.at[which] for which in range(3)] + grads
+    summed_last = take(1)[0]
     extras = take(4)
-    small_out, packed_out = take(2)
+    small_out, qkv_out, *matrix_outs = take(5)
+    targets = [qkv_out.at[which] for which in range(3)] + matrix_outs
     extra_outs = take(2)
     small_in, small_rows, vector_own, vector_parts, summed = take(5)
     extra_sends = take(2)
@@ -804,19 +807,28 @@
         vector_copies.append(copy)
     first_layer.finish(summed.at[0])
     handed.wait()
-    result = pltpu.make_async_remote_copy(
-        src_ref=summed.at[1 - section],
-        dst_ref=packed_out.at[section],
-        send_sem=result_send,
-        recv_sem=result_recv,
-        device_id=other,
-        device_id_type=MESH,
-    )
-    result.start()
-    own_result = pltpu.make_async_copy(summed.at[section], packed_out.at[section], result_local)
-    own_result.start()
-    own_result.wait()
-    result.wait()
+    half = depth // 2
+    mine = half_of(section, half)
+    results = []
+    for i, (row, column, columns) in enumerate(half_places(half, qkv_out.shape[2], summed.shape[2])):
+        area = (pl.ds(row, half), pl.ds(column, columns))
+        copy = pltpu.make_async_remote_copy(
+            src_ref=summed.at[(1 - section,) + area],
+            dst_ref=targets[i].at[mine],
+            send_sem=result_send.at[i],
+            recv_sem=result_recv.at[i],
+            device_id=other,
+            device_id_type=MESH,
+        )
+        copy.start()
+        results.append(copy)
+        copy = pltpu.make_async_copy(
+            summed.at[(section,) + area], targets[i].at[mine], result_local.at[i]
+        )
+        copy.start()
+        results.append(copy)
+    for copy in results:
+        copy.wait()
     for copy in vector_copies:
         copy.wait()
     total = vector_parts[0]
@@ -840,11 +852,12 @@
         final_kernel,
         out_shape=[
             jax.ShapeDtypeStruct((SMALL, 128), F32),
-            jax.ShapeDtypeStruct((2, HALF_ROWS, hidden), F32),
+            jax.ShapeDtypeStruct((3,) + grads[1].shape[2:], F32),
         ]
+        + [jax.ShapeDtypeStruct(value.shape[2:], F32) for value in grads[1:]]
         + [jax.ShapeDtypeStruct((2,) + value.shape, value.dtype) for value in extras[::2]],
         in_specs=[vmem_spec()] * len(sums) + [any_spec()] * (len(grads) + 1) + [vmem_spec()] * extra,
-        out_specs=[vmem_spec()] * 4,
+        out_specs=[vmem_spec()] * 7,
         scratch_shapes=[
             pltpu.VMEM((RING, RING, 2 * SMALL, 128), F32),
             pltpu.VMEM((2 * SMALL, width), F32),
@@ -860,9 +873,9 @@
             pltpu.SemaphoreType.DMA((RING,)),
             pltpu.SemaphoreType.DMA((extra,)),
             pltpu.SemaphoreType.DMA((extra,)),
-            pltpu.SemaphoreType.DMA,
-            pltpu.SemaphoreType.DMA,
-            pltpu.SemaphoreType.DMA,
+            pltpu.SemaphoreType.DMA((6,)),
+            pltpu.SemaphoreType.DMA((6,)),
+            pltpu.SemaphoreType.DMA((6,)),
             pltpu.SemaphoreType.DMA,
         ],
         compiler_params=comm_params(cid),
@@ -976,21 +989,21 @@
     ring.near()
     for i in ring.every:
         ring.relay(i, 0)
-        ring.other(i, 0)
-    attend_all(2, lambda t: (t * 0, side(t)))
     for i in ring.every:
         ring.far(i)
-    attend_all(2, lambda t: (side(t), t * 0))
+        ring.other(i, 0)
+    attend_all(4, lambda t: (side(t) * (t // 2), side(t) * (1 - t // 2)))
     for i in ring.every:
         ring.relay(i, MINUS)
         ring.relay(i, PLUS)
     for i in ring.every:
         ring.other(i, MINUS)
         ring.other(i, PLUS)
-    attend_all(4, lambda t: (side(t // 2), side(t)))
+    attend_all(2, lambda t: (t * 0 + PLUS, side(t)))
     for i in ring.every:
         ring.relay(i, FAR)
         ring.relayed[i, 0].wait_recv()
+    attend_all(2, lambda t: (t * 0 + MINUS, side(t)))
     attend_all(2, lambda t: (2 * t, 2 - 2 * t))
     for i in ring.every:
         ring.other(i, FAR)
@@ -1136,9 +1149,10 @@
     values.join()
     for j in (FAR, PLUS, MINUS):
         keys.join_one(j)
-    attend_all(1, 4, lambda t: (t * 0, step(t, FAR)))
+    attend_all(0, 2, lambda t: (t * 0, 1 + 2 * t))
     keys.send_direct(0)
     keys.join_one(0)
+    attend_all(0, 1, lambda t: (t, t))
     values.turn()
     keys.turn()
     values.join_two()
@@ -1623,24 +1637,19 @@
         [close.sums_last, middle.sums_middle, middle.sums_last[2:], attend_first, middle.bias_grad],
         [middle.sums_last, last.sums_middle, last.sums_end, attend_last, last.bias_grad],
     ]
-    grads = [close.grad_qkv[which] for which in range(3)]
-    grads += [close.grad_out, middle.grad_up, middle.grad_down]
+    grads = [close.grad_qkv, close.grad_out, middle.grad_up, middle.grad_down]
     first_grad = input_grad
 
-    small_sum, packed_sum, out_pair, grad_pair = final_call(
+    small_sum, sum_qkv, sum_out, sum_up, sum_down, out_pair, grad_pair = final_call(
         10, sums[0] + sums[1], grads, middle.summed, [outputs, between, last_grad, first_grad]
     )
-    half = depth // 2
-    columns = lambda which: packed_sum[
-        :, :half, which * local_width : (which + 1) * local_width
-    ].reshape(depth, local_width)
     return (
         out_pair[None],
         grad_pair[None],
-        jnp.stack([columns(0), columns(1), columns(2)])[None],
-        columns(3)[None],
-        packed_sum[:, half : 2 * half].reshape(1, depth, local_hidden),
-        packed_sum[:, 2 * half :].reshape(1, depth, local_hidden),
+        sum_qkv[None],
+        sum_out[None],
+        sum_up[None],
+        sum_down[None],
         small_sum[:13, :depth][None],
         small_sum[13:14, :depth],
     )

time: 398 us -> 397 us (level)
    unnamed x9 -> x13, local copies, waits for them, and re-layouts: 2.11 us -> 8.66 us
where the time goes in v8:
time: 397 us; the launch traced here: 391 us
  Pallas kernels  377 us (95%)
  local copies, waits for them, and re-layouts  11.2 us (3%)
    pallas_call x4, Pallas kernels, chain_call(): pl.pallas_call(kernel, out_shape=[jax.ShapeDtypeStruct(shape, dtype) for...  145 us
    pallas_call x2, Pallas kernels, attend_call(): pl.pallas_call(functools.partial(attend_kernel, layer), out_shape=[jax.Sh...  74.5 us
    pallas_call x2, Pallas kernels, attend_back_call(): pl.pallas_call(attend_back_kernel, out_shape=[jax.ShapeDtypeStruct((3, gr...  73.8 us
    pallas_call x1, Pallas kernels, final_call(): pl.pallas_call(final_kernel, out_shape=[jax.ShapeDtypeStruct((SMALL, 128)...  41.9 us
    pallas_call x1, Pallas kernels, first_call(): pl.pallas_call(first_kernel, out_shape=[jax.ShapeDtypeStruct((2, RING, RI...  41.4 us
    unnamed x13, local copies, waits for them, and re-layouts  8.66 us

profile of v8, /device:TPU:1, one launch (start us, length us, event | category | flops | bytes accessed | tf_op | source)
XLA Modules:
  0.0 390.9 jit_solution(9387532854989941727)
XLA Ops:
  0.6 0.8 fusion.9
  1.4 1.3 fusion.8.small_in
  2.7 41.4 %shard_map.152 = (bf16[2,4,4,96,1024]{4,3,2,1,0:T(8,128)(2,1)}, bf16[2,96,1024]{2,1,0:T(8,128)(2,1)}, f32[2,16,1024]{2,1,0:T(8,128)}, bf16[4,64,1024]{2,1,0:T(8,...) custom-call(bf16[2,64,1024]{2,1,0:T(8,128)(2,1)} %tokens_in.1, ...), custom_call_target="tpu_custom_call" | custom-call | tf_op jit(solution)/shard_map/pallas_call | solution.py:420
  44.2 38.2 %shard_map.153 = (bf16[256,256]{1,0:T(8,128)(2,1)}, bf16[4,4,256,256]{3,2,1,0:T(8,128)(2,1)}, bf16[4,4,256,256]{3,2,1,0:T(8,128)(2,1)}, bf16[256,256]{1,0:T(8,12...) custom-call(bf16[256,1024]{1,0:T(8,128)(2,1)} %bitcast.17, ...), custom_call_target="tpu_custom_call" | custom-call | tf_op jit(solution)/shard_map/pallas_call | solution.py:1041
  82.3 35.6 %shard_map.154 = (f32[64,1024]{1,0:T(8,128)}, f32[64,1024]{1,0:T(8,128)}, bf16[4,64,1024]{2,1,0:T(8,128)(2,1)}, bf16[4,64,1024]{2,1,0:T(8,128)(2,1)}, f32[4,64,1...) custom-call(bf16[2,4,4,96,1024]{4,3,2,1,0:T(8,128)(2,1)} %get-tuple-, ...), custom_call_target="tpu_custom_call" | custom-call | tf_op jit(solution)/shard_map/pallas_call | solution.py:1387
  118.0 36.3 %shard_map.155 = (bf16[256,256]{1,0:T(8,128)(2,1)}, bf16[4,4,256,256]{3,2,1,0:T(8,128)(2,1)}, bf16[4,4,256,256]{3,2,1,0:T(8,128)(2,1)}, bf16[256,256]{1,0:T(8,12...) custom-call(bf16[256,1024]{1,0:T(8,128)(2,1)} %bitcast.18, ...), custom_call_target="tpu_custom_call" | custom-call | tf_op jit(solution)/shard_map/pallas_call | solution.py:1041
  154.3 44.7 %shard_map.156 = (bf16[64,1024]{1,0:T(8,128)(2,1)}, f32[8,1024]{1,0:T(8,128)}, f32[64,1024]{1,0:T(8,128)}, f32[8,1024]{1,0:T(8,128)}, bf16[4,64,1024]{2,1,0:T(8,...) custom-call(bf16[2,4,4,96,1024]{4,3,2,1,0:T(8,128)(2,1)} %get-tuple-element.81.pack, ...), custom_call_target="tpu_custom_call" | custom-call | tf_op jit(solution)/shard_map/pallas_call | solution.py:1387
  199.0 34.9 %shard_map.157 = (bf16[3,256,256]{2,1,0:T(8,128)(2,1)}, f32[8,256]{1,0:T(8,128)}, bf16[4,64,1024]{2,1,0:T(8,128)(2,1)}) custom-call(bf16[256,1024]{1,0:T(8,128)(2,1)} %bitcast.20, bf16[2,4,4,96,1024]{4,3,2,1,0:T(8,128)(2,1)} %get-tuple-element.81.packed_any.refs_0_, bf16[256,256]{1,0:T(8,128)(2,1)} %get-tuple-element.87.q_ref, ...), custom_call_target="tpu_custom_call" | custom-call | tf_op jit(solution)/shard_map/pallas_call | solution.py:1183
  233.8 51.5 %shard_map.158 = (f32[96,1024]{1,0:T(8,128)}, f32[64,1024]{1,0:T(8,128)}, f32[8,1024]{1,0:T(8,128)}, f32[64,1024]{1,0:T(8,128)}, f32[8,1024]{1,0:T(8,128)}, /*in...) custom-call(bf16[2,4,4,96,1024]{4,3,2,1,0:T(8,128)(2,1)} %get-tuple-, ...), custom_call_target="tpu_custom_call" | custom-call | tf_op jit(solution)/shard_map/pallas_call | solution.py:1387
  285.3 39.0 %shard_map.159 = (bf16[3,256,256]{2,1,0:T(8,128)(2,1)}, f32[8,256]{1,0:T(8,128)}, bf16[4,64,1024]{2,1,0:T(8,128)(2,1)}) custom-call(bf16[256,1024]{1,0:T(8,128)(2,1)} %bitcast.19, bf16[2,4,4,96,1024]{4,3,2,1,0:T(8,128)(2,1)} %get-tuple-element.73.packed_any.refs_0_, bf16[256,256]{1,0:T(8,128)(2,1)} %get-tuple-element.105.q_ref, ...), custom_call_target="tpu_custom_call" | custom-call | tf_op jit(solution)/shard_map/pallas_call | solution.py:1183
  324.3 0.0 copy-start.2
  324.3 13.3 %shard_map.160 = (f32[64,1024]{1,0:T(8,128)}, f32[8,1024]{1,0:T(8,128)}, bf16[4,4,64,256]{3,2,1,0:T(8,128)(2,1)}, bf16[3,4,4,64,256]{4,3,2,1,0:T(8,128)(2,1)}) custom-call(bf16[4,64,1024]{2,1,0:T(8,128)(2,1)} %get-tuple-element.110.refs_0_, f32[64,1024]{1,0:T(8,128)} %get-tuple-element.111.refs_1_, bf16[64,1024]{1,0:T(8,128)(2,1)} %get-tuple-element.79.refs_2_, ...), custom_call_target="tpu_custom_call" | custom-call | tf_op jit(solution)/shard_map/pallas_call | solution.py:1387
  337.6 0.0 copy-done.2
  337.6 0.6 slice.17.refs_2_
  338.2 41.9 %shard_map.161 = (f32[16,128]{1,0:T(8,128)}, f32[3,64,256]{2,1,0:T(8,128)}, f32[64,256]{1,0:T(8,128)}, f32[64,1024]{1,0:T(8,128)}, f32[64,1024]{1,0:T(8,128)}, /...) custom-call(f32[8,1024]{1,0:T(8,128)} %get-tuple-element.114.refs_0_, f32[8,1024]{1,0:T(8,128)} %get-tuple-element.115.refs_1_, ...), custom_call_target="tpu_custom_call" | custom-call | tf_op jit(solution)/shard_map/pallas_call | solution.py:851
  380.1 0.0 copy-start.1
  380.1 0.0 copy-start
  380.1 1.2 slice.19
  381.4 0.7 slice_bitcast_fusion
  382.1 0.6 copy.17
  382.7 1.7 copy.24
  384.3 1.9 copy.25
  386.2 1.6 copy.26
  387.8 1.5 copy.27
  389.3 0.0 copy-done.1
  389.3 0.7 copy.28
  390.0 0.0 copy-done
  390.0 0.7 copy.29
Async XLA Ops:
  324.3 13.3 %copy-start.2 = (f32[8,1024]{1,0:T(8,128)S(1)}, f32[8,1024]{1,0:T(8,128)}, u32[]{:S(2)}) copy-start(f32[8,1024]{1,0:T(8,128)} %get-tuple-element.116.refs_5_) | copy-start | bytes 98308
  380.1 9.2 %copy-start.1 = (f32[64,1024]{1,0:T(8,128)S(1)}, f32[64,1024]{1,0:T(8,128)}, u32[]{:S(2)}) copy-start(f32[64,1024]{1,0:T(8,128)} %get-tuple-element.135) | copy-start | bytes 786436
  380.1 9.9 %copy-start = (f32[64,1024]{1,0:T(8,128)S(1)}, f32[64,1024]{1,0:T(8,128)}, u32[]{:S(2)}) copy-start(f32[64,1024]{1,0:T(8,128)} %get-tuple-element.136) | copy-start | bytes 786436

commit v9 on v8

--- a/solution.py
+++ b/solution.py
@@ -601,6 +601,7 @@
     def __init__(self, grads, buffers, semaphores, y, z, section, push):
         self.grads, self.buffers, self.y, self.z = grads, buffers, y, z
         self.section, self.push = section, push
+        self.keeps, self.swaps, self.parts = {}, {}, {}
         self.swap_send, self.swap_recv, self.keep_local = semaphores
         depth, width = grads[0].shape[2:]
         hidden = grads[5].shape[3]
@@ -612,63 +613,59 @@
         piece, row, column, columns = place
         return self.buffers[piece][which].at[:, :, pl.ds(row, self.half), pl.ds(column, columns)]
 
-    def keep(self):
+    def keep(self, piece):
         mine = half_of(self.section, self.half)
-        self.keeps = []
         for i, place in enumerate(self.places):
-            copy = pltpu.make_async_copy(
-                self.grads[i].at[:, :, mine], self.region(0, place), self.keep_local.at[i]
-            )
-            copy.start()
-            self.keeps.append(copy)
-
-    def swap(self):
+            if place[0] == piece:
+                self.keeps[i] = pltpu.make_async_copy(
+                    self.grads[i].at[:, :, mine], self.region(0, place), self.keep_local.at[i]
+                )
+                self.keeps[i].start()
+
+    def swap(self, piece):
         others = half_of(1 - self.section, self.half)
-        self.swaps = []
         for i, place in enumerate(self.places):
-            copy = pltpu.make_async_remote_copy(
-                src_ref=self.grads[i].at[:, :, others],
-                dst_ref=self.region(1, place),
-                send_sem=self.swap_send.at[i],
-                recv_sem=self.swap_recv.at[i],
-                device_id={"section": 1 - self.section},
-                device_id_type=MESH,
-            )
-            copy.start()
-            self.swaps.append(copy)
-
-    def begin(self):
-        self.parts = []
-        for piece in range(2):
-            for i, place in enumerate(self.places):
-                if place[0] == piece:
-                    self.keeps[i].wait()
-                    self.swaps[i].wait_recv()
-            own, sibling = self.buffers[piece][:2]
-            add_blocks(own, own, sibling)
-            self.parts.append(
-                Scatter(piece, piece == 0, own, self.buffers[piece][2:], self.y, self.z, self.push)
-            )
-            self.parts[piece].begin()
+            if place[0] == piece:
+                self.swaps[i] = pltpu.make_async_remote_copy(
+                    src_ref=self.grads[i].at[:, :, others],
+                    dst_ref=self.region(1, place),
+                    send_sem=self.swap_send.at[i],
+                    recv_sem=self.swap_recv.at[i],
+                    device_id={"section": 1 - self.section},
+                    device_id_type=MESH,
+                )
+                self.swaps[i].start()
+
+    def begin(self, piece):
+        for i, place in enumerate(self.places):
+            if place[0] == piece:
+                self.keeps[i].wait()
+                self.swaps[i].wait_recv()
+        own, sibling = self.buffers[piece][:2]
+        add_blocks(own, own, sibling)
+        self.parts[piece] = Scatter(
+            piece, piece == 0, own, self.buffers[piece][2:], self.y, self.z, self.push
+        )
+        self.parts[piece].begin()
 
     def join(self):
-        for part in self.parts:
-            part.join()
+        for piece in (1, 0):
+            self.parts[piece].join()
 
     def turn(self):
-        for part in self.parts:
-            part.turn()
+        for piece in (1, 0):
+            self.parts[piece].turn()
 
     def join_two(self):
-        for part in self.parts:
-            part.join_two()
+        for piece in (1, 0):
+            self.parts[piece].join_two()
 
     def finish(self, out):
         self.parts[0].finish(out.at[pl.ds(0, self.half)])
         self.parts[1].finish(out.at[pl.ds(self.half, 2 * self.half)])
 
     def end(self):
-        for copy in self.swaps:
+        for copy in self.swaps.values():
             copy.wait_send()
 
     @staticmethod
@@ -731,7 +728,8 @@
     started = []
     first_layer = layer_gradients(grads, layer_scratch, y, z, section, started)
     push = first_layer.push
-    first_layer.keep()
+    first_layer.keep(1)
+    first_layer.keep(0)
     handed = pltpu.make_async_copy(summed_last, summed.at[1], hand_local)
     handed.start()
     depth = grads[0].shape[2]
@@ -765,7 +763,8 @@
             :, number * depth : (number + 1) * depth
         ]
     pl.semaphore_wait(barrier, count)
-    first_layer.swap()
+    first_layer.swap(1)
+    first_layer.swap(0)
     small_swap = push(2, 6, 0, small_in.at[:, :, half_of(1 - section, SMALL)], small_buffers[1], other)
     extra_copies = []
     for i in range(2):
@@ -780,7 +779,8 @@
         copy.start()
         extra_copies.append(copy)
 
-    first_layer.begin()
+    first_layer.begin(1)
+    first_layer.begin(0)
     small_swap.wait_recv()
     add_blocks(small_buffers[0], small_in.at[:, :, half_of(section, SMALL)], small_buffers[1])
     small_part = Scatter(2, True, small_buffers[0], small_buffers[2:], y, z, push)
@@ -1473,14 +1473,17 @@
     def swap():
         for work in attention_products(env):
             work()
-        layer.keep()
-        layer.swap()
-
+        layer.keep(0)
+        layer.swap(0)
+        layer.begin(1)
+
+    layer.swap(1)
+    layer.keep(1)
     rings[0].reduce(env.part)
     rings[0].run(
         env.part, back_end_rows_last, [env.hidden_grad_in, env.inputs, env.mlp_out],
         [env.vectors.at[1], env.vectors.at[0]], [env.input_grad], env.sums_last, env.mlp_rows,
-        [swap, layer.begin],
+        [swap, lambda: layer.begin(0)],
     )
     for copy in loads:
         copy.wait()

time: 397 us -> 393 us (0.990)
  Pallas kernels: 377 us -> 373 us
    pallas_call x4, Pallas kernels: 145 us -> 140 us  [chain_call(): pl.pallas_call(kernel, out_shape=[jax.ShapeDtypeStruct(shape, dtype) for...]
where the time goes in v9:
time: 393 us; the launch traced here: 387 us
  Pallas kernels  373 us (95%)
  local copies, waits for them, and re-layouts  11.2 us (3%)
    pallas_call x4, Pallas kernels, chain_call(): pl.pallas_call(kernel, out_shape=[jax.ShapeDtypeStruct(shape, dtype) for...  140 us
    pallas_call x2, Pallas kernels, attend_call(): pl.pallas_call(functools.partial(attend_kernel, layer), out_shape=[jax.Sh...  74.5 us
    pallas_call x2, Pallas kernels, attend_back_call(): pl.pallas_call(attend_back_kernel, out_shape=[jax.ShapeDtypeStruct((3, gr...  71 us
    pallas_call x1, Pallas kernels, final_call(): pl.pallas_call(final_kernel, out_shape=[jax.ShapeDtypeStruct((SMALL, 128)...  45.7 us
    pallas_call x1, Pallas kernels, first_call(): pl.pallas_call(first_kernel, out_shape=[jax.ShapeDtypeStruct((2, RING, RI...  41.4 us
    unnamed x13, local copies, waits for them, and re-layouts  8.66 us

profile of v9, /device:TPU:1, one launch (start us, length us, event | category | flops | bytes accessed | tf_op | source)
XLA Modules:
  0.0 387.1 jit_solution(17950471710641869810)
XLA Ops:
  0.6 0.8 fusion.9
  1.4 1.3 fusion.8.small_in
  2.7 41.4 %shard_map.152 = (bf16[2,4,4,96,1024]{4,3,2,1,0:T(8,128)(2,1)}, bf16[2,96,1024]{2,1,0:T(8,128)(2,1)}, f32[2,16,1024]{2,1,0:T(8,128)}, bf16[4,64,1024]{2,1,0:T(8,...) custom-call(bf16[2,64,1024]{2,1,0:T(8,128)(2,1)} %tokens_in.1, ...), custom_call_target="tpu_custom_call" | custom-call | tf_op jit(solution)/shard_map/pallas_call | solution.py:420
  44.2 38.2 %shard_map.153 = (bf16[256,256]{1,0:T(8,128)(2,1)}, bf16[4,4,256,256]{3,2,1,0:T(8,128)(2,1)}, bf16[4,4,256,256]{3,2,1,0:T(8,128)(2,1)}, bf16[256,256]{1,0:T(8,12...) custom-call(bf16[256,1024]{1,0:T(8,128)(2,1)} %bitcast.17, ...), custom_call_target="tpu_custom_call" | custom-call | tf_op jit(solution)/shard_map/pallas_call | solution.py:1041
  82.3 35.6 %shard_map.154 = (f32[64,1024]{1,0:T(8,128)}, f32[64,1024]{1,0:T(8,128)}, bf16[4,64,1024]{2,1,0:T(8,128)(2,1)}, bf16[4,64,1024]{2,1,0:T(8,128)(2,1)}, f32[4,64,1...) custom-call(bf16[2,4,4,96,1024]{4,3,2,1,0:T(8,128)(2,1)} %get-tuple-, ...), custom_call_target="tpu_custom_call" | custom-call | tf_op jit(solution)/shard_map/pallas_call | solution.py:1387
  118.0 36.3 %shard_map.155 = (bf16[256,256]{1,0:T(8,128)(2,1)}, bf16[4,4,256,256]{3,2,1,0:T(8,128)(2,1)}, bf16[4,4,256,256]{3,2,1,0:T(8,128)(2,1)}, bf16[256,256]{1,0:T(8,12...) custom-call(bf16[256,1024]{1,0:T(8,128)(2,1)} %bitcast.18, ...), custom_call_target="tpu_custom_call" | custom-call | tf_op jit(solution)/shard_map/pallas_call | solution.py:1041
  154.3 44.7 %shard_map.156 = (bf16[64,1024]{1,0:T(8,128)(2,1)}, f32[8,1024]{1,0:T(8,128)}, f32[64,1024]{1,0:T(8,128)}, f32[8,1024]{1,0:T(8,128)}, bf16[4,64,1024]{2,1,0:T(8,...) custom-call(bf16[2,4,4,96,1024]{4,3,2,1,0:T(8,128)(2,1)} %get-tuple-element.81.pack, ...), custom_call_target="tpu_custom_call" | custom-call | tf_op jit(solution)/shard_map/pallas_call | solution.py:1387
  199.0 34.9 %shard_map.157 = (bf16[3,256,256]{2,1,0:T(8,128)(2,1)}, f32[8,256]{1,0:T(8,128)}, bf16[4,64,1024]{2,1,0:T(8,128)(2,1)}) custom-call(bf16[256,1024]{1,0:T(8,128)(2,1)} %bitcast.20, bf16[2,4,4,96,1024]{4,3,2,1,0:T(8,128)(2,1)} %get-tuple-element.81.packed_any.refs_0_, bf16[256,256]{1,0:T(8,128)(2,1)} %get-tuple-element.87.q_ref, ...), custom_call_target="tpu_custom_call" | custom-call | tf_op jit(solution)/shard_map/pallas_call | solution.py:1183
  233.8 46.7 %shard_map.158 = (f32[96,1024]{1,0:T(8,128)}, f32[64,1024]{1,0:T(8,128)}, f32[8,1024]{1,0:T(8,128)}, f32[64,1024]{1,0:T(8,128)}, f32[8,1024]{1,0:T(8,128)}, /*in...) custom-call(bf16[2,4,4,96,1024]{4,3,2,1,0:T(8,128)(2,1)} %get-tuple-, ...), custom_call_target="tpu_custom_call" | custom-call | tf_op jit(solution)/shard_map/pallas_call | solution.py:1387
  280.5 36.1 %shard_map.159 = (bf16[3,256,256]{2,1,0:T(8,128)(2,1)}, f32[8,256]{1,0:T(8,128)}, bf16[4,64,1024]{2,1,0:T(8,128)(2,1)}) custom-call(bf16[256,1024]{1,0:T(8,128)(2,1)} %bitcast.19, bf16[2,4,4,96,1024]{4,3,2,1,0:T(8,128)(2,1)} %get-tuple-element.73.packed_any.refs_0_, bf16[256,256]{1,0:T(8,128)(2,1)} %get-tuple-element.105.q_ref, ...), custom_call_target="tpu_custom_call" | custom-call | tf_op jit(solution)/shard_map/pallas_call | solution.py:1183
  316.6 0.0 copy-start.2
  316.7 13.2 %shard_map.160 = (f32[64,1024]{1,0:T(8,128)}, f32[8,1024]{1,0:T(8,128)}, bf16[4,4,64,256]{3,2,1,0:T(8,128)(2,1)}, bf16[3,4,4,64,256]{4,3,2,1,0:T(8,128)(2,1)}) custom-call(bf16[4,64,1024]{2,1,0:T(8,128)(2,1)} %get-tuple-element.110.refs_0_, f32[64,1024]{1,0:T(8,128)} %get-tuple-element.111.refs_1_, bf16[64,1024]{1,0:T(8,128)(2,1)} %get-tuple-element.79.refs_2_, ...), custom_call_target="tpu_custom_call" | custom-call | tf_op jit(solution)/shard_map/pallas_call | solution.py:1387
  329.9 0.0 copy-done.2
  329.9 0.6 slice.17.refs_2_
  330.5 45.7 %shard_map.161 = (f32[16,128]{1,0:T(8,128)}, f32[3,64,256]{2,1,0:T(8,128)}, f32[64,256]{1,0:T(8,128)}, f32[64,1024]{1,0:T(8,128)}, f32[64,1024]{1,0:T(8,128)}, /...) custom-call(f32[8,1024]{1,0:T(8,128)} %get-tuple-element.114.refs_0_, f32[8,1024]{1,0:T(8,128)} %get-tuple-element.115.refs_1_, ...), custom_call_target="tpu_custom_call" | custom-call | tf_op jit(solution)/shard_map/pallas_call | solution.py:851
  376.3 0.0 copy-start.1
  376.3 0.0 copy-start
  376.3 1.2 slice.19
  377.5 0.7 slice_bitcast_fusion
  378.2 0.6 copy.17
  378.8 1.7 copy.24
  380.5 1.9 copy.25
  382.4 1.6 copy.26
  384.0 1.5 copy.27
  385.5 0.0 copy-done.1
  385.5 0.7 copy.28
  386.2 0.0 copy-done
  386.2 0.7 copy.29
Async XLA Ops:
  316.6 13.3 %copy-start.2 = (f32[8,1024]{1,0:T(8,128)S(1)}, f32[8,1024]{1,0:T(8,128)}, u32[]{:S(2)}) copy-start(f32[8,1024]{1,0:T(8,128)} %get-tuple-element.116.refs_5_) | copy-start | bytes 98308
  376.3 9.2 %copy-start.1 = (f32[64,1024]{1,0:T(8,128)S(1)}, f32[64,1024]{1,0:T(8,128)}, u32[]{:S(2)}) copy-start(f32[64,1024]{1,0:T(8,128)} %get-tuple-element.135) | copy-start | bytes 786436
  376.3 9.9 %copy-start = (f32[64,1024]{1,0:T(8,128)S(1)}, f32[64,1024]{1,0:T(8,128)}, u32[]{:S(2)}) copy-start(f32[64,1024]{1,0:T(8,128)} %get-tuple-element.136) | copy-start | bytes 786436

commit v10 on v9

--- a/solution.py
+++ b/solution.py
@@ -1410,9 +1410,8 @@
     rings[0].reduce(env.part)
     rings[0].run(
         env.part, middle_rows, [env.inputs], [env.vectors.at[0]],
-        [env.attn_out, env.hidden], None, env.normed, [begin, near],
-    )
-    middle()
+        [env.attn_out, env.hidden], None, env.normed, [begin, near, middle],
+    )
     for copy in loads:
         copy.wait()
     mlp_forward(

time: 393 us -> 393 us (level)
  no operation moved by 1% of the time
where the time goes in v10:
time: 393 us; the launch traced here: 387 us
  Pallas kernels  373 us (95%)
  local copies, waits for them, and re-layouts  11.2 us (3%)
    pallas_call x4, Pallas kernels, chain_call(): pl.pallas_call(kernel, out_shape=[jax.ShapeDtypeStruct(shape, dtype) for...  141 us
    pallas_call x2, Pallas kernels, attend_call(): pl.pallas_call(functools.partial(attend_kernel, layer), out_shape=[jax.Sh...  74.1 us
    pallas_call x2, Pallas kernels, attend_back_call(): pl.pallas_call(attend_back_kernel, out_shape=[jax.ShapeDtypeStruct((3, gr...  70.8 us
    pallas_call x1, Pallas kernels, final_call(): pl.pallas_call(final_kernel, out_shape=[jax.ShapeDtypeStruct((SMALL, 128)...  45.5 us
    pallas_call x1, Pallas kernels, first_call(): pl.pallas_call(first_kernel, out_shape=[jax.ShapeDtypeStruct((2, RING, RI...  41.4 us
    unnamed x13, local copies, waits for them, and re-layouts  8.66 us

profile of v10, /device:TPU:1, one launch (start us, length us, event | category | flops | bytes accessed | tf_op | source)
XLA Modules:
  0.0 386.9 jit_solution(6128325092563029871)
XLA Ops:
  0.6 0.8 fusion.9
  1.4 1.3 fusion.8.small_in
  2.7 41.4 %shard_map.152 = (bf16[2,4,4,96,1024]{4,3,2,1,0:T(8,128)(2,1)}, bf16[2,96,1024]{2,1,0:T(8,128)(2,1)}, f32[2,16,1024]{2,1,0:T(8,128)}, bf16[4,64,1024]{2,1,0:T(8,...) custom-call(bf16[2,64,1024]{2,1,0:T(8,128)(2,1)} %tokens_in.1, ...), custom_call_target="tpu_custom_call" | custom-call | tf_op jit(solution)/shard_map/pallas_call | solution.py:420
  44.2 38.2 %shard_map.153 = (bf16[256,256]{1,0:T(8,128)(2,1)}, bf16[4,4,256,256]{3,2,1,0:T(8,128)(2,1)}, bf16[4,4,256,256]{3,2,1,0:T(8,128)(2,1)}, bf16[256,256]{1,0:T(8,12...) custom-call(bf16[256,1024]{1,0:T(8,128)(2,1)} %bitcast.17, ...), custom_call_target="tpu_custom_call" | custom-call | tf_op jit(solution)/shard_map/pallas_call | solution.py:1041
  82.3 35.7 %shard_map.154 = (f32[64,1024]{1,0:T(8,128)}, f32[64,1024]{1,0:T(8,128)}, bf16[4,64,1024]{2,1,0:T(8,128)(2,1)}, bf16[4,64,1024]{2,1,0:T(8,128)(2,1)}, f32[4,64,1...) custom-call(bf16[2,4,4,96,1024]{4,3,2,1,0:T(8,128)(2,1)} %get-tuple-, ...), custom_call_target="tpu_custom_call" | custom-call | tf_op jit(solution)/shard_map/pallas_call | solution.py:1387
  118.0 35.9 %shard_map.155 = (bf16[256,256]{1,0:T(8,128)(2,1)}, bf16[4,4,256,256]{3,2,1,0:T(8,128)(2,1)}, bf16[4,4,256,256]{3,2,1,0:T(8,128)(2,1)}, bf16[256,256]{1,0:T(8,12...) custom-call(bf16[256,1024]{1,0:T(8,128)(2,1)} %bitcast.18, ...), custom_call_target="tpu_custom_call" | custom-call | tf_op jit(solution)/shard_map/pallas_call | solution.py:1041
  153.9 44.9 %shard_map.156 = (bf16[64,1024]{1,0:T(8,128)(2,1)}, f32[8,1024]{1,0:T(8,128)}, f32[64,1024]{1,0:T(8,128)}, f32[8,1024]{1,0:T(8,128)}, bf16[4,64,1024]{2,1,0:T(8,...) custom-call(bf16[2,4,4,96,1024]{4,3,2,1,0:T(8,128)(2,1)} %get-tuple-element.81.pack, ...), custom_call_target="tpu_custom_call" | custom-call | tf_op jit(solution)/shard_map/pallas_call | solution.py:1387
  198.8 34.9 %shard_map.157 = (bf16[3,256,256]{2,1,0:T(8,128)(2,1)}, f32[8,256]{1,0:T(8,128)}, bf16[4,64,1024]{2,1,0:T(8,128)(2,1)}) custom-call(bf16[256,1024]{1,0:T(8,128)(2,1)} %bitcast.20, bf16[2,4,4,96,1024]{4,3,2,1,0:T(8,128)(2,1)} %get-tuple-element.81.packed_any.refs_0_, bf16[256,256]{1,0:T(8,128)(2,1)} %get-tuple-element.87.q_ref, ...), custom_call_target="tpu_custom_call" | custom-call | tf_op jit(solution)/shard_map/pallas_call | solution.py:1183
  233.7 47.2 %shard_map.158 = (f32[96,1024]{1,0:T(8,128)}, f32[64,1024]{1,0:T(8,128)}, f32[8,1024]{1,0:T(8,128)}, f32[64,1024]{1,0:T(8,128)}, f32[8,1024]{1,0:T(8,128)}, /*in...) custom-call(bf16[2,4,4,96,1024]{4,3,2,1,0:T(8,128)(2,1)} %get-tuple-, ...), custom_call_target="tpu_custom_call" | custom-call | tf_op jit(solution)/shard_map/pallas_call | solution.py:1387
  280.9 35.8 %shard_map.159 = (bf16[3,256,256]{2,1,0:T(8,128)(2,1)}, f32[8,256]{1,0:T(8,128)}, bf16[4,64,1024]{2,1,0:T(8,128)(2,1)}) custom-call(bf16[256,1024]{1,0:T(8,128)(2,1)} %bitcast.19, bf16[2,4,4,96,1024]{4,3,2,1,0:T(8,128)(2,1)} %get-tuple-element.73.packed_any.refs_0_, bf16[256,256]{1,0:T(8,128)(2,1)} %get-tuple-element.105.q_ref, ...), custom_call_target="tpu_custom_call" | custom-call | tf_op jit(solution)/shard_map/pallas_call | solution.py:1183
  316.7 0.0 copy-start.2
  316.8 13.2 %shard_map.160 = (f32[64,1024]{1,0:T(8,128)}, f32[8,1024]{1,0:T(8,128)}, bf16[4,4,64,256]{3,2,1,0:T(8,128)(2,1)}, bf16[3,4,4,64,256]{4,3,2,1,0:T(8,128)(2,1)}) custom-call(bf16[4,64,1024]{2,1,0:T(8,128)(2,1)} %get-tuple-element.110.refs_0_, f32[64,1024]{1,0:T(8,128)} %get-tuple-element.111.refs_1_, bf16[64,1024]{1,0:T(8,128)(2,1)} %get-tuple-element.79.refs_2_, ...), custom_call_target="tpu_custom_call" | custom-call | tf_op jit(solution)/shard_map/pallas_call | solution.py:1387
  330.0 0.0 copy-done.2
  330.0 0.6 slice.17.refs_2_
  330.6 45.5 %shard_map.161 = (f32[16,128]{1,0:T(8,128)}, f32[3,64,256]{2,1,0:T(8,128)}, f32[64,256]{1,0:T(8,128)}, f32[64,1024]{1,0:T(8,128)}, f32[64,1024]{1,0:T(8,128)}, /...) custom-call(f32[8,1024]{1,0:T(8,128)} %get-tuple-element.114.refs_0_, f32[8,1024]{1,0:T(8,128)} %get-tuple-element.115.refs_1_, ...), custom_call_target="tpu_custom_call" | custom-call | tf_op jit(solution)/shard_map/pallas_call | solution.py:851
  376.1 0.0 copy-start.1
  376.1 0.0 copy-start
  376.1 1.2 slice.19
  377.4 0.7 slice_bitcast_fusion
  378.1 0.6 copy.17
  378.7 1.7 copy.24
  380.3 1.9 copy.25
  382.2 1.6 copy.26
  383.8 1.5 copy.27
  385.3 0.0 copy-done.1
  385.3 0.7 copy.28
  386.0 0.0 copy-done
  386.0 0.7 copy.29
Async XLA Ops:
  316.7 13.3 %copy-start.2 = (f32[8,1024]{1,0:T(8,128)S(1)}, f32[8,1024]{1,0:T(8,128)}, u32[]{:S(2)}) copy-start(f32[8,1024]{1,0:T(8,128)} %get-tuple-element.116.refs_5_) | copy-start | bytes 98308
  376.1 9.2 %copy-start.1 = (f32[64,1024]{1,0:T(8,128)S(1)}, f32[64,1024]{1,0:T(8,128)}, u32[]{:S(2)}) copy-start(f32[64,1024]{1,0:T(8,128)} %get-tuple-element.135) | copy-start | bytes 786436
  376.1 9.9 %copy-start = (f32[64,1024]{1,0:T(8,128)S(1)}, f32[64,1024]{1,0:T(8,128)}, u32[]{:S(2)}) copy-start(f32[64,1024]{1,0:T(8,128)} %get-tuple-element.136) | copy-start | bytes 786436
